TPU v7x, 32 devices: a whole 2x2x4 slice. The times are simulated.
32 devices in a mesh: dp: 16 (over z, y, x), tensor: 2 (over core).
Axes of the slice: x: 2, y: 2, z: 4, core: 2. Of those that a mesh axis runs over, the one named last changes fastest.
Arguments:
- tokens: bfloat16 [32768, 1024], P(('dp', 'tensor')), may hold values from -6 to 6
- block_ids: int32 [32, 1024], P('dp'), may hold values from 0 to 4, never falling along the last dimension, each value on 1 to 256 neighbouring positions
- memory_index: int32 [32768, 8, 32], P('dp', 'tensor'), may hold values from 0 to 16383
- memory_keys: bfloat16 [8, 16384, 128], P('tensor'), may hold values from -6 to 6
- memory_values: bfloat16 [8, 16384, 128], P('tensor'), may hold values from -6 to 6
- attn_gain: float32 [1024], replicated, may hold values from 0.5 to 1.5
- query_weight: bfloat16 [1024, 1024], P(None, 'tensor'), may hold values from -0.1875 to 0.1875
- key_weight: bfloat16 [1024, 1024], P(None, 'tensor'), may hold values from -0.1875 to 0.1875
- value_weight: bfloat16 [1024, 1024], P(None, 'tensor'), may hold values from -0.1875 to 0.1875
- output_weight: bfloat16 [1024, 1024], P('tensor'), may hold values from -1.5 to 1.5
- position_table: float32 [32, 8], P(None, 'tensor'), may hold values from -3 to 3
- memory_gate: float32 [8], P('tensor'), may hold values from -4 to 4
- mlp_gain: float32 [1024], replicated, may hold values from 0.5 to 1.5
- hidden_weight: bfloat16 [1024, 4096], P(None, 'tensor'), may hold values from -0.1875 to 0.1875
- return_weight: bfloat16 [4096, 1024], P('tensor'), may hold values from -0.09375 to 0.09375
- grad_output: bfloat16 [32768, 1024], P(('dp', 'tensor')), may hold values from -6 to 6
Outputs:
- layer_output: bfloat16 [32768, 1024], P(('dp', 'tensor'))
- tokens_grad: bfloat16 [32768, 1024], P(('dp', 'tensor'))
- attn_gain_grad: float32 [1024], replicated
- query_grad: float32 [1024, 1024], P(None, 'tensor')
- key_grad: float32 [1024, 1024], P(None, 'tensor')
- value_grad: float32 [1024, 1024], P(None, 'tensor')
- output_weight_grad: float32 [1024, 1024], P('tensor')
- table_grad: float32 [32, 8], P(None, 'tensor')
- gate_grad: float32 [8], P('tensor')
- mlp_gain_grad: float32 [1024], replicated
- hidden_grad: float32 [1024, 4096], P(None, 'tensor')
- return_grad: float32 [4096, 1024], P('tensor')
Inputs may be any that keep to these rules, and one draw needn't show every extreme that they name: `block_ids`: inside each sequence block numbers never fall; each of the 5 blocks holds 1 to 256 positions, one exactly 256.
All inputs are finite; a program needn't handle non-finite values.
Results may differ from a plain program's by a relative error of at most 0.023.
Values may be sent and summed in bfloat16 or wider, within the bound.
No kernel may reach another device: no remote copies, remote signals or barrier semaphores. Data moves between devices by JAX's collectives and lax.ppermute only.
A program may use at most 512 MiB of HBM per device.

v0:
```python
import jax
import jax.numpy as jnp
from jax import lax
from jax.sharding import PartitionSpec as P

eps_norm = 1e-06
far_steps = (12, 16, 23, 32, 46, 64, 91)
exact_mode = lax.Precision.HIGHEST


def bucket_of(relative):
    upper_half = jnp.where(relative > 0, 16, 0).astype(jnp.int32)
    distance = jnp.abs(relative)
    far_bucket = 8 + sum(((distance >= step_size).astype(jnp.int32) for step_size in far_steps))
    return upper_half + jnp.where(distance < 8, distance, far_bucket)


def rms_scaled(rows, gain):
    return rows * lax.rsqrt(jnp.mean(rows * rows, -1, keepdims=True) + eps_norm) * gain


def dot_rows(left, right):
    return jnp.dot(left, right, preferred_element_type=jnp.float32)


def dot_outer(left, right):
    return lax.dot_general(
        left, right, (((0,), (0,)), ((), ())), preferred_element_type=jnp.float32
    )


def dot_inner(left, right):
    return lax.dot_general(
        left, right, (((1,), (1,)), ((), ())), preferred_element_type=jnp.float32
    )


def bucket_table(seq_len):
    relative = jnp.arange(1 - seq_len, seq_len, dtype=jnp.int32)
    return (bucket_of(relative)[:, None] == jnp.arange(32, dtype=jnp.int32)[None, :]).astype(
        jnp.float32
    )


def toeplitz(column, seq_len):
    tiled = jnp.tile(column, seq_len + 1)
    flat = tiled[seq_len - 1 : seq_len - 1 + seq_len * (2 * seq_len - 2)]
    return flat.reshape(seq_len, 2 * seq_len - 2)[:, :seq_len]


def diagonal_sums(matrix, seq_len):
    flipped = matrix[::-1]
    padded = jnp.pad(flipped, ((0, 0), (0, seq_len)))
    flat = padded.reshape(-1)[: seq_len * (2 * seq_len - 1)].reshape(seq_len, 2 * seq_len - 1)
    return jnp.sum(flat, 0)


def to_pairs(rows, seq_count, head_count):
    seq_len = rows.shape[0] // seq_count
    return (
        rows.reshape(seq_count, seq_len, head_count, -1)
        .transpose(0, 2, 1, 3)
        .reshape(seq_count * head_count, seq_len, -1)
    )


def from_pairs(pairs, seq_count, head_count):
    seq_len = pairs.shape[1]
    return (
        pairs.reshape(seq_count, head_count, seq_len, -1)
        .transpose(0, 2, 1, 3)
        .reshape(seq_count * seq_len, -1)
    )


def block_scores(query_rows, key_pair, bias_rows, block_rows, block_all, score_scale):
    scores = dot_inner(query_rows, key_pair) * score_scale + bias_rows
    step_gap = block_rows[:, None] - block_all[None, :]
    allowed = (step_gap >= 0) & (step_gap <= 1)
    return jnp.where(allowed, scores, -jnp.inf)


def memory_lookup(query_rows, found_rows, score_scale):
    head_width = found_rows.shape[-1] // 2
    keys_found = found_rows[..., :head_width]
    values_found = found_rows[..., head_width:].astype(jnp.float32)
    memory_scores = (
        jnp.einsum("qd,qkd->qk", query_rows, keys_found, preferred_element_type=jnp.float32)
        * score_scale
    )
    row_top = jnp.max(memory_scores, -1, keepdims=True)
    exponent = jnp.exp(memory_scores - row_top)
    memory_weights = exponent / jnp.sum(exponent, -1, keepdims=True)
    memory_read = jnp.einsum("qk,qkd->qd", memory_weights, values_found, precision=exact_mode)
    return (memory_read, memory_weights, keys_found.astype(jnp.float32), values_found)


def forward_pair(pair_items, bias_mats, memory_table, score_scale):
    query_pair, key_pair, value_pair, index_pair, block_row, head_index = pair_items
    seq_len = query_pair.shape[0]
    step_rows = min(512, seq_len)
    bias_matrix = lax.dynamic_index_in_dim(bias_mats, head_index, 0, False)
    table_head = lax.dynamic_index_in_dim(memory_table, head_index, 0, False)
    found_pair = jnp.take(table_head, index_pair, axis=0)
    local_parts = []
    memory_parts = []
    lse_parts = []
    for row_start in range(0, seq_len, step_rows):
        row_stop = row_start + step_rows
        query_rows = query_pair[row_start:row_stop]
        scores = block_scores(
            query_rows,
            key_pair,
            bias_matrix[row_start:row_stop],
            block_row[row_start:row_stop],
            block_row,
            score_scale,
        )
        row_top = jnp.max(scores, -1, keepdims=True)
        exponent = jnp.exp(scores - row_top)
        row_total = jnp.sum(exponent, -1, keepdims=True)
        weights_low = (exponent / row_total).astype(jnp.bfloat16)
        local_parts.append(dot_rows(weights_low, value_pair))
        lse_parts.append(row_top[:, 0] + jnp.log(row_total[:, 0]))
        memory_parts.append(
            memory_lookup(query_rows, found_pair[row_start:row_stop], score_scale)[0]
        )
    return (
        jnp.concatenate(local_parts, 0),
        jnp.concatenate(memory_parts, 0),
        jnp.concatenate(lse_parts, 0),
        found_pair,
    )


def backward_pair(pair_items, bias_mats, gate_values, score_scale):
    query_pair, key_pair, value_pair, found_pair, block_row, head_index, lse_pair, mixed_delta = (
        pair_items
    )
    seq_len = query_pair.shape[0]
    step_rows = min(512, seq_len)
    bias_matrix = lax.dynamic_index_in_dim(bias_mats, head_index, 0, False)
    gate_value = lax.dynamic_index_in_dim(gate_values, head_index, 0, False)
    delta_full = mixed_delta.astype(jnp.float32)
    local_delta = ((1.0 - gate_value) * delta_full).astype(jnp.bfloat16)
    memory_delta = gate_value * delta_full
    key_grad = jnp.zeros(key_pair.shape, jnp.float32)
    value_grad = jnp.zeros(value_pair.shape, jnp.float32)
    query_parts = []
    score_parts = []
    for row_start in range(0, seq_len, step_rows):
        row_stop = row_start + step_rows
        query_rows = query_pair[row_start:row_stop]
        scores = block_scores(
            query_rows,
            key_pair,
            bias_matrix[row_start:row_stop],
            block_row[row_start:row_stop],
            block_row,
            score_scale,
        )
        weights = jnp.exp(scores - lse_pair[row_start:row_stop, None])
        delta_rows = local_delta[row_start:row_stop]
        value_grad = value_grad + dot_outer(weights.astype(jnp.bfloat16), delta_rows)
        weight_delta = dot_inner(delta_rows, value_pair)
        score_delta = (
            weights * (weight_delta - jnp.sum(weights * weight_delta, -1, keepdims=True))
        ).astype(jnp.bfloat16)
        key_grad = key_grad + dot_outer(score_delta, query_rows) * score_scale
        unused, memory_weights, keys_found, values_found = memory_lookup(
            query_rows, found_pair[row_start:row_stop], score_scale
        )
        read_delta = jnp.einsum(
            "qd,qkd->qk", memory_delta[row_start:row_stop], values_found, precision=exact_mode
        )
        memory_score_delta = memory_weights * (
            read_delta - jnp.sum(memory_weights * read_delta, -1, keepdims=True)
        )
        memory_query = (
            jnp.einsum("qk,qkd->qd", memory_score_delta, keys_found, precision=exact_mode)
            * score_scale
        )
        query_parts.append(dot_rows(score_delta, key_pair) * score_scale + memory_query)
        score_parts.append(score_delta.astype(jnp.float32))
    diagonal = diagonal_sums(jnp.concatenate(score_parts, 0), seq_len)
    return (
        jnp.concatenate(query_parts, 0).astype(jnp.bfloat16),
        key_grad.astype(jnp.bfloat16),
        value_grad.astype(jnp.bfloat16),
        diagonal,
    )


def body(
    tokens,
    block_ids,
    memory_index,
    memory_keys,
    memory_values,
    attn_gain,
    query_weight,
    key_weight,
    value_weight,
    output_weight,
    position_table,
    memory_gate,
    mlp_gain,
    hidden_weight,
    return_weight,
    grad_output,
):
    share_rows = tokens.shape[0]
    seq_count = block_ids.shape[0]
    seq_len = block_ids.shape[1]
    head_count = memory_keys.shape[0]
    head_width = memory_keys.shape[2]
    inner_width = head_count * head_width
    score_scale = head_width ** (-0.5)
    token_full = tokens.astype(jnp.float32)
    normed_rows = rms_scaled(token_full, attn_gain).astype(jnp.bfloat16)
    normed = lax.all_gather(normed_rows, "tensor", axis=0, tiled=True)
    joined = jnp.concatenate([query_weight, key_weight, value_weight], 1)
    projected = dot_rows(normed, joined).astype(jnp.bfloat16)
    q_pairs = to_pairs(projected[:, :inner_width], seq_count, head_count)
    k_pairs = to_pairs(projected[:, inner_width : 2 * inner_width], seq_count, head_count)
    v_pairs = to_pairs(projected[:, 2 * inner_width :], seq_count, head_count)
    index_pairs = to_pairs(memory_index.reshape(memory_index.shape[0], -1), seq_count, head_count)
    memory_table = jnp.concatenate([memory_keys, memory_values], 2)
    onehot = bucket_table(seq_len)
    bias_columns = jnp.dot(onehot, position_table, precision=exact_mode)
    bias_mats = jax.vmap(lambda column: toeplitz(column, seq_len))(bias_columns.T)
    pair_heads = jnp.tile(jnp.arange(head_count, dtype=jnp.int32), seq_count)
    pair_blocks = jnp.repeat(block_ids, head_count, axis=0)
    gate_values = jax.nn.sigmoid(memory_gate)

    def run_forward(pair_items):
        return forward_pair(pair_items, bias_mats, memory_table, score_scale)

    local_pairs, recall_pairs, lse_pairs, found_pairs = lax.map(
        run_forward, (q_pairs, k_pairs, v_pairs, index_pairs, pair_blocks, pair_heads)
    )
    gate_pairs = jnp.tile(gate_values, seq_count)[:, None, None]
    mixed_pairs = gate_pairs * recall_pairs + (1.0 - gate_pairs) * local_pairs
    mixed_rows = from_pairs(mixed_pairs, seq_count, head_count).astype(jnp.bfloat16)
    middle = token_full + lax.psum_scatter(
        dot_rows(
            lax.slice_in_dim(mixed_rows, 0, share_rows * lax.axis_size("tensor"), axis=0),
            output_weight,
        ),
        "tensor",
        scatter_dimension=0,
        tiled=True,
    )
    second_rows = rms_scaled(middle, mlp_gain).astype(jnp.bfloat16)
    grad_rows = grad_output.astype(jnp.float32)
    second = lax.all_gather(second_rows, "tensor", axis=0, tiled=True)
    hidden = dot_rows(second, hidden_weight)
    active = jax.nn.gelu(hidden).astype(jnp.bfloat16)
    layer_output = (
        middle
        + lax.psum_scatter(
            dot_rows(active, return_weight).astype(jnp.bfloat16),
            "tensor",
            scatter_dimension=0,
            tiled=True,
        ).astype(jnp.float32)
    ).astype(jnp.bfloat16)
    grad_full = lax.all_gather(grad_output, "tensor", axis=0, tiled=True)
    return_part = dot_outer(active, grad_full)
    active_delta = dot_inner(grad_full, return_weight)
    gelu_back = jax.vjp(jax.nn.gelu, hidden)[1]
    hidden_delta = gelu_back(active_delta)[0].astype(jnp.bfloat16)
    hidden_part = dot_outer(second, hidden_delta)
    second_delta = lax.psum_scatter(
        dot_inner(hidden_delta, hidden_weight), "tensor", scatter_dimension=0, tiled=True
    )
    second_back = jax.vjp(rms_scaled, middle, mlp_gain)[1]
    middle_part, mlp_gain_part = second_back(second_delta)
    middle_delta = grad_rows + middle_part
    middle_low = middle_delta.astype(jnp.bfloat16)
    middle_full = lax.all_gather(middle_low, "tensor", axis=0, tiled=True)
    output_part = dot_outer(mixed_rows, middle_full)
    mixed_delta = dot_inner(middle_full, output_weight).astype(jnp.bfloat16)
    delta_pairs = to_pairs(mixed_delta, seq_count, head_count)
    gate_sums = jnp.sum(delta_pairs.astype(jnp.float32) * (recall_pairs - local_pairs), axis=(1, 2))
    gate_part = (
        jnp.sum(gate_sums.reshape(seq_count, head_count), 0) * gate_values * (1.0 - gate_values)
    )

    def run_backward(pair_items):
        return backward_pair(pair_items, bias_mats, gate_values, score_scale)

    query_pairs, key_pairs, value_pairs, diagonal_pairs = lax.map(
        run_backward,
        (q_pairs, k_pairs, v_pairs, found_pairs, pair_blocks, pair_heads, lse_pairs, delta_pairs),
    )
    diagonal_heads = jnp.sum(diagonal_pairs.reshape(seq_count, head_count, -1), 0)
    table_part = lax.dot_general(
        onehot, diagonal_heads, (((0,), (1,)), ((), ())), precision=exact_mode
    )
    project_delta = jnp.concatenate(
        [
            from_pairs(query_pairs, seq_count, head_count),
            from_pairs(key_pairs, seq_count, head_count),
            from_pairs(value_pairs, seq_count, head_count),
        ],
        1,
    )
    normed_used = lax.all_gather(normed_rows, "tensor", axis=0, tiled=True)
    joined_part = dot_outer(normed_used, project_delta)
    query_part = joined_part[:, :inner_width]
    key_part = joined_part[:, inner_width : 2 * inner_width]
    value_part = joined_part[:, 2 * inner_width :]
    normed_delta = lax.psum_scatter(
        dot_inner(
            lax.slice_in_dim(project_delta, 0, share_rows * lax.axis_size("tensor"), axis=0), joined
        ).astype(jnp.bfloat16),
        "tensor",
        scatter_dimension=0,
        tiled=True,
    ).astype(jnp.float32)
    first_back = jax.vjp(rms_scaled, token_full, attn_gain)[1]
    token_part, attn_gain_part = first_back(normed_delta)
    tokens_grad = (middle_delta + token_part).astype(jnp.bfloat16)
    (
        query_grad,
        key_grad,
        value_grad,
        output_weight_grad,
        table_grad,
        gate_grad,
        hidden_grad,
        return_grad,
    ) = (
        lax.psum(query_part.astype(jnp.bfloat16), "dp").astype(jnp.float32),
        lax.psum(key_part.astype(jnp.bfloat16), "dp").astype(jnp.float32),
        lax.psum(value_part.astype(jnp.bfloat16), "dp").astype(jnp.float32),
        lax.psum(output_part.astype(jnp.bfloat16), "dp").astype(jnp.float32),
        lax.psum(table_part.astype(jnp.bfloat16), "dp").astype(jnp.float32),
        lax.psum(gate_part.astype(jnp.bfloat16), "dp").astype(jnp.float32),
        lax.psum(hidden_part.astype(jnp.bfloat16), "dp").astype(jnp.float32),
        lax.psum(return_part.astype(jnp.bfloat16), "dp").astype(jnp.float32),
    )
    attn_gain_grad, mlp_gain_grad = lax.psum((attn_gain_part, mlp_gain_part), ("dp", "tensor"))
    return (
        layer_output,
        tokens_grad,
        attn_gain_grad,
        query_grad,
        key_grad,
        value_grad,
        output_weight_grad,
        table_grad,
        gate_grad,
        mlp_gain_grad,
        hidden_grad,
        return_grad,
    )


def solution(mesh):
    return jax.shard_map(
        body,
        mesh=mesh,
        in_specs=(
            P(("dp", "tensor"), None),
            P("dp", None),
            P("dp", "tensor", None),
            P("tensor", None, None),
            P("tensor", None, None),
            P(),
            P(None, "tensor"),
            P(None, "tensor"),
            P(None, "tensor"),
            P("tensor", None),
            P(None, "tensor"),
            P("tensor"),
            P(),
            P(None, "tensor"),
            P("tensor", None),
            P(("dp", "tensor"), None),
        ),
        out_specs=(
            P(("dp", "tensor"), None),
            P(("dp", "tensor"), None),
            P(),
            P(None, "tensor"),
            P(None, "tensor"),
            P(None, "tensor"),
            P("tensor", None),
            P(None, "tensor"),
            P("tensor"),
            P(),
            P(None, "tensor"),
            P("tensor", None),
        ),
        check_vma=False,
    )
```

profile of v0, /device:TPU:1, one launch (start us, length us, event | category | flops | bytes accessed | tf_op | source)
XLA Modules:
  0.0 4142.2 jit_solution(11963079640464935723)
XLA Ops:
  41.2 384.7 %while.37 = (u32[]{:T(128)}, f32[4,1025,2047]{2,1,0:T(8,128)}, f32[8392700]{0:T(1024)}, u32[]{}, u32[]{}, /*index=5*/u32[]{}, u32[]{}, u32[]{}) while((u32[]{:T(128)}, f32[4,1025,2047]{2,1,0:T(8,128)}, f32[8392700]{0:T(1024)}, u32[]{}, u32[]{}, /*index=5*/u32[]{}, u32[]{}, u32[]{}) %tuple.138), condition=%wide.cond, body=%wide.body.sunk | while | flops 9 | bytes 25153716
  52.7 36.6 dynamic-update-slice.22
  100.8 36.7 dynamic-update-slice.22
  148.9 36.6 dynamic-update-slice.22
  197.0 36.6 dynamic-update-slice.22
  245.1 36.6 dynamic-update-slice.22
  293.2 36.6 dynamic-update-slice.22
  341.3 36.6 dynamic-update-slice.22
  389.3 36.4 dynamic-update-slice.22
  426.0 44.9 %tile.32 = f32[4,2098175]{1,0:T(4,128)} reshape(f32[8392700]{0:T(1024)} %get-tuple-element.282) | data formatting | bytes 67141600 | tf_op jit(solution)/shard_map/vmap()/tile | solution.py:46
  470.9 23.5 slice.250
  494.3 93.9 %reshape.386 = f32[8380416]{0:T(1024)} reshape(f32[4,2095104]{1,0:T(4,128)} %slice.250) | data formatting | bytes 67043328
  588.2 30.1 reshape.336
  639.3 22.8 pad_maximum_fusion.1
  687.0 1622.8 %while.35 = (s32[]{:T(128)}, f32[8,1024,128]{2,1,0:T(8,128)}, f32[8,1024,128]{2,1,0:T(8,128)}, f32[8,1024]{1,0:T(8,128)}, bf16[8,1024,32,256]{3,2,1,0:T(8,128)(2...) while((s32[]{:T(128)}, f32[8,1024,128]{2,1,0:T(8,128)}, ...), condition=%wide.region_10.11_spmd, body=%wide.region_1.10_spmd.sunk | while | flops 626849792 | bytes 209131344 | solution.py:239
  698.1 125.9 %gather_fusion = bf16[32768,256]{1,0:T(8,128)(2,1)} fusion(bf16[16384,256]{1,0:T(8,128)(2,1)} %dynamic-slice_bitcast_fusion.15, s32[32768]{0:T(1024)S(1)} %broadcast_clamp_fusion.2), kind=kCustom, calls=%fused_computation.clone.1 | custom fusion | bytes 33685504 | tf_op jit(solution)/shard_map/while/body/eval_jaxpr/jit(_take)/gather | solution.py:104
  841.1 14.8 broadcast_select_fusion.2
  900.9 125.9 %gather_fusion = bf16[32768,256]{1,0:T(8,128)(2,1)} fusion(bf16[16384,256]{1,0:T(8,128)(2,1)} %dynamic-slice_bitcast_fusion.15, s32[32768]{0:T(1024)S(1)} %broadcast_clamp_fusion.2), kind=kCustom, calls=%fused_computation.clone.1 | custom fusion | bytes 33685504 | tf_op jit(solution)/shard_map/while/body/eval_jaxpr/jit(_take)/gather | solution.py:104
  1043.9 14.8 broadcast_select_fusion.2
  1103.7 125.9 %gather_fusion = bf16[32768,256]{1,0:T(8,128)(2,1)} fusion(bf16[16384,256]{1,0:T(8,128)(2,1)} %dynamic-slice_bitcast_fusion.15, s32[32768]{0:T(1024)S(1)} %broadcast_clamp_fusion.2), kind=kCustom, calls=%fused_computation.clone.1 | custom fusion | bytes 33685504 | tf_op jit(solution)/shard_map/while/body/eval_jaxpr/jit(_take)/gather | solution.py:104
  1246.7 14.8 broadcast_select_fusion.2
  1306.6 125.9 %gather_fusion = bf16[32768,256]{1,0:T(8,128)(2,1)} fusion(bf16[16384,256]{1,0:T(8,128)(2,1)} %dynamic-slice_bitcast_fusion.15, s32[32768]{0:T(1024)S(1)} %broadcast_clamp_fusion.2), kind=kCustom, calls=%fused_computation.clone.1 | custom fusion | bytes 33685504 | tf_op jit(solution)/shard_map/while/body/eval_jaxpr/jit(_take)/gather | solution.py:104
  1449.6 14.8 broadcast_select_fusion.2
  1509.3 125.9 %gather_fusion = bf16[32768,256]{1,0:T(8,128)(2,1)} fusion(bf16[16384,256]{1,0:T(8,128)(2,1)} %dynamic-slice_bitcast_fusion.15, s32[32768]{0:T(1024)S(1)} %broadcast_clamp_fusion.2), kind=kCustom, calls=%fused_computation.clone.1 | custom fusion | bytes 33685504 | tf_op jit(solution)/shard_map/while/body/eval_jaxpr/jit(_take)/gather | solution.py:104
  1652.3 14.8 broadcast_select_fusion.2
  1712.1 125.9 %gather_fusion = bf16[32768,256]{1,0:T(8,128)(2,1)} fusion(bf16[16384,256]{1,0:T(8,128)(2,1)} %dynamic-slice_bitcast_fusion.15, s32[32768]{0:T(1024)S(1)} %broadcast_clamp_fusion.2), kind=kCustom, calls=%fused_computation.clone.1 | custom fusion | bytes 33685504 | tf_op jit(solution)/shard_map/while/body/eval_jaxpr/jit(_take)/gather | solution.py:104
  1855.1 14.8 broadcast_select_fusion.2
  1914.9 125.9 %gather_fusion = bf16[32768,256]{1,0:T(8,128)(2,1)} fusion(bf16[16384,256]{1,0:T(8,128)(2,1)} %dynamic-slice_bitcast_fusion.15, s32[32768]{0:T(1024)S(1)} %broadcast_clamp_fusion.2), kind=kCustom, calls=%fused_computation.clone.1 | custom fusion | bytes 33685504 | tf_op jit(solution)/shard_map/while/body/eval_jaxpr/jit(_take)/gather | solution.py:104
  2117.8 125.9 %gather_fusion = bf16[32768,256]{1,0:T(8,128)(2,1)} fusion(bf16[16384,256]{1,0:T(8,128)(2,1)} %dynamic-slice_bitcast_fusion.15, s32[32768]{0:T(1024)S(1)} %broadcast_clamp_fusion.2), kind=kCustom, calls=%fused_computation.clone.1 | custom fusion | bytes 33685504 | tf_op jit(solution)/shard_map/while/body/eval_jaxpr/jit(_take)/gather | solution.py:104
  2323.5 18.7 reduce-scatter.5.cloned.1.call-done
  2358.7 15.7 fusion.172
  2375.7 28.9 fusion.132
  2419.4 18.2 reduce-scatter.9.cloned.1.call-done
  2446.0 14.9 all-gather.11.cloned.1.call-done
  2471.0 1197.6 %while.36 = (s32[]{:T(128)}, bf16[8,1024,128]{2,1,0:T(8,128)(2,1)}, bf16[8,1024,128]{2,1,0:T(8,128)(2,1)}, bf16[8,1024,128]{2,1,0:T(8,128)(2,1)}, f32[8,2047]{1,...) while((s32[]{:T(128)}, bf16[8,1024,128]{2,1,0:T(8,128)(2,1)}, ...), condition=%wide.region_26.27_spmd, body=%wide.region_16.26_spmd.sunk | while | flops 1474782208 | bytes 277643808 | solution.py:293
  2511.8 32.7 rev.7
  2658.2 32.7 rev.7
  2804.7 32.7 rev.7
  2951.1 32.7 rev.7
  3097.5 32.7 rev.7
  3244.0 32.7 rev.7
  3390.4 32.7 rev.7
  3536.9 32.7 rev.7
  3689.1 16.4 convolution_convert_fusion.4
  3719.8 16.1 convolution_convert_fusion.5
  3757.5 37.3 all-reduce.2
  3799.4 47.4 %all-reduce.1 = (f32[1024]{0:T(1024)}, f32[1024]{0:T(1024)}) all-reduce(f32[1024]{0:T(1024)S(1)} %get-tuple-element.285, f32[1024]{0:T(1024)S(1)} %copy-done.41), channel_id=1, replica_groups=mesh['dp'=16,'tensor'=2] {'dp','tensor'}, use_global_device_ids=true, to_apply=%region_30.31 | all-reduce | flops 2048 | bytes 16384 | tf_op jit(solution)/shard_map/psum | solution.py:344
  3855.0 262.6 %all-reduce.6.cloned.1.call-done = (bf16[1024,512]{1,0:T(8,128)(2,1)}, bf16[1024,512]{1,0:T(8,128)(2,1)}, bf16[1024,512]{1,0:T(8,128)(2,1)}, bf16[512,1024]{1,0:...) async-done(((bf16[1024,512]{1,0:T(8,128)(2,1)}, bf16[1024,512]{1,0:T(8,128)(2,1)}, bf16[1024,512]{1,0:T(8,128)(2,1)}, bf16[512,1024]{1,0:T(8,128)(2,1)}, ...) | async-done | bytes 12582928 | tf_op jit(solution)/shard_map/psum | solution.py:335
  (1087 shorter events, 1720.0 us)
Async XLA Ops:
  7.2 2309.8 %copy-start = (bf16[512,1024]{1,0:T(8,128)(2,1)S(1)}, bf16[512,1024]{1,0:T(8,128)(2,1)}, u32[]{:S(2)}) copy-start(bf16[512,1024]{1,0:T(8,128)(2,1)} %param.29) | copy-start | bytes 3145732
  7.2 654.9 %all-gather.5.cloned.1.call-start = ((), (), s32[]{:S(2)}) async-start(), calls=%async_computation.4 | async-start | bytes 6291456 | tf_op jit(solution)/shard_map/all_gather | solution.py:221
  14.1 2328.2 %reduce-scatter.5.cloned.1.call-start = ((), (), s32[]{:S(2)}) async-start(), calls=%async_computation.5 | async-start | bytes 12582912 | tf_op jit(solution)/shard_map/reduce_scatter | solution.py:245
  635.4 26.7 copy-start.54
  635.5 26.6 copy-start.45
  687.0 1622.8 %copy-start.46 = (f32[8]{0:T(128)S(1)}, f32[8]{0:T(128)}, u32[]{:S(2)}) copy-start(f32[8]{0:T(128)} %copy-done.45) | copy-start | bytes 100
  687.0 1622.9 %copy-start.47 = (f32[8]{0:T(128)S(1)}, f32[8]{0:T(128)}, u32[]{:S(2)}) copy-start(f32[8]{0:T(128)} %broadcast_subtract_fusion) | copy-start | bytes 100
  825.3 14.6 slice-start.2
  825.3 15.8 slice-start.3
  1026.8 14.1 slice-start
  1028.1 14.6 slice-start.2
  1028.1 15.8 slice-start.3
  1230.9 14.6 slice-start.2
  1230.9 15.8 slice-start.3
  1433.8 14.6 slice-start.2
  1433.8 15.8 slice-start.3
  1636.6 14.6 slice-start.2
  1636.6 15.8 slice-start.3
  1838.0 14.1 slice-start
  1839.4 14.6 slice-start.2
  1839.4 15.8 slice-start.3
  2042.1 14.6 slice-start.2
  2042.2 15.8 slice-start.3
  2245.0 14.6 slice-start.2
  2245.0 15.8 slice-start.3
  2322.7 19.5 copy-start.11
  2322.7 36.0 all-gather.9.cloned.1.call-start
  2323.5 23.6 copy-start.32
  2323.5 52.2 %all-gather.7.cloned.1.call-start = ((), (), s32[]{:S(2)}) async-start(), calls=%async_computation.6 | async-start | bytes 6291456 | tf_op jit(solution)/shard_map/all_gather | solution.py:256
  2345.1 97.7 %copy-start.30 = (f32[1024]{0:T(1024)}, f32[1024]{0:T(1024)S(1)}, u32[]{:S(2)}) copy-start(f32[1024]{0:T(1024)S(1)} %fusion.164) | copy-start | bytes 12292
  2348.8 88.8 %reduce-scatter.9.cloned.1.call-start = ((), (), s32[]{:S(2)}) async-start(), calls=%async_computation.9 | async-start | bytes 12582912 | tf_op jit(solution)/shard_map/reduce_scatter | solution.py:274
  2419.3 24.1 copy-start.14
  2419.3 41.6 %all-gather.11.cloned.1.call-start = ((), (), s32[]{:S(2)}) async-start(), calls=%async_computation.10 | async-start | bytes 6291456 | tf_op jit(solution)/shard_map/all_gather | solution.py:281
  2445.9 1350.0 %reduce-scatter.11.cloned.1.call-start = ((), (), s32[]{:S(2)}) async-start(), calls=%async_computation.11 | async-start | bytes 6291456 | tf_op jit(solution)/shard_map/reduce_scatter | solution.py:314
  3689.0 157.8 %reduce-scatter.7.cloned.1.call-start = ((), (), s32[]{:S(2)}) async-start(), calls=%async_computation.7 | async-start | bytes 6291456 | tf_op jit(solution)/shard_map/reduce_scatter | solution.py:261
  3705.5 412.0 %all-reduce.6.cloned.1.call-start = ((), (), s32[]{:S(2)}) async-start(), calls=%async_computation.12 | async-start | bytes 25165824 | tf_op jit(solution)/shard_map/psum | solution.py:335
  3705.5 14.2 copy-start.49
  3705.6 30.3 slice-start.4
  3719.7 16.2 slice-start.5
  3719.7 16.2 copy-start.48
  3750.9 45.0 %copy-start.12 = (bf16[1024,1024]{1,0:T(8,128)(2,1)S(1)}, bf16[1024,1024]{1,0:T(8,128)(2,1)}, u32[]{:S(2)}) copy-start(bf16[1024,1024]{1,0:T(8,128)(2,1)} %param.20) | copy-start | bytes 6291460
  3751.0 45.0 %copy-start.35 = (f32[1024]{0:T(1024)S(1)}, f32[1024]{0:T(1024)}, u32[]{:S(2)}) copy-start(f32[1024]{0:T(1024)} %copy-done.34) | copy-start | bytes 12292
  3751.0 44.9 %copy-start.40 = (f32[1024]{0:T(1024)S(1)}, f32[1024]{0:T(1024)}, u32[]{:S(2)}) copy-start(f32[1024]{0:T(1024)} %param.25) | copy-start | bytes 12292
  3755.9 43.6 %copy-start.41 = (f32[1024]{0:T(1024)S(1)}, f32[1024]{0:T(1024)}, u32[]{:S(2)}) copy-start(f32[1024]{0:T(1024)} %get-tuple-element.283) | copy-start | bytes 12292
  3755.9 91.0 %copy-start.37 = (f32[1024]{0:T(1024)S(1)}, f32[1024]{0:T(1024)}, u32[]{:S(2)}) copy-start(f32[1024]{0:T(1024)} %copy-done.36) | copy-start | bytes 12292
  3755.9 91.0 %copy-start.31 = (f32[1024]{0:T(1024)S(1)}, f32[1024]{0:T(1024)}, u32[]{:S(2)}) copy-start(f32[1024]{0:T(1024)} %copy-done.30) | copy-start | bytes 12292
  3755.9 91.0 %copy-start.33 = (f32[1024]{0:T(1024)S(1)}, f32[1024]{0:T(1024)}, u32[]{:S(2)}) copy-start(f32[1024]{0:T(1024)} %param.32) | copy-start | bytes 12292
  3755.9 91.0 %copy-start.39 = (f32[1024]{0:T(1024)S(1)}, f32[1024]{0:T(1024)}, u32[]{:S(2)}) copy-start(f32[1024]{0:T(1024)} %copy-done.38) | copy-start | bytes 12292
  (107 other events, 651.3 us)
Sparse Core Ops, SparseCore 0:
  14.2 16.1 all-gather.4
  2322.8 19.3 reduce-scatter.4
  2343.9 14.8 all-gather.8
  2360.8 14.8 all-gather.6
  2419.5 18.0 reduce-scatter.8
  2446.0 14.8 all-gather.10
  3689.2 13.3 reduce-scatter.10
  3705.6 13.3 reduce-scatter.6
  3751.0 366.4 all-reduce.5
where the time goes:
time: 4200 us; the launch traced here: 4140 us
  local copies, waits for them, and re-layouts  2430 us (58%)
  matrix products  788 us (19%)
  other arithmetic  429 us (10%)
  waiting for transfers between devices  326 us (8%)
  blocking collectives  84.7 us (2%)
  loops' own time  65.5 us (2%)
    gather x8, local copies, waits for them, and re-layouts, forward_pair(): found_pair = jnp.take(table_head, index_pair, axis=0)  1010 us
    unnamed x135, local copies, waits for them, and re-layouts  512 us
    psum x1, waiting for transfers between devices, body(): lax.psum(query_part.astype(jnp.bfloat16), 'dp').astype(jnp.float32)  263 us
    rev x8, local copies, waits for them, and re-layouts, diagonal_sums(): flipped = matrix[::-1]  262 us
    dot_general x52, matrix products, dot_inner(): lax.dot_general(left, right, (((1,), (1,)), ((), ())), preferred_element_...  156 us
    dot_general x16, matrix products, backward_pair(): jnp.einsum('qd,qkd->qk', memory_delta[row_start:row_stop], values_found,...  142 us
    dot_general x32, matrix products, memory_lookup(): jnp.einsum('qd,qkd->qk', query_rows, keys_found, preferred_element_type=j...  130 us
    select_n x16, other arithmetic, forward_pair(): found_pair = jnp.take(table_head, index_pair, axis=0)  127 us
  transfers between devices with their start and end apart: 9, of which 6 were waited for; matrix products, arithmetic and copies ran while one was open for 18% of the time, Pallas kernels for 0%

commit v1 on v0

v1 whole, which is shorter than its diff:
```python
import functools
import math

import jax
import jax.numpy as jnp
from jax import lax
from jax.experimental import pallas as pl
from jax.experimental.pallas import tpu as pltpu
from jax.sharding import PartitionSpec as P

eps_norm = 1e-06
far_steps = (12, 16, 23, 32, 46, 64, 91)
exact_mode = lax.Precision.HIGHEST
low_type = jnp.bfloat16
full_type = jnp.float32
log2_e = math.log2(math.e)
tile = 256
span = 3 * tile
ring = 1024
mask_gap = -(2.0**100)
vmem_most = 60 * 2**20


def bucket_of(relative):
    upper_half = jnp.where(relative > 0, 16, 0).astype(jnp.int32)
    distance = jnp.abs(relative)
    far_bucket = 8 + sum(((distance >= step_size).astype(jnp.int32) for step_size in far_steps))
    return upper_half + jnp.where(distance < 8, distance, far_bucket)


def rms_scaled(rows, gain):
    return rows * lax.rsqrt(jnp.mean(rows * rows, -1, keepdims=True) + eps_norm) * gain


def dot_rows(left, right):
    return jnp.dot(left, right, preferred_element_type=full_type)


def dot_outer(left, right):
    return lax.dot_general(
        left, right, (((0,), (0,)), ((), ())), preferred_element_type=full_type
    )


def dot_inner(left, right):
    return lax.dot_general(
        left, right, (((1,), (1,)), ((), ())), preferred_element_type=full_type
    )


def interleave_kernel(key_ref, value_ref, table_ref):
    rows = key_ref.shape[1]
    flat = table_ref.reshape(1, 2 * rows, 128)
    row = lax.broadcasted_iota(jnp.int32, (256, 256), 0)
    column = lax.broadcasted_iota(jnp.int32, (256, 256), 1)
    order = jnp.where(column == (row // 2 + (row % 2) * 128), 1.0, 0.0).astype(low_type)
    for part in range(rows // 128):
        both = jnp.concatenate(
            [key_ref[0, pl.ds(part * 128, 128)], value_ref[0, pl.ds(part * 128, 128)]], 0
        )
        flat[0, pl.ds(part * 256, 256)] = dot_rows(order, both).astype(low_type)


def interleave(memory_keys, memory_values):
    heads, rows, width = memory_keys.shape
    step = min(2048, rows)
    spec = pl.BlockSpec((1, step, width), lambda h, i: (h, i, 0))
    return pl.pallas_call(
        interleave_kernel,
        grid=(heads, rows // step),
        in_specs=[spec, spec],
        out_specs=pl.BlockSpec((1, step, 2, width), lambda h, i: (h, i, 0, 0)),
        out_shape=jax.ShapeDtypeStruct((heads, rows, 2, width), low_type),
        name="interleave",
    )(memory_keys, memory_values)


def gather_kernel(
    index_hbm, table_hbm, found_ref, table_ref, table_sems, index_a, index_b, index_sems
):
    heads = pl.num_programs(0)
    head = pl.program_id(0)
    step = head * pl.num_programs(1) + pl.program_id(1)
    steps = heads * pl.num_programs(1)
    chunk = found_ref.shape[0] // 2
    rows = table_ref.shape[0] // table_sems.shape[0]
    slots = (index_a, index_b)

    def index_copy(number, slot):
        return pltpu.make_async_copy(index_hbm.at[number], slots[slot], index_sems.at[slot])

    def table_copy(number):
        where = pl.ds(number * rows, rows)
        return pltpu.make_async_copy(
            table_hbm.at[where], table_ref.at[where], table_sems.at[number]
        )

    @pl.when(step == 0)
    def start_all():
        index_copy(0, 0).start()
        index_copy(1, 1).start()
        for number in range(table_sems.shape[0]):
            table_copy(number).start()

    @pl.when(pl.program_id(1) == 0)
    def wait_table():
        table_copy(head).wait()

    following = jnp.minimum(step + 1, steps - 1)
    for slot in range(2):
        index_copy(2 * step + slot, slot).wait()
        picked = slots[slot]
        for start in range(0, chunk, 8):
            rows_now = [
                table_ref[picked[(start + j) // 128, (start + j) % 128]] for j in range(8)
            ]
            for j in range(8):
                found_ref[slot * chunk + start + j] = rows_now[j]
        index_copy(2 * following + slot, slot).start()

    @pl.when(step == steps - 1)
    def drain():
        index_copy(2 * following, 0).wait()
        index_copy(2 * following + 1, 1).wait()


def gather_found(index_rows, table):
    heads, rows, unused, width = table.shape
    total = index_rows.size // heads
    chunk = min(4096, total // 2)
    blocks = total // (2 * chunk)
    return pl.pallas_call(
        gather_kernel,
        grid=(heads, blocks),
        in_specs=[pl.BlockSpec(memory_space=pl.ANY), pl.BlockSpec(memory_space=pl.ANY)],
        out_specs=pl.BlockSpec((2 * chunk, 2, width), lambda h, i: (h * blocks + i, 0, 0)),
        out_shape=jax.ShapeDtypeStruct((heads * total, 2, width), low_type),
        scratch_shapes=[
            pltpu.VMEM((heads * rows, 2, width), low_type),
            pltpu.SemaphoreType.DMA((heads,)),
            pltpu.SMEM((chunk // 128, 128), jnp.int32),
            pltpu.SMEM((chunk // 128, 128), jnp.int32),
            pltpu.SemaphoreType.DMA((2,)),
        ],
        compiler_params=pltpu.CompilerParams(vmem_limit_bytes=vmem_most),
        name="gather_found",
    )(index_rows.reshape(-1, chunk // 128, 128), table.reshape(heads * rows, 2, width))


def own_columns(picks):
    shape = (8, 8 * picks * 2)
    lane = lax.broadcasted_iota(jnp.int32, shape, 1)
    row = lax.broadcasted_iota(jnp.int32, shape, 0)
    return jnp.logical_and(lane // (2 * picks) == row, lane % 2 == 0)


def recall_kernel(picks, scale, found_ref, query_ref, read_ref):
    tokens = query_ref.shape[0]
    wide = 8 * picks * 2
    own = own_columns(picks)
    groups = range(tokens // 8)
    scores = [
        dot_inner(query_ref[pl.ds(g * 8, 8), :], found_ref[pl.ds(g * wide, wide), :])
        for g in groups
    ]
    for g in groups:
        masked = jnp.where(own, scores[g] * (scale * log2_e), -jnp.inf)
        exponent = jnp.exp2(masked - jnp.max(masked, 1, keepdims=True))
        total = jnp.sum(exponent, 1, keepdims=True)
        shifted = pltpu.roll(exponent, 1, 1).astype(low_type)
        read_ref[pl.ds(g * 8, 8), :] = (
            dot_rows(shifted, found_ref[pl.ds(g * wide, wide), :]) / total
        )


def recall(found, queries, heads, picks, scale):
    tokens = queries.shape[0]
    width = queries.shape[1] // (3 * heads)
    step = min(256, tokens)
    blocks = tokens // step
    return pl.pallas_call(
        functools.partial(recall_kernel, picks, scale),
        grid=(heads, blocks),
        in_specs=[
            pl.BlockSpec((step * picks * 2, width), lambda h, i: (h * blocks + i, 0)),
            pl.BlockSpec((step, width), lambda h, i: (i, h)),
        ],
        out_specs=pl.BlockSpec((step, width), lambda h, i: (i, h)),
        out_shape=jax.ShapeDtypeStruct((tokens, heads * width), full_type),
        compiler_params=pltpu.CompilerParams(vmem_limit_bytes=vmem_most),
        name="recall",
    )(found, queries)


def recall_back_kernel(
    picks, scale, gate_ref, found_ref, query_ref, delta_ref, query_delta_ref, sums_ref
):
    tokens = query_ref.shape[0]
    wide = 8 * picks * 2
    own = own_columns(picks)
    gate = gate_ref[pl.program_id(0)]
    groups = range(tokens // 8)
    both = []
    for g in groups:
        rows = jnp.concatenate(
            [query_ref[pl.ds(g * 8, 8), :], delta_ref[pl.ds(g * 8, 8), :]], 0
        )
        both.append(dot_inner(rows, found_ref[pl.ds(g * wide, wide), :]))
    gained = jnp.zeros((8, 1), full_type)
    for g in groups:
        masked = jnp.where(own, both[g][:8] * (scale * log2_e), -jnp.inf)
        exponent = jnp.exp2(masked - jnp.max(masked, 1, keepdims=True))
        weights = exponent / jnp.sum(exponent, 1, keepdims=True)
        reads = pltpu.roll(both[g][8:], wide - 1, 1)
        expected = jnp.sum(weights * reads, 1, keepdims=True)
        gained = gained + expected
        score_delta = (weights * (reads - expected)).astype(low_type)
        query_delta_ref[pl.ds(g * 8, 8), :] = dot_rows(
            score_delta, found_ref[pl.ds(g * wide, wide), :]
        ) * (scale * gate)

    @pl.when(pl.program_id(1) == 0)
    def clear():
        sums_ref[...] = jnp.zeros(sums_ref.shape, full_type)

    sums_ref[0] += jnp.broadcast_to(gained, (8, 128))


def recall_back(found, queries, mixed_delta, gates, heads, picks, scale):
    tokens = queries.shape[0]
    width = mixed_delta.shape[1] // heads
    step = min(256, tokens)
    blocks = tokens // step
    rows_spec = pl.BlockSpec((step, width), lambda h, i: (i, h))
    return pl.pallas_call(
        functools.partial(recall_back_kernel, picks, scale),
        grid=(heads, blocks),
        in_specs=[
            pl.BlockSpec(memory_space=pltpu.SMEM),
            pl.BlockSpec((step * picks * 2, width), lambda h, i: (h * blocks + i, 0)),
            rows_spec,
            rows_spec,
        ],
        out_specs=[rows_spec, pl.BlockSpec((1, 8, 128), lambda h, i: (h, 0, 0))],
        out_shape=[
            jax.ShapeDtypeStruct((tokens, heads * width), full_type),
            jax.ShapeDtypeStruct((heads, 8, 128), full_type),
        ],
        compiler_params=pltpu.CompilerParams(vmem_limit_bytes=vmem_most),
        name="recall_back",
    )(gates, found, queries, mixed_delta)


def band(column_ref):
    wide = jnp.broadcast_to(column_ref[0], (tile, ring))
    return pltpu.roll(wide, 0, 1, stride=1, stride_axis=0)[:, :span]


def local_kernel(
    scale, gate_ref, far_ref, column_ref, query_ref, key_ref, value_ref, query_mask_ref,
    key_mask_ref, recall_ref, mixed_ref, bias_ref,
):
    head = pl.program_id(0)

    @pl.when(pl.program_id(1) == 0)
    def make_band():
        bias_ref[...] = band(column_ref)

    gate = gate_ref[head]
    count = query_ref.shape[0] // tile
    at = [pl.ds(t * tile, tile) for t in range(count)]
    keys = [jnp.concatenate([key_ref[a, :], key_mask_ref[0, a, :]], 1) for a in at]
    for t in range(count):
        rows = jnp.concatenate([query_ref[at[t], :], query_mask_ref[0, at[t], :]], 1)
        parts = []
        for j in range(count):
            step = j - t
            if step < -1:
                bias = far_ref[head, 0]
            elif step > 1:
                bias = far_ref[head, 1]
            else:
                bias = bias_ref[:, pl.ds((step + 1) * tile, tile)]
            parts.append(dot_inner(rows, keys[j]) * (scale * log2_e) + bias)
        top = jnp.max(functools.reduce(jnp.maximum, parts), 1, keepdims=True)
        parts = [jnp.exp2(part - top) for part in parts]
        total = jnp.sum(functools.reduce(jnp.add, parts), 1, keepdims=True)
        read = sum(dot_rows(parts[j].astype(low_type), value_ref[at[j], :]) for j in range(count))
        mixed_ref[at[t], :] = (
            gate * recall_ref[at[t], :] + ((1.0 - gate) / total) * read
        ).astype(low_type)


def local_read(projected, query_mask, key_mask, recalled, columns, far, gates, seq_len, scale):
    tokens = recalled.shape[0]
    heads = gates.shape[0]
    width = recalled.shape[1] // heads

    def rows_of(shift):
        return pl.BlockSpec((seq_len, width), lambda h, s: (s, h + shift * heads))

    mask_spec = pl.BlockSpec((1, seq_len, 128), lambda h, s: (s, 0, 0))
    smem = pl.BlockSpec(memory_space=pltpu.SMEM)
    return pl.pallas_call(
        functools.partial(local_kernel, scale),
        grid=(heads, tokens // seq_len),
        in_specs=[
            smem,
            smem,
            pl.BlockSpec((1, 1, ring), lambda h, s: (h, 0, 0)),
            rows_of(0),
            rows_of(1),
            rows_of(2),
            mask_spec,
            mask_spec,
            rows_of(0),
        ],
        out_specs=rows_of(0),
        out_shape=jax.ShapeDtypeStruct((tokens, heads * width), low_type),
        scratch_shapes=[pltpu.VMEM((tile, span), full_type)],
        compiler_params=pltpu.CompilerParams(vmem_limit_bytes=vmem_most),
        name="local_read",
    )(gates, far, columns, projected, projected, projected, query_mask, key_mask, recalled)


def local_back_kernel(
    scale, gate_ref, far_ref, column_ref, query_ref, key_ref, value_ref, query_mask_ref,
    key_mask_ref, delta_ref, recall_delta_ref, query_delta_ref, key_delta_ref, value_delta_ref,
    diagonal_ref, sums_ref, bias_ref, near_ref, key_sum_ref, value_sum_ref,
):
    head = pl.program_id(0)
    last = pl.program_id(1) == pl.num_programs(1) - 1

    @pl.when(pl.program_id(1) == 0)
    def make_band():
        bias_ref[...] = band(column_ref)
        near_ref[...] = jnp.zeros(near_ref.shape, full_type)
        sums_ref[...] = jnp.zeros(sums_ref.shape, full_type)

    gate = gate_ref[head]
    count = query_ref.shape[0] // tile
    at = [pl.ds(t * tile, tile) for t in range(count)]
    keys = [jnp.concatenate([key_ref[a, :], key_mask_ref[0, a, :]], 1) for a in at]
    turned = [key_ref[a, :].astype(full_type).T.astype(low_type) for a in at]
    gained = jnp.zeros((1, tile), full_type)
    far_sums = [jnp.zeros((8, tile), full_type) for side in range(2)]
    for t in range(count):
        rows = jnp.concatenate([query_ref[at[t], :], query_mask_ref[0, at[t], :]], 1)
        delta = ((1.0 - gate) * delta_ref[at[t], :].astype(full_type)).astype(low_type)
        parts = []
        for j in range(count):
            step = j - t
            if step < -1:
                bias = far_ref[head, 0]
            elif step > 1:
                bias = far_ref[head, 1]
            else:
                bias = bias_ref[:, pl.ds((1 - step) * tile, tile)]
            parts.append(dot_inner(keys[j], rows) * (scale * log2_e) + bias)
        top = jnp.max(functools.reduce(jnp.maximum, parts), 0, keepdims=True)
        parts = [jnp.exp2(part - top) for part in parts]
        total = jnp.sum(functools.reduce(jnp.add, parts), 0, keepdims=True)
        inverse = 1.0 / total
        parts = [part * inverse for part in parts]
        moves = [dot_inner(value_ref[at[j], :], delta) for j in range(count)]
        expected = jnp.sum(
            functools.reduce(jnp.add, [parts[j] * moves[j] for j in range(count)]),
            0,
            keepdims=True,
        )
        gained = gained + expected
        query_sum = None
        for j in range(count):
            step = j - t
            score_delta = parts[j] * (moves[j] - expected)
            if abs(step) > 1:
                side = 0 if step < 0 else 1
                far_sums[side] = far_sums[side] + jnp.sum(
                    score_delta.reshape(tile // 8, 8, tile), 0
                )
            else:
                near_ref[:, pl.ds((1 - step) * tile, tile)] += score_delta
            low_delta = score_delta.astype(low_type)
            value_part = dot_rows(parts[j].astype(low_type), delta)
            key_part = dot_rows(low_delta, query_ref[at[t], :])
            query_part = dot_rows(turned[j], low_delta)
            if t == 0:
                value_sum_ref[at[j], :] = value_part
                key_sum_ref[at[j], :] = key_part
            else:
                value_sum_ref[at[j], :] += value_part
                key_sum_ref[at[j], :] += key_part
            query_sum = query_part if j == 0 else query_sum + query_part
        query_delta_ref[at[t], :] = (
            query_sum.T * scale + recall_delta_ref[at[t], :]
        ).astype(low_type)
    key_delta_ref[...] = (key_sum_ref[...] * scale).astype(low_type)
    value_delta_ref[...] = value_sum_ref[...].astype(low_type)
    sums_ref[0, 0:1] += gained
    sums_ref[0, 8:16] += far_sums[0]
    sums_ref[0, 16:24] += far_sums[1]

    @pl.when(last)
    def fold_diagonals():
        total = jnp.zeros((8, ring), full_type)
        for g in range(tile // 8):
            part = jnp.concatenate(
                [near_ref[pl.ds(g * 8, 8), :], jnp.zeros((8, ring - span), full_type)], 1
            )
            total = total + (pltpu.roll(part, ring - 8 * g, 1) if g else part)
        row = lax.broadcasted_iota(jnp.int32, (8, ring), 0)
        for bit in (1, 2, 4):
            total = jnp.where((row & bit) != 0, pltpu.roll(total, ring - bit, 1), total)
        diagonal_ref[0] = total


def local_back(
    projected, query_mask, key_mask, mixed_delta, recall_delta, columns, far, gates, seq_len, scale
):
    tokens = mixed_delta.shape[0]
    heads = gates.shape[0]
    width = mixed_delta.shape[1] // heads

    def rows_of(shift):
        return pl.BlockSpec((seq_len, width), lambda h, s: (s, h + shift * heads))

    mask_spec = pl.BlockSpec((1, seq_len, 128), lambda h, s: (s, 0, 0))
    smem = pl.BlockSpec(memory_space=pltpu.SMEM)
    rows_shape = jax.ShapeDtypeStruct((tokens, heads * width), low_type)
    return pl.pallas_call(
        functools.partial(local_back_kernel, scale),
        grid=(heads, tokens // seq_len),
        in_specs=[
            smem,
            smem,
            pl.BlockSpec((1, 1, ring), lambda h, s: (h, 0, 0)),
            rows_of(0),
            rows_of(1),
            rows_of(2),
            mask_spec,
            mask_spec,
            rows_of(0),
            rows_of(0),
        ],
        out_specs=[
            rows_of(0),
            rows_of(0),
            rows_of(0),
            pl.BlockSpec((1, 8, ring), lambda h, s: (h, 0, 0)),
            pl.BlockSpec((1, 24, tile), lambda h, s: (h, 0, 0)),
        ],
        out_shape=[
            rows_shape,
            rows_shape,
            rows_shape,
            jax.ShapeDtypeStruct((heads, 8, ring), full_type),
            jax.ShapeDtypeStruct((heads, 24, tile), full_type),
        ],
        scratch_shapes=[
            pltpu.VMEM((tile, span), full_type),
            pltpu.VMEM((tile, span), full_type),
            pltpu.VMEM((seq_len, width), full_type),
            pltpu.VMEM((seq_len, width), full_type),
        ],
        compiler_params=pltpu.CompilerParams(vmem_limit_bytes=vmem_most),
        name="local_back",
    )(
        gates, far, columns, projected, projected, projected, query_mask, key_mask, mixed_delta,
        recall_delta,
    )


def mask_rows(block_ids):
    level = jnp.arange(128, dtype=jnp.int32)
    gap = block_ids[:, :, None] - level
    query_mask = jnp.where((gap >= 0) & (gap <= 1), 0.0, mask_gap).astype(low_type)
    key_mask = (gap == 0).astype(low_type)
    return query_mask, key_mask


def body(
    tokens,
    block_ids,
    memory_index,
    memory_keys,
    memory_values,
    attn_gain,
    query_weight,
    key_weight,
    value_weight,
    output_weight,
    position_table,
    memory_gate,
    mlp_gain,
    hidden_weight,
    return_weight,
    grad_output,
):
    share_rows = tokens.shape[0]
    seq_len = block_ids.shape[1]
    head_count, memory_rows, head_width = memory_keys.shape
    picks = memory_index.shape[2]
    inner_width = head_count * head_width
    scale = head_width ** (-0.5)
    group = lax.axis_size("tensor")
    group_rows = share_rows * group

    offsets = jnp.arange(head_count, dtype=jnp.int32) * memory_rows
    index_rows = memory_index.transpose(1, 0, 2) + offsets[:, None, None]
    found = gather_found(index_rows, interleave(memory_keys, memory_values))
    found = found.reshape(-1, head_width)

    token_full = tokens.astype(full_type)
    normed_rows = rms_scaled(token_full, attn_gain).astype(low_type)
    normed = lax.all_gather(normed_rows, "tensor", axis=0, tiled=True)
    joined = jnp.concatenate([query_weight, key_weight, value_weight], 1)
    projected = dot_rows(normed, joined).astype(low_type)

    query_mask, key_mask = mask_rows(block_ids)
    place = jnp.arange(ring, dtype=jnp.int32)
    place = jnp.where(place < span, place, place - ring)
    ahead = bucket_of(place - tile)
    behind = bucket_of(tile - place)
    level = jnp.arange(32, dtype=jnp.int32)
    ahead_hot = (ahead[:, None] == level).astype(full_type)
    behind_hot = (behind[:, None] == level).astype(full_type)
    scaled_table = position_table * log2_e
    ahead_columns = jnp.dot(ahead_hot, scaled_table, precision=exact_mode).T[:, None, :]
    behind_columns = jnp.dot(behind_hot, scaled_table, precision=exact_mode).T[:, None, :]
    far = jnp.stack([scaled_table[15], scaled_table[31]], 1)
    gates = jax.nn.sigmoid(memory_gate)

    recalled = recall(found, projected, head_count, picks, scale)
    mixed_rows = local_read(
        projected, query_mask, key_mask, recalled, ahead_columns, far, gates, seq_len, scale
    )
    middle = token_full + lax.psum_scatter(
        dot_rows(mixed_rows, output_weight), "tensor", scatter_dimension=0, tiled=True
    )
    second_rows = rms_scaled(middle, mlp_gain).astype(low_type)
    grad_rows = grad_output.astype(full_type)
    second = lax.all_gather(second_rows, "tensor", axis=0, tiled=True)
    hidden = dot_rows(second, hidden_weight)
    active = jax.nn.gelu(hidden).astype(low_type)
    layer_output = (
        middle
        + lax.psum_scatter(
            dot_rows(active, return_weight).astype(low_type),
            "tensor",
            scatter_dimension=0,
            tiled=True,
        ).astype(full_type)
    ).astype(low_type)
    grad_full = lax.all_gather(grad_output, "tensor", axis=0, tiled=True)
    return_part = dot_outer(active, grad_full)
    active_delta = dot_inner(grad_full, return_weight)
    gelu_back = jax.vjp(jax.nn.gelu, hidden)[1]
    hidden_delta = gelu_back(active_delta)[0].astype(low_type)
    hidden_part = dot_outer(second, hidden_delta)
    second_delta = lax.psum_scatter(
        dot_inner(hidden_delta, hidden_weight), "tensor", scatter_dimension=0, tiled=True
    )
    second_back = jax.vjp(rms_scaled, middle, mlp_gain)[1]
    middle_part, mlp_gain_part = second_back(second_delta)
    middle_delta = grad_rows + middle_part
    middle_low = middle_delta.astype(low_type)
    middle_full = lax.all_gather(middle_low, "tensor", axis=0, tiled=True)
    output_part = dot_outer(mixed_rows, middle_full)
    mixed_delta = dot_inner(middle_full, output_weight).astype(low_type)

    recall_delta, recall_sums = recall_back(
        found, projected, mixed_delta, gates, head_count, picks, scale
    )
    query_delta, key_delta, value_delta, diagonals, local_sums = local_back(
        projected, query_mask, key_mask, mixed_delta, recall_delta, behind_columns, far, gates,
        seq_len, scale,
    )
    recall_gain = jnp.sum(recall_sums[:, :, 0], 1)
    local_gain = jnp.sum(local_sums[:, 0], 1)
    gate_part = gates * (1.0 - gates) * recall_gain - gates * local_gain
    diagonal_sums = jnp.sum(diagonals, 1)
    table_part = jnp.dot(diagonal_sums, behind_hot, precision=exact_mode).T
    far_left = jnp.sum(local_sums[:, 8:16], (1, 2))
    far_right = jnp.sum(local_sums[:, 16:24], (1, 2))
    table_part = table_part.at[15].add(far_left).at[31].add(far_right)

    project_delta = jnp.concatenate([query_delta, key_delta, value_delta], 1)
    joined_part = dot_outer(normed, project_delta)
    query_part = joined_part[:, :inner_width]
    key_part = joined_part[:, inner_width : 2 * inner_width]
    value_part = joined_part[:, 2 * inner_width :]
    normed_delta = lax.psum_scatter(
        dot_inner(project_delta, joined).astype(low_type),
        "tensor",
        scatter_dimension=0,
        tiled=True,
    ).astype(full_type)
    first_back = jax.vjp(rms_scaled, token_full, attn_gain)[1]
    token_part, attn_gain_part = first_back(normed_delta)
    tokens_grad = (middle_delta + token_part).astype(low_type)
    (
        query_grad,
        key_grad,
        value_grad,
        output_weight_grad,
        table_grad,
        gate_grad,
        hidden_grad,
        return_grad,
    ) = (
        lax.psum(part.astype(low_type), "dp").astype(full_type)
        for part in (
            query_part,
            key_part,
            value_part,
            output_part,
            table_part,
            gate_part,
            hidden_part,
            return_part,
        )
    )
    attn_gain_grad, mlp_gain_grad = lax.psum((attn_gain_part, mlp_gain_part), ("dp", "tensor"))
    return (
        layer_output,
        tokens_grad,
        attn_gain_grad,
        query_grad,
        key_grad,
        value_grad,
        output_weight_grad,
        table_grad,
        gate_grad,
        mlp_gain_grad,
        hidden_grad,
        return_grad,
    )


def solution(mesh):
    def run(*arrays):
        with jax.sharding.use_abstract_mesh(mesh.abstract_mesh):
            return jax.shard_map(
                body,
                mesh=mesh,
                in_specs=(
                    P(("dp", "tensor"), None),
                    P("dp", None),
                    P("dp", "tensor", None),
                    P("tensor", None, None),
                    P("tensor", None, None),
                    P(),
                    P(None, "tensor"),
                    P(None, "tensor"),
                    P(None, "tensor"),
                    P("tensor", None),
                    P(None, "tensor"),
                    P("tensor"),
                    P(),
                    P(None, "tensor"),
                    P("tensor", None),
                    P(("dp", "tensor"), None),
                ),
                out_specs=(
                    P(("dp", "tensor"), None),
                    P(("dp", "tensor"), None),
                    P(),
                    P(None, "tensor"),
                    P(None, "tensor"),
                    P(None, "tensor"),
                    P("tensor", None),
                    P(None, "tensor"),
                    P("tensor"),
                    P(),
                    P(None, "tensor"),
                    P("tensor", None),
                ),
                check_vma=False,
            )(*arrays)

    return run
```

time: 4200 us -> 1060 us (0.25); the launches traced: 4140 us -> 1050 us
  local copies, waits for them, and re-layouts: 2430 us -> 25.1 us
  matrix products: 788 us -> 151 us
  Pallas kernels: 0 us -> 390 us
  other arithmetic: 429 us -> 52.3 us
  loops' own time: 65.5 us -> 0 us
    gather x8 -> x0, local copies, waits for them, and re-layouts: 1010 us -> none  [forward_pair(): found_pair = jnp.take(table_head, index_pair, axis=0)]
    unnamed x135 -> x100, local copies, waits for them, and re-layouts: 512 us -> 14.7 us
    dot_general x118 -> x7, matrix products: 550 us -> 65.4 us  [the longest x4 64.1 us: dot_rows(): return jnp.dot(left, right, preferred_element_type=full_type)]
    pallas_call x0 -> x6, Pallas kernels: none -> 390 us  [the longest x1 149 us: gather_found(): pl.pallas_call(gather_kernel, grid=(heads, blocks), in_specs=[pl.BlockSpe...]
    rev x8 -> x0, local copies, waits for them, and re-layouts: 262 us -> none  [diagonal_sums(): flipped = matrix[::-1]]
    slice x67 -> x0, local copies, waits for them, and re-layouts: 197 us -> none  [the longest x8 75.3 us: backward_pair(): found_pair[row_start:row_stop]]
    reshape x19 -> x1, local copies, waits for them, and re-layouts: 150 us -> 4.1 us  [gather_found(): index_rows.reshape(-1, chunk // 128, 128)]
    select_n x16 -> x0, other arithmetic: 127 us -> none  [forward_pair(): found_pair = jnp.take(table_head, index_pair, axis=0)]
  transfers between devices with their start and end apart: 9 -> 9, of which waited for: 6 -> 6; matrix products, arithmetic and copies ran while one was open for 18% -> 10% of each run, Pallas kernels for 0% -> 18%
where the time goes in v1:
time: 1060 us; the launch traced here: 1050 us
  Pallas kernels  390 us (37%)
  waiting for transfers between devices  330 us (31%)
  matrix products  151 us (14%)
  blocking collectives  84.7 us (8%)
  other arithmetic  52.3 us (5%)
  local copies, waits for them, and re-layouts  25.1 us (2%)
  between operations  14.6 us (1%)
    psum x1, waiting for transfers between devices, body(): lax.psum(part.astype(low_type), 'dp').astype(full_type)  267 us
    pallas_call x1, Pallas kernels, gather_found(): pl.pallas_call(gather_kernel, grid=(heads, blocks), in_specs=[pl.BlockSpe...  149 us
    pallas_call x1, Pallas kernels, recall_back(): pl.pallas_call(functools.partial(recall_back_kernel, picks, scale), grid=...  68.4 us
    pallas_call x1, Pallas kernels, recall(): pl.pallas_call(functools.partial(recall_kernel, picks, scale), grid=(head...  67.7 us
    dot_general x4, matrix products, dot_rows(): return jnp.dot(left, right, preferred_element_type=full_type)  64.1 us
    psum x1, blocking collectives, body(): lax.psum((attn_gain_part, mlp_gain_part), ('dp', 'tensor'))  47.7 us
    dot_general x4, matrix products, dot_inner(): lax.dot_general(left, right, (((1,), (1,)), ((), ())), preferred_element_...  44.6 us
    pallas_call x1, Pallas kernels, local_back(): pl.pallas_call(functools.partial(local_back_kernel, scale), grid=(heads,...  42.1 us
  transfers between devices with their start and end apart: 9, of which 6 were waited for; matrix products, arithmetic and copies ran while one was open for 10% of the time, Pallas kernels for 18%

profile of v1, /device:TPU:1, one launch (start us, length us, event | category | flops | bytes accessed | tf_op | source)
XLA Modules:
  0.0 1047.6 jit_solution(14108237459199075508)
XLA Ops:
  7.3 2.2 fusion.14
  10.7 3.5 fusion.9
  14.4 2.7 copy.35
  17.1 4.1 reshape.195.index_hbm
  22.3 41.5 %interleave.1 = bf16[4,16384,2,128]{3,2,1,0:T(2,128)(2,1)} custom-call(bf16[4,16384,128]{2,1,0:T(8,128)(2,1)} %key_ref.1, bf16[4,16384,128]{2,1,0:T(8,128)(2,1)} %value_ref.1), custom_call_target="tpu_custom_call" | custom-call | tf_op jit(solution)/shard_map/interleave/pallas_call | solution.py:68
  63.8 149.0 %gather_found.1 = bf16[262144,2,128]{2,1,0:T(2,128)(2,1)} custom-call(s32[64,32,128]{2,1,0:T(8,128)} %reshape.195.index_hbm, bf16[65536,2,128]{2,1,0:T(2,128)(2,1)} %bitcast.33), custom_call_target="tpu_custom_call" | custom-call | tf_op jit(solution)/shard_map/gather_found/pallas_call | solution.py:132
  214.1 1.7 copy-done.21
  218.6 11.3 %convolution_convert_fusion.query_ref.key_ref.value_ref = bf16[2048,1536]{1,0:T(8,128)(2,1)} fusion(bf16[2048,1024]{1,0:T(8,128)(2,1)} %all-gather.5.cloned.1.call-done, bf16[1024,1536]{1,0:T(8,128)(2,1)} %copy-done.21), kind=kOutput, calls=%fused_computation.15 | convolution fusion | flops 6445596672 | bytes 13631488 | tf_op jit(solution)/shard_map/dot_general | solution.py:36
  230.0 67.7 %recall.1.recall_ref = f32[2048,512]{1,0:T(8,128)} custom-call(bf16[524288,128]{1,0:T(8,128)(2,1)} %bitcast.4.found_ref, bf16[2048,1536]{1,0:T(8,128)(2,1)} %convolution_convert_fusion.query_ref.key_ref.value_ref), custom_call_target="tpu_custom_call" | custom-call | tf_op jit(solution)/shard_map/recall/pallas_call | solution.py:181
  297.7 21.0 %local_read.1 = bf16[2048,512]{1,0:T(8,128)(2,1)} custom-call(f32[4]{0:T(128)} %add_divide_fusion.gate_ref, f32[4,2]{1,0:T(4,128)} %pad_maximum_fusion.far_ref, f32[4,1,1024]{2,1,0:T(1,128)} %broadcast_in_dim.25.column_ref, bf16[2048,1536]{1,0:T(8,128)(2,1)} %convolution_convert_fusion.query_ref.key_ref.value_ref, ...), custom_call_target="tpu_custom_call" | custom-call | tf_op jit(solution)/shard_map/local_read/pallas_call | solution.py:304
  318.6 7.3 fusion.56
  326.8 18.8 %reduce-scatter.5.cloned.1.call-done = f32[1024,1024]{1,0:T(8,128)} async-done(((f32[2048,1024]{1,0:T(8,128)}), f32[1024,1024]{1,0:T(8,128)}) %reduce-scatter.5.cloned.1.call-update) | async-done | bytes 4194320 | tf_op jit(solution)/shard_map/reduce_scatter | solution.py:537
  345.6 2.8 multiply_reduce_fusion.2
  348.4 2.0 copy-done.2
  350.5 1.7 multiply_convert_fusion.1
  352.3 9.8 all-gather.9.cloned.1.call-done
  362.1 15.7 %fusion.57 = f32[2048,2048]{1,0:T(8,128)} fusion(bf16[2048,1024]{1,0:T(8,128)(2,1)} %all-gather.9.cloned.1.call-done, bf16[2048,1024]{1,0:T(8,128)(2,1)} %param.34), kind=kOutput, calls=%fused_computation.113 | convolution fusion | flops 8589934592 | bytes 25165824 | tf_op jit(solution)/shard_map/dot_general | solution.py:46
  377.7 1.3 all-gather.7.cloned.1.call-done
  379.0 28.9 %fusion.6 = (bf16[2048,2048]{1,0:T(8,128)(2,1)}, f32[2048,2048]{1,0:T(8,128)}) fusion(f32[2048,2048]{1,0:T(8,128)} %fusion.57, bf16[2048,1024]{1,0:T(8,128)(2,1)} %all-gather.7.cloned.1.call-done, bf16[1024,2048]{1,0:T(8,128)(2,1)} %param.33), kind=kOutput, calls=%fused_computation.8 | convolution fusion | flops 8673820672 | bytes 50331648 | tf_op jit(solution)/shard_map/dot_general | solution.py:36
  407.9 14.7 %fusion.58 = f32[2048,1024]{1,0:T(8,128)} fusion(bf16[2048,2048]{1,0:T(8,128)(2,1)} %get-tuple-element.75, bf16[1024,2048]{1,0:T(8,128)(2,1)} %param.33), kind=kOutput, calls=%fused_computation.114 | convolution fusion | flops 8589934592 | bytes 20971520 | tf_op jit(solution)/shard_map/dot_general | solution.py:46
  422.7 18.2 %reduce-scatter.9.cloned.1.call-done = f32[1024,1024]{1,0:T(8,128)} async-done(((f32[2048,1024]{1,0:T(8,128)}), f32[1024,1024]{1,0:T(8,128)}) %reduce-scatter.9.cloned.1.call-update) | async-done | bytes 4194320 | tf_op jit(solution)/shard_map/reduce_scatter | solution.py:560
  440.9 5.2 multiply_reduce_fusion
  446.8 2.4 fusion.54
  450.4 13.9 %all-gather.11.cloned.1.call-done = bf16[2048,1024]{1,0:T(8,128)(2,1)} async-done(((bf16[1024,1024]{1,0:T(8,128)(2,1)}), bf16[2048,1024]{1,0:T(8,128)(2,1)}) %all-gather.11.cloned.1.call-update) | async-done | bytes 4194320 | tf_op jit(solution)/shard_map/all_gather | solution.py:567
  464.2 5.9 convolution_convert_fusion.6.delta_ref
  470.1 68.4 %recall_back.1 = (f32[2048,512]{1,0:T(8,128)}, f32[4,8,128]{2,1,0:T(8,128)}) custom-call(f32[4]{0:T(128)} %add_divide_fusion.gate_ref, bf16[524288,128]{1,0:T(8,128)(2,1)} %bitcast.4.found_ref, bf16[2048,1536]{1,0:T(8,128)(2,1)} %convolution_convert_fusion.query_ref.key_ref.value_ref, bf16[2048,512]{1,0:T(8,128)(2,1)} %convolution_convert_fusion.6.delta_ref), custom_call_target="tpu_custom_call" | custom-call | tf_op jit(solution)/shard_map/recall_back/pallas_call | solution.py:235
  538.5 42.1 %local_back.1 = (bf16[2048,512]{1,0:T(8,128)(2,1)}, bf16[2048,512]{1,0:T(8,128)(2,1)}, bf16[2048,512]{1,0:T(8,128)(2,1)}, f32[4,8,1024]{2,1,0:T(8,128)}, f32[4,24,256]{2,1,0:T(8,128)}) custom-call(f32[4]{0:T(128)} %add_divide_fusion.gate_ref, f32[4,2]{1,0:T(4,128)} %pad_maximum_fusion.far_ref, f32[4,1,1024]{2,1,0:T(1,128)} %broadcast_in_dim.48.column_ref, ...), custom_call_target="tpu_custom_call" | custom-call | tf_op jit(solution)/shard_map/local_back/pallas_call | solution.py:430
  580.6 1.9 constant_dynamic-update-slice_fusion.5
  583.6 2.7 copy-done.20
  586.3 8.3 convolution_convert_fusion.2
  594.7 16.5 %convolution_convert_fusion.4 = bf16[2048,1024]{1,0:T(8,128)(2,1)} fusion(bf16[2048,1024]{1,0:T(8,128)(2,1)} %param.34, f32[2048,2048]{1,0:T(8,128)} %get-tuple-element.76), kind=kOutput, calls=%fused_computation.37 | convolution fusion | flops 8629780480 | bytes 25165824 | tf_op jit(solution)/shard_map/dot_general | solution.py:36
  611.3 14.2 %convolution_convert_fusion.3 = bf16[1024,2048]{1,0:T(8,128)(2,1)} fusion(bf16[2048,1024]{1,0:T(8,128)(2,1)} %all-gather.7.cloned.1.call-done, bf16[2048,2048]{1,0:T(8,128)(2,1)} %get-tuple-element.75), kind=kOutput, calls=%fused_computation.36 | convolution fusion | flops 8592031744 | bytes 16777216 | tf_op jit(solution)/shard_map/dot_general | solution.py:40
  625.5 16.1 %convolution_convert_fusion.5 = bf16[2048,1024]{1,0:T(8,128)(2,1)} fusion(bf16[2048,1024]{1,0:T(8,128)(2,1)S(1)} %copy-done.44, f32[2048,2048]{1,0:T(8,128)} %get-tuple-element.76), kind=kOutput, calls=%fused_computation.38 | convolution fusion | flops 8629780480 | bytes 25165824 | tf_op jit(solution)/shard_map/dot_general | solution.py:40
  641.7 7.6 convolution_convert_fusion.1
  649.3 1.7 fusion.55
  652.0 1.2 copy-done.45
  653.2 3.4 convolution_convert_fusion.7
  658.8 37.0 %all-reduce.1 = (bf16[32,4]{0,1:T(4,128)(2,1)S(1)}, bf16[4]{0:T(256)(128)(2,1)S(1)}) all-reduce(bf16[32,4]{0,1:T(4,128)(2,1)S(1)} %convert_element_type.243, bf16[4]{0:T(256)(128)(2,1)S(1)} %fusion.53), channel_id=1, replica_groups=mesh['dp'=16,'tensor'=2] {'dp'}, use_global_device_ids=true, to_apply=%region_17.18 | all-reduce | flops 132 | bytes 528 | tf_op jit(solution)/shard_map/psum | solution.py:611
  696.9 3.4 fusion.10
  700.3 47.7 %all-reduce = (f32[1024]{0:T(1024)}, f32[1024]{0:T(1024)}) all-reduce(f32[1024]{0:T(1024)S(1)} %get-tuple-element.52, f32[1024]{0:T(1024)S(1)} %copy-done.37), channel_id=1, replica_groups=mesh['dp'=16,'tensor'=2] {'dp','tensor'}, use_global_device_ids=true, to_apply=%region_9.10 | all-reduce | flops 2048 | bytes 16384 | tf_op jit(solution)/shard_map/psum | solution.py:623
  748.0 8.1 fusion.13
  756.1 267.1 %all-reduce.5.cloned.1.call-done = (bf16[1024,512]{1,0:T(8,128)(2,1)}, bf16[1024,512]{1,0:T(8,128)(2,1)}, bf16[1024,512]{1,0:T(8,128)(2,1)}, bf16[512,1024]{1,0:...) async-done(((bf16[1024,512]{1,0:T(8,128)(2,1)}, bf16[1024,512]{1,0:T(8,128)(2,1)}, bf16[1024,512]{1,0:T(8,128)(2,1)}, bf16[512,1024]{1,0:T(8,128)(2,1)}, ...) | async-done | bytes 12582928 | tf_op jit(solution)/shard_map/psum | solution.py:611
  1023.2 6.8 convert_element_type.248
  1030.0 4.4 convert_element_type.250
  1034.5 1.6 convert_element_type.238
  1036.1 1.6 convert_element_type.239
  1037.7 1.6 convert_element_type.240
  1039.3 1.6 convert_element_type.242
  (152 shorter events, 14.9 us)
Async XLA Ops:
  7.2 311.5 %copy-start = (bf16[512,1024]{1,0:T(8,128)(2,1)S(1)}, bf16[512,1024]{1,0:T(8,128)(2,1)}, u32[]{:S(2)}) copy-start(bf16[512,1024]{1,0:T(8,128)(2,1)} %param.29) | copy-start | bytes 3145732
  7.2 7.0 copy-start.16
  7.2 211.4 %all-gather.5.cloned.1.call-start = ((), (), s32[]{:S(2)}) async-start(), calls=%async_computation.4 | async-start | bytes 6291456 | tf_op jit(solution)/shard_map/all_gather | solution.py:515
  14.1 331.4 %reduce-scatter.5.cloned.1.call-start = ((), (), s32[]{:S(2)}) async-start(), calls=%async_computation.5 | async-start | bytes 12582912 | tf_op jit(solution)/shard_map/reduce_scatter | solution.py:537
  14.4 6.8 copy-start.39
  63.8 149.8 %copy-start.17 = (bf16[1024,512]{1,0:T(8,128)(2,1)S(1)}, bf16[1024,512]{1,0:T(8,128)(2,1)}, u32[]{:S(2)}) copy-start(bf16[1024,512]{1,0:T(8,128)(2,1)} %param.26) | copy-start | bytes 3145732
  63.8 149.9 %copy-start.18 = (bf16[1024,512]{1,0:T(8,128)(2,1)S(1)}, bf16[1024,512]{1,0:T(8,128)(2,1)}, u32[]{:S(2)}) copy-start(bf16[1024,512]{1,0:T(8,128)(2,1)} %param.27) | copy-start | bytes 3145732
  212.8 3.0 copy-start.41
  212.9 3.5 copy-start.36
  326.0 19.6 %copy-start.4 = (bf16[1024,1024]{1,0:T(8,128)(2,1)S(1)}, bf16[1024,1024]{1,0:T(8,128)(2,1)}, u32[]{:S(2)}) copy-start(bf16[1024,1024]{1,0:T(8,128)(2,1)} %param.20) | copy-start | bytes 6291460
  326.0 36.0 %all-gather.9.cloned.1.call-start = ((), (), s32[]{:S(2)}) async-start(), calls=%async_computation.8 | async-start | bytes 6291456 | tf_op jit(solution)/shard_map/all_gather | solution.py:554
  326.7 23.7 %copy-start.26 = (f32[1024]{0:T(1024)S(1)}, f32[1024]{0:T(1024)}, u32[]{:S(2)}) copy-start(f32[1024]{0:T(1024)} %param.32) | copy-start | bytes 12292
  326.8 52.2 %all-gather.7.cloned.1.call-start = ((), (), s32[]{:S(2)}) async-start(), calls=%async_computation.6 | async-start | bytes 6291456 | tf_op jit(solution)/shard_map/all_gather | solution.py:542
  348.4 97.7 %copy-start.24 = (f32[1024]{0:T(1024)}, f32[1024]{0:T(1024)S(1)}, u32[]{:S(2)}) copy-start(f32[1024]{0:T(1024)S(1)} %fusion.50) | copy-start | bytes 12292
  352.2 88.6 %reduce-scatter.9.cloned.1.call-start = ((), (), s32[]{:S(2)}) async-start(), calls=%async_computation.9 | async-start | bytes 12582912 | tf_op jit(solution)/shard_map/reduce_scatter | solution.py:560
  422.6 24.1 %copy-start.7 = (bf16[1024,1024]{1,0:T(8,128)(2,1)S(1)}, bf16[1024,1024]{1,0:T(8,128)(2,1)}, u32[]{:S(2)}) copy-start(bf16[1024,1024]{1,0:T(8,128)(2,1)} %param.35) | copy-start | bytes 6291460
  422.6 41.6 %all-gather.11.cloned.1.call-start = ((), (), s32[]{:S(2)}) async-start(), calls=%async_computation.10 | async-start | bytes 6291456 | tf_op jit(solution)/shard_map/all_gather | solution.py:567
  440.9 5.8 copy-start.3
  440.9 5.9 copy-start.6
  446.8 2.5 copy-start.40
  449.2 247.7 %reduce-scatter.11.cloned.1.call-start = ((), (), s32[]{:S(2)}) async-start(), calls=%async_computation.11 | async-start | bytes 6291456 | tf_op jit(solution)/shard_map/reduce_scatter | solution.py:592
  580.6 2.2 copy-start.10
  580.6 2.8 copy-start.9
  582.8 3.5 copy-start.22
  583.6 2.7 copy-start.20
  594.6 153.4 %reduce-scatter.7.cloned.1.call-start = ((), (), s32[]{:S(2)}) async-start(), calls=%async_computation.7 | async-start | bytes 6291456 | tf_op jit(solution)/shard_map/reduce_scatter | solution.py:547
  611.2 412.0 %all-reduce.5.cloned.1.call-start = ((), (), s32[]{:S(2)}) async-start(), calls=%async_computation.12 | async-start | bytes 25165824 | tf_op jit(solution)/shard_map/psum | solution.py:611
  611.3 14.2 %copy-start.44 = (bf16[2048,1024]{1,0:T(8,128)(2,1)S(1)}, bf16[2048,1024]{1,0:T(8,128)(2,1)}, u32[]{:S(2)}) copy-start(bf16[2048,1024]{1,0:T(8,128)(2,1)} %all-gather.9.cloned.1.call-done) | copy-start | bytes 12582916
  611.3 30.4 %slice-start = ((s8[6291456]{0:T(1024)(128)(4,1)}), s8[4194304]{0:T(1024)(128)(4,1)S(1)}, s32[]{:S(2)}) async-start(s8[6291456]{0:T(1024)(128)(4,1)} %bitcast.34), calls=%async_computation.13 | async-start | bytes 8388608
  625.5 16.2 %slice-start.1 = ((s8[6291456]{0:T(1024)(128)(4,1)}), s8[2097152]{0:T(1024)(128)(4,1)S(1)}, s32[]{:S(2)}) async-start(s8[6291456]{0:T(1024)(128)(4,1)} %bitcast.34), calls=%async_computation.14 | async-start | bytes 4194304
  625.5 16.2 %copy-start.43 = (bf16[2048,1024]{1,0:T(8,128)(2,1)S(1)}, bf16[2048,1024]{1,0:T(8,128)(2,1)}, u32[]{:S(2)}) copy-start(bf16[2048,1024]{1,0:T(8,128)(2,1)} %all-gather.5.cloned.1.call-done) | copy-start | bytes 12582916
  649.2 2.7 copy-start.11
  649.2 4.0 copy-start.45
  656.6 2.2 copy-start.42
  656.6 40.3 %copy-start.5 = (bf16[1024,1024]{1,0:T(8,128)(2,1)S(1)}, bf16[1024,1024]{1,0:T(8,128)(2,1)}, u32[]{:S(2)}) copy-start(bf16[1024,1024]{1,0:T(8,128)(2,1)} %param.20) | copy-start | bytes 6291460
  656.6 40.3 %copy-start.29 = (f32[1024]{0:T(1024)S(1)}, f32[1024]{0:T(1024)}, u32[]{:S(2)}) copy-start(f32[1024]{0:T(1024)} %copy-done.28) | copy-start | bytes 12292
  656.6 40.3 %copy-start.35 = (f32[1024]{0:T(1024)S(1)}, f32[1024]{0:T(1024)}, u32[]{:S(2)}) copy-start(f32[1024]{0:T(1024)} %param.25) | copy-start | bytes 12292
  656.6 43.6 %copy-start.37 = (f32[1024]{0:T(1024)S(1)}, f32[1024]{0:T(1024)}, u32[]{:S(2)}) copy-start(f32[1024]{0:T(1024)} %get-tuple-element.50) | copy-start | bytes 12292
  656.7 91.3 %copy-start.32 = (f32[1024]{0:T(1024)S(1)}, f32[1024]{0:T(1024)}, u32[]{:S(2)}) copy-start(f32[1024]{0:T(1024)} %copy-done.31) | copy-start | bytes 12292
  656.7 91.4 %copy-start.25 = (f32[1024]{0:T(1024)S(1)}, f32[1024]{0:T(1024)}, u32[]{:S(2)}) copy-start(f32[1024]{0:T(1024)} %copy-done.24) | copy-start | bytes 12292
  656.7 91.4 %copy-start.27 = (f32[1024]{0:T(1024)S(1)}, f32[1024]{0:T(1024)}, u32[]{:S(2)}) copy-start(f32[1024]{0:T(1024)} %param.32) | copy-start | bytes 12292
  656.7 91.3 %copy-start.34 = (f32[1024]{0:T(1024)S(1)}, f32[1024]{0:T(1024)}, u32[]{:S(2)}) copy-start(f32[1024]{0:T(1024)} %copy-done.33) | copy-start | bytes 12292
  1023.2 6.8 copy-start.8
  1030.0 4.4 copy-start.15
  1030.0 6.1 copy-start.14
  1034.4 3.2 copy-start.13
  1034.5 4.8 copy-start.12
  1036.1 4.8 copy-start.1
  (9 other events, 10.8 us)
Sparse Core Ops, SparseCore 0:
  14.3 16.1 all-gather.4
  326.1 19.4 reduce-scatter.4
  347.2 14.8 all-gather.8
  364.1 14.8 all-gather.6
  422.8 18.0 reduce-scatter.8
  449.4 14.8 all-gather.10
  594.8 13.2 reduce-scatter.10
  611.3 13.2 reduce-scatter.6
  656.8 366.3 all-reduce.4

commit v2 on v1

--- a/solution.py
+++ b/solution.py
@@ -50,7 +50,6 @@
 
 def interleave_kernel(key_ref, value_ref, table_ref):
     rows = key_ref.shape[1]
-    flat = table_ref.reshape(1, 2 * rows, 128)
     row = lax.broadcasted_iota(jnp.int32, (256, 256), 0)
     column = lax.broadcasted_iota(jnp.int32, (256, 256), 1)
     order = jnp.where(column == (row // 2 + (row % 2) * 128), 1.0, 0.0).astype(low_type)
@@ -58,7 +57,7 @@
         both = jnp.concatenate(
             [key_ref[0, pl.ds(part * 128, 128)], value_ref[0, pl.ds(part * 128, 128)]], 0
         )
-        flat[0, pl.ds(part * 256, 256)] = dot_rows(order, both).astype(low_type)
+        table_ref[pl.ds(part * 256, 256), :] = dot_rows(order, both).astype(low_type)
 
 
 def interleave(memory_keys, memory_values):
@@ -69,10 +68,15 @@
         interleave_kernel,
         grid=(heads, rows // step),
         in_specs=[spec, spec],
-        out_specs=pl.BlockSpec((1, step, 2, width), lambda h, i: (h, i, 0, 0)),
-        out_shape=jax.ShapeDtypeStruct((heads, rows, 2, width), low_type),
+        out_specs=pl.BlockSpec((2 * step, width), lambda h, i: (h * (rows // step) + i, 0)),
+        out_shape=jax.ShapeDtypeStruct((heads * rows * 2, width), low_type),
+        cost_estimate=pl.CostEstimate(
+            flops=heads * rows * 4 * 256 * width,
+            bytes_accessed=heads * rows * width * 8,
+            transcendentals=0,
+        ),
         name="interleave",
-    )(memory_keys, memory_values)
+    )(memory_keys, memory_values).reshape(heads, rows, 2, width)
 
 
 def gather_kernel(
@@ -143,6 +147,9 @@
             pltpu.SemaphoreType.DMA((2,)),
         ],
         compiler_params=pltpu.CompilerParams(vmem_limit_bytes=vmem_most),
+        cost_estimate=pl.CostEstimate(
+            flops=0, bytes_accessed=4 * heads * total * width * 4, transcendentals=0
+        ),
         name="gather_found",
     )(index_rows.reshape(-1, chunk // 128, 128), table.reshape(heads * rows, 2, width))
 
@@ -176,7 +183,7 @@
 def recall(found, queries, heads, picks, scale):
     tokens = queries.shape[0]
     width = queries.shape[1] // (3 * heads)
-    step = min(256, tokens)
+    step = min(512, tokens)
     blocks = tokens // step
     return pl.pallas_call(
         functools.partial(recall_kernel, picks, scale),
@@ -188,6 +195,9 @@
         out_specs=pl.BlockSpec((step, width), lambda h, i: (i, h)),
         out_shape=jax.ShapeDtypeStruct((tokens, heads * width), full_type),
         compiler_params=pltpu.CompilerParams(vmem_limit_bytes=vmem_most),
+        cost_estimate=pl.CostEstimate(
+            flops=0, bytes_accessed=heads * tokens * picks * width * 8, transcendentals=0
+        ),
         name="recall",
     )(found, queries)
 
@@ -229,7 +239,7 @@
 def recall_back(found, queries, mixed_delta, gates, heads, picks, scale):
     tokens = queries.shape[0]
     width = mixed_delta.shape[1] // heads
-    step = min(256, tokens)
+    step = min(512, tokens)
     blocks = tokens // step
     rows_spec = pl.BlockSpec((step, width), lambda h, i: (i, h))
     return pl.pallas_call(
@@ -247,6 +257,9 @@
             jax.ShapeDtypeStruct((heads, 8, 128), full_type),
         ],
         compiler_params=pltpu.CompilerParams(vmem_limit_bytes=vmem_most),
+        cost_estimate=pl.CostEstimate(
+            flops=0, bytes_accessed=heads * tokens * picks * width * 8, transcendentals=0
+        ),
         name="recall_back",
     )(gates, found, queries, mixed_delta)
 
@@ -319,6 +332,9 @@
         out_shape=jax.ShapeDtypeStruct((tokens, heads * width), low_type),
         scratch_shapes=[pltpu.VMEM((tile, span), full_type)],
         compiler_params=pltpu.CompilerParams(vmem_limit_bytes=vmem_most),
+        cost_estimate=pl.CostEstimate(
+            flops=0, bytes_accessed=heads * tokens * seq_len * 20, transcendentals=0
+        ),
         name="local_read",
     )(gates, far, columns, projected, projected, projected, query_mask, key_mask, recalled)
 
@@ -463,6 +479,9 @@
             pltpu.VMEM((seq_len, width), full_type),
         ],
         compiler_params=pltpu.CompilerParams(vmem_limit_bytes=vmem_most),
+        cost_estimate=pl.CostEstimate(
+            flops=0, bytes_accessed=heads * tokens * seq_len * 40, transcendentals=0
+        ),
         name="local_back",
     )(
         gates, far, columns, projected, projected, projected, query_mask, key_mask, mixed_delta,
@@ -476,6 +495,40 @@
     query_mask = jnp.where((gap >= 0) & (gap <= 1), 0.0, mask_gap).astype(low_type)
     key_mask = (gap == 0).astype(low_type)
     return query_mask, key_mask
+
+
+def fetch(rows):
+    group = lax.axis_size("tensor")
+    return [rows] + [
+        lax.ppermute(rows, "tensor", [((i + k) % group, i) for i in range(group)])
+        for k in range(1, group)
+    ]
+
+
+def in_order(shares):
+    group = lax.axis_size("tensor")
+    rows = shares[0].shape[0]
+    whole = jnp.zeros((group * rows,) + shares[0].shape[1:], shares[0].dtype)
+    for k in range(group):
+        start = ((lax.axis_index("tensor") + k) % group) * rows
+        whole = lax.dynamic_update_slice_in_dim(whole, shares[k], start, 0)
+    return whole
+
+
+def share_of(whole, k, rows):
+    start = ((lax.axis_index("tensor") + k) % lax.axis_size("tensor")) * rows
+    return lax.dynamic_slice_in_dim(whole, start, rows, 0)
+
+
+def fold(term, piece):
+    group = lax.axis_size("tensor")
+    sent = [
+        lax.ppermute(
+            term(piece(k)).astype(low_type), "tensor", [(i, (i + k) % group) for i in range(group)]
+        )
+        for k in range(1, group)
+    ]
+    return sum((part.astype(full_type) for part in sent), term(piece(0)))
 
 
 def body(
@@ -502,8 +555,6 @@
     picks = memory_index.shape[2]
     inner_width = head_count * head_width
     scale = head_width ** (-0.5)
-    group = lax.axis_size("tensor")
-    group_rows = share_rows * group
 
     offsets = jnp.arange(head_count, dtype=jnp.int32) * memory_rows
     index_rows = memory_index.transpose(1, 0, 2) + offsets[:, None, None]
@@ -534,39 +585,38 @@
     mixed_rows = local_read(
         projected, query_mask, key_mask, recalled, ahead_columns, far, gates, seq_len, scale
     )
-    middle = token_full + lax.psum_scatter(
-        dot_rows(mixed_rows, output_weight), "tensor", scatter_dimension=0, tiled=True
+    middle = token_full + fold(
+        lambda rows: dot_rows(rows, output_weight), lambda k: share_of(mixed_rows, k, share_rows)
     )
     second_rows = rms_scaled(middle, mlp_gain).astype(low_type)
-    grad_rows = grad_output.astype(full_type)
-    second = lax.all_gather(second_rows, "tensor", axis=0, tiled=True)
+    grad_full = jnp.concatenate(fetch(grad_output), 0)
+    second = jnp.concatenate(fetch(second_rows), 0)
     hidden = dot_rows(second, hidden_weight)
     active = jax.nn.gelu(hidden).astype(low_type)
-    layer_output = (
-        middle
-        + lax.psum_scatter(
-            dot_rows(active, return_weight).astype(low_type),
-            "tensor",
-            scatter_dimension=0,
-            tiled=True,
-        ).astype(full_type)
-    ).astype(low_type)
-    grad_full = lax.all_gather(grad_output, "tensor", axis=0, tiled=True)
-    return_part = dot_outer(active, grad_full)
+    return_low = dot_outer(active, grad_full).astype(low_type)
+    return_sum = lax.psum(return_low, "dp")
     active_delta = dot_inner(grad_full, return_weight)
     gelu_back = jax.vjp(jax.nn.gelu, hidden)[1]
     hidden_delta = gelu_back(active_delta)[0].astype(low_type)
-    hidden_part = dot_outer(second, hidden_delta)
-    second_delta = lax.psum_scatter(
-        dot_inner(hidden_delta, hidden_weight), "tensor", scatter_dimension=0, tiled=True
-    )
+    second_delta = fold(
+        lambda rows: dot_inner(rows, hidden_weight),
+        lambda k: lax.slice_in_dim(hidden_delta, k * share_rows, (k + 1) * share_rows),
+    )
+    hidden_low = dot_outer(second, hidden_delta).astype(low_type)
+    hidden_low, return_sum = lax.optimization_barrier((hidden_low, return_sum))
+    hidden_sum = lax.psum(hidden_low, "dp")
     second_back = jax.vjp(rms_scaled, middle, mlp_gain)[1]
     middle_part, mlp_gain_part = second_back(second_delta)
-    middle_delta = grad_rows + middle_part
-    middle_low = middle_delta.astype(low_type)
-    middle_full = lax.all_gather(middle_low, "tensor", axis=0, tiled=True)
-    output_part = dot_outer(mixed_rows, middle_full)
+    middle_delta = grad_output.astype(full_type) + middle_part
+    middle_full = in_order(fetch(middle_delta.astype(low_type)))
     mixed_delta = dot_inner(middle_full, output_weight).astype(low_type)
+    layer_output = (
+        middle
+        + fold(
+            lambda rows: dot_rows(rows, return_weight),
+            lambda k: lax.slice_in_dim(active, k * share_rows, (k + 1) * share_rows),
+        )
+    ).astype(low_type)
 
     recall_delta, recall_sums = recall_back(
         found, projected, mixed_delta, gates, head_count, picks, scale
@@ -575,65 +625,55 @@
         projected, query_mask, key_mask, mixed_delta, recall_delta, behind_columns, far, gates,
         seq_len, scale,
     )
+    output_part = dot_outer(mixed_rows, middle_full)
     recall_gain = jnp.sum(recall_sums[:, :, 0], 1)
     local_gain = jnp.sum(local_sums[:, 0], 1)
     gate_part = gates * (1.0 - gates) * recall_gain - gates * local_gain
     diagonal_sums = jnp.sum(diagonals, 1)
-    table_part = jnp.dot(diagonal_sums, behind_hot, precision=exact_mode).T
+    table_part = jnp.dot(diagonal_sums, behind_hot, precision=exact_mode)
     far_left = jnp.sum(local_sums[:, 8:16], (1, 2))
     far_right = jnp.sum(local_sums[:, 16:24], (1, 2))
-    table_part = table_part.at[15].add(far_left).at[31].add(far_right)
+    table_part = table_part + far_left[:, None] * (level == 15) + far_right[:, None] * (level == 31)
 
     project_delta = jnp.concatenate([query_delta, key_delta, value_delta], 1)
     joined_part = dot_outer(normed, project_delta)
-    query_part = joined_part[:, :inner_width]
-    key_part = joined_part[:, inner_width : 2 * inner_width]
-    value_part = joined_part[:, 2 * inner_width :]
-    normed_delta = lax.psum_scatter(
-        dot_inner(project_delta, joined).astype(low_type),
-        "tensor",
-        scatter_dimension=0,
-        tiled=True,
-    ).astype(full_type)
+    attn_gain_part = jnp.sum(joined_part * joined.astype(full_type), 1) / attn_gain
+    model_width = tokens.shape[1]
+    small = jnp.concatenate([table_part.reshape(-1), gate_part])
+    small = jnp.pad(small, (0, model_width - small.shape[0]))
+    extra = jnp.stack([attn_gain_part, mlp_gain_part, small])
+    extra = jnp.pad(extra, ((0, 13), (0, 0)))
+    last_low = (
+        jnp.concatenate([output_part, extra], 0).astype(low_type),
+        joined_part.astype(low_type),
+    )
+    last_low, hidden_sum = lax.optimization_barrier((last_low, hidden_sum))
+    output_sum, joined_sum = lax.psum(last_low, "dp")
+
+    normed_delta = fold(
+        lambda rows: dot_inner(rows, joined), lambda k: share_of(project_delta, k, share_rows)
+    )
     first_back = jax.vjp(rms_scaled, token_full, attn_gain)[1]
-    token_part, attn_gain_part = first_back(normed_delta)
-    tokens_grad = (middle_delta + token_part).astype(low_type)
-    (
-        query_grad,
-        key_grad,
-        value_grad,
-        output_weight_grad,
-        table_grad,
-        gate_grad,
-        hidden_grad,
-        return_grad,
-    ) = (
-        lax.psum(part.astype(low_type), "dp").astype(full_type)
-        for part in (
-            query_part,
-            key_part,
-            value_part,
-            output_part,
-            table_part,
-            gate_part,
-            hidden_part,
-            return_part,
-        )
-    )
-    attn_gain_grad, mlp_gain_grad = lax.psum((attn_gain_part, mlp_gain_part), ("dp", "tensor"))
+    tokens_grad = (middle_delta + first_back(normed_delta)[0]).astype(low_type)
+
+    joined_grad = joined_sum.astype(full_type)
+    output_grad = output_sum.astype(full_type)
+    gains = sum(fetch(output_grad[inner_width : inner_width + 2]))
+    small_sum = output_grad[inner_width + 2]
+    table_size = head_count * 32
     return (
         layer_output,
         tokens_grad,
-        attn_gain_grad,
-        query_grad,
-        key_grad,
-        value_grad,
-        output_weight_grad,
-        table_grad,
-        gate_grad,
-        mlp_gain_grad,
-        hidden_grad,
-        return_grad,
+        gains[0],
+        joined_grad[:, :inner_width],
+        joined_grad[:, inner_width : 2 * inner_width],
+        joined_grad[:, 2 * inner_width :],
+        output_grad[:inner_width],
+        small_sum[:table_size].reshape(head_count, 32).T,
+        small_sum[table_size : table_size + head_count],
+        gains[1],
+        hidden_sum.astype(full_type),
+        return_sum.astype(full_type),
     )
 
 

time: 1060 us -> 937 us (0.88)
  blocking collectives: 84.7 us -> 0 us
  other arithmetic: 52.3 us -> 30.2 us
  Pallas kernels: 390 us -> 372 us
  local copies, waits for them, and re-layouts: 25.1 us -> 35.7 us
    psum x2 -> x0, blocking collectives: 84.7 us -> none  [the longest x1 47.7 us: body(): lax.psum((attn_gain_part, mlp_gain_part), ('dp', 'tensor'))]
    psum x1 -> x3, waiting for transfers between devices: 267 us -> 321 us  [the longest x1 153 us: body(): output_sum, joined_sum = lax.psum(last_low, 'dp')]
    reduce_scatter x4 -> x0, waiting for transfers between devices: 37 us -> none  [the longest x1 18.8 us: body(): lax.psum_scatter(dot_rows(mixed_rows, output_weight), 'tensor', scatter_d...]
    all_gather x3 -> x0, waiting for transfers between devices: 24.9 us -> none  [the longest x1 13.9 us: body(): middle_full = lax.all_gather(middle_low, 'tensor', axis=0, tiled=True)]
    convert_element_type x12 -> x5, other arithmetic: 29.2 us -> 13.3 us  [the longest x1 4.65 us: body(): return_sum.astype(full_type)]
    dot_general x4 -> x6, matrix products: 64.1 us -> 62.4 us  [dot_rows(): return jnp.dot(left, right, preferred_element_type=full_type)]
    dot_general x4 -> x6, matrix products: 44.6 us -> 45.6 us  [dot_inner(): lax.dot_general(left, right, (((1,), (1,)), ((), ())), preferred_element_...]
  transfers between devices with their start and end apart: 9 -> 12, of which waited for: 6 -> 4; matrix products, arithmetic and copies ran while one was open for 10% -> 15% of each run, Pallas kernels for 18% -> 31%
where the time goes in v2:
time: 937 us; the launch traced here: 927 us
  Pallas kernels  372 us (40%)
  waiting for transfers between devices  323 us (34%)
  matrix products  148 us (16%)
  local copies, waits for them, and re-layouts  35.7 us (4%)
  other arithmetic  30.2 us (3%)
  between operations  14.9 us (2%)
    psum x1, waiting for transfers between devices, body(): output_sum, joined_sum = lax.psum(last_low, 'dp')  153 us
    pallas_call x1, Pallas kernels, gather_found(): pl.pallas_call(gather_kernel, grid=(heads, blocks), in_specs=[pl.BlockSpe...  149 us
    psum x1, waiting for transfers between devices, body(): return_sum = lax.psum(return_low, 'dp')  126 us
    dot_general x6, matrix products, dot_rows(): return jnp.dot(left, right, preferred_element_type=full_type)  62.4 us
    pallas_call x1, Pallas kernels, recall_back(): pl.pallas_call(functools.partial(recall_back_kernel, picks, scale), grid=...  60.8 us
    pallas_call x1, Pallas kernels, recall(): pl.pallas_call(functools.partial(recall_kernel, picks, scale), grid=(head...  59.2 us
    dot_general x6, matrix products, dot_inner(): lax.dot_general(left, right, (((1,), (1,)), ((), ())), preferred_element_...  45.6 us
    pallas_call x1, Pallas kernels, local_back(): pl.pallas_call(functools.partial(local_back_kernel, scale), grid=(heads,...  42.1 us
  transfers between devices with their start and end apart: 12, of which 4 were waited for; matrix products, arithmetic and copies ran while one was open for 15% of the time, Pallas kernels for 31%

profile of v2, /device:TPU:1, one launch (start us, length us, event | category | flops | bytes accessed | tf_op | source)
XLA Modules:
  0.0 927.2 jit_solution(8838448312893660446)
XLA Ops:
  7.2 2.2 fusion.10
  10.7 3.5 fusion.12
  14.4 2.7 copy.34
  17.1 4.1 reshape.162.index_hbm
  22.3 39.9 %interleave.1 = bf16[131072,128]{1,0:T(8,128)(2,1)} custom-call(bf16[4,16384,128]{2,1,0:T(8,128)(2,1)} %key_ref.1, bf16[4,16384,128]{2,1,0:T(8,128)(2,1)} %value_ref.1), custom_call_target="tpu_custom_call" | custom-call | flops 8589934592 | bytes 67108864 | tf_op jit(solution)/shard_map/interleave/pallas_call | solution.py:67
  62.2 149.0 %gather_found.1 = bf16[262144,2,128]{2,1,0:T(2,128)(2,1)} custom-call(s32[64,32,128]{2,1,0:T(8,128)} %reshape.162.index_hbm, bf16[65536,2,128]{2,1,0:T(2,128)(2,1)} %bitcast.36), custom_call_target="tpu_custom_call" | custom-call | bytes 536870912 | tf_op jit(solution)/shard_map/gather_found/pallas_call | solution.py:136
  212.5 1.6 copy-done.22
  214.6 1.1 fusion.47.key_mask_ref
  215.8 1.2 select_convert_fusion.query_mask_ref
  216.9 11.3 %convolution_convert_fusion.query_ref.key_ref.value_ref = bf16[2048,1536]{1,0:T(8,128)(2,1)} fusion(bf16[2048,1024]{1,0:T(8,128)(2,1)} %all-gather.2.cloned.1.call-done, bf16[1024,1536]{1,0:T(8,128)(2,1)} %copy-done.22), kind=kOutput, calls=%fused_computation.15 | convolution fusion | flops 6445596672 | bytes 13631488 | tf_op jit(solution)/shard_map/dot_general | solution.py:36
  228.2 59.2 %recall.1.recall_ref = f32[2048,512]{1,0:T(8,128)} custom-call(bf16[524288,128]{1,0:T(8,128)(2,1)} %bitcast.4.found_ref, bf16[2048,1536]{1,0:T(8,128)(2,1)} %convolution_convert_fusion.query_ref.key_ref.value_ref), custom_call_target="tpu_custom_call" | custom-call | bytes 268435456 | tf_op jit(solution)/shard_map/recall/pallas_call | solution.py:188
  287.5 21.0 %local_read.1 = bf16[2048,512]{1,0:T(8,128)(2,1)} custom-call(f32[4]{0:T(128)} %add_divide_fusion.gate_ref, f32[4,2]{1,0:T(4,128)} %pad_maximum_fusion.4.far_ref, f32[4,1,1024]{2,1,0:T(1,128)} %broadcast_in_dim.27.column_ref, bf16[2048,1536]{1,0:T(8,128)(2,1)} %convolution_convert_fusion.query_ref.key_ref.value_ref, ...), custom_call_target="tpu_custom_call" | custom-call | bytes 167772160 | tf_op jit(solution)/shard_map/local_read/pallas_call | solution.py:317
  308.4 3.8 convolution_convert_fusion.4
  312.8 1.9 constant_dynamic-update-slice_fusion.4
  314.7 2.0 collective-permute-done
  316.7 3.2 multiply_reduce_fusion.3
  320.0 2.1 copy-done.1
  322.7 2.8 constant_dynamic-update-slice_fusion.3
  325.6 11.7 %fusion.98 = f32[2048,2048]{1,0:T(8,128)} fusion(bf16[2048,1024]{1,0:T(8,128)(2,1)S(1)} %constant_dynamic-update-slice_fusion.3, bf16[2048,1024]{1,0:T(8,128)(2,1)S(1)} %copy-done.39), kind=kOutput, calls=%fused_computation.157 | convolution fusion | flops 8589934592 | bytes 25165824 | tf_op jit(solution)/shard_map/dot_general | solution.py:46
  337.3 26.0 %fusion.6 = (bf16[2048,2048]{1,0:T(8,128)(2,1)}, bf16[2048,2048]{1,0:T(8,128)(2,1)}) fusion(f32[2048,2048]{1,0:T(8,128)} %fusion.98, bf16[1024,2048]{1,0:T(8,128)(2,1)S(1)} %copy-done.40, bf16[1024,1024]{1,0:T(8,128)(2,1)} %collective-permute-done.1, bf16[1024,1024]{1,0:T(8,128)(2,1)S(1)} %multiply_convert_fusion.1), kind=kOutput, calls=%fused_computation.8 | convolution fusion | flops 8690597888 | bytes 41943040 | tf_op jit(solution)/shard_map/dot_general | solution.py:36
  363.3 8.0 fusion.27
  371.7 5.7 fusion.30
  377.5 13.2 %convolution_convert_fusion.2 = bf16[2048,1024]{1,0:T(8,128)(2,1)} fusion(bf16[2048,2048]{1,0:T(8,128)(2,1)} %get-tuple-element.46, bf16[2048,1024]{1,0:T(8,128)(2,1)S(1)} %constant_dynamic-update-slice_fusion.3), kind=kOutput, calls=%fused_computation.43 | convolution fusion | flops 8592031744 | bytes 16777216 | tf_op jit(solution)/shard_map/dot_general | solution.py:40
  390.9 10.1 %fusion.20 = f32[1024,1024]{1,0:T(8,128)} fusion(bf16[2048,1024]{1,0:T(8,128)(2,1)} %param.30, bf16[2048,2048]{1,0:T(8,128)(2,1)} %get-tuple-element.46), kind=kOutput, calls=%fused_computation.32 | convolution fusion | flops 4294967296 | bytes 12582912 | tf_op jit(solution)/shard_map/dot_general | solution.py:36
  401.0 12.1 %multiply_reduce_fusion.1 = (bf16[1024]{0:T(1024)(128)(2,1)S(1)}, f32[1024]{0:T(1024)S(1)}, bf16[1024,1024]{1,0:T(8,128)(2,1)}, f32[1024,1024]{1,0:T(8,128)S(1)}) fusion(f32[1024,1024]{1,0:T(8,128)S(1)} %copy-done.2, f32[1024]{0:T(1024)S(1)} %fusion.83, bf16[1024,1024]{1,0:T(8,128)(2,1)S(1)} %collective-permute-done.4, f32[1024]{0:T(1024)S(1)} %copy-done.33, ...), kind=kOutput, calls=%fused_computation.35 | convolution fusion | flops 4307548160 | bytes 27277312 | tf_op jit(solution)/shard_map/dot_general | solution.py:46
  413.7 5.6 constant_dynamic-update-slice_fusion.9
  419.3 2.0 copy-done.12
  422.6 12.3 %convolution_convert_fusion.1 = bf16[1024,2048]{1,0:T(8,128)(2,1)} fusion(bf16[2048,2048]{1,0:T(8,128)(2,1)S(1)} %bitcast.43, bf16[1024,1024]{1,0:T(8,128)(2,1)} %collective-permute-done.1, bf16[1024,1024]{1,0:T(8,128)(2,1)S(1)} %copy-done.14), kind=kOutput, calls=%fused_computation.42 | convolution fusion | flops 8600420352 | bytes 16777216 | tf_op jit(solution)/shard_map/dot_general | solution.py:40
  434.9 126.2 %all-reduce.7.cloned.1.call-done = bf16[2048,1024]{1,0:T(8,128)(2,1)} async-done(((bf16[2048,1024]{1,0:T(8,128)(2,1)}), bf16[2048,1024]{1,0:T(8,128)(2,1)}) %all-reduce.7.cloned.1.call-update) | async-done | bytes 4194320 | tf_op jit(solution)/shard_map/psum | solution.py:597
  561.1 1.5 constant_dynamic-update-slice_fusion.8
  562.7 5.9 convolution_convert_fusion.3.delta_ref
  568.6 60.8 %recall_back.1 = (f32[2048,512]{1,0:T(8,128)}, f32[4,8,128]{2,1,0:T(8,128)}) custom-call(f32[4]{0:T(128)} %add_divide_fusion.gate_ref, bf16[524288,128]{1,0:T(8,128)(2,1)} %bitcast.4.found_ref, bf16[2048,1536]{1,0:T(8,128)(2,1)} %convolution_convert_fusion.query_ref.key_ref.value_ref, bf16[2048,512]{1,0:T(8,128)(2,1)} %convolution_convert_fusion.3.delta_ref), custom_call_target="tpu_custom_call" | custom-call | bytes 268435456 | tf_op jit(solution)/shard_map/recall_back/pallas_call | solution.py:245
  629.4 42.1 %local_back.1 = (bf16[2048,512]{1,0:T(8,128)(2,1)}, bf16[2048,512]{1,0:T(8,128)(2,1)}, bf16[2048,512]{1,0:T(8,128)(2,1)}, f32[4,8,1024]{2,1,0:T(8,128)}, f32[4,24,256]{2,1,0:T(8,128)}) custom-call(f32[4]{0:T(128)} %add_divide_fusion.gate_ref, f32[4,2]{1,0:T(4,128)} %pad_maximum_fusion.4.far_ref, f32[4,1,1024]{2,1,0:T(1,128)} %broadcast_in_dim.31.column_ref, ...), custom_call_target="tpu_custom_call" | custom-call | bytes 335544320 | tf_op jit(solution)/shard_map/local_back/pallas_call | solution.py:446
  671.5 1.9 constant_dynamic-update-slice_fusion.7
  674.5 1.4 copy-done.23
  676.0 1.5 copy-done.41
  677.5 9.1 fusion.95
  687.7 4.5 convolution_convert_fusion.5
  693.3 41.5 %all-reduce.9.cloned.1.call-done = bf16[1024,2048]{1,0:T(8,128)(2,1)} async-done(((bf16[1024,2048]{1,0:T(8,128)(2,1)}), bf16[1024,2048]{1,0:T(8,128)(2,1)}) %all-reduce.9.cloned.1.call-update) | async-done | bytes 4194320 | tf_op jit(solution)/shard_map/psum | solution.py:607
  734.8 6.4 fusion.33
  742.0 4.7 convert_element_type.264
  746.8 3.7 fusion.13
  750.5 2.6 fusion.9
  753.1 4.4 convert_element_type.263
  757.6 153.2 %all-reduce.11.cloned.1.call-done = (bf16[528,1024]{1,0:T(8,128)(2,1)}, bf16[1024,1536]{1,0:T(8,128)(2,1)}) async-done(((bf16[528,1024]{1,0:T(8,128)(2,1)}, bf16[1024,1536]{1,0:T(8,128)(2,1)}), (bf16[528,1024]{1,0:T(8,128)(2,1)}, bf16[1024,1536]{1,0:T(8,128)(2,1)})) %all-reduce.11.cloned.1.call-update) | async-done | bytes 4227088 | tf_op jit(solution)/shard_map/psum | solution.py:651
  910.8 1.6 convert_element_type.261
  913.2 3.0 fusion.96
  917.4 1.6 slice.93
  (159 shorter events, 15.2 us)
Async XLA Ops:
  7.2 301.2 %copy-start = (bf16[512,1024]{1,0:T(8,128)(2,1)S(1)}, bf16[512,1024]{1,0:T(8,128)(2,1)}, u32[]{:S(2)}) copy-start(bf16[512,1024]{1,0:T(8,128)(2,1)} %param.25) | copy-start | bytes 3145732
  7.2 7.0 copy-start.17
  7.2 209.7 %all-gather.2.cloned.1.call-start = ((), (), s32[]{:S(2)}) async-start(), calls=%async_computation | async-start | bytes 6291456 | tf_op jit(solution)/shard_map/all_gather | solution.py:566
  14.1 546.9 %all-reduce.7.cloned.1.call-start = ((), (), s32[]{:S(2)}) async-start(), calls=%async_computation.1 | async-start | bytes 8388608 | tf_op jit(solution)/shard_map/psum | solution.py:597
  14.4 6.8 copy-start.35
  62.2 149.8 %copy-start.18 = (bf16[1024,512]{1,0:T(8,128)(2,1)S(1)}, bf16[1024,512]{1,0:T(8,128)(2,1)}, u32[]{:S(2)}) copy-start(bf16[1024,512]{1,0:T(8,128)(2,1)} %param.22) | copy-start | bytes 3145732
  62.2 149.9 %copy-start.19 = (bf16[1024,512]{1,0:T(8,128)(2,1)S(1)}, bf16[1024,512]{1,0:T(8,128)(2,1)}, u32[]{:S(2)}) copy-start(bf16[1024,512]{1,0:T(8,128)(2,1)} %param.23) | copy-start | bytes 3145732
  211.2 2.9 copy-start.37
  211.2 3.4 copy-start.32
  312.2 4.5 copy-start.3
  312.2 4.5 collective-permute-start
  312.3 10.4 %collective-permute-start.3 = (bf16[1024,1024]{1,0:T(8,128)(2,1)}, bf16[1024,1024]{1,0:T(8,128)(2,1)}, u32[]{:S(2)}, u32[]{:S(2)}) collective-permute-start(bf16[1024,1024]{1,0:T(8,128)(2,1)} %param.31), channel_id=1, source_target_pairs={{1,0},{0,1},{3,2},{2,3},{5,4},{4,5},{7,6},{6,7},{9,8},{8,9},{11,10... | collective-permute-start | bytes 6291464 | tf_op jit(solution)/shard_map/ppermute | solution.py:503
  312.7 4.0 copy-start.8
  314.7 7.3 copy-start.33
  322.0 3.6 copy-start.39
  322.4 14.9 %copy-start.13 = (bf16[1024,1024]{1,0:T(8,128)(2,1)}, bf16[1024,1024]{1,0:T(8,128)(2,1)S(1)}, u32[]{:S(2)}) copy-start(bf16[1024,1024]{1,0:T(8,128)(2,1)S(1)} %multiply_convert_fusion.1) | copy-start | bytes 6291460
  322.5 14.9 %collective-permute-start.1 = (bf16[1024,1024]{1,0:T(8,128)(2,1)S(1)}, bf16[1024,1024]{1,0:T(8,128)(2,1)}, u32[]{:S(2)}, u32[]{:S(2)}) collective-permute-start(bf16[1024,1024]{1,0:T(8,128)(2,1)S(1)} %multiply_convert_fusion.1), channel_id=1, source_target_pairs={{1,0},{0,1},{3,2},{2,3},{5,4},{4,5},{7,6},{6,7},{9,8},{8,9},{11,10... | collective-permute-start | bytes 6291464 | tf_op jit(solution)/shard_map/ppermute | solution.py:503
  325.6 11.7 %copy-start.40 = (bf16[1024,2048]{1,0:T(8,128)(2,1)S(1)}, bf16[1024,2048]{1,0:T(8,128)(2,1)}, u32[]{:S(2)}) copy-start(bf16[1024,2048]{1,0:T(8,128)(2,1)} %param.29) | copy-start | bytes 12582916
  363.3 8.4 copy-start.42
  371.3 29.7 %collective-permute-start.2 = (bf16[1024,1024]{1,0:T(8,128)(2,1)}, bf16[1024,1024]{1,0:T(8,128)(2,1)}, u32[]{:S(2)}, u32[]{:S(2)}) collective-permute-start(bf16[1024,1024]{1,0:T(8,128)(2,1)} %fusion.27), channel_id=1, source_target_pairs={{0,1},{1,0},{2,3},{3,2},{4,5},{5,4},{6,7},{7,6},{8,9},{9,8},{10,11... | collective-permute-start | bytes 6291464 | tf_op jit(solution)/shard_map/ppermute | solution.py:526
  377.4 23.6 %collective-permute-start.4 = (bf16[1024,1024]{1,0:T(8,128)(2,1)}, bf16[1024,1024]{1,0:T(8,128)(2,1)S(1)}, u32[]{:S(2)}, u32[]{:S(2)}) collective-permute-start(bf16[1024,1024]{1,0:T(8,128)(2,1)} %fusion.30), channel_id=1, source_target_pairs={{0,1},{1,0},{2,3},{3,2},{4,5},{5,4},{6,7},{7,6},{8,9},{9,8},{10,11... | collective-permute-start | bytes 6291464 | tf_op jit(solution)/shard_map/ppermute | solution.py:526
  390.8 344.0 %all-reduce.9.cloned.1.call-start = ((), (), s32[]{:S(2)}) async-start(), calls=%async_computation.2 | async-start | bytes 8388608 | tf_op jit(solution)/shard_map/psum | solution.py:607
  390.8 10.1 %copy-start.2 = (f32[1024,1024]{1,0:T(8,128)S(1)}, f32[1024,1024]{1,0:T(8,128)}, u32[]{:S(2)}) copy-start(f32[1024,1024]{1,0:T(8,128)} %copy-done.1) | copy-start | bytes 12582916
  413.1 9.4 %slice-start.2 = ((s8[8388608]{0:T(1024)(128)(4,1)}), s8[4194304]{0:T(1024)(128)(4,1)S(1)}, s32[]{:S(2)}) async-start(s8[8388608]{0:T(1024)(128)(4,1)} %bitcast.42), calls=%async_computation.6 | async-start | bytes 8388608
  413.7 7.8 copy-start.36
  413.7 8.9 copy-start.14
  413.7 8.9 slice-start.3
  421.3 139.8 %collective-permute-start.5 = (bf16[1024,1024]{1,0:T(8,128)(2,1)}, bf16[1024,1024]{1,0:T(8,128)(2,1)S(1)}, u32[]{:S(2)}, u32[]{:S(2)}) collective-permute-start(bf16[1024,1024]{1,0:T(8,128)(2,1)} %get-tuple-element.43), channel_id=1, source_target_pairs={{1,0},{0,1},{3,2},{2,3},{5,4},{4,5},{7,6},{6,7},{9,8},{8,9},{11,10... | collective-permute-start | bytes 6291464 | tf_op jit(solution)/shard_map/ppermute | solution.py:503
  561.1 349.8 %all-reduce.11.cloned.1.call-start = ((), (), s32[]{:S(2)}) async-start(), calls=%async_computation.3 | async-start | bytes 8454144 | tf_op jit(solution)/shard_map/psum | solution.py:651
  673.7 3.8 copy-start.41
  677.5 9.2 copy-start.21
  677.5 9.2 copy-start.29
  677.5 9.2 copy-start.25
  677.5 9.3 copy-start.26
  677.5 9.9 %copy-start.34 = (f32[4,8,128]{2,1,0:T(8,128)S(1)}, f32[4,8,128]{2,1,0:T(8,128)}, u32[]{:S(2)}) copy-start(f32[4,8,128]{2,1,0:T(8,128)} %get-tuple-element.30) | copy-start | bytes 49156
  677.5 10.1 %copy-start.38 = (f32[4]{0:T(128)S(1)}, f32[4]{0:T(128)}, u32[]{:S(2)}) copy-start(f32[4]{0:T(128)} %param.27) | copy-start | bytes 52
  677.5 10.2 %copy-start.9 = (bf16[2048,512]{1,0:T(8,128)(2,1)S(1)}, bf16[2048,512]{1,0:T(8,128)(2,1)}, u32[]{:S(2)}) copy-start(bf16[2048,512]{1,0:T(8,128)(2,1)} %local_read.1) | copy-start | bytes 6291460
  734.8 11.9 %slice-start = ((s8[6291456]{0:T(1024)(128)(4,1)}), s8[2097152]{0:T(1024)(128)(4,1)S(1)}, s32[]{:S(2)}) async-start(s8[6291456]{0:T(1024)(128)(4,1)} %bitcast.37), calls=%async_computation.4 | async-start | bytes 4194304
  734.8 7.2 copy-start.10
  734.8 11.9 %slice-start.1 = ((s8[6291456]{0:T(1024)(128)(4,1)}), s8[4194304]{0:T(1024)(128)(4,1)S(1)}, s32[]{:S(2)}) async-start(s8[6291456]{0:T(1024)(128)(4,1)} %bitcast.37), calls=%async_computation.5 | async-start | bytes 8388608
  741.3 5.5 copy-start.4
  741.3 5.5 copy-start.24
  741.3 5.4 collective-permute-start.6
  746.7 3.8 copy-start.28
  746.7 3.8 copy-start.5
  746.7 3.8 copy-start.31
  913.2 4.2 copy-start.7
  916.2 3.4 collective-permute-start.7
  (11 other events, 20.5 us)
Sparse Core Ops, SparseCore 0:
  14.3 16.1 all-gather.1
  390.9 170.0 all-reduce.6
  567.6 167.1 all-reduce.8
  741.1 169.7 all-reduce.10

commit v3 on v2

--- a/solution.py
+++ b/solution.py
@@ -208,7 +208,7 @@
     tokens = query_ref.shape[0]
     wide = 8 * picks * 2
     own = own_columns(picks)
-    gate = gate_ref[pl.program_id(0)]
+    gate = gate_ref[0]
     groups = range(tokens // 8)
     both = []
     for g in groups:
@@ -229,39 +229,55 @@
             score_delta, found_ref[pl.ds(g * wide, wide), :]
         ) * (scale * gate)
 
-    @pl.when(pl.program_id(1) == 0)
+    @pl.when(pl.program_id(0) == 0)
     def clear():
         sums_ref[...] = jnp.zeros(sums_ref.shape, full_type)
 
     sums_ref[0] += jnp.broadcast_to(gained, (8, 128))
 
 
-def recall_back(found, queries, mixed_delta, gates, heads, picks, scale):
+def recall_back(found, queries, mixed_delta, gates, head, carried, kept, heads, picks, scale):
     tokens = queries.shape[0]
     width = mixed_delta.shape[1] // heads
     step = min(512, tokens)
     blocks = tokens // step
-    rows_spec = pl.BlockSpec((step, width), lambda h, i: (i, h))
-    return pl.pallas_call(
-        functools.partial(recall_back_kernel, picks, scale),
-        grid=(heads, blocks),
+    rows_spec = pl.BlockSpec((step, width), lambda i: (i, head))
+    anywhere = pl.BlockSpec(memory_space=pl.ANY)
+    extra = [kept] if kept is not None else []
+    first = 4 + len(extra)
+
+    def kernel(gate_ref, found_ref, query_ref, delta_ref, *rest):
+        query_delta_ref, sums_ref = rest[len(extra) + len(carried) :][:2]
+        recall_back_kernel(
+            picks, scale, gate_ref, found_ref, query_ref, delta_ref, query_delta_ref, sums_ref
+        )
+
+    out = pl.pallas_call(
+        kernel,
+        grid=(blocks,),
         in_specs=[
             pl.BlockSpec(memory_space=pltpu.SMEM),
-            pl.BlockSpec((step * picks * 2, width), lambda h, i: (h * blocks + i, 0)),
+            pl.BlockSpec((step * picks * 2, width), lambda i: (head * blocks + i, 0)),
             rows_spec,
             rows_spec,
-        ],
-        out_specs=[rows_spec, pl.BlockSpec((1, 8, 128), lambda h, i: (h, 0, 0))],
+        ]
+        + [anywhere] * (len(extra) + len(carried)),
+        out_specs=[rows_spec, pl.BlockSpec((1, 8, 128), lambda i: (0, 0, 0))]
+        + [anywhere] * len(carried),
         out_shape=[
             jax.ShapeDtypeStruct((tokens, heads * width), full_type),
-            jax.ShapeDtypeStruct((heads, 8, 128), full_type),
-        ],
+            jax.ShapeDtypeStruct((1, 8, 128), full_type),
+        ]
+        + [jax.ShapeDtypeStruct(part.shape, part.dtype) for part in carried],
+        input_output_aliases=({4: 0} if extra else {})
+        | {first + i: 2 + i for i in range(len(carried))},
         compiler_params=pltpu.CompilerParams(vmem_limit_bytes=vmem_most),
         cost_estimate=pl.CostEstimate(
-            flops=0, bytes_accessed=heads * tokens * picks * width * 8, transcendentals=0
+            flops=0, bytes_accessed=tokens * picks * width * 8, transcendentals=0
         ),
         name="recall_back",
-    )(gates, found, queries, mixed_delta)
+    )(gates[head : head + 1], found, queries, mixed_delta, *extra, *carried)
+    return out[0], out[1], list(out[2:])
 
 
 def band(column_ref):
@@ -431,21 +447,30 @@
 
 
 def local_back(
-    projected, query_mask, key_mask, mixed_delta, recall_delta, columns, far, gates, seq_len, scale
+    projected, query_mask, key_mask, mixed_delta, recall_delta, columns, far, gates, seq_len, scale,
+    heads_now, carried, kept, after,
 ):
     tokens = mixed_delta.shape[0]
     heads = gates.shape[0]
     width = mixed_delta.shape[1] // heads
+    start, count = heads_now
+    anywhere = pl.BlockSpec(memory_space=pl.ANY)
+    chosen = slice(start, start + count)
 
     def rows_of(shift):
-        return pl.BlockSpec((seq_len, width), lambda h, s: (s, h + shift * heads))
+        return pl.BlockSpec((seq_len, width), lambda h, s: (s, h + start + shift * heads))
+
+    def kernel(*refs):
+        inputs, rest = refs[:10], refs[10 + len(kept) + len(carried) + len(after) :]
+        local_back_kernel(scale, *inputs, *rest[:5], *rest[5 + len(carried) :])
 
     mask_spec = pl.BlockSpec((1, seq_len, 128), lambda h, s: (s, 0, 0))
     smem = pl.BlockSpec(memory_space=pltpu.SMEM)
     rows_shape = jax.ShapeDtypeStruct((tokens, heads * width), low_type)
-    return pl.pallas_call(
-        functools.partial(local_back_kernel, scale),
-        grid=(heads, tokens // seq_len),
+    first = 10 + len(kept)
+    out = pl.pallas_call(
+        kernel,
+        grid=(count, tokens // seq_len),
         in_specs=[
             smem,
             smem,
@@ -457,21 +482,26 @@
             mask_spec,
             rows_of(0),
             rows_of(0),
-        ],
+        ]
+        + [anywhere] * (len(kept) + len(carried) + len(after)),
         out_specs=[
             rows_of(0),
             rows_of(0),
             rows_of(0),
             pl.BlockSpec((1, 8, ring), lambda h, s: (h, 0, 0)),
             pl.BlockSpec((1, 24, tile), lambda h, s: (h, 0, 0)),
-        ],
+        ]
+        + [anywhere] * len(carried),
         out_shape=[
             rows_shape,
             rows_shape,
             rows_shape,
-            jax.ShapeDtypeStruct((heads, 8, ring), full_type),
-            jax.ShapeDtypeStruct((heads, 24, tile), full_type),
-        ],
+            jax.ShapeDtypeStruct((count, 8, ring), full_type),
+            jax.ShapeDtypeStruct((count, 24, tile), full_type),
+        ]
+        + [jax.ShapeDtypeStruct(part.shape, part.dtype) for part in carried],
+        input_output_aliases={10 + i: i for i in range(len(kept))}
+        | {first + i: 5 + i for i in range(len(carried))},
         scratch_shapes=[
             pltpu.VMEM((tile, span), full_type),
             pltpu.VMEM((tile, span), full_type),
@@ -480,13 +510,14 @@
         ],
         compiler_params=pltpu.CompilerParams(vmem_limit_bytes=vmem_most),
         cost_estimate=pl.CostEstimate(
-            flops=0, bytes_accessed=heads * tokens * seq_len * 40, transcendentals=0
+            flops=0, bytes_accessed=count * tokens * seq_len * 40, transcendentals=0
         ),
         name="local_back",
     )(
-        gates, far, columns, projected, projected, projected, query_mask, key_mask, mixed_delta,
-        recall_delta,
-    )
+        gates[chosen], far[chosen], columns[chosen], projected, projected, projected, query_mask,
+        key_mask, mixed_delta, recall_delta, *kept, *carried, *after,
+    )
+    return list(out[:3]), out[3], out[4], list(out[5:])
 
 
 def mask_rows(block_ids):
@@ -529,6 +560,85 @@
         for k in range(1, group)
     ]
     return sum((part.astype(full_type) for part in sent), term(piece(0)))
+
+
+def bit_orders():
+    bits = lax.axis_size("dp").bit_length() - 1
+    near = [(0, 1, 2), (1, 2, 0), (2, 0, 1)]
+    return [list(head) + list(range(3, bits)) for head in near]
+
+
+def swap_over(rows, bit):
+    return lax.ppermute(rows, "dp", [(i, i ^ (1 << bit)) for i in range(lax.axis_size("dp"))])
+
+
+def side_of(bit):
+    return (lax.axis_index("dp") >> bit) & 1
+
+
+def halve_step(parts, step):
+    kept, sent = [], []
+    for part, order in zip(parts, bit_orders()):
+        half = part.shape[0] // 2
+        side = side_of(order[step])
+        sent.append(
+            swap_over(
+                lax.dynamic_slice_in_dim(part, (1 - side) * half, half, 0), order[step]
+            )
+        )
+        kept.append(lax.dynamic_slice_in_dim(part, side * half, half, 0))
+    return kept, sent
+
+
+def add_low(kept, sent):
+    return [
+        (a.astype(full_type) + b.astype(full_type)).astype(low_type) for a, b in zip(kept, sent)
+    ]
+
+
+def double_all(parts):
+    orders = bit_orders()
+    for step in reversed(range(len(orders[0]))):
+        got = [swap_over(part, order[step]) for part, order in zip(parts, orders)]
+        wider = []
+        for part, other, order in zip(parts, got, orders):
+            rows = part.shape[0]
+            side = side_of(order[step])
+            whole = jnp.zeros((2 * rows,) + part.shape[1:], part.dtype)
+            whole = lax.dynamic_update_slice_in_dim(whole, part, side * rows, 0)
+            wider.append(lax.dynamic_update_slice_in_dim(whole, other, (1 - side) * rows, 0))
+        parts = wider
+    return parts
+
+
+def pack(parts):
+    width = min(part.shape[1] for part in parts)
+    return jnp.concatenate(
+        [
+            part[:, start : start + width]
+            for part in parts
+            for start in range(0, part.shape[1], width)
+        ],
+        0,
+    )
+
+
+def gather_all(packed, parts):
+    whole = lax.all_gather(packed, "dp", axis=0)
+    width = packed.shape[1]
+    wide = []
+    start = 0
+    for part, order in zip(parts, bit_orders()):
+        bits = len(order)
+        rows = part.shape[0]
+        columns = []
+        for unused in range(part.shape[1] // width):
+            piece = whole[:, start : start + rows].reshape((2,) * bits + (rows, width))
+            piece = piece.transpose([bits - 1 - bit for bit in order] + [bits, bits + 1])
+            columns.append(piece.reshape(-1, width))
+            start += rows
+        wide.append(jnp.concatenate(columns, 1).astype(full_type))
+    return wide
 
 
 def body(
@@ -594,7 +704,6 @@
     hidden = dot_rows(second, hidden_weight)
     active = jax.nn.gelu(hidden).astype(low_type)
     return_low = dot_outer(active, grad_full).astype(low_type)
-    return_sum = lax.psum(return_low, "dp")
     active_delta = dot_inner(grad_full, return_weight)
     gelu_back = jax.vjp(jax.nn.gelu, hidden)[1]
     hidden_delta = gelu_back(active_delta)[0].astype(low_type)
@@ -603,8 +712,6 @@
         lambda k: lax.slice_in_dim(hidden_delta, k * share_rows, (k + 1) * share_rows),
     )
     hidden_low = dot_outer(second, hidden_delta).astype(low_type)
-    hidden_low, return_sum = lax.optimization_barrier((hidden_low, return_sum))
-    hidden_sum = lax.psum(hidden_low, "dp")
     second_back = jax.vjp(rms_scaled, middle, mlp_gain)[1]
     middle_part, mlp_gain_part = second_back(second_delta)
     middle_delta = grad_output.astype(full_type) + middle_part
@@ -618,14 +725,53 @@
         )
     ).astype(low_type)
 
-    recall_delta, recall_sums = recall_back(
-        found, projected, mixed_delta, gates, head_count, picks, scale
-    )
-    query_delta, key_delta, value_delta, diagonals, local_sums = local_back(
-        projected, query_mask, key_mask, mixed_delta, recall_delta, behind_columns, far, gates,
-        seq_len, scale,
-    )
-    output_part = dot_outer(mixed_rows, middle_full)
+    return_half = return_low.shape[0] // 2
+    steps = len(bit_orders()[0])
+    output_low = dot_outer(mixed_rows, middle_full).astype(low_type)
+    kept, sent = halve_step(
+        [
+            hidden_low,
+            return_low[:return_half],
+            jnp.concatenate([return_low[return_half:], output_low], 0),
+        ],
+        0,
+    )
+    taken = 0
+    waits = (0, 2, 3)
+    recall_delta = None
+    recall_sums = []
+    for head in range(head_count):
+        recall_delta, head_sums, kept = recall_back(
+            found, projected, mixed_delta, gates, head, kept, recall_delta, head_count, picks, scale
+        )
+        recall_sums.append(head_sums)
+        if head in waits and taken < steps - 1:
+            taken += 1
+            kept, sent = halve_step(add_low(kept, sent), taken)
+    while taken < steps - 1:
+        taken += 1
+        kept, sent = halve_step(add_low(kept, sent), taken)
+    recall_sums = jnp.concatenate(recall_sums, 0)
+    half_heads = max(1, head_count // 2)
+    deltas = []
+    diagonals = []
+    local_sums = []
+    shards = []
+    packed = []
+    for start in range(0, head_count, half_heads):
+        deltas, diagonal_now, sums_now, kept = local_back(
+            projected, query_mask, key_mask, mixed_delta, recall_delta, behind_columns, far, gates,
+            seq_len, scale, (start, half_heads), [] if shards else kept, deltas, packed,
+        )
+        if not shards:
+            shards = add_low(kept, sent)
+            packed = [pack(shards)]
+        diagonals.append(diagonal_now)
+        local_sums.append(sums_now)
+    hidden_sum, return_sum, mixed_sum = gather_all(packed[0], shards)
+    query_delta, key_delta, value_delta = deltas
+    diagonals = jnp.concatenate(diagonals, 0)
+    local_sums = jnp.concatenate(local_sums, 0)
     recall_gain = jnp.sum(recall_sums[:, :, 0], 1)
     local_gain = jnp.sum(local_sums[:, 0], 1)
     gate_part = gates * (1.0 - gates) * recall_gain - gates * local_gain
@@ -641,14 +787,18 @@
     model_width = tokens.shape[1]
     small = jnp.concatenate([table_part.reshape(-1), gate_part])
     small = jnp.pad(small, (0, model_width - small.shape[0]))
-    extra = jnp.stack([attn_gain_part, mlp_gain_part, small])
-    extra = jnp.pad(extra, ((0, 13), (0, 0)))
-    last_low = (
-        jnp.concatenate([output_part, extra], 0).astype(low_type),
-        joined_part.astype(low_type),
-    )
-    last_low, hidden_sum = lax.optimization_barrier((last_low, hidden_sum))
-    output_sum, joined_sum = lax.psum(last_low, "dp")
+    extra = jnp.stack([attn_gain_part, mlp_gain_part, small], 1)
+    extra = jnp.pad(extra, ((0, 0), (0, 125)))
+    joined_low = jnp.concatenate([joined_part, extra], 1).astype(low_type)
+    quarter = joined_low.shape[0] // 4
+    last = [
+        joined_low[: 2 * quarter],
+        joined_low[2 * quarter : 3 * quarter],
+        joined_low[3 * quarter :],
+    ]
+    for step in range(steps):
+        last = add_low(*halve_step(last, step))
+    joined_sum = double_all(last)
 
     normed_delta = fold(
         lambda rows: dot_inner(rows, joined), lambda k: share_of(project_delta, k, share_rows)
@@ -656,24 +806,23 @@
     first_back = jax.vjp(rms_scaled, token_full, attn_gain)[1]
     tokens_grad = (middle_delta + first_back(normed_delta)[0]).astype(low_type)
 
-    joined_grad = joined_sum.astype(full_type)
-    output_grad = output_sum.astype(full_type)
-    gains = sum(fetch(output_grad[inner_width : inner_width + 2]))
-    small_sum = output_grad[inner_width + 2]
+    joined_grad = jnp.concatenate(joined_sum, 0).astype(full_type)
+    gains = sum(fetch(joined_grad[:, 3 * inner_width : 3 * inner_width + 2]))
+    small_sum = joined_grad[:, 3 * inner_width + 2]
     table_size = head_count * 32
     return (
         layer_output,
         tokens_grad,
-        gains[0],
+        gains[:, 0],
         joined_grad[:, :inner_width],
         joined_grad[:, inner_width : 2 * inner_width],
-        joined_grad[:, 2 * inner_width :],
-        output_grad[:inner_width],
+        joined_grad[:, 2 * inner_width : 3 * inner_width],
+        mixed_sum[return_half:],
         small_sum[:table_size].reshape(head_count, 32).T,
         small_sum[table_size : table_size + head_count],
-        gains[1],
-        hidden_sum.astype(full_type),
-        return_sum.astype(full_type),
+        gains[:, 1],
+        hidden_sum,
+        jnp.concatenate([return_sum, mixed_sum[:return_half]], 0),
     )
 
 

time: 937 us -> 836 us (0.89)
  waiting for transfers between devices: 323 us -> 81.1 us
  starting transfers between devices: 2.97 us -> 82.2 us
  other arithmetic: 30.2 us -> 53.5 us
  local copies, waits for them, and re-layouts: 35.7 us -> 58.8 us
  Pallas kernels: 372 us -> 389 us
    psum x3 -> x0, waiting for transfers between devices: 321 us -> none  [the longest x1 153 us: body(): output_sum, joined_sum = lax.psum(last_low, 'dp')]
    ppermute x0 -> x36, waiting for transfers between devices: none -> 81.1 us  [swap_over(): lax.ppermute(rows, 'dp', [(i, i ^ 1 << bit) for i in range(lax.axis_size(...]
    ppermute x0 -> x36, starting transfers between devices: none -> 62.6 us  [swap_over(): lax.ppermute(rows, 'dp', [(i, i ^ 1 << bit) for i in range(lax.axis_size(...]
    pallas_call x2 -> x6, Pallas kernels: 103 us -> 120 us  [the longest x4 75 us: recall_back(): pl.pallas_call(kernel, grid=(blocks,), in_specs=[pl.BlockSpec(memory_spac...]
    ppermute x4, starting transfers between devices: 1.5 us -> 15.1 us  [fetch(): lax.ppermute(rows, 'tensor', [((i + k) % group, i) for i in range(group)])]
    dynamic_slice x0 -> x23, local copies, waits for them, and re-layouts: none -> 11.4 us  [halve_step(): lax.dynamic_slice_in_dim(part, (1 - side) * half, half, 0)]
    convert_element_type x3 -> x23, other arithmetic: 10.7 us -> 21 us  [the longest x21 16.1 us: add_low(): (a.astype(full_type) + b.astype(full_type)).astype(low_type)]
    slice x6 -> x16, local copies, waits for them, and re-layouts: 6.42 us -> 16.2 us  [the longest x2 6.42 us: gather_all(): piece = whole[:, start:start + rows].reshape((2,) * bits + (rows, width))]
  transfers between devices with their start and end apart: 12 -> 46, of which waited for: 4 -> 20; matrix products, arithmetic and copies ran while one was open for 15% -> 21% of each run, Pallas kernels for 31% -> 37%
where the time goes in v3:
time: 836 us; the launch traced here: 825 us
  Pallas kernels  389 us (47%)
  matrix products  145 us (17%)
  starting transfers between devices  82.2 us (10%)
  waiting for transfers between devices  81.1 us (10%)
  local copies, waits for them, and re-layouts  58.8 us (7%)
  other arithmetic  53.5 us (6%)
  between operations  15.9 us (2%)
    pallas_call x1, Pallas kernels, gather_found(): pl.pallas_call(gather_kernel, grid=(heads, blocks), in_specs=[pl.BlockSpe...  149 us
    ppermute x36, waiting for transfers between devices, swap_over(): lax.ppermute(rows, 'dp', [(i, i ^ 1 << bit) for i in range(lax.axis_size(...  81.1 us
    pallas_call x4, Pallas kernels, recall_back(): pl.pallas_call(kernel, grid=(blocks,), in_specs=[pl.BlockSpec(memory_spac...  75 us
    ppermute x36, starting transfers between devices, swap_over(): lax.ppermute(rows, 'dp', [(i, i ^ 1 << bit) for i in range(lax.axis_size(...  62.6 us
    dot_general x6, matrix products, dot_rows(): return jnp.dot(left, right, preferred_element_type=full_type)  62.1 us
    pallas_call x1, Pallas kernels, recall(): pl.pallas_call(functools.partial(recall_kernel, picks, scale), grid=(head...  59.3 us
    dot_general x6, matrix products, dot_inner(): lax.dot_general(left, right, (((1,), (1,)), ((), ())), preferred_element_...  45.2 us
    pallas_call x2, Pallas kernels, local_back(): pl.pallas_call(kernel, grid=(count, tokens // seq_len), in_specs=[smem, s...  44.7 us
  transfers between devices with their start and end apart: 46, of which 20 were waited for; matrix products, arithmetic and copies ran while one was open for 21% of the time, Pallas kernels for 37%

profile of v3, /device:TPU:1, one launch (start us, length us, event | category | flops | bytes accessed | tf_op | source)
XLA Modules:
  0.0 825.3 jit_solution(18379501745141284104)
XLA Ops:
  9.5 3.5 fusion.13
  16.0 4.1 reshape.187.index_hbm
  21.2 39.8 %interleave.1 = bf16[131072,128]{1,0:T(8,128)(2,1)} custom-call(bf16[4,16384,128]{2,1,0:T(8,128)(2,1)} %key_ref.1, bf16[4,16384,128]{2,1,0:T(8,128)(2,1)} %value_ref.1), custom_call_target="tpu_custom_call" | custom-call | flops 8589934592 | bytes 67108864 | tf_op jit(solution)/shard_map/interleave/pallas_call | solution.py:67
  61.0 149.0 %gather_found.1 = bf16[262144,2,128]{2,1,0:T(2,128)(2,1)} custom-call(s32[64,32,128]{2,1,0:T(8,128)} %reshape.187.index_hbm, bf16[65536,2,128]{2,1,0:T(2,128)(2,1)} %bitcast.51), custom_call_target="tpu_custom_call" | custom-call | bytes 536870912 | tf_op jit(solution)/shard_map/gather_found/pallas_call | solution.py:136
  216.9 11.3 %convolution_convert_fusion.query_ref.key_ref.value_ref.refs_3_.refs_4_.refs_5_ = bf16[2048,1536]{1,0:T(8,128)(2,1)} fusion(bf16[2048,1024]{1,0:T(8,128)(2,1)} %all-gather.4.cloned.1.call-done, bf16[1024,1536]{1,0:T(8,128)(2,1)} %constant_dynamic-update-slice_fusion), kind=kOutput, calls=%fused_computation.16 | convolution fusion | flops 6445596672 | bytes 13631488 | tf_op jit(solution)/shard_map/dot_general | solution.py:36
  228.2 59.3 %recall.1.recall_ref = f32[2048,512]{1,0:T(8,128)} custom-call(bf16[524288,128]{1,0:T(8,128)(2,1)} %bitcast.4.found_ref, bf16[2048,1536]{1,0:T(8,128)(2,1)} %convolution_convert_fusion.query_ref.key_ref.value_ref.refs_3_.refs_4_.refs_5_), custom_call_target="tpu_custom_call" | custom-call | bytes 268435456 | tf_op jit(solution)/shard_map/recall/pallas_call | solution.py:188
  287.5 21.0 %local_read.1 = bf16[2048,512]{1,0:T(8,128)(2,1)} custom-call(f32[4]{0:T(128)} %add_divide_fusion.gate_ref, f32[4,2]{1,0:T(4,128)} %pad_maximum_fusion.9.far_ref, f32[4,1,1024]{2,1,0:T(1,128)} %broadcast_in_dim.27.column_ref, bf16[2048,1536]{1,0:T(8,128)(2,1)} %convolution_convert_fusion.query_ref.key_ref.value_ref.refs_3_.refs_4_.refs_5_, ...), custom_call_target="tpu_custom_call" | custom-call | bytes 167772160 | tf_op jit(solution)/shard_map/local_read/pallas_call | solution.py:333
  308.5 3.8 convolution_convert_fusion.4
  324.2 11.8 %fusion.105 = f32[2048,2048]{1,0:T(8,128)} fusion(bf16[2048,1024]{1,0:T(8,128)(2,1)S(1)} %constant_dynamic-update-slice_fusion.3, bf16[2048,1024]{1,0:T(8,128)(2,1)S(1)} %copy-done.41), kind=kOutput, calls=%fused_computation.261 | convolution fusion | flops 8589934592 | bytes 25165824 | tf_op jit(solution)/shard_map/dot_general | solution.py:46
  336.1 28.5 %fusion.6 = (bf16[2048,2048]{1,0:T(8,128)(2,1)}, bf16[2048,2048]{1,0:T(8,128)(2,1)}) fusion(f32[2048,2048]{1,0:T(8,128)} %fusion.105, bf16[1024,2048]{1,0:T(8,128)(2,1)} %param.29, bf16[1024,1024]{1,0:T(8,128)(2,1)S(1)} %collective-permute-done.1, bf16[1024,1024]{1,0:T(8,128)(2,1)S(1)} %multiply_convert_fusion.1), kind=kOutput, calls=%fused_computation.8 | convolution fusion | flops 8690597888 | bytes 41943040 | tf_op jit(solution)/shard_map/dot_general | solution.py:36
  364.6 7.1 fusion.29
  372.1 7.1 fusion.32
  379.5 11.8 %convolution_convert_fusion.1 = bf16[1024,2048]{1,0:T(8,128)(2,1)S(1)} fusion(bf16[2048,2048]{1,0:T(8,128)(2,1)} %get-tuple-element.93, bf16[1024,1024]{1,0:T(8,128)(2,1)S(1)} %copy-done.49, bf16[1024,1024]{1,0:T(8,128)(2,1)S(1)} %multiply_convert_fusion.1), kind=kOutput, calls=%fused_computation.49 | convolution fusion | flops 8600420352 | bytes 16777216 | tf_op jit(solution)/shard_map/dot_general | solution.py:40
  395.2 8.2 fusion.21
  404.8 10.9 %multiply_reduce_fusion.1 = (bf16[1024]{0:T(1024)(128)(2,1)S(1)}, f32[1024]{0:T(1024)S(1)}, bf16[1024,1024]{1,0:T(8,128)(2,1)}, f32[1024,1024]{1,0:T(8,128)}) fusion(f32[1024,1024]{1,0:T(8,128)S(1)} %get-tuple-element.147, f32[1024]{0:T(1024)S(1)} %fusion.87, bf16[1024,1024]{1,0:T(8,128)(2,1)S(1)} %collective-permute-done.4, f32[1024]{0:T(1024)S(1)} %copy-done.31, ...), kind=kOutput, calls=%fused_computation.39 | convolution fusion | flops 4307548160 | bytes 27277312 | tf_op jit(solution)/shard_map/dot_general | solution.py:46
  417.9 4.4 constant_dynamic-update-slice_fusion.35
  422.7 11.8 %convolution_convert_fusion.2 = bf16[2048,1024]{1,0:T(8,128)(2,1)S(1)} fusion(bf16[2048,2048]{1,0:T(8,128)(2,1)} %get-tuple-element.94, bf16[2048,1024]{1,0:T(8,128)(2,1)S(1)} %copy-done.16), kind=kOutput, calls=%fused_computation.50 | convolution fusion | flops 8592031744 | bytes 16777216 | tf_op jit(solution)/shard_map/dot_general | solution.py:40
  440.4 5.4 fusion.38
  447.2 3.8 convolution_convert_fusion.3.delta_ref.refs_8_
  451.0 19.0 %recall_back.4 = (f32[2048,512]{1,0:T(8,128)}, f32[1,8,128]{2,1,0:T(8,128)}, bf16[512,2048]{1,0:T(8,128)(2,1)}, bf16[512,1024]{1,0:T(8,128)(2,1)}, bf16[768,1024]{1,0:T(8,128)(2,1)}) custom-call(f32[1]{0:T(128)} %get-tuple-element.142.gate_ref, bf16[524288,128]{1,0:T(8,128)(2,1)} %bitcast.4.found_ref, ...), custom_call_target="tpu_custom_call", output_to_operand_aliasing={{2}: (4, {}), {3}: (5, {}), {4}: (6, {})} | custom-call | bytes 67108864 | tf_op jit(solution)/shard_map/recall_back/pallas_call | solution.py:255
  485.8 18.6 %recall_back.5 = (f32[2048,512]{1,0:T(8,128)}, f32[1,8,128]{2,1,0:T(8,128)}, bf16[256,2048]{1,0:T(8,128)(2,1)}, bf16[256,1024]{1,0:T(8,128)(2,1)}, bf16[384,1024]{1,0:T(8,128)(2,1)}) custom-call(f32[1]{0:T(128)} %get-tuple-element.143.gate_ref, ...), custom_call_target="tpu_custom_call", output_to_operand_aliasing={{0}: (4, {}), {2}: (5, {}), {3}: (6, {}), {4}: (7, {})} | custom-call | bytes 67108864 | tf_op jit(solution)/shard_map/recall_back/pallas_call | solution.py:255
  504.4 18.7 %recall_back.6 = (f32[2048,512]{1,0:T(8,128)}, f32[1,8,128]{2,1,0:T(8,128)}, bf16[256,2048]{1,0:T(8,128)(2,1)}, bf16[256,1024]{1,0:T(8,128)(2,1)}, bf16[384,1024]{1,0:T(8,128)(2,1)}) custom-call(f32[1]{0:T(128)} %get-tuple-element.144.gate_ref, ...), custom_call_target="tpu_custom_call", output_to_operand_aliasing={{0}: (4, {}), {2}: (5, {}), {3}: (6, {}), {4}: (7, {})} | custom-call | bytes 67108864 | tf_op jit(solution)/shard_map/recall_back/pallas_call | solution.py:255
  530.6 18.7 %recall_back.7 = (f32[2048,512]{1,0:T(8,128)}, f32[1,8,128]{2,1,0:T(8,128)}, bf16[128,2048]{1,0:T(8,128)(2,1)}, bf16[128,1024]{1,0:T(8,128)(2,1)}, bf16[192,1024]{1,0:T(8,128)(2,1)}) custom-call(f32[1]{0:T(128)} %get-tuple-element.145.gate_ref, ...), custom_call_target="tpu_custom_call", output_to_operand_aliasing={{0}: (4, {}), {2}: (5, {}), {3}: (6, {}), {4}: (7, {})} | custom-call | bytes 67108864 | tf_op jit(solution)/shard_map/recall_back/pallas_call | solution.py:255
  557.2 22.2 %local_back.2 = (bf16[2048,512]{1,0:T(8,128)(2,1)}, bf16[2048,512]{1,0:T(8,128)(2,1)}, bf16[2048,512]{1,0:T(8,128)(2,1)}, f32[2,8,1024]{2,1,0:T(8,128)}, f32[2,2...) custom-call(f32[2]{0:T(128)} %get-tuple-element.140.refs_0_, ...), custom_call_target="tpu_custom_call", output_to_operand_aliasing={{5}: (10, {}), {6}: (11, {}), {7}: (12, {})} | custom-call | bytes 167772160 | tf_op jit(solution)/shard_map/local_back/pallas_call | solution.py:471
  584.6 5.9 collective-permute-done.17
  592.4 22.5 %local_back.3 = (bf16[2048,512]{1,0:T(8,128)(2,1)}, bf16[2048,512]{1,0:T(8,128)(2,1)}, bf16[2048,512]{1,0:T(8,128)(2,1)}, f32[2,8,1024]{2,1,0:T(8,128)}, f32[2,24,256]{2,1,0:T(8,128)}) custom-call(f32[2]{0:T(128)} %get-tuple-element.141.refs_0_, f32[2,2]{1,0:T(2,128)} %get-tuple-element.137.refs_1_, ...), custom_call_target="tpu_custom_call", output_to_operand_aliasing={{0}: (10, {}), {1}: (11, {}), {2}: (12, {})} | custom-call | bytes 167772160 | tf_op jit(solution)/shard_map/local_back/pallas_call | solution.py:471
  620.3 10.5 %fusion.97 = (bf16[1024,1536]{1,0:T(8,128)(2,1)S(1)}, f32[1024]{0:T(1024)S(1)}) fusion(bf16[1024,1536]{1,0:T(8,128)(2,1)} %constant_dynamic-update-slice_fusion, bf16[2048,1024]{1,0:T(8,128)(2,1)S(1)} %copy-done.46, bf16[2048,1536]{1,0:T(8,128)(2,1)S(1)} %constant_dynamic-update-slice_fusion.5), kind=kOutput, calls=%fused_computation.253 | convolution fusion | flops 6448741376 | bytes 16781312 | tf_op jit(solution)/shard_map/dot_general | solution.py:40
  634.7 5.8 fusion.35
  640.5 3.7 collective-permute-start.18
  646.1 3.9 collective-permute-done.35
  650.2 3.8 collective-permute-start.36
  658.8 7.5 collective-permute-done.36
  677.2 4.4 collective-permute-done.31
  682.4 3.7 collective-permute-done.39
  687.9 4.6 collective-permute-start.33
  692.5 6.8 collective-permute-done.40
  699.6 10.8 %collective-permute-done.33 = bf16[64,1664]{1,0:T(8,128)(2,1)S(1)} collective-permute-done((bf16[64,1664]{1,0:T(8,128)(2,1)S(1)}, bf16[64,1664]{1,0:T(8,128)(2,1)S(1)}, u32[]{:S(2)}, u32[]{:S(2)}) %collective-permute-start.33) | collective-permute-done | bytes 213024 | tf_op jit(solution)/shard_map/ppermute | solution.py:572
  715.2 9.6 %collective-permute-done.21 = bf16[64,1664]{1,0:T(8,128)(2,1)S(1)} collective-permute-done((bf16[64,1664]{1,0:T(8,128)(2,1)S(1)}, bf16[64,1664]{1,0:T(8,128)(2,1)S(1)}, u32[]{:S(2)}, u32[]{:S(2)}) %collective-permute-start.21) | collective-permute-done | bytes 213024 | tf_op jit(solution)/shard_map/ppermute | solution.py:572
  724.9 17.9 %collective-permute-start.22 = (bf16[32,1664]{1,0:T(8,128)(2,1)S(1)}, bf16[32,1664]{1,0:T(8,128)(2,1)S(1)}, u32[]{:S(2)}, u32[]{:S(2)}) collective-permute-start(bf16[32,1664]{1,0:T(8,128)(2,1)S(1)} %constant_dynamic-slice_fusion.8), channel_id=1, source_target_pairs={{0,16},{2,18},{4,20},{6,22},{8,24},{10,26},{12,28},{14,30},{16,0},... | collective-permute-start | bytes 319496 | tf_op jit(solution)/shard_map/ppermute | solution.py:572
  742.9 3.8 collective-permute-done.22
  746.8 3.3 collective-permute-start.23
  754.6 3.2 collective-permute-done.24
  758.4 5.8 fusion.14
  768.1 8.7 %collective-permute-done.26 = bf16[256,1664]{1,0:T(8,128)(2,1)S(1)} collective-permute-done((bf16[256,1664]{1,0:T(8,128)(2,1)S(1)}, bf16[256,1664]{1,0:T(8,128)(2,1)S(1)}, u32[]{:S(2)}, u32[]{:S(2)}) %collective-permute-start.26) | collective-permute-done | bytes 852000 | tf_op jit(solution)/shard_map/ppermute | solution.py:572
  777.8 14.0 %collective-permute-start.43 = (f32[1024,2]{1,0:T(8,128)}, f32[1024,2]{1,0:T(8,128)}, u32[]{:S(2)}, u32[]{:S(2)}) collective-permute-start(f32[1024,2]{1,0:T(8,128)} %maximum_convert_fusion.2), channel_id=1, source_target_pairs={{1,0},{0,1},{3,2},{2,3},{5,4},{4,5},{7,6},{6,7},{9,8},{8,9},{11,10... | collective-permute-start | bytes 24584 | tf_op jit(solution)/shard_map/ppermute | solution.py:534
  801.5 4.1 fusion.95
  809.2 4.2 pad_maximum_fusion
  813.5 4.4 maximum_convert_fusion
  (342 shorter events, 136.6 us)
Async XLA Ops:
  7.2 301.3 %copy-start = (bf16[512,1024]{1,0:T(8,128)(2,1)S(1)}, bf16[512,1024]{1,0:T(8,128)(2,1)}, u32[]{:S(2)}) copy-start(bf16[512,1024]{1,0:T(8,128)(2,1)} %param.25) | copy-start | bytes 3145732
  7.2 209.7 %all-gather.4.cloned.1.call-start = ((), (), s32[]{:S(2)}) async-start(), calls=%async_computation | async-start | bytes 6291456 | tf_op jit(solution)/shard_map/all_gather | solution.py:676
  13.0 786.2 %all-gather.6.cloned.1.call-start = ((), (), s32[]{:S(2)}) async-start(), calls=%async_computation.1 | async-start | bytes 10027008 | tf_op jit(solution)/shard_map/all_gather | solution.py:627
  20.1 292.7 %copy-start.33 = (s32[1024]{0:T(1024)}, s32[1024]{0:T(1024)S(1)}, u32[]{:S(2)}) copy-start(s32[1024]{0:T(1024)S(1)} %get-tuple-element.152) | copy-start | bytes 12292
  312.3 5.9 collective-permute-start
  312.4 9.6 %collective-permute-start.3 = (bf16[1024,1024]{1,0:T(8,128)(2,1)}, bf16[1024,1024]{1,0:T(8,128)(2,1)}, u32[]{:S(2)}, u32[]{:S(2)}) collective-permute-start(bf16[1024,1024]{1,0:T(8,128)(2,1)} %param.31), channel_id=1, source_target_pairs={{1,0},{0,1},{3,2},{2,3},{5,4},{4,5},{7,6},{6,7},{9,8},{8,9},{11,10... | collective-permute-start | bytes 6291464 | tf_op jit(solution)/shard_map/ppermute | solution.py:534
  321.8 14.2 %collective-permute-start.1 = (bf16[1024,1024]{1,0:T(8,128)(2,1)S(1)}, bf16[1024,1024]{1,0:T(8,128)(2,1)S(1)}, u32[]{:S(2)}, u32[]{:S(2)}) collective-permute-start(bf16[1024,1024]{1,0:T(8,128)(2,1)S(1)} %multiply_convert_fusion.1), channel_id=1, source_target_pairs={{1,0},{0,1},{3,2},{2,3},{5,4},{4,5},{7,6},{6,7},{9,8},{8,9},{11,10... | collective-permute-start | bytes 6291464 | tf_op jit(solution)/shard_map/ppermute | solution.py:534
  371.7 31.8 %collective-permute-start.2 = (bf16[1024,1024]{1,0:T(8,128)(2,1)S(1)}, bf16[1024,1024]{1,0:T(8,128)(2,1)S(1)}, u32[]{:S(2)}, u32[]{:S(2)}) collective-permute-start(bf16[1024,1024]{1,0:T(8,128)(2,1)S(1)} %fusion.29), channel_id=1, source_target_pairs={{0,1},{1,0},{2,3},{3,2},{4,5},{5,4},{6,7},{7,6},{8,9},{9,8},{10,11... | collective-permute-start | bytes 6291464 | tf_op jit(solution)/shard_map/ppermute | solution.py:557
  379.2 25.6 %collective-permute-start.4 = (bf16[1024,1024]{1,0:T(8,128)(2,1)S(1)}, bf16[1024,1024]{1,0:T(8,128)(2,1)S(1)}, u32[]{:S(2)}, u32[]{:S(2)}) collective-permute-start(bf16[1024,1024]{1,0:T(8,128)(2,1)S(1)} %fusion.32), channel_id=1, source_target_pairs={{0,1},{1,0},{2,3},{3,2},{4,5},{5,4},{6,7},{7,6},{8,9},{9,8},{10,11... | collective-permute-start | bytes 6291464 | tf_op jit(solution)/shard_map/ppermute | solution.py:557
  393.0 76.9 %collective-permute-start.6 = (bf16[512,2048]{1,0:T(8,128)(2,1)S(1)}, bf16[512,2048]{1,0:T(8,128)(2,1)}, u32[]{:S(2)}, u32[]{:S(2)}) collective-permute-start(bf16[512,2048]{1,0:T(8,128)(2,1)S(1)} %get-tuple-element.103), channel_id=1, source_target_pairs={{0,2},{2,0},{4,6},{6,4},{8,10},{10,8},{12,14},{14,12},{16,18},{18,... | collective-permute-start | bytes 6291464 | tf_op jit(solution)/shard_map/ppermute | solution.py:572
  422.3 15.5 %collective-permute-start.5 = (bf16[1024,1024]{1,0:T(8,128)(2,1)S(1)}, bf16[1024,1024]{1,0:T(8,128)(2,1)S(1)}, u32[]{:S(2)}, u32[]{:S(2)}) collective-permute-start(bf16[1024,1024]{1,0:T(8,128)(2,1)S(1)} %get-tuple-element.91), channel_id=1, source_target_pairs={{1,0},{0,1},{3,2},{2,3},{5,4},{4,5},{7,6},{6,7},{9,8},{8,9},{11,10... | collective-permute-start | bytes 6291464 | tf_op jit(solution)/shard_map/ppermute | solution.py:534
  436.5 39.1 %collective-permute-start.7 = (bf16[512,1024]{1,0:T(8,128)(2,1)}, bf16[512,1024]{1,0:T(8,128)(2,1)}, u32[]{:S(2)}, u32[]{:S(2)}) collective-permute-start(bf16[512,1024]{1,0:T(8,128)(2,1)} %get-tuple-element.114), channel_id=1, source_target_pairs={{0,4},{2,6},{4,0},{6,2},{8,12},{10,14},{12,8},{14,10},{16,20},{18,... | collective-permute-start | bytes 3145736 | tf_op jit(solution)/shard_map/ppermute | solution.py:572
  445.8 35.7 %collective-permute-start.8 = (bf16[768,1024]{1,0:T(8,128)(2,1)}, bf16[768,1024]{1,0:T(8,128)(2,1)}, u32[]{:S(2)}, u32[]{:S(2)}) collective-permute-start(bf16[768,1024]{1,0:T(8,128)(2,1)} %get-tuple-element.110), channel_id=1, source_target_pairs={{0,8},{2,10},{4,12},{6,14},{8,0},{10,2},{12,4},{14,6},{16,24},{18,... | collective-permute-start | bytes 4718600 | tf_op jit(solution)/shard_map/ppermute | solution.py:572
  474.2 48.9 %collective-permute-start.9 = (bf16[256,2048]{1,0:T(8,128)(2,1)S(1)}, bf16[256,2048]{1,0:T(8,128)(2,1)S(1)}, u32[]{:S(2)}, u32[]{:S(2)}) collective-permute-start(bf16[256,2048]{1,0:T(8,128)(2,1)S(1)} %get-tuple-element.112), channel_id=1, source_target_pairs={{0,4},{2,6},{4,0},{6,2},{8,12},{10,14},{12,8},{14,10},{16,20},{18,... | collective-permute-start | bytes 3145736 | tf_op jit(solution)/shard_map/ppermute | solution.py:572
  478.2 48.8 %collective-permute-start.10 = (bf16[256,1024]{1,0:T(8,128)(2,1)}, bf16[256,1024]{1,0:T(8,128)(2,1)}, u32[]{:S(2)}, u32[]{:S(2)}) collective-permute-start(bf16[256,1024]{1,0:T(8,128)(2,1)} %get-tuple-element.120), channel_id=1, source_target_pairs={{0,8},{2,10},{4,12},{6,14},{8,0},{10,2},{12,4},{14,6},{16,24},{18,... | collective-permute-start | bytes 1572872 | tf_op jit(solution)/shard_map/ppermute | solution.py:572
  484.6 44.8 %collective-permute-start.11 = (bf16[384,1024]{1,0:T(8,128)(2,1)S(1)}, bf16[384,1024]{1,0:T(8,128)(2,1)S(1)}, u32[]{:S(2)}, u32[]{:S(2)}) collective-permute-start(bf16[384,1024]{1,0:T(8,128)(2,1)S(1)} %get-tuple-element.116), channel_id=1, source_target_pairs={{0,2},{2,0},{4,6},{6,4},{8,10},{10,8},{12,14},{14,12},{16,18},{18,... | collective-permute-start | bytes 2359304 | tf_op jit(solution)/shard_map/ppermute | solution.py:572
  525.7 23.7 %collective-permute-start.12 = (bf16[128,2048]{1,0:T(8,128)(2,1)S(1)}, bf16[128,2048]{1,0:T(8,128)(2,1)S(1)}, u32[]{:S(2)}, u32[]{:S(2)}) collective-permute-start(bf16[128,2048]{1,0:T(8,128)(2,1)S(1)} %get-tuple-element.118), channel_id=1, source_target_pairs={{0,8},{2,10},{4,12},{6,14},{8,0},{10,2},{12,4},{14,6},{16,24},{18,... | collective-permute-start | bytes 1572872 | tf_op jit(solution)/shard_map/ppermute | solution.py:572
  529.0 24.7 %collective-permute-start.13 = (bf16[128,1024]{1,0:T(8,128)(2,1)S(1)}, bf16[128,1024]{1,0:T(8,128)(2,1)S(1)}, u32[]{:S(2)}, u32[]{:S(2)}) collective-permute-start(bf16[128,1024]{1,0:T(8,128)(2,1)S(1)} %get-tuple-element.126), channel_id=1, source_target_pairs={{0,2},{2,0},{4,6},{6,4},{8,10},{10,8},{12,14},{14,12},{16,18},{18,... | collective-permute-start | bytes 786440 | tf_op jit(solution)/shard_map/ppermute | solution.py:572
  530.5 25.8 %collective-permute-start.14 = (bf16[192,1024]{1,0:T(8,128)(2,1)S(1)}, bf16[192,1024]{1,0:T(8,128)(2,1)S(1)}, u32[]{:S(2)}, u32[]{:S(2)}) collective-permute-start(bf16[192,1024]{1,0:T(8,128)(2,1)S(1)} %get-tuple-element.122), channel_id=1, source_target_pairs={{0,4},{2,6},{4,0},{6,2},{8,12},{10,14},{12,8},{14,10},{16,20},{18,... | collective-permute-start | bytes 1179656 | tf_op jit(solution)/shard_map/ppermute | solution.py:572
  551.4 28.1 %collective-permute-start.15 = (bf16[64,2048]{1,0:T(8,128)(2,1)S(1)}, bf16[64,2048]{1,0:T(8,128)(2,1)S(1)}, u32[]{:S(2)}, u32[]{:S(2)}) collective-permute-start(bf16[64,2048]{1,0:T(8,128)(2,1)S(1)} %get-tuple-element.124), channel_id=1, source_target_pairs={{0,16},{2,18},{4,20},{6,22},{8,24},{10,26},{12,28},{14,30},{16,0},... | collective-permute-start | bytes 786440 | tf_op jit(solution)/shard_map/ppermute | solution.py:572
  555.5 28.2 %collective-permute-start.16 = (bf16[64,1024]{1,0:T(8,128)(2,1)S(1)}, bf16[64,1024]{1,0:T(8,128)(2,1)S(1)}, u32[]{:S(2)}, u32[]{:S(2)}) collective-permute-start(bf16[64,1024]{1,0:T(8,128)(2,1)S(1)} %get-tuple-element.132), channel_id=1, source_target_pairs={{0,16},{2,18},{4,20},{6,22},{8,24},{10,26},{12,28},{14,30},{16,0},... | collective-permute-start | bytes 393224 | tf_op jit(solution)/shard_map/ppermute | solution.py:572
  580.5 10.0 %collective-permute-start.17 = (bf16[96,1024]{1,0:T(8,128)(2,1)S(1)}, bf16[96,1024]{1,0:T(8,128)(2,1)S(1)}, u32[]{:S(2)}, u32[]{:S(2)}) collective-permute-start(bf16[96,1024]{1,0:T(8,128)(2,1)S(1)} %get-tuple-element.128), channel_id=1, source_target_pairs={{0,16},{2,18},{4,20},{6,22},{8,24},{10,26},{12,28},{14,30},{16,0},... | collective-permute-start | bytes 589832 | tf_op jit(solution)/shard_map/ppermute | solution.py:572
  632.2 44.3 %collective-permute-start.19 = (bf16[256,1664]{1,0:T(8,128)(2,1)S(1)}, bf16[256,1664]{1,0:T(8,128)(2,1)S(1)}, u32[]{:S(2)}, u32[]{:S(2)}) collective-permute-start(bf16[256,1664]{1,0:T(8,128)(2,1)S(1)} %constant_dynamic-slice_fusion.11), channel_id=1, source_target_pairs={{0,2},{2,0},{4,6},{6,4},{8,10},{10,8},{12,14},{14,12},{16,18},{18,... | collective-permute-start | bytes 2555912 | tf_op jit(solution)/shard_map/ppermute | solution.py:572
  632.5 11.8 %collective-permute-start.27 = (bf16[128,1664]{1,0:T(8,128)(2,1)S(1)}, bf16[128,1664]{1,0:T(8,128)(2,1)S(1)}, u32[]{:S(2)}, u32[]{:S(2)}) collective-permute-start(bf16[128,1664]{1,0:T(8,128)(2,1)S(1)} %constant_dynamic-slice_fusion.7), channel_id=1, source_target_pairs={{0,4},{2,6},{4,0},{6,2},{8,12},{10,14},{12,8},{14,10},{16,20},{18,... | collective-permute-start | bytes 1277960 | tf_op jit(solution)/shard_map/ppermute | solution.py:572
  632.6 17.4 %collective-permute-start.35 = (bf16[128,1664]{1,0:T(8,128)(2,1)S(1)}, bf16[128,1664]{1,0:T(8,128)(2,1)S(1)}, u32[]{:S(2)}, u32[]{:S(2)}) collective-permute-start(bf16[128,1664]{1,0:T(8,128)(2,1)S(1)} %constant_dynamic-slice_fusion.3), channel_id=1, source_target_pairs={{0,8},{2,10},{4,12},{6,14},{8,0},{10,2},{12,4},{14,6},{16,24},{18,... | collective-permute-start | bytes 1277960 | tf_op jit(solution)/shard_map/ppermute | solution.py:572
  640.5 117.9 %collective-permute-start.18 = (bf16[1024,1024]{1,0:T(8,128)(2,1)S(1)}, bf16[1024,1024]{1,0:T(8,128)(2,1)S(1)}, u32[]{:S(2)}, u32[]{:S(2)}) collective-permute-start(bf16[1024,1024]{1,0:T(8,128)(2,1)S(1)} %fusion.35), channel_id=1, source_target_pairs={{0,1},{1,0},{2,3},{3,2},{4,5},{5,4},{6,7},{7,6},{8,9},{9,8},{10,11... | collective-permute-start | bytes 6291464 | tf_op jit(solution)/shard_map/ppermute | solution.py:557
  644.4 12.2 %collective-permute-start.28 = (bf16[64,1664]{1,0:T(8,128)(2,1)S(1)}, bf16[64,1664]{1,0:T(8,128)(2,1)S(1)}, u32[]{:S(2)}, u32[]{:S(2)}) collective-permute-start(bf16[64,1664]{1,0:T(8,128)(2,1)S(1)} %constant_dynamic-slice_fusion.6), channel_id=1, source_target_pairs={{0,8},{2,10},{4,12},{6,14},{8,0},{10,2},{12,4},{14,6},{16,24},{18,... | collective-permute-start | bytes 638984 | tf_op jit(solution)/shard_map/ppermute | solution.py:572
  650.2 16.1 %collective-permute-start.36 = (bf16[64,1664]{1,0:T(8,128)(2,1)S(1)}, bf16[64,1664]{1,0:T(8,128)(2,1)S(1)}, u32[]{:S(2)}, u32[]{:S(2)}) collective-permute-start(bf16[64,1664]{1,0:T(8,128)(2,1)S(1)} %constant_dynamic-slice_fusion.2), channel_id=1, source_target_pairs={{0,2},{2,0},{4,6},{6,4},{8,10},{10,8},{12,14},{14,12},{16,18},{18,... | collective-permute-start | bytes 638984 | tf_op jit(solution)/shard_map/ppermute | solution.py:572
  656.7 11.8 %collective-permute-start.29 = (bf16[32,1664]{1,0:T(8,128)(2,1)S(1)}, bf16[32,1664]{1,0:T(8,128)(2,1)S(1)}, u32[]{:S(2)}, u32[]{:S(2)}) collective-permute-start(bf16[32,1664]{1,0:T(8,128)(2,1)S(1)} %constant_dynamic-slice_fusion.5), channel_id=1, source_target_pairs={{0,2},{2,0},{4,6},{6,4},{8,10},{10,8},{12,14},{14,12},{16,18},{18,... | collective-permute-start | bytes 319496 | tf_op jit(solution)/shard_map/ppermute | solution.py:572
  666.4 3.6 collective-permute-start.37
  668.5 4.5 collective-permute-start.30
  670.0 3.9 collective-permute-start.38
  673.1 8.5 %collective-permute-start.31 = (bf16[16,1664]{1,0:T(8,128)(2,1)S(1)}, bf16[16,1664]{1,0:T(8,128)(2,1)S(1)}, u32[]{:S(2)}, u32[]{:S(2)}) collective-permute-start(bf16[16,1664]{1,0:T(8,128)(2,1)S(1)} %get-tuple-element.87), channel_id=1, source_target_pairs={{0,16},{2,18},{4,20},{6,22},{8,24},{10,26},{12,28},{14,30},{16,0},... | collective-permute-start | bytes 159752 | tf_op jit(solution)/shard_map/ppermute | solution.py:572
  674.0 12.0 %collective-permute-start.39 = (bf16[16,1664]{1,0:T(8,128)(2,1)S(1)}, bf16[16,1664]{1,0:T(8,128)(2,1)S(1)}, u32[]{:S(2)}, u32[]{:S(2)}) collective-permute-start(bf16[16,1664]{1,0:T(8,128)(2,1)S(1)} %get-tuple-element.89), channel_id=1, source_target_pairs={{0,16},{2,18},{4,20},{6,22},{8,24},{10,26},{12,28},{14,30},{16,0},... | collective-permute-start | bytes 159752 | tf_op jit(solution)/shard_map/ppermute | solution.py:572
  676.7 38.1 %collective-permute-start.20 = (bf16[128,1664]{1,0:T(8,128)(2,1)S(1)}, bf16[128,1664]{1,0:T(8,128)(2,1)S(1)}, u32[]{:S(2)}, u32[]{:S(2)}) collective-permute-start(bf16[128,1664]{1,0:T(8,128)(2,1)S(1)} %constant_dynamic-slice_fusion.10), channel_id=1, source_target_pairs={{0,4},{2,6},{4,0},{6,2},{8,12},{10,14},{12,8},{14,10},{16,20},{18,... | collective-permute-start | bytes 1277960 | tf_op jit(solution)/shard_map/ppermute | solution.py:572
  681.6 6.3 collective-permute-start.32
  686.0 13.3 %collective-permute-start.40 = (bf16[32,1664]{1,0:T(8,128)(2,1)S(1)}, bf16[32,1664]{1,0:T(8,128)(2,1)S(1)}, u32[]{:S(2)}, u32[]{:S(2)}) collective-permute-start(bf16[32,1664]{1,0:T(8,128)(2,1)S(1)} %constant_dynamic-update-slice_fusion.16), channel_id=1, source_target_pairs={{0,4},{2,6},{4,0},{6,2},{8,12},{10,14},{12,8},{14,10},{16,20},{18,... | collective-permute-start | bytes 319496 | tf_op jit(solution)/shard_map/ppermute | solution.py:572
  687.9 22.5 %collective-permute-start.33 = (bf16[64,1664]{1,0:T(8,128)(2,1)S(1)}, bf16[64,1664]{1,0:T(8,128)(2,1)S(1)}, u32[]{:S(2)}, u32[]{:S(2)}) collective-permute-start(bf16[64,1664]{1,0:T(8,128)(2,1)S(1)} %constant_dynamic-update-slice_fusion.22), channel_id=1, source_target_pairs={{0,8},{2,10},{4,12},{6,14},{8,0},{10,2},{12,4},{14,6},{16,24},{18,... | collective-permute-start | bytes 638984 | tf_op jit(solution)/shard_map/ppermute | solution.py:572
  699.3 12.8 %collective-permute-start.41 = (bf16[64,1664]{1,0:T(8,128)(2,1)S(1)}, bf16[64,1664]{1,0:T(8,128)(2,1)S(1)}, u32[]{:S(2)}, u32[]{:S(2)}) collective-permute-start(bf16[64,1664]{1,0:T(8,128)(2,1)S(1)} %constant_dynamic-update-slice_fusion.14), channel_id=1, source_target_pairs={{0,2},{2,0},{4,6},{6,4},{8,10},{10,8},{12,14},{14,12},{16,18},{18,... | collective-permute-start | bytes 638984 | tf_op jit(solution)/shard_map/ppermute | solution.py:572
  710.4 39.6 %collective-permute-start.34 = (bf16[128,1664]{1,0:T(8,128)(2,1)S(1)}, bf16[128,1664]{1,0:T(8,128)(2,1)S(1)}, u32[]{:S(2)}, u32[]{:S(2)}) collective-permute-start(bf16[128,1664]{1,0:T(8,128)(2,1)S(1)} %constant_dynamic-update-slice_fusion.20), channel_id=1, source_target_pairs={{0,4},{2,6},{4,0},{6,2},{8,12},{10,14},{12,8},{14,10},{16,20},{18,... | collective-permute-start | bytes 1277960 | tf_op jit(solution)/shard_map/ppermute | solution.py:572
  712.2 37.9 %collective-permute-start.42 = (bf16[128,1664]{1,0:T(8,128)(2,1)S(1)}, bf16[128,1664]{1,0:T(8,128)(2,1)S(1)}, u32[]{:S(2)}, u32[]{:S(2)}) collective-permute-start(bf16[128,1664]{1,0:T(8,128)(2,1)S(1)} %constant_dynamic-update-slice_fusion.12), channel_id=1, source_target_pairs={{0,8},{2,10},{4,12},{6,14},{8,0},{10,2},{12,4},{14,6},{16,24},{18,... | collective-permute-start | bytes 1277960 | tf_op jit(solution)/shard_map/ppermute | solution.py:572
  715.0 9.8 %collective-permute-start.21 = (bf16[64,1664]{1,0:T(8,128)(2,1)S(1)}, bf16[64,1664]{1,0:T(8,128)(2,1)S(1)}, u32[]{:S(2)}, u32[]{:S(2)}) collective-permute-start(bf16[64,1664]{1,0:T(8,128)(2,1)S(1)} %constant_dynamic-slice_fusion.9), channel_id=1, source_target_pairs={{0,8},{2,10},{4,12},{6,14},{8,0},{10,2},{12,4},{14,6},{16,24},{18,... | collective-permute-start | bytes 638984 | tf_op jit(solution)/shard_map/ppermute | solution.py:572
  724.9 21.8 %collective-permute-start.22 = (bf16[32,1664]{1,0:T(8,128)(2,1)S(1)}, bf16[32,1664]{1,0:T(8,128)(2,1)S(1)}, u32[]{:S(2)}, u32[]{:S(2)}) collective-permute-start(bf16[32,1664]{1,0:T(8,128)(2,1)S(1)} %constant_dynamic-slice_fusion.8), channel_id=1, source_target_pairs={{0,16},{2,18},{4,20},{6,22},{8,24},{10,26},{12,28},{14,30},{16,0},... | collective-permute-start | bytes 319496 | tf_op jit(solution)/shard_map/ppermute | solution.py:572
  746.8 5.4 collective-permute-start.23
  752.1 5.7 collective-permute-start.24
  757.9 7.0 collective-permute-start.25
  764.9 11.9 %collective-permute-start.26 = (bf16[256,1664]{1,0:T(8,128)(2,1)S(1)}, bf16[256,1664]{1,0:T(8,128)(2,1)S(1)}, u32[]{:S(2)}, u32[]{:S(2)}) collective-permute-start(bf16[256,1664]{1,0:T(8,128)(2,1)S(1)} %constant_dynamic-update-slice_fusion.28), channel_id=1, source_target_pairs={{0,2},{2,0},{4,6},{6,4},{8,10},{10,8},{12,14},{14,12},{16,18},{18,... | collective-permute-start | bytes 2555912 | tf_op jit(solution)/shard_map/ppermute | solution.py:572
  777.8 19.0 %collective-permute-start.43 = (f32[1024,2]{1,0:T(8,128)}, f32[1024,2]{1,0:T(8,128)}, u32[]{:S(2)}, u32[]{:S(2)}) collective-permute-start(f32[1024,2]{1,0:T(8,128)} %maximum_convert_fusion.2), channel_id=1, source_target_pairs={{1,0},{0,1},{3,2},{2,3},{5,4},{4,5},{7,6},{6,7},{9,8},{8,9},{11,10... | collective-permute-start | bytes 24584 | tf_op jit(solution)/shard_map/ppermute | solution.py:534
  (52 other events, 749.2 us)
Sparse Core Ops, SparseCore 0:
  13.1 16.1 all-gather.3
  592.5 156.5 all-gather.5

commit v4 on v3

--- a/solution.py
+++ b/solution.py
@@ -79,16 +79,70 @@
     )(memory_keys, memory_values).reshape(heads, rows, 2, width)
 
 
+def own_columns(picks):
+    shape = (8, 8 * picks * 2)
+    lane = lax.broadcasted_iota(jnp.int32, shape, 1)
+    row = lax.broadcasted_iota(jnp.int32, shape, 0)
+    return jnp.logical_and(lane // (2 * picks) == row, lane % 2 == 0)
+
+
+def copy_rows(picked, first, table_ref, found_ref, start, count):
+    for at in range(0, count, 8):
+        rows_now = [
+            table_ref[picked[(first + at + j) // 128, (first + at + j) % 128]] for j in range(8)
+        ]
+        for j in range(8):
+            found_ref[start + at + j] = rows_now[j]
+        yield
+
+
+def recall_rows(picks, scale, own, query_ref, query_at, rows_ref, read_ref, read_at, tokens):
+    wide = 8 * picks * 2
+    groups = range(tokens // 8)
+    scores = []
+    for g in groups:
+        rows = rows_ref[pl.ds(g * wide, wide), :]
+        scores.append(dot_inner(query_ref[pl.ds(query_at + g * 8, 8), :], rows))
+        yield
+    shifted = []
+    totals = []
+    for g in groups:
+        masked = jnp.where(own, scores[g] * (scale * log2_e), -jnp.inf)
+        exponent = jnp.exp2(masked - jnp.max(masked, 1, keepdims=True))
+        totals.append(jnp.sum(exponent, 1, keepdims=True))
+        shifted.append(pltpu.roll(exponent, 1, 1).astype(low_type))
+        yield
+    for g in groups:
+        rows = rows_ref[pl.ds(g * wide, wide), :]
+        read_ref[pl.ds(read_at + g * 8, 8), :] = dot_rows(shifted[g], rows) / totals[g]
+        yield
+
+
+def weave(many, many_count, few, few_count):
+    done = 0
+    for number in range(few_count):
+        until = (number + 1) * many_count // few_count
+        while done < until:
+            next(many)
+            done += 1
+        next(few)
+
+
 def gather_kernel(
-    index_hbm, table_hbm, found_ref, table_ref, table_sems, index_a, index_b, index_sems
+    picks, scale, index_hbm, table_hbm, now_ref, before_ref, found_ref, late_ref, early_ref,
+    table_ref, table_sems, index_a, index_b, index_sems, stage_ref, stage_sems,
 ):
-    heads = pl.num_programs(0)
-    head = pl.program_id(0)
-    step = head * pl.num_programs(1) + pl.program_id(1)
-    steps = heads * pl.num_programs(1)
+    step = pl.program_id(0)
+    steps = pl.num_programs(0) - 1
+    heads = table_sems.shape[0]
+    blocks = steps // heads
     chunk = found_ref.shape[0] // 2
-    rows = table_ref.shape[0] // table_sems.shape[0]
+    rows = table_ref.shape[0] // heads
     slots = (index_a, index_b)
+    part = chunk // 2
+    tokens = part // picks
+    own = own_columns(picks)
+    flat = found_ref.reshape(4 * chunk, 128)
 
     def index_copy(number, slot):
         return pltpu.make_async_copy(index_hbm.at[number], slots[slot], index_sems.at[slot])
@@ -99,107 +153,113 @@
             table_hbm.at[where], table_ref.at[where], table_sems.at[number]
         )
 
+    def stage_copy(number):
+        return pltpu.make_async_copy(
+            flat.at[pl.ds(number * 2 * part, 2 * part)], stage_ref.at[number], stage_sems.at[number]
+        )
+
+    def reads(number, query_ref, read_ref):
+        return recall_rows(
+            picks, scale, own, query_ref, (number % 2) * tokens, stage_ref.at[number], read_ref,
+            (number % 2) * tokens, tokens,
+        )
+
     @pl.when(step == 0)
     def start_all():
         index_copy(0, 0).start()
         index_copy(1, 1).start()
-        for number in range(table_sems.shape[0]):
+        for number in range(heads):
             table_copy(number).start()
-
-    @pl.when(pl.program_id(1) == 0)
+        stage_copy(2).start()
+        stage_copy(3).start()
+
+    @pl.when(jnp.logical_and(step < steps, step % blocks == 0))
     def wait_table():
-        table_copy(head).wait()
-
-    following = jnp.minimum(step + 1, steps - 1)
-    for slot in range(2):
-        index_copy(2 * step + slot, slot).wait()
-        picked = slots[slot]
-        for start in range(0, chunk, 8):
-            rows_now = [
-                table_ref[picked[(start + j) // 128, (start + j) % 128]] for j in range(8)
-            ]
-            for j in range(8):
-                found_ref[slot * chunk + start + j] = rows_now[j]
-        index_copy(2 * following + slot, slot).start()
-
-    @pl.when(step == steps - 1)
-    def drain():
-        index_copy(2 * following, 0).wait()
-        index_copy(2 * following + 1, 1).wait()
-
-
-def gather_found(index_rows, table):
+        table_copy(step // blocks).wait()
+
+    @pl.when(step < steps)
+    def work():
+        following = jnp.minimum(step + 1, steps - 1)
+        for number in range(4):
+            slot = number // 2
+            if number % 2 == 0:
+                index_copy(2 * step + slot, slot).wait()
+            finished = (number + 2) % 4
+            stage_copy(finished).wait()
+            copied = copy_rows(
+                slots[slot], (number % 2) * part, table_ref, found_ref, number * part, part
+            )
+            if number < 2:
+                read = reads(finished, before_ref, late_ref)
+            else:
+                read = reads(finished, now_ref, early_ref)
+            weave(copied, part // 8, read, 3 * (tokens // 8))
+            stage_copy(number).start()
+            if number % 2 == 1:
+                index_copy(2 * following + slot, slot).start()
+
+    @pl.when(step == steps)
+    def finish():
+        for number in (2, 3):
+            stage_copy(number).wait()
+            for unused in reads(number, before_ref, late_ref):
+                pass
+        for slot in range(2):
+            index_copy(2 * (steps - 1) + slot, slot).wait()
+
+
+def gather_found(index_rows, table, queries, picks, scale):
     heads, rows, unused, width = table.shape
-    total = index_rows.size // heads
-    chunk = min(4096, total // 2)
-    blocks = total // (2 * chunk)
+    tokens = queries.shape[0]
+    half = 128
+    blocks = tokens // (2 * half)
+    steps = heads * blocks
+    chunk = half * picks
+
+    def query_spec(shift):
+        def place(t):
+            at = jnp.clip(t - shift, 0, steps - 1)
+            return (2 * (at % blocks) + shift, at // blocks)
+
+        return pl.BlockSpec((half, width), place)
+
     return pl.pallas_call(
-        gather_kernel,
-        grid=(heads, blocks),
-        in_specs=[pl.BlockSpec(memory_space=pl.ANY), pl.BlockSpec(memory_space=pl.ANY)],
-        out_specs=pl.BlockSpec((2 * chunk, 2, width), lambda h, i: (h * blocks + i, 0, 0)),
-        out_shape=jax.ShapeDtypeStruct((heads * total, 2, width), low_type),
+        functools.partial(gather_kernel, picks, scale),
+        grid=(steps + 1,),
+        in_specs=[
+            pl.BlockSpec(memory_space=pl.ANY),
+            pl.BlockSpec(memory_space=pl.ANY),
+            query_spec(0),
+            query_spec(1),
+        ],
+        out_specs=[
+            pl.BlockSpec((2 * chunk, 2, width), lambda t: (jnp.minimum(t, steps - 1), 0, 0)),
+            pl.BlockSpec((half, width), lambda t: (jnp.maximum(t - 1, 0), 0)),
+            pl.BlockSpec((half, width), lambda t: (jnp.minimum(t, steps - 1), 0)),
+        ],
+        out_shape=[
+            jax.ShapeDtypeStruct((heads * tokens * picks, 2, width), low_type),
+            jax.ShapeDtypeStruct((heads * tokens // 2, width), full_type),
+            jax.ShapeDtypeStruct((heads * tokens // 2, width), full_type),
+        ],
         scratch_shapes=[
             pltpu.VMEM((heads * rows, 2, width), low_type),
             pltpu.SemaphoreType.DMA((heads,)),
             pltpu.SMEM((chunk // 128, 128), jnp.int32),
             pltpu.SMEM((chunk // 128, 128), jnp.int32),
             pltpu.SemaphoreType.DMA((2,)),
+            pltpu.VMEM((4, chunk, width), low_type),
+            pltpu.SemaphoreType.DMA((4,)),
         ],
         compiler_params=pltpu.CompilerParams(vmem_limit_bytes=vmem_most),
         cost_estimate=pl.CostEstimate(
-            flops=0, bytes_accessed=4 * heads * total * width * 4, transcendentals=0
+            flops=0, bytes_accessed=4 * heads * tokens * picks * width * 4, transcendentals=0
         ),
         name="gather_found",
-    )(index_rows.reshape(-1, chunk // 128, 128), table.reshape(heads * rows, 2, width))
-
-
-def own_columns(picks):
-    shape = (8, 8 * picks * 2)
-    lane = lax.broadcasted_iota(jnp.int32, shape, 1)
-    row = lax.broadcasted_iota(jnp.int32, shape, 0)
-    return jnp.logical_and(lane // (2 * picks) == row, lane % 2 == 0)
-
-
-def recall_kernel(picks, scale, found_ref, query_ref, read_ref):
-    tokens = query_ref.shape[0]
-    wide = 8 * picks * 2
-    own = own_columns(picks)
-    groups = range(tokens // 8)
-    scores = [
-        dot_inner(query_ref[pl.ds(g * 8, 8), :], found_ref[pl.ds(g * wide, wide), :])
-        for g in groups
-    ]
-    for g in groups:
-        masked = jnp.where(own, scores[g] * (scale * log2_e), -jnp.inf)
-        exponent = jnp.exp2(masked - jnp.max(masked, 1, keepdims=True))
-        total = jnp.sum(exponent, 1, keepdims=True)
-        shifted = pltpu.roll(exponent, 1, 1).astype(low_type)
-        read_ref[pl.ds(g * 8, 8), :] = (
-            dot_rows(shifted, found_ref[pl.ds(g * wide, wide), :]) / total
-        )
-
-
-def recall(found, queries, heads, picks, scale):
-    tokens = queries.shape[0]
-    width = queries.shape[1] // (3 * heads)
-    step = min(512, tokens)
-    blocks = tokens // step
-    return pl.pallas_call(
-        functools.partial(recall_kernel, picks, scale),
-        grid=(heads, blocks),
-        in_specs=[
-            pl.BlockSpec((step * picks * 2, width), lambda h, i: (h * blocks + i, 0)),
-            pl.BlockSpec((step, width), lambda h, i: (i, h)),
-        ],
-        out_specs=pl.BlockSpec((step, width), lambda h, i: (i, h)),
-        out_shape=jax.ShapeDtypeStruct((tokens, heads * width), full_type),
-        compiler_params=pltpu.CompilerParams(vmem_limit_bytes=vmem_most),
-        cost_estimate=pl.CostEstimate(
-            flops=0, bytes_accessed=heads * tokens * picks * width * 8, transcendentals=0
-        ),
-        name="recall",
-    )(found, queries)
+    )(
+        index_rows.reshape(-1, chunk // 128, 128), table.reshape(heads * rows, 2, width), queries,
+        queries,
+    )
 
 
 def recall_back_kernel(
@@ -236,7 +296,9 @@
     sums_ref[0] += jnp.broadcast_to(gained, (8, 128))
 
 
-def recall_back(found, queries, mixed_delta, gates, head, carried, kept, heads, picks, scale):
+def recall_back(
+    found, queries, mixed_delta, gates, head, carried, after, kept, heads, picks, scale
+):
     tokens = queries.shape[0]
     width = mixed_delta.shape[1] // heads
     step = min(512, tokens)
@@ -247,7 +309,7 @@
     first = 4 + len(extra)
 
     def kernel(gate_ref, found_ref, query_ref, delta_ref, *rest):
-        query_delta_ref, sums_ref = rest[len(extra) + len(carried) :][:2]
+        query_delta_ref, sums_ref = rest[len(extra) + len(carried) + len(after) :][:2]
         recall_back_kernel(
             picks, scale, gate_ref, found_ref, query_ref, delta_ref, query_delta_ref, sums_ref
         )
@@ -261,7 +323,7 @@
             rows_spec,
             rows_spec,
         ]
-        + [anywhere] * (len(extra) + len(carried)),
+        + [anywhere] * (len(extra) + len(carried) + len(after)),
         out_specs=[rows_spec, pl.BlockSpec((1, 8, 128), lambda i: (0, 0, 0))]
         + [anywhere] * len(carried),
         out_shape=[
@@ -276,7 +338,7 @@
             flops=0, bytes_accessed=tokens * picks * width * 8, transcendentals=0
         ),
         name="recall_back",
-    )(gates[head : head + 1], found, queries, mixed_delta, *extra, *carried)
+    )(gates[head : head + 1], found, queries, mixed_delta, *extra, *carried, *after)
     return out[0], out[1], list(out[2:])
 
 
@@ -287,7 +349,7 @@
 
 def local_kernel(
     scale, gate_ref, far_ref, column_ref, query_ref, key_ref, value_ref, query_mask_ref,
-    key_mask_ref, recall_ref, mixed_ref, bias_ref,
+    key_mask_ref, early_ref, late_ref, mixed_ref, bias_ref,
 ):
     head = pl.program_id(0)
 
@@ -315,15 +377,17 @@
         parts = [jnp.exp2(part - top) for part in parts]
         total = jnp.sum(functools.reduce(jnp.add, parts), 1, keepdims=True)
         read = sum(dot_rows(parts[j].astype(low_type), value_ref[at[j], :]) for j in range(count))
-        mixed_ref[at[t], :] = (
-            gate * recall_ref[at[t], :] + ((1.0 - gate) / total) * read
-        ).astype(low_type)
-
-
-def local_read(projected, query_mask, key_mask, recalled, columns, far, gates, seq_len, scale):
-    tokens = recalled.shape[0]
+        half = pl.ds(t * (tile // 2), tile // 2)
+        recalled = jnp.concatenate([early_ref[half, :], late_ref[half, :]], 0)
+        mixed_ref[at[t], :] = (gate * recalled + ((1.0 - gate) / total) * read).astype(low_type)
+
+
+def local_read(projected, query_mask, key_mask, early, late, columns, far, gates, seq_len, scale):
+    tokens, width = projected.shape
     heads = gates.shape[0]
-    width = recalled.shape[1] // heads
+    width = width // (3 * heads)
+    sequences = tokens // seq_len
+    half_spec = pl.BlockSpec((seq_len // 2, width), lambda h, s: (h * sequences + s, 0))
 
     def rows_of(shift):
         return pl.BlockSpec((seq_len, width), lambda h, s: (s, h + shift * heads))
@@ -342,7 +406,8 @@
             rows_of(2),
             mask_spec,
             mask_spec,
-            rows_of(0),
+            half_spec,
+            half_spec,
         ],
         out_specs=rows_of(0),
         out_shape=jax.ShapeDtypeStruct((tokens, heads * width), low_type),
@@ -352,7 +417,7 @@
             flops=0, bytes_accessed=heads * tokens * seq_len * 20, transcendentals=0
         ),
         name="local_read",
-    )(gates, far, columns, projected, projected, projected, query_mask, key_mask, recalled)
+    )(gates, far, columns, projected, projected, projected, query_mask, key_mask, early, late)
 
 
 def local_back_kernel(
@@ -576,9 +641,9 @@
     return (lax.axis_index("dp") >> bit) & 1
 
 
-def halve_step(parts, step):
+def halve_step(parts, orders, step):
     kept, sent = [], []
-    for part, order in zip(parts, bit_orders()):
+    for part, order in zip(parts, orders):
         half = part.shape[0] // 2
         side = side_of(order[step])
         sent.append(
@@ -623,12 +688,12 @@
     )
 
 
-def gather_all(packed, parts):
+def gather_all(packed, parts, orders):
     whole = lax.all_gather(packed, "dp", axis=0)
     width = packed.shape[1]
     wide = []
     start = 0
-    for part, order in zip(parts, bit_orders()):
+    for part, order in zip(parts, orders):
         bits = len(order)
         rows = part.shape[0]
         columns = []
@@ -668,14 +733,15 @@
 
     offsets = jnp.arange(head_count, dtype=jnp.int32) * memory_rows
     index_rows = memory_index.transpose(1, 0, 2) + offsets[:, None, None]
-    found = gather_found(index_rows, interleave(memory_keys, memory_values))
-    found = found.reshape(-1, head_width)
+    table = interleave(memory_keys, memory_values)
 
     token_full = tokens.astype(full_type)
     normed_rows = rms_scaled(token_full, attn_gain).astype(low_type)
     normed = lax.all_gather(normed_rows, "tensor", axis=0, tiled=True)
     joined = jnp.concatenate([query_weight, key_weight, value_weight], 1)
     projected = dot_rows(normed, joined).astype(low_type)
+    found, late, early = gather_found(index_rows, table, projected, picks, scale)
+    found = found.reshape(-1, head_width)
 
     query_mask, key_mask = mask_rows(block_ids)
     place = jnp.arange(ring, dtype=jnp.int32)
@@ -691,9 +757,8 @@
     far = jnp.stack([scaled_table[15], scaled_table[31]], 1)
     gates = jax.nn.sigmoid(memory_gate)
 
-    recalled = recall(found, projected, head_count, picks, scale)
     mixed_rows = local_read(
-        projected, query_mask, key_mask, recalled, ahead_columns, far, gates, seq_len, scale
+        projected, query_mask, key_mask, early, late, ahead_columns, far, gates, seq_len, scale
     )
     middle = token_full + fold(
         lambda rows: dot_rows(rows, output_weight), lambda k: share_of(mixed_rows, k, share_rows)
@@ -704,6 +769,12 @@
     hidden = dot_rows(second, hidden_weight)
     active = jax.nn.gelu(hidden).astype(low_type)
     return_low = dot_outer(active, grad_full).astype(low_type)
+    orders = bit_orders()
+    steps = len(orders[0])
+    return_half = return_low.shape[0] // 2
+    return_parts = [return_low[:return_half], return_low[return_half:]]
+    for step in range(steps):
+        return_parts = add_low(*halve_step(return_parts, orders[1:], step))
     active_delta = dot_inner(grad_full, return_weight)
     gelu_back = jax.vjp(jax.nn.gelu, hidden)[1]
     hidden_delta = gelu_back(active_delta)[0].astype(low_type)
@@ -712,6 +783,10 @@
         lambda k: lax.slice_in_dim(hidden_delta, k * share_rows, (k + 1) * share_rows),
     )
     hidden_low = dot_outer(second, hidden_delta).astype(low_type)
+    hidden_half = hidden_low.shape[0] // 2
+    hidden_parts = [hidden_low[:hidden_half], hidden_low[hidden_half:]]
+    hidden_parts = add_low(*halve_step(hidden_parts, orders[:2], 0))
+    kept, sent = halve_step(hidden_parts, orders[:2], 1)
     second_back = jax.vjp(rms_scaled, middle, mlp_gain)[1]
     middle_part, mlp_gain_part = second_back(second_delta)
     middle_delta = grad_output.astype(full_type) + middle_part
@@ -725,50 +800,46 @@
         )
     ).astype(low_type)
 
-    return_half = return_low.shape[0] // 2
-    steps = len(bit_orders()[0])
-    output_low = dot_outer(mixed_rows, middle_full).astype(low_type)
-    kept, sent = halve_step(
-        [
-            hidden_low,
-            return_low[:return_half],
-            jnp.concatenate([return_low[return_half:], output_low], 0),
-        ],
-        0,
-    )
-    taken = 0
-    waits = (0, 2, 3)
+    taken = 1
+    shards, packed = [], []
     recall_delta = None
     recall_sums = []
     for head in range(head_count):
         recall_delta, head_sums, kept = recall_back(
-            found, projected, mixed_delta, gates, head, kept, recall_delta, head_count, picks, scale
+            found, projected, mixed_delta, gates, head, kept, packed, recall_delta, head_count,
+            picks, scale,
         )
         recall_sums.append(head_sums)
-        if head in waits and taken < steps - 1:
+        if taken < steps - 1:
             taken += 1
-            kept, sent = halve_step(add_low(kept, sent), taken)
+            kept, sent = halve_step(add_low(kept, sent), orders[:2], taken)
+        elif not shards:
+            shards = add_low(kept, sent) + return_parts
+            packed = [pack(shards)]
+            kept = []
     while taken < steps - 1:
         taken += 1
-        kept, sent = halve_step(add_low(kept, sent), taken)
+        kept, sent = halve_step(add_low(kept, sent), orders[:2], taken)
+    if not shards:
+        shards = add_low(kept, sent) + return_parts
+        packed = [pack(shards)]
+    hidden_low_sum, hidden_high_sum, return_low_sum, return_high_sum = gather_all(
+        packed[0], shards, orders[:2] + orders[1:]
+    )
+    hidden_sum = jnp.concatenate([hidden_low_sum, hidden_high_sum], 0)
+    return_sum = jnp.concatenate([return_low_sum, return_high_sum], 0)
     recall_sums = jnp.concatenate(recall_sums, 0)
     half_heads = max(1, head_count // 2)
     deltas = []
     diagonals = []
     local_sums = []
-    shards = []
-    packed = []
     for start in range(0, head_count, half_heads):
-        deltas, diagonal_now, sums_now, kept = local_back(
+        deltas, diagonal_now, sums_now, unused = local_back(
             projected, query_mask, key_mask, mixed_delta, recall_delta, behind_columns, far, gates,
-            seq_len, scale, (start, half_heads), [] if shards else kept, deltas, packed,
-        )
-        if not shards:
-            shards = add_low(kept, sent)
-            packed = [pack(shards)]
+            seq_len, scale, (start, half_heads), [], deltas, packed,
+        )
         diagonals.append(diagonal_now)
         local_sums.append(sums_now)
-    hidden_sum, return_sum, mixed_sum = gather_all(packed[0], shards)
     query_delta, key_delta, value_delta = deltas
     diagonals = jnp.concatenate(diagonals, 0)
     local_sums = jnp.concatenate(local_sums, 0)
@@ -790,15 +861,16 @@
     extra = jnp.stack([attn_gain_part, mlp_gain_part, small], 1)
     extra = jnp.pad(extra, ((0, 0), (0, 125)))
     joined_low = jnp.concatenate([joined_part, extra], 1).astype(low_type)
-    quarter = joined_low.shape[0] // 4
+    joined_half = joined_low.shape[0] // 2
     last = [
-        joined_low[: 2 * quarter],
-        joined_low[2 * quarter : 3 * quarter],
-        joined_low[3 * quarter :],
+        joined_low[:joined_half],
+        joined_low[joined_half:],
+        dot_outer(mixed_rows, middle_full).astype(low_type),
     ]
     for step in range(steps):
-        last = add_low(*halve_step(last, step))
-    joined_sum = double_all(last)
+        last = add_low(*halve_step(last, orders, step))
+    last, hidden_sum, return_sum = lax.optimization_barrier((last, hidden_sum, return_sum))
+    *joined_sum, output_sum = double_all(last)
 
     normed_delta = fold(
         lambda rows: dot_inner(rows, joined), lambda k: share_of(project_delta, k, share_rows)
@@ -806,23 +878,26 @@
     first_back = jax.vjp(rms_scaled, token_full, attn_gain)[1]
     tokens_grad = (middle_delta + first_back(normed_delta)[0]).astype(low_type)
 
-    joined_grad = jnp.concatenate(joined_sum, 0).astype(full_type)
-    gains = sum(fetch(joined_grad[:, 3 * inner_width : 3 * inner_width + 2]))
-    small_sum = joined_grad[:, 3 * inner_width + 2]
+    def joined_columns(start, stop):
+        return jnp.concatenate([part[:, start:stop].astype(full_type) for part in joined_sum], 0)
+
+    last_columns = joined_columns(3 * inner_width, 3 * inner_width + 128)
+    gains = sum(fetch(last_columns[:, :2].T))
+    small_sum = last_columns[:, 2]
     table_size = head_count * 32
     return (
         layer_output,
         tokens_grad,
-        gains[:, 0],
-        joined_grad[:, :inner_width],
-        joined_grad[:, inner_width : 2 * inner_width],
-        joined_grad[:, 2 * inner_width : 3 * inner_width],
-        mixed_sum[return_half:],
+        gains[0],
+        joined_columns(0, inner_width),
+        joined_columns(inner_width, 2 * inner_width),
+        joined_columns(2 * inner_width, 3 * inner_width),
+        output_sum.astype(full_type),
         small_sum[:table_size].reshape(head_count, 32).T,
         small_sum[table_size : table_size + head_count],
-        gains[:, 1],
+        gains[1],
         hidden_sum,
-        jnp.concatenate([return_sum, mixed_sum[:return_half]], 0),
+        return_sum,
     )
 
 

time: 836 us -> 807 us (0.965)
  waiting for transfers between devices: 81.1 us -> 113 us
  starting transfers between devices: 82.2 us -> 54.2 us
  Pallas kernels: 389 us -> 369 us
  local copies, waits for them, and re-layouts: 58.8 us -> 46.1 us
  other arithmetic: 53.5 us -> 62.9 us
    ppermute x36 -> x40, waiting for transfers between devices: 81.1 us -> 113 us  [swap_over(): lax.ppermute(rows, 'dp', [(i, i ^ 1 << bit) for i in range(lax.axis_size(...]
    ppermute x36 -> x40, starting transfers between devices: 62.6 us -> 39.2 us  [swap_over(): lax.ppermute(rows, 'dp', [(i, i ^ 1 << bit) for i in range(lax.axis_size(...]
    pallas_call x2 -> x1, Pallas kernels: 208 us -> 189 us  [gather_found(): pl.pallas_call(functools.partial(gather_kernel, picks, scale), grid=(step...]
    concatenate x2 -> x5, other arithmetic: 9.67 us -> 27.9 us  [the longest x1 18.5 us: body(): hidden_sum = jnp.concatenate([hidden_low_sum, hidden_high_sum], 0)]
  transfers between devices with their start and end apart: 46 -> 50, of which waited for: 20 -> 20; matrix products, arithmetic and copies ran while one was open for 21% -> 17% of each run, Pallas kernels for 37% -> 20%
where the time goes in v4:
time: 807 us; the launch traced here: 800 us
  Pallas kernels  369 us (46%)
  matrix products  138 us (17%)
  waiting for transfers between devices  113 us (14%)
  other arithmetic  62.9 us (8%)
  starting transfers between devices  54.2 us (7%)
  local copies, waits for them, and re-layouts  46.1 us (6%)
  between operations  15.8 us (2%)
    pallas_call x1, Pallas kernels, gather_found(): pl.pallas_call(functools.partial(gather_kernel, picks, scale), grid=(step...  189 us
    ppermute x40, waiting for transfers between devices, swap_over(): lax.ppermute(rows, 'dp', [(i, i ^ 1 << bit) for i in range(lax.axis_size(...  113 us
    pallas_call x4, Pallas kernels, recall_back(): pl.pallas_call(kernel, grid=(blocks,), in_specs=[pl.BlockSpec(memory_spac...  75 us
    dot_general x6, matrix products, dot_rows(): return jnp.dot(left, right, preferred_element_type=full_type)  56.7 us
    pallas_call x2, Pallas kernels, local_back(): pl.pallas_call(kernel, grid=(count, tokens // seq_len), in_specs=[smem, s...  44.6 us
    dot_general x6, matrix products, dot_inner(): lax.dot_general(left, right, (((1,), (1,)), ((), ())), preferred_element_...  42.9 us
    ppermute x40, starting transfers between devices, swap_over(): lax.ppermute(rows, 'dp', [(i, i ^ 1 << bit) for i in range(lax.axis_size(...  39.2 us
    pallas_call x1, Pallas kernels, interleave(): pl.pallas_call(interleave_kernel, grid=(heads, rows // step), in_specs=[s...  39.1 us
  transfers between devices with their start and end apart: 50, of which 20 were waited for; matrix products, arithmetic and copies ran while one was open for 17% of the time, Pallas kernels for 20%

profile of v4, /device:TPU:1, one launch (start us, length us, event | category | flops | bytes accessed | tf_op | source)
XLA Modules:
  0.0 799.9 jit_solution(4539219934849410708)
XLA Ops:
  10.7 3.5 fusion.13
  14.4 2.7 copy.65
  17.1 4.2 reshape.199.index_hbm
  28.4 39.1 %interleave.1 = bf16[131072,128]{1,0:T(8,128)(2,1)} custom-call(bf16[4,16384,128]{2,1,0:T(8,128)(2,1)} %key_ref.1, bf16[4,16384,128]{2,1,0:T(8,128)(2,1)} %value_ref.1), custom_call_target="tpu_custom_call" | custom-call | flops 8589934592 | bytes 67108864 | tf_op jit(solution)/shard_map/interleave/pallas_call | solution.py:67
  67.4 11.3 %convolution_convert_fusion.now_ref.before_ref.query_ref.key_ref.value_ref.refs_3_.refs_4_.refs_5_ = bf16[2048,1536]{1,0:T(8,128)(2,1)} fusion(bf16[2048,1024]{1,0:T(8,128)(2,1)} %all-gather.4.cloned.1.call-done, bf16[1024,1536]{1,0:T(8,128)(2,1)} %copy-done.19), kind=kOutput, calls=%fused_computation.15 | convolution fusion | flops 6445596672 | bytes 13631488 | tf_op jit(solution)/shard_map/dot_general | solution.py:36
  78.7 189.5 %gather_found.1 = (bf16[262144,2,128]{2,1,0:T(2,128)(2,1)}, f32[4096,128]{1,0:T(8,128)}, f32[4096,128]{1,0:T(8,128)}) custom-call(s32[64,32,128]{2,1,0:T(8,128)} %reshape.199.index_hbm, bf16[65536,2,128]{2,1,0:T(2,128)(2,1)} %bitcast.61, bf16[2048,1536]{1,0:T(8,128)(2,1)} %convolution_convert_fusion.now_ref.before_ref.query_ref.key_ref.value_ref.refs_3_.refs_4_.refs_5_, ...), custom_call_target="tpu_custom_call" | custom-call | bytes 536870912 | tf_op jit(solution)/shard_map/gather_found/pallas_call | solution.py:226
  268.2 21.2 %local_read.1 = bf16[2048,512]{1,0:T(8,128)(2,1)} custom-call(f32[4]{0:T(128)} %add_divide_fusion.gate_ref, f32[4,2]{1,0:T(4,128)} %pad_maximum_fusion.8.far_ref, f32[4,1,1024]{2,1,0:T(1,128)} %broadcast_in_dim.33.column_ref, bf16[2048,1536]{1,0:T(8,128)(2,1)} %convolution_convert_fusion.now_ref.before_ref.query_ref.key_ref.value_ref.refs_3_.refs_4_.refs_5_, ...), custom_call_target="tpu_custom_call" | custom-call | bytes 167772160 | tf_op jit(solution)/shard_map/local_read/pallas_call | solution.py:397
  289.5 3.8 convolution_convert_fusion.4
  299.0 3.2 multiply_reduce_fusion.3
  305.1 11.7 %fusion.109 = f32[2048,2048]{1,0:T(8,128)} fusion(bf16[2048,1024]{1,0:T(8,128)(2,1)S(1)} %constant_dynamic-update-slice_fusion.3, bf16[2048,1024]{1,0:T(8,128)(2,1)S(1)} %copy-done.45), kind=kOutput, calls=%fused_computation.272 | convolution fusion | flops 8589934592 | bytes 25165824 | tf_op jit(solution)/shard_map/dot_general | solution.py:46
  316.8 27.0 %fusion.6 = (bf16[2048,2048]{1,0:T(8,128)(2,1)}, bf16[2048,2048]{1,0:T(8,128)(2,1)}) fusion(f32[2048,2048]{1,0:T(8,128)} %fusion.109, bf16[1024,2048]{1,0:T(8,128)(2,1)} %param.29, bf16[1024,1024]{1,0:T(8,128)(2,1)} %collective-permute-done.1, bf16[1024,1024]{1,0:T(8,128)(2,1)S(1)} %multiply_convert_fusion.1), kind=kOutput, calls=%fused_computation.8 | convolution fusion | flops 8690597888 | bytes 41943040 | tf_op jit(solution)/shard_map/dot_general | solution.py:36
  343.8 11.7 %convolution_convert_fusion.2 = bf16[2048,1024]{1,0:T(8,128)(2,1)S(1)} fusion(bf16[2048,2048]{1,0:T(8,128)(2,1)} %get-tuple-element.86, bf16[2048,1024]{1,0:T(8,128)(2,1)S(1)} %constant_dynamic-update-slice_fusion.3), kind=kOutput, calls=%fused_computation.47 | convolution fusion | flops 8592031744 | bytes 16777216 | tf_op jit(solution)/shard_map/dot_general | solution.py:40
  355.5 5.2 fusion.29
  360.8 6.1 fusion.21
  367.4 2.7 collective-permute-start.18
  372.2 7.9 fusion.32
  380.1 12.4 %convolution_convert_fusion.1 = bf16[1024,2048]{1,0:T(8,128)(2,1)S(1)} fusion(bf16[2048,2048]{1,0:T(8,128)(2,1)} %get-tuple-element.85, bf16[1024,1024]{1,0:T(8,128)(2,1)} %collective-permute-done.1, bf16[1024,1024]{1,0:T(8,128)(2,1)S(1)} %multiply_convert_fusion.1), kind=kOutput, calls=%fused_computation.46 | convolution fusion | flops 8600420352 | bytes 16777216 | tf_op jit(solution)/shard_map/dot_general | solution.py:40
  398.3 18.9 %collective-permute-done.7 = bf16[256,2048]{1,0:T(8,128)(2,1)S(1)} collective-permute-done((bf16[256,2048]{1,0:T(8,128)(2,1)S(1)}, bf16[256,2048]{1,0:T(8,128)(2,1)S(1)}, u32[]{:S(2)}, u32[]{:S(2)}) %collective-permute-start.7) | collective-permute-done | bytes 1048608 | tf_op jit(solution)/shard_map/ppermute | solution.py:637
  420.3 12.1 %multiply_reduce_fusion.1 = (bf16[1024]{0:T(1024)(128)(2,1)S(1)}, f32[1024]{0:T(1024)S(1)}, bf16[1024,1024]{1,0:T(8,128)(2,1)}, f32[1024,1024]{1,0:T(8,128)S(1)}) fusion(f32[1024,1024]{1,0:T(8,128)S(1)} %get-tuple-element.133, f32[1024]{0:T(1024)S(1)} %fusion.88, bf16[1024,1024]{1,0:T(8,128)(2,1)S(1)} %collective-permute-done.4, f32[1024]{0:T(1024)S(1)} %copy-done.35, ...), kind=kOutput, calls=%fused_computation.39 | convolution fusion | flops 4307548160 | bytes 27277312 | tf_op jit(solution)/shard_map/dot_general | solution.py:46
  432.9 4.4 constant_dynamic-update-slice_fusion.35
  447.0 13.7 %collective-permute-done.20 = bf16[128,1024]{1,0:T(8,128)(2,1)S(1)} collective-permute-done((bf16[128,1024]{1,0:T(8,128)(2,1)S(1)}, bf16[128,1024]{1,0:T(8,128)(2,1)S(1)}, u32[]{:S(2)}, u32[]{:S(2)}) %collective-permute-start.20) | collective-permute-done | bytes 262176 | tf_op jit(solution)/shard_map/ppermute | solution.py:637
  460.8 2.4 collective-permute-start.21
  464.3 3.8 convolution_convert_fusion.3.delta_ref.refs_8_
  468.1 18.6 %recall_back.4 = (f32[2048,512]{1,0:T(8,128)}, f32[1,8,128]{2,1,0:T(8,128)}, bf16[128,2048]{1,0:T(8,128)(2,1)}, bf16[128,2048]{1,0:T(8,128)(2,1)}) custom-call(f32[1]{0:T(128)} %get-tuple-element.128.gate_ref, bf16[524288,128]{1,0:T(8,128)(2,1)} %bitcast.4.found_ref, ...), custom_call_target="tpu_custom_call", output_to_operand_aliasing={{2}: (4, {}), {3}: (5, {})} | custom-call | bytes 67108864 | tf_op jit(solution)/shard_map/recall_back/pallas_call | solution.py:317
  493.1 18.6 %recall_back.5 = (f32[2048,512]{1,0:T(8,128)}, f32[1,8,128]{2,1,0:T(8,128)}, bf16[64,2048]{1,0:T(8,128)(2,1)}, bf16[64,2048]{1,0:T(8,128)(2,1)}) custom-call(f32[1]{0:T(128)} %get-tuple-element.129.gate_ref, bf16[524288,128]{1,0:T(8,128)(2,1)} %bitcast.4.found_ref, ...), custom_call_target="tpu_custom_call", output_to_operand_aliasing={{0}: (4, {}), {2}: (5, {}), {3}: (6, {})} | custom-call | bytes 67108864 | tf_op jit(solution)/shard_map/recall_back/pallas_call | solution.py:317
  517.4 19.1 %recall_back.6 = (f32[2048,512]{1,0:T(8,128)}, f32[1,8,128]{2,1,0:T(8,128)}, bf16[32,2048]{1,0:T(8,128)(2,1)}, bf16[32,2048]{1,0:T(8,128)(2,1)}) custom-call(f32[1]{0:T(128)} %get-tuple-element.130.gate_ref, bf16[524288,128]{1,0:T(8,128)(2,1)} %bitcast.4.found_ref, ...), custom_call_target="tpu_custom_call", output_to_operand_aliasing={{0}: (4, {}), {2}: (5, {}), {3}: (6, {})} | custom-call | bytes 67108864 | tf_op jit(solution)/shard_map/recall_back/pallas_call | solution.py:317
  540.0 4.5 convolution_convert_fusion.5
  545.1 18.7 %recall_back.7 = (f32[2048,512]{1,0:T(8,128)}, f32[1,8,128]{2,1,0:T(8,128)}) custom-call(f32[1]{0:T(128)} %get-tuple-element.131.gate_ref, bf16[524288,128]{1,0:T(8,128)(2,1)} %bitcast.4.found_ref, bf16[2048,1536]{1,0:T(8,128)(2,1)} %convolution_convert_fusion.now_ref.before_ref.query_ref.key_ref.value_ref.refs_3_.refs_4_.refs_5_, ...), custom_call_target="tpu_custom_call", output_to_operand_aliasing={{0}: (4, {})} | custom-call | bytes 67108864 | tf_op jit(solution)/shard_map/recall_back/pallas_call | solution.py:317
  563.8 22.4 %local_back.2 = (bf16[2048,512]{1,0:T(8,128)(2,1)}, bf16[2048,512]{1,0:T(8,128)(2,1)}, bf16[2048,512]{1,0:T(8,128)(2,1)}, f32[2,8,1024]{2,1,0:T(8,128)}, f32[2,24,256]{2,1,0:T(8,128)}) custom-call(f32[2]{0:T(128)} %get-tuple-element.126.refs_0_, f32[2,2]{1,0:T(2,128)} %get-tuple-element.122.refs_1_, f32[2,1,1024]{2,1,0:T(1,128)} %slice.187.refs_2_, ...), custom_call_target="tpu_custom_call" | custom-call | bytes 167772160 | tf_op jit(solution)/shard_map/local_back/pallas_call | solution.py:536
  586.2 22.2 %local_back.3 = (bf16[2048,512]{1,0:T(8,128)(2,1)}, bf16[2048,512]{1,0:T(8,128)(2,1)}, bf16[2048,512]{1,0:T(8,128)(2,1)}, f32[2,8,1024]{2,1,0:T(8,128)}, f32[2,24,256]{2,1,0:T(8,128)}) custom-call(f32[2]{0:T(128)} %get-tuple-element.127.refs_0_, f32[2,2]{1,0:T(2,128)} %get-tuple-element.123.refs_1_, ...), custom_call_target="tpu_custom_call", output_to_operand_aliasing={{0}: (10, {}), {1}: (11, {}), {2}: (12, {})} | custom-call | bytes 167772160 | tf_op jit(solution)/shard_map/local_back/pallas_call | solution.py:536
  614.1 9.1 %fusion.99 = (bf16[1024,1536]{1,0:T(8,128)(2,1)}, f32[1024]{0:T(1024)S(1)}) fusion(bf16[1024,1536]{1,0:T(8,128)(2,1)S(1)} %copy-done.20, bf16[2048,1024]{1,0:T(8,128)(2,1)S(1)} %copy-done.47, bf16[2048,1536]{1,0:T(8,128)(2,1)S(1)} %constant_dynamic-update-slice_fusion.5), kind=kOutput, calls=%fused_computation.262 | convolution fusion | flops 6448741376 | bytes 16781312 | tf_op jit(solution)/shard_map/dot_general | solution.py:40
  629.3 10.5 %collective-permute-done.32 = bf16[128,1024]{1,0:T(8,128)(2,1)S(1)} collective-permute-done((bf16[128,1024]{1,0:T(8,128)(2,1)S(1)}, bf16[128,1024]{1,0:T(8,128)(2,1)S(1)}, u32[]{:S(2)}, u32[]{:S(2)}) %collective-permute-start.32) | collective-permute-done | bytes 262176 | tf_op jit(solution)/shard_map/ppermute | solution.py:637
  641.2 3.7 fusion.35
  644.9 14.2 %collective-permute-done.33 = bf16[64,1024]{1,0:T(8,128)(2,1)S(1)} collective-permute-done((bf16[64,1024]{1,0:T(8,128)(2,1)S(1)}, bf16[64,1024]{1,0:T(8,128)(2,1)S(1)}, u32[]{:S(2)}, u32[]{:S(2)}) %collective-permute-start.33) | collective-permute-done | bytes 131104 | tf_op jit(solution)/shard_map/ppermute | solution.py:637
  667.2 13.0 %collective-permute-done.23 = bf16[256,1664]{1,0:T(8,128)(2,1)S(1)} collective-permute-done((bf16[256,1664]{1,0:T(8,128)(2,1)S(1)}, bf16[256,1664]{1,0:T(8,128)(2,1)S(1)}, u32[]{:S(2)}, u32[]{:S(2)}) %collective-permute-start.23) | collective-permute-done | bytes 852000 | tf_op jit(solution)/shard_map/ppermute | solution.py:637
  682.2 7.0 collective-permute-done.24
  691.4 2.6 collective-permute-done.25
  696.7 4.8 collective-permute-done.26
  701.6 3.7 fusion.14
  705.4 2.9 fusion.10
  708.4 2.9 fusion.97
  714.3 4.5 maximum_convert_fusion.1
  718.8 18.5 %maximum_convert_fusion = f32[1024,2048]{1,0:T(8,128)} fusion(bf16[512,1024]{1,0:T(8,128)(2,1)S(1)} %bitcast.70, bf16[512,1024]{1,0:T(8,128)(2,1)S(1)} %bitcast.69, bf16[512,1024]{1,0:T(8,128)(2,1)S(1)} %bitcast.68, bf16[512,1024]{1,0:T(8,128)(2,1)S(1)} %bitcast.71), kind=kLoop, calls=%fused_computation.37 | loop fusion | flops 16777216 | bytes 12582912 | tf_op jit(solution)/shard_map/concatenate | solution.py:829
  741.5 3.2 collective-permute-start.45
  747.9 4.1 collective-permute-done.36
  754.8 4.6 collective-permute-done.37
  762.3 9.2 %collective-permute-done.47 = bf16[256,1024]{1,0:T(8,128)(2,1)S(1)} collective-permute-done((bf16[256,1024]{1,0:T(8,128)(2,1)S(1)}, bf16[256,1024]{1,0:T(8,128)(2,1)S(1)}, u32[]{:S(2)}, u32[]{:S(2)}) %collective-permute-start.47) | collective-permute-done | bytes 524320 | tf_op jit(solution)/shard_map/ppermute | solution.py:637
  776.1 9.5 %collective-permute-start.43 = (f32[2,1024]{0,1:T(8,128)S(1)}, f32[2,1024]{0,1:T(8,128)S(1)}, u32[]{:S(2)}, u32[]{:S(2)}) collective-permute-start(f32[2,1024]{0,1:T(8,128)S(1)} %fusion.50), channel_id=1, source_target_pairs={{1,0},{0,1},{3,2},{2,3},{5,4},{4,5},{7,6},{6,7},{9,8},{8,9},{11,10... | collective-permute-start | bytes 24584 | tf_op jit(solution)/shard_map/ppermute | solution.py:599
  (368 shorter events, 113.6 us)
Async XLA Ops:
  7.2 60.2 %all-gather.4.cloned.1.call-start = ((), (), s32[]{:S(2)}) async-start(), calls=%async_computation | async-start | bytes 6291456 | tf_op jit(solution)/shard_map/all_gather | solution.py:740
  14.1 694.2 %all-gather.6.cloned.1.call-start = ((), (), s32[]{:S(2)}) async-start(), calls=%async_computation.1 | async-start | bytes 8912896 | tf_op jit(solution)/shard_map/all_gather | solution.py:692
  293.3 5.8 collective-permute-start
  293.3 9.6 %collective-permute-start.3 = (bf16[1024,1024]{1,0:T(8,128)(2,1)}, bf16[1024,1024]{1,0:T(8,128)(2,1)}, u32[]{:S(2)}, u32[]{:S(2)}) collective-permute-start(bf16[1024,1024]{1,0:T(8,128)(2,1)} %param.31), channel_id=1, source_target_pairs={{1,0},{0,1},{3,2},{2,3},{5,4},{4,5},{7,6},{6,7},{9,8},{8,9},{11,10... | collective-permute-start | bytes 6291464 | tf_op jit(solution)/shard_map/ppermute | solution.py:599
  302.7 14.1 %collective-permute-start.1 = (bf16[1024,1024]{1,0:T(8,128)(2,1)S(1)}, bf16[1024,1024]{1,0:T(8,128)(2,1)}, u32[]{:S(2)}, u32[]{:S(2)}) collective-permute-start(bf16[1024,1024]{1,0:T(8,128)(2,1)S(1)} %multiply_convert_fusion.1), channel_id=1, source_target_pairs={{1,0},{0,1},{3,2},{2,3},{5,4},{4,5},{7,6},{6,7},{9,8},{8,9},{11,10... | collective-permute-start | bytes 6291464 | tf_op jit(solution)/shard_map/ppermute | solution.py:599
  367.4 26.9 %collective-permute-start.18 = (bf16[512,1024]{1,0:T(8,128)(2,1)S(1)}, bf16[512,1024]{1,0:T(8,128)(2,1)S(1)}, u32[]{:S(2)}, u32[]{:S(2)}) collective-permute-start(bf16[512,1024]{1,0:T(8,128)(2,1)S(1)} %constant_dynamic-slice_fusion.15), channel_id=1, source_target_pairs={{0,8},{2,10},{4,12},{6,14},{8,0},{10,2},{12,4},{14,6},{16,24},{18,... | collective-permute-start | bytes 3145736 | tf_op jit(solution)/shard_map/ppermute | solution.py:637
  370.2 26.6 %collective-permute-start.14 = (bf16[512,1024]{1,0:T(8,128)(2,1)S(1)}, bf16[512,1024]{1,0:T(8,128)(2,1)S(1)}, u32[]{:S(2)}, u32[]{:S(2)}) collective-permute-start(bf16[512,1024]{1,0:T(8,128)(2,1)S(1)} %constant_dynamic-slice_fusion.19), channel_id=1, source_target_pairs={{0,4},{2,6},{4,0},{6,2},{8,12},{10,14},{12,8},{14,10},{16,20},{18,... | collective-permute-start | bytes 3145736 | tf_op jit(solution)/shard_map/ppermute | solution.py:637
  371.4 47.5 %collective-permute-start.2 = (bf16[1024,1024]{1,0:T(8,128)(2,1)S(1)}, bf16[1024,1024]{1,0:T(8,128)(2,1)S(1)}, u32[]{:S(2)}, u32[]{:S(2)}) collective-permute-start(bf16[1024,1024]{1,0:T(8,128)(2,1)S(1)} %fusion.29), channel_id=1, source_target_pairs={{0,1},{1,0},{2,3},{3,2},{4,5},{5,4},{6,7},{7,6},{8,9},{9,8},{10,11... | collective-permute-start | bytes 6291464 | tf_op jit(solution)/shard_map/ppermute | solution.py:622
  380.1 40.2 %collective-permute-start.4 = (bf16[1024,1024]{1,0:T(8,128)(2,1)}, bf16[1024,1024]{1,0:T(8,128)(2,1)S(1)}, u32[]{:S(2)}, u32[]{:S(2)}) collective-permute-start(bf16[1024,1024]{1,0:T(8,128)(2,1)} %fusion.32), channel_id=1, source_target_pairs={{0,1},{1,0},{2,3},{3,2},{4,5},{5,4},{6,7},{7,6},{8,9},{9,8},{10,11... | collective-permute-start | bytes 6291464 | tf_op jit(solution)/shard_map/ppermute | solution.py:622
  392.9 24.4 %collective-permute-start.7 = (bf16[256,2048]{1,0:T(8,128)(2,1)S(1)}, bf16[256,2048]{1,0:T(8,128)(2,1)S(1)}, u32[]{:S(2)}, u32[]{:S(2)}) collective-permute-start(bf16[256,2048]{1,0:T(8,128)(2,1)S(1)} %constant_dynamic-slice_fusion.31), channel_id=1, source_target_pairs={{0,4},{2,6},{4,0},{6,2},{8,12},{10,14},{12,8},{14,10},{16,20},{18,... | collective-permute-start | bytes 3145736 | tf_op jit(solution)/shard_map/ppermute | solution.py:637
  394.3 44.8 %collective-permute-start.6 = (bf16[256,2048]{1,0:T(8,128)(2,1)}, bf16[256,2048]{1,0:T(8,128)(2,1)}, u32[]{:S(2)}, u32[]{:S(2)}) collective-permute-start(bf16[256,2048]{1,0:T(8,128)(2,1)} %constant_dynamic-slice_fusion.33), channel_id=1, source_target_pairs={{0,2},{2,0},{4,6},{6,4},{8,10},{10,8},{12,14},{14,12},{16,18},{18,... | collective-permute-start | bytes 3145736 | tf_op jit(solution)/shard_map/ppermute | solution.py:637
  396.8 45.7 %collective-permute-start.19 = (bf16[256,1024]{1,0:T(8,128)(2,1)}, bf16[256,1024]{1,0:T(8,128)(2,1)}, u32[]{:S(2)}, u32[]{:S(2)}) collective-permute-start(bf16[256,1024]{1,0:T(8,128)(2,1)} %constant_dynamic-slice_fusion.14), channel_id=1, source_target_pairs={{0,2},{2,0},{4,6},{6,4},{8,10},{10,8},{12,14},{14,12},{16,18},{18,... | collective-permute-start | bytes 1572872 | tf_op jit(solution)/shard_map/ppermute | solution.py:637
  417.3 27.1 %collective-permute-start.15 = (bf16[256,1024]{1,0:T(8,128)(2,1)}, bf16[256,1024]{1,0:T(8,128)(2,1)}, u32[]{:S(2)}, u32[]{:S(2)}) collective-permute-start(bf16[256,1024]{1,0:T(8,128)(2,1)} %constant_dynamic-slice_fusion.18), channel_id=1, source_target_pairs={{0,8},{2,10},{4,12},{6,14},{8,0},{10,2},{12,4},{14,6},{16,24},{18,... | collective-permute-start | bytes 1572872 | tf_op jit(solution)/shard_map/ppermute | solution.py:637
  419.0 70.7 %collective-permute-start.9 = (bf16[128,2048]{1,0:T(8,128)(2,1)}, bf16[128,2048]{1,0:T(8,128)(2,1)}, u32[]{:S(2)}, u32[]{:S(2)}) collective-permute-start(bf16[128,2048]{1,0:T(8,128)(2,1)} %get-tuple-element.108), channel_id=1, source_target_pairs={{0,8},{2,10},{4,12},{6,14},{8,0},{10,2},{12,4},{14,6},{16,24},{18,... | collective-permute-start | bytes 1572872 | tf_op jit(solution)/shard_map/ppermute | solution.py:637
  437.3 26.8 %collective-permute-start.5 = (bf16[1024,1024]{1,0:T(8,128)(2,1)S(1)}, bf16[1024,1024]{1,0:T(8,128)(2,1)S(1)}, u32[]{:S(2)}, u32[]{:S(2)}) collective-permute-start(bf16[1024,1024]{1,0:T(8,128)(2,1)S(1)} %get-tuple-element.83), channel_id=1, source_target_pairs={{1,0},{0,1},{3,2},{2,3},{5,4},{4,5},{7,6},{6,7},{9,8},{8,9},{11,10... | collective-permute-start | bytes 6291464 | tf_op jit(solution)/shard_map/ppermute | solution.py:599
  441.6 45.2 %collective-permute-start.8 = (bf16[128,2048]{1,0:T(8,128)(2,1)S(1)}, bf16[128,2048]{1,0:T(8,128)(2,1)S(1)}, u32[]{:S(2)}, u32[]{:S(2)}) collective-permute-start(bf16[128,2048]{1,0:T(8,128)(2,1)S(1)} %get-tuple-element.110), channel_id=1, source_target_pairs={{0,4},{2,6},{4,0},{6,2},{8,12},{10,14},{12,8},{14,10},{16,20},{18,... | collective-permute-start | bytes 1572872 | tf_op jit(solution)/shard_map/ppermute | solution.py:637
  443.8 16.9 %collective-permute-start.20 = (bf16[128,1024]{1,0:T(8,128)(2,1)S(1)}, bf16[128,1024]{1,0:T(8,128)(2,1)S(1)}, u32[]{:S(2)}, u32[]{:S(2)}) collective-permute-start(bf16[128,1024]{1,0:T(8,128)(2,1)S(1)} %constant_dynamic-slice_fusion.13), channel_id=1, source_target_pairs={{0,4},{2,6},{4,0},{6,2},{8,12},{10,14},{12,8},{14,10},{16,20},{18,... | collective-permute-start | bytes 786440 | tf_op jit(solution)/shard_map/ppermute | solution.py:637
  445.7 17.6 %collective-permute-start.16 = (bf16[128,1024]{1,0:T(8,128)(2,1)S(1)}, bf16[128,1024]{1,0:T(8,128)(2,1)S(1)}, u32[]{:S(2)}, u32[]{:S(2)}) collective-permute-start(bf16[128,1024]{1,0:T(8,128)(2,1)S(1)} %constant_dynamic-slice_fusion.17), channel_id=1, source_target_pairs={{0,2},{2,0},{4,6},{6,4},{8,10},{10,8},{12,14},{14,12},{16,18},{18,... | collective-permute-start | bytes 786440 | tf_op jit(solution)/shard_map/ppermute | solution.py:637
  460.8 77.7 %collective-permute-start.21 = (bf16[64,1024]{1,0:T(8,128)(2,1)S(1)}, bf16[64,1024]{1,0:T(8,128)(2,1)S(1)}, u32[]{:S(2)}, u32[]{:S(2)}) collective-permute-start(bf16[64,1024]{1,0:T(8,128)(2,1)S(1)} %constant_dynamic-slice_fusion.12), channel_id=1, source_target_pairs={{0,16},{2,18},{4,20},{6,22},{8,24},{10,26},{12,28},{14,30},{16,0},... | collective-permute-start | bytes 393224 | tf_op jit(solution)/shard_map/ppermute | solution.py:637
  464.0 74.5 %collective-permute-start.17 = (bf16[64,1024]{1,0:T(8,128)(2,1)}, bf16[64,1024]{1,0:T(8,128)(2,1)S(1)}, u32[]{:S(2)}, u32[]{:S(2)}) collective-permute-start(bf16[64,1024]{1,0:T(8,128)(2,1)} %constant_dynamic-slice_fusion.16), channel_id=1, source_target_pairs={{0,16},{2,18},{4,20},{6,22},{8,24},{10,26},{12,28},{14,30},{16,0},... | collective-permute-start | bytes 393224 | tf_op jit(solution)/shard_map/ppermute | solution.py:637
  488.7 23.0 %collective-permute-start.10 = (bf16[64,2048]{1,0:T(8,128)(2,1)S(1)}, bf16[64,2048]{1,0:T(8,128)(2,1)S(1)}, u32[]{:S(2)}, u32[]{:S(2)}) collective-permute-start(bf16[64,2048]{1,0:T(8,128)(2,1)S(1)} %get-tuple-element.114), channel_id=1, source_target_pairs={{0,8},{2,10},{4,12},{6,14},{8,0},{10,2},{12,4},{14,6},{16,24},{18,... | collective-permute-start | bytes 786440 | tf_op jit(solution)/shard_map/ppermute | solution.py:637
  491.8 23.9 %collective-permute-start.11 = (bf16[64,2048]{1,0:T(8,128)(2,1)S(1)}, bf16[64,2048]{1,0:T(8,128)(2,1)S(1)}, u32[]{:S(2)}, u32[]{:S(2)}) collective-permute-start(bf16[64,2048]{1,0:T(8,128)(2,1)S(1)} %get-tuple-element.112), channel_id=1, source_target_pairs={{0,2},{2,0},{4,6},{6,4},{8,10},{10,8},{12,14},{14,12},{16,18},{18,... | collective-permute-start | bytes 786440 | tf_op jit(solution)/shard_map/ppermute | solution.py:637
  513.4 23.2 %collective-permute-start.12 = (bf16[32,2048]{1,0:T(8,128)(2,1)S(1)}, bf16[32,2048]{1,0:T(8,128)(2,1)S(1)}, u32[]{:S(2)}, u32[]{:S(2)}) collective-permute-start(bf16[32,2048]{1,0:T(8,128)(2,1)S(1)} %get-tuple-element.118), channel_id=1, source_target_pairs={{0,16},{2,18},{4,20},{6,22},{8,24},{10,26},{12,28},{14,30},{16,0},... | collective-permute-start | bytes 393224 | tf_op jit(solution)/shard_map/ppermute | solution.py:637
  517.4 20.1 %collective-permute-start.13 = (bf16[32,2048]{1,0:T(8,128)(2,1)S(1)}, bf16[32,2048]{1,0:T(8,128)(2,1)S(1)}, u32[]{:S(2)}, u32[]{:S(2)}) collective-permute-start(bf16[32,2048]{1,0:T(8,128)(2,1)S(1)} %get-tuple-element.116), channel_id=1, source_target_pairs={{0,16},{2,18},{4,20},{6,22},{8,24},{10,26},{12,28},{14,30},{16,0},... | collective-permute-start | bytes 393224 | tf_op jit(solution)/shard_map/ppermute | solution.py:637
  544.6 82.1 %collective-permute-start.31 = (bf16[256,1024]{1,0:T(8,128)(2,1)S(1)}, bf16[256,1024]{1,0:T(8,128)(2,1)S(1)}, u32[]{:S(2)}, u32[]{:S(2)}) collective-permute-start(bf16[256,1024]{1,0:T(8,128)(2,1)S(1)} %constant_dynamic-slice_fusion.3), channel_id=1, source_target_pairs={{0,8},{2,10},{4,12},{6,14},{8,0},{10,2},{12,4},{14,6},{16,24},{18,... | collective-permute-start | bytes 1572872 | tf_op jit(solution)/shard_map/ppermute | solution.py:637
  627.0 12.9 %collective-permute-start.32 = (bf16[128,1024]{1,0:T(8,128)(2,1)S(1)}, bf16[128,1024]{1,0:T(8,128)(2,1)S(1)}, u32[]{:S(2)}, u32[]{:S(2)}) collective-permute-start(bf16[128,1024]{1,0:T(8,128)(2,1)S(1)} %constant_dynamic-slice_fusion.2), channel_id=1, source_target_pairs={{0,2},{2,0},{4,6},{6,4},{8,10},{10,8},{12,14},{14,12},{16,18},{18,... | collective-permute-start | bytes 786440 | tf_op jit(solution)/shard_map/ppermute | solution.py:637
  628.2 38.6 %collective-permute-start.27 = (bf16[256,1664]{1,0:T(8,128)(2,1)S(1)}, bf16[256,1664]{1,0:T(8,128)(2,1)S(1)}, u32[]{:S(2)}, u32[]{:S(2)}) collective-permute-start(bf16[256,1664]{1,0:T(8,128)(2,1)S(1)} %constant_dynamic-slice_fusion.7), channel_id=1, source_target_pairs={{0,4},{2,6},{4,0},{6,2},{8,12},{10,14},{12,8},{14,10},{16,20},{18,... | collective-permute-start | bytes 2555912 | tf_op jit(solution)/shard_map/ppermute | solution.py:637
  640.0 19.2 %collective-permute-start.33 = (bf16[64,1024]{1,0:T(8,128)(2,1)S(1)}, bf16[64,1024]{1,0:T(8,128)(2,1)S(1)}, u32[]{:S(2)}, u32[]{:S(2)}) collective-permute-start(bf16[64,1024]{1,0:T(8,128)(2,1)S(1)} %constant_dynamic-slice_fusion.1), channel_id=1, source_target_pairs={{0,4},{2,6},{4,0},{6,2},{8,12},{10,14},{12,8},{14,10},{16,20},{18,... | collective-permute-start | bytes 393224 | tf_op jit(solution)/shard_map/ppermute | solution.py:637
  659.2 7.5 collective-permute-start.34
  661.4 18.8 %collective-permute-start.23 = (bf16[256,1664]{1,0:T(8,128)(2,1)S(1)}, bf16[256,1664]{1,0:T(8,128)(2,1)S(1)}, u32[]{:S(2)}, u32[]{:S(2)}) collective-permute-start(bf16[256,1664]{1,0:T(8,128)(2,1)S(1)} %constant_dynamic-slice_fusion.11), channel_id=1, source_target_pairs={{0,2},{2,0},{4,6},{6,4},{8,10},{10,8},{12,14},{14,12},{16,18},{18,... | collective-permute-start | bytes 2555912 | tf_op jit(solution)/shard_map/ppermute | solution.py:637
  662.4 39.2 %collective-permute-start.22 = (bf16[1024,1024]{1,0:T(8,128)(2,1)S(1)}, bf16[1024,1024]{1,0:T(8,128)(2,1)S(1)}, u32[]{:S(2)}, u32[]{:S(2)}) collective-permute-start(bf16[1024,1024]{1,0:T(8,128)(2,1)S(1)} %fusion.35), channel_id=1, source_target_pairs={{0,1},{1,0},{2,3},{3,2},{4,5},{5,4},{6,7},{7,6},{8,9},{9,8},{10,11... | collective-permute-start | bytes 6291464 | tf_op jit(solution)/shard_map/ppermute | solution.py:622
  667.1 13.9 %collective-permute-start.28 = (bf16[128,1664]{1,0:T(8,128)(2,1)S(1)}, bf16[128,1664]{1,0:T(8,128)(2,1)S(1)}, u32[]{:S(2)}, u32[]{:S(2)}) collective-permute-start(bf16[128,1664]{1,0:T(8,128)(2,1)S(1)} %constant_dynamic-slice_fusion.6), channel_id=1, source_target_pairs={{0,8},{2,10},{4,12},{6,14},{8,0},{10,2},{12,4},{14,6},{16,24},{18,... | collective-permute-start | bytes 1277960 | tf_op jit(solution)/shard_map/ppermute | solution.py:637
  680.4 8.7 %collective-permute-start.24 = (bf16[128,1664]{1,0:T(8,128)(2,1)S(1)}, bf16[128,1664]{1,0:T(8,128)(2,1)S(1)}, u32[]{:S(2)}, u32[]{:S(2)}) collective-permute-start(bf16[128,1664]{1,0:T(8,128)(2,1)S(1)} %constant_dynamic-slice_fusion.10), channel_id=1, source_target_pairs={{0,4},{2,6},{4,0},{6,2},{8,12},{10,14},{12,8},{14,10},{16,20},{18,... | collective-permute-start | bytes 1277960 | tf_op jit(solution)/shard_map/ppermute | solution.py:637
  681.2 9.7 %collective-permute-start.29 = (bf16[64,1664]{1,0:T(8,128)(2,1)S(1)}, bf16[64,1664]{1,0:T(8,128)(2,1)S(1)}, u32[]{:S(2)}, u32[]{:S(2)}) collective-permute-start(bf16[64,1664]{1,0:T(8,128)(2,1)S(1)} %constant_dynamic-slice_fusion.5), channel_id=1, source_target_pairs={{0,2},{2,0},{4,6},{6,4},{8,10},{10,8},{12,14},{14,12},{16,18},{18,... | collective-permute-start | bytes 638984 | tf_op jit(solution)/shard_map/ppermute | solution.py:637
  690.9 5.7 collective-permute-start.30
  694.2 7.3 collective-permute-start.26
  737.4 7.4 collective-permute-start.35
  739.8 6.2 collective-permute-start.39
  741.5 5.5 collective-permute-start.45
  744.9 7.1 collective-permute-start.36
  746.0 6.8 collective-permute-start.40
  747.0 6.7 collective-permute-start.46
  752.0 7.3 collective-permute-start.37
  752.8 8.6 %collective-permute-start.41 = (bf16[128,1664]{1,0:T(8,128)(2,1)S(1)}, bf16[128,1664]{1,0:T(8,128)(2,1)S(1)}, u32[]{:S(2)}, u32[]{:S(2)}) collective-permute-start(bf16[128,1664]{1,0:T(8,128)(2,1)S(1)} %constant_dynamic-update-slice_fusion.22), channel_id=1, source_target_pairs={{0,8},{2,10},{4,12},{6,14},{8,0},{10,2},{12,4},{14,6},{16,24},{18,... | collective-permute-start | bytes 1277960 | tf_op jit(solution)/shard_map/ppermute | solution.py:637
  753.7 17.7 %collective-permute-start.47 = (bf16[256,1024]{1,0:T(8,128)(2,1)S(1)}, bf16[256,1024]{1,0:T(8,128)(2,1)S(1)}, u32[]{:S(2)}, u32[]{:S(2)}) collective-permute-start(bf16[256,1024]{1,0:T(8,128)(2,1)S(1)} %constant_dynamic-update-slice_fusion.12), channel_id=1, source_target_pairs={{0,8},{2,10},{4,12},{6,14},{8,0},{10,2},{12,4},{14,6},{16,24},{18,... | collective-permute-start | bytes 1572872 | tf_op jit(solution)/shard_map/ppermute | solution.py:637
  759.4 13.7 %collective-permute-start.38 = (bf16[256,1664]{1,0:T(8,128)(2,1)S(1)}, bf16[256,1664]{1,0:T(8,128)(2,1)S(1)}, u32[]{:S(2)}, u32[]{:S(2)}) collective-permute-start(bf16[256,1664]{1,0:T(8,128)(2,1)S(1)} %constant_dynamic-update-slice_fusion.28), channel_id=1, source_target_pairs={{0,2},{2,0},{4,6},{6,4},{8,10},{10,8},{12,14},{14,12},{16,18},{18,... | collective-permute-start | bytes 2555912 | tf_op jit(solution)/shard_map/ppermute | solution.py:637
  761.5 14.1 %collective-permute-start.42 = (bf16[256,1664]{1,0:T(8,128)(2,1)S(1)}, bf16[256,1664]{1,0:T(8,128)(2,1)S(1)}, u32[]{:S(2)}, u32[]{:S(2)}) collective-permute-start(bf16[256,1664]{1,0:T(8,128)(2,1)S(1)} %constant_dynamic-update-slice_fusion.20), channel_id=1, source_target_pairs={{0,4},{2,6},{4,0},{6,2},{8,12},{10,14},{12,8},{14,10},{16,20},{18,... | collective-permute-start | bytes 2555912 | tf_op jit(solution)/shard_map/ppermute | solution.py:637
  776.1 15.6 %collective-permute-start.43 = (f32[2,1024]{0,1:T(8,128)S(1)}, f32[2,1024]{0,1:T(8,128)S(1)}, u32[]{:S(2)}, u32[]{:S(2)}) collective-permute-start(f32[2,1024]{0,1:T(8,128)S(1)} %fusion.50), channel_id=1, source_target_pairs={{1,0},{0,1},{3,2},{2,3},{5,4},{4,5},{7,6},{6,7},{9,8},{8,9},{11,10... | collective-permute-start | bytes 24584 | tf_op jit(solution)/shard_map/ppermute | solution.py:599
  (56 other events, 965.7 us)
Sparse Core Ops, SparseCore 0:
  14.3 16.2 all-gather.3
  539.5 123.3 all-gather.5

commit v5 on v4

--- a/solution.py
+++ b/solution.py
@@ -32,6 +32,15 @@
     return rows * lax.rsqrt(jnp.mean(rows * rows, -1, keepdims=True) + eps_norm) * gain
 
 
+def gelu_pair(rows):
+    reach = math.sqrt(2.0 / math.pi)
+    square = rows * rows
+    turn = jnp.tanh(reach * rows * (1.0 + 0.044715 * square))
+    share = 0.5 * (1.0 + turn)
+    steep = 0.5 * (1.0 - turn * turn) * reach * (1.0 + 3.0 * 0.044715 * square)
+    return (rows * share).astype(low_type), (share + rows * steep).astype(low_type)
+
+
 def dot_rows(left, right):
     return jnp.dot(left, right, preferred_element_type=full_type)
 
@@ -53,11 +62,18 @@
     row = lax.broadcasted_iota(jnp.int32, (256, 256), 0)
     column = lax.broadcasted_iota(jnp.int32, (256, 256), 1)
     order = jnp.where(column == (row // 2 + (row % 2) * 128), 1.0, 0.0).astype(low_type)
-    for part in range(rows // 128):
+    for part in range(rows // 256):
+        low, high = pl.ds(part * 256, 128), pl.ds(part * 256 + 128, 128)
         both = jnp.concatenate(
-            [key_ref[0, pl.ds(part * 128, 128)], value_ref[0, pl.ds(part * 128, 128)]], 0
-        )
-        table_ref[pl.ds(part * 256, 256), :] = dot_rows(order, both).astype(low_type)
+            [
+                jnp.concatenate([key_ref[0, low], key_ref[0, high]], 1),
+                jnp.concatenate([value_ref[0, low], value_ref[0, high]], 1),
+            ],
+            0,
+        )
+        mixed = dot_rows(order, both).astype(low_type)
+        table_ref[pl.ds(part * 512, 256), :] = mixed[:, :128]
+        table_ref[pl.ds(part * 512 + 256, 256), :] = mixed[:, 128:]
 
 
 def interleave(memory_keys, memory_values):
@@ -297,13 +313,15 @@
 
 
 def recall_back(
-    found, queries, mixed_delta, gates, head, carried, after, kept, heads, picks, scale
+    found, queries, mixed_delta, gates, head, heads_now, carried, after, kept, picks, scale
 ):
     tokens = queries.shape[0]
-    width = mixed_delta.shape[1] // heads
+    width = mixed_delta.shape[1] // gates.shape[0]
+    start, count = heads_now
     step = min(512, tokens)
     blocks = tokens // step
     rows_spec = pl.BlockSpec((step, width), lambda i: (i, head))
+    out_spec = pl.BlockSpec((step, width), lambda i: (i, head - start))
     anywhere = pl.BlockSpec(memory_space=pl.ANY)
     extra = [kept] if kept is not None else []
     first = 4 + len(extra)
@@ -324,10 +342,10 @@
             rows_spec,
         ]
         + [anywhere] * (len(extra) + len(carried) + len(after)),
-        out_specs=[rows_spec, pl.BlockSpec((1, 8, 128), lambda i: (0, 0, 0))]
+        out_specs=[out_spec, pl.BlockSpec((1, 8, 128), lambda i: (0, 0, 0))]
         + [anywhere] * len(carried),
         out_shape=[
-            jax.ShapeDtypeStruct((tokens, heads * width), full_type),
+            jax.ShapeDtypeStruct((tokens, count * width), full_type),
             jax.ShapeDtypeStruct((1, 8, 128), full_type),
         ]
         + [jax.ShapeDtypeStruct(part.shape, part.dtype) for part in carried],
@@ -513,7 +531,7 @@
 
 def local_back(
     projected, query_mask, key_mask, mixed_delta, recall_delta, columns, far, gates, seq_len, scale,
-    heads_now, carried, kept, after,
+    heads_now, carried, after,
 ):
     tokens = mixed_delta.shape[0]
     heads = gates.shape[0]
@@ -525,14 +543,15 @@
     def rows_of(shift):
         return pl.BlockSpec((seq_len, width), lambda h, s: (s, h + start + shift * heads))
 
+    own_spec = pl.BlockSpec((seq_len, width), lambda h, s: (s, h))
+
     def kernel(*refs):
-        inputs, rest = refs[:10], refs[10 + len(kept) + len(carried) + len(after) :]
+        inputs, rest = refs[:10], refs[10 + len(carried) + len(after) :]
         local_back_kernel(scale, *inputs, *rest[:5], *rest[5 + len(carried) :])
 
     mask_spec = pl.BlockSpec((1, seq_len, 128), lambda h, s: (s, 0, 0))
     smem = pl.BlockSpec(memory_space=pltpu.SMEM)
-    rows_shape = jax.ShapeDtypeStruct((tokens, heads * width), low_type)
-    first = 10 + len(kept)
+    rows_shape = jax.ShapeDtypeStruct((tokens, count * width), low_type)
     out = pl.pallas_call(
         kernel,
         grid=(count, tokens // seq_len),
@@ -546,13 +565,13 @@
             mask_spec,
             mask_spec,
             rows_of(0),
-            rows_of(0),
+            own_spec,
         ]
-        + [anywhere] * (len(kept) + len(carried) + len(after)),
+        + [anywhere] * (len(carried) + len(after)),
         out_specs=[
-            rows_of(0),
-            rows_of(0),
-            rows_of(0),
+            own_spec,
+            own_spec,
+            own_spec,
             pl.BlockSpec((1, 8, ring), lambda h, s: (h, 0, 0)),
             pl.BlockSpec((1, 24, tile), lambda h, s: (h, 0, 0)),
         ]
@@ -565,8 +584,7 @@
             jax.ShapeDtypeStruct((count, 24, tile), full_type),
         ]
         + [jax.ShapeDtypeStruct(part.shape, part.dtype) for part in carried],
-        input_output_aliases={10 + i: i for i in range(len(kept))}
-        | {first + i: 5 + i for i in range(len(carried))},
+        input_output_aliases={10 + i: 5 + i for i in range(len(carried))},
         scratch_shapes=[
             pltpu.VMEM((tile, span), full_type),
             pltpu.VMEM((tile, span), full_type),
@@ -580,7 +598,7 @@
         name="local_back",
     )(
         gates[chosen], far[chosen], columns[chosen], projected, projected, projected, query_mask,
-        key_mask, mixed_delta, recall_delta, *kept, *carried, *after,
+        key_mask, mixed_delta, recall_delta, *carried, *after,
     )
     return list(out[:3]), out[3], out[4], list(out[5:])
 
@@ -661,10 +679,12 @@
     ]
 
 
-def double_all(parts):
+def double_all(parts, beside):
     orders = bit_orders()
     for step in reversed(range(len(orders[0]))):
         got = [swap_over(part, order[step]) for part, order in zip(parts, orders)]
+        if step == 1:
+            got[2], beside = lax.optimization_barrier((got[2], beside))
         wider = []
         for part, other, order in zip(parts, got, orders):
             rows = part.shape[0]
@@ -673,7 +693,7 @@
             whole = lax.dynamic_update_slice_in_dim(whole, part, side * rows, 0)
             wider.append(lax.dynamic_update_slice_in_dim(whole, other, (1 - side) * rows, 0))
         parts = wider
-    return parts
+    return parts, beside
 
 
 def pack(parts):
@@ -766,32 +786,47 @@
     second_rows = rms_scaled(middle, mlp_gain).astype(low_type)
     grad_full = jnp.concatenate(fetch(grad_output), 0)
     second = jnp.concatenate(fetch(second_rows), 0)
-    hidden = dot_rows(second, hidden_weight)
-    active = jax.nn.gelu(hidden).astype(low_type)
-    return_low = dot_outer(active, grad_full).astype(low_type)
+    active, slope = gelu_pair(dot_rows(second, hidden_weight))
+    slope = lax.optimization_barrier(slope)
     orders = bit_orders()
     steps = len(orders[0])
+
+    return_low = dot_outer(active, grad_full).astype(low_type)
     return_half = return_low.shape[0] // 2
-    return_parts = [return_low[:return_half], return_low[return_half:]]
-    for step in range(steps):
-        return_parts = add_low(*halve_step(return_parts, orders[1:], step))
+    kept_back, sent_back = halve_step(
+        [return_low[:return_half], return_low[return_half:]], orders[1:], 0
+    )
     active_delta = dot_inner(grad_full, return_weight)
-    gelu_back = jax.vjp(jax.nn.gelu, hidden)[1]
-    hidden_delta = gelu_back(active_delta)[0].astype(low_type)
+    hidden_delta = (active_delta * slope.astype(full_type)).astype(low_type)
     second_delta = fold(
         lambda rows: dot_inner(rows, hidden_weight),
         lambda k: lax.slice_in_dim(hidden_delta, k * share_rows, (k + 1) * share_rows),
     )
-    hidden_low = dot_outer(second, hidden_delta).astype(low_type)
-    hidden_half = hidden_low.shape[0] // 2
-    hidden_parts = [hidden_low[:hidden_half], hidden_low[hidden_half:]]
-    hidden_parts = add_low(*halve_step(hidden_parts, orders[:2], 0))
-    kept, sent = halve_step(hidden_parts, orders[:2], 1)
+    hidden_half = hidden_delta.shape[1] // 2
+    hidden_parts = [
+        dot_outer(second, hidden_delta[:, :hidden_half]).astype(low_type),
+        dot_outer(second, hidden_delta[:, hidden_half:]).astype(low_type),
+    ]
+    kept, sent = halve_step(hidden_parts, orders[:2], 0)
+
+    kept_back, kept = lax.optimization_barrier((kept_back, kept))
+    kept_back, sent_back = halve_step(add_low(kept_back, sent_back), orders[1:], 1)
+
     second_back = jax.vjp(rms_scaled, middle, mlp_gain)[1]
     middle_part, mlp_gain_part = second_back(second_delta)
     middle_delta = grad_output.astype(full_type) + middle_part
-    middle_full = in_order(fetch(middle_delta.astype(low_type)))
+    middle_low = middle_delta.astype(low_type)
+    kept, kept_back, middle_low = lax.optimization_barrier((kept, kept_back, middle_low))
+    kept, sent = halve_step(add_low(kept, sent), orders[:2], 1)
+    kept_back, sent_back = halve_step(add_low(kept_back, sent_back), orders[1:], 2)
+    middle_full = in_order(fetch(middle_low))
     mixed_delta = dot_inner(middle_full, output_weight).astype(low_type)
+    kept, kept_back, mixed_delta = lax.optimization_barrier((kept, kept_back, mixed_delta))
+    kept, sent = halve_step(add_low(kept, sent), orders[:2], 2)
+    kept_back, sent_back = halve_step(add_low(kept_back, sent_back), orders[1:], 3)
+    taken = 2
+    for step in range(4, steps):
+        kept_back, sent_back = halve_step(add_low(kept_back, sent_back), orders[1:], step)
     layer_output = (
         middle
         + fold(
@@ -800,61 +835,90 @@
         )
     ).astype(low_type)
 
-    taken = 1
     shards, packed = [], []
-    recall_delta = None
-    recall_sums = []
-    for head in range(head_count):
-        recall_delta, head_sums, kept = recall_back(
-            found, projected, mixed_delta, gates, head, kept, packed, recall_delta, head_count,
-            picks, scale,
-        )
-        recall_sums.append(head_sums)
-        if taken < steps - 1:
-            taken += 1
-            kept, sent = halve_step(add_low(kept, sent), orders[:2], taken)
-        elif not shards:
-            shards = add_low(kept, sent) + return_parts
-            packed = [pack(shards)]
-            kept = []
+    half_heads = max(1, head_count // 2)
+    recall_gain, local_gain, diagonals, far_left, far_right = [], [], [], [], []
+    attn_gain_part = jnp.zeros_like(attn_gain)
+    joined_parts = []
+    early_kept, early_sent, early_taken = [], [], 0
+    early_shards = []
+    normed_terms = []
+
+    def early_step(parts):
+        if early_taken + 1 < steps:
+            return *halve_step(add_low(parts, early_sent), orders, early_taken + 1), early_taken + 1
+        return parts, early_sent, early_taken
+
+    for start in range(0, head_count, half_heads):
+        recall_delta = None
+        for head in range(start, start + half_heads):
+            count_kept = len(kept)
+            recall_delta, head_sums, passed = recall_back(
+                found, projected, mixed_delta, gates, head, (start, half_heads), kept + early_kept,
+                packed, recall_delta, picks, scale,
+            )
+            recall_gain.append(jnp.sum(head_sums[:, :, 0], 1))
+            if early_kept:
+                early_kept, early_sent, early_taken = early_step(passed[count_kept:])
+            if shards:
+                continue
+            kept = passed[:count_kept]
+            if taken < steps - 1:
+                taken += 1
+                kept, sent = halve_step(add_low(kept, sent), orders[:2], taken)
+            else:
+                shards = add_low(kept, sent) + add_low(kept_back, sent_back)
+                packed = [pack(shards)]
+                kept = []
+        deltas, diagonal_now, local_sums, passed = local_back(
+            projected, query_mask, key_mask, mixed_delta, recall_delta, behind_columns, far, gates,
+            seq_len, scale, (start, half_heads), early_kept, packed,
+        )
+        diagonals.append(diagonal_now)
+        local_gain.append(jnp.sum(local_sums[:, 0], 1))
+        far_left.append(jnp.sum(local_sums[:, 8:16], (1, 2)))
+        far_right.append(jnp.sum(local_sums[:, 16:24], (1, 2)))
+        if early_kept:
+            early_kept = passed
+            while early_taken + 1 < steps:
+                early_kept, early_sent, early_taken = early_step(early_kept)
+            early_shards = add_low(early_kept, early_sent)
+            early_kept = []
+        columns = slice(start * head_width, (start + half_heads) * head_width)
+        weights_now = jnp.concatenate(
+            [query_weight[:, columns], key_weight[:, columns], value_weight[:, columns]], 1
+        )
+        project_delta = jnp.concatenate(deltas, 1)
+        joined_part = dot_outer(normed, project_delta)
+        attn_gain_part += jnp.sum(joined_part * weights_now.astype(full_type), 1) / attn_gain
+        normed_terms.append((project_delta, weights_now))
+        if start + half_heads < head_count:
+            joined_low = joined_part.astype(low_type)
+            joined_half = joined_low.shape[0] // 2
+            early_kept, early_sent = halve_step(
+                [joined_low[:joined_half], joined_low[joined_half:]], orders, 0
+            )
     while taken < steps - 1:
         taken += 1
         kept, sent = halve_step(add_low(kept, sent), orders[:2], taken)
     if not shards:
-        shards = add_low(kept, sent) + return_parts
+        shards = add_low(kept, sent) + add_low(kept_back, sent_back)
         packed = [pack(shards)]
     hidden_low_sum, hidden_high_sum, return_low_sum, return_high_sum = gather_all(
         packed[0], shards, orders[:2] + orders[1:]
     )
-    hidden_sum = jnp.concatenate([hidden_low_sum, hidden_high_sum], 0)
+    hidden_sum = jnp.concatenate([hidden_low_sum, hidden_high_sum], 1)
     return_sum = jnp.concatenate([return_low_sum, return_high_sum], 0)
-    recall_sums = jnp.concatenate(recall_sums, 0)
-    half_heads = max(1, head_count // 2)
-    deltas = []
-    diagonals = []
-    local_sums = []
-    for start in range(0, head_count, half_heads):
-        deltas, diagonal_now, sums_now, unused = local_back(
-            projected, query_mask, key_mask, mixed_delta, recall_delta, behind_columns, far, gates,
-            seq_len, scale, (start, half_heads), [], deltas, packed,
-        )
-        diagonals.append(diagonal_now)
-        local_sums.append(sums_now)
-    query_delta, key_delta, value_delta = deltas
-    diagonals = jnp.concatenate(diagonals, 0)
-    local_sums = jnp.concatenate(local_sums, 0)
-    recall_gain = jnp.sum(recall_sums[:, :, 0], 1)
-    local_gain = jnp.sum(local_sums[:, 0], 1)
-    gate_part = gates * (1.0 - gates) * recall_gain - gates * local_gain
-    diagonal_sums = jnp.sum(diagonals, 1)
-    table_part = jnp.dot(diagonal_sums, behind_hot, precision=exact_mode)
-    far_left = jnp.sum(local_sums[:, 8:16], (1, 2))
-    far_right = jnp.sum(local_sums[:, 16:24], (1, 2))
-    table_part = table_part + far_left[:, None] * (level == 15) + far_right[:, None] * (level == 31)
-
-    project_delta = jnp.concatenate([query_delta, key_delta, value_delta], 1)
-    joined_part = dot_outer(normed, project_delta)
-    attn_gain_part = jnp.sum(joined_part * joined.astype(full_type), 1) / attn_gain
+    gate_part = gates * (1.0 - gates) * jnp.concatenate(recall_gain)
+    gate_part = gate_part - gates * jnp.concatenate(local_gain)
+    table_part = jnp.dot(
+        jnp.sum(jnp.concatenate(diagonals, 0), 1), behind_hot, precision=exact_mode
+    )
+    table_part = (
+        table_part
+        + jnp.concatenate(far_left)[:, None] * (level == 15)
+        + jnp.concatenate(far_right)[:, None] * (level == 31)
+    )
     model_width = tokens.shape[1]
     small = jnp.concatenate([table_part.reshape(-1), gate_part])
     small = jnp.pad(small, (0, model_width - small.shape[0]))
@@ -869,12 +933,18 @@
     ]
     for step in range(steps):
         last = add_low(*halve_step(last, orders, step))
-    last, hidden_sum, return_sum = lax.optimization_barrier((last, hidden_sum, return_sum))
-    *joined_sum, output_sum = double_all(last)
-
-    normed_delta = fold(
-        lambda rows: dot_inner(rows, joined), lambda k: share_of(project_delta, k, share_rows)
-    )
+    if early_shards:
+        last[:2] = [jnp.concatenate(pair, 1) for pair in zip(early_shards, last[:2])]
+    last, (hidden_sum, return_sum) = double_all(last, (hidden_sum, return_sum))
+    *joined_sum, output_sum = last
+
+    def normed_term(k):
+        terms = [
+            dot_inner(share_of(delta, k, share_rows), weights) for delta, weights in normed_terms
+        ]
+        return functools.reduce(jnp.add, terms)
+
+    normed_delta = fold(lambda term: term, normed_term)
     first_back = jax.vjp(rms_scaled, token_full, attn_gain)[1]
     tokens_grad = (middle_delta + first_back(normed_delta)[0]).astype(low_type)
 
@@ -885,13 +955,22 @@
     gains = sum(fetch(last_columns[:, :2].T))
     small_sum = last_columns[:, 2]
     table_size = head_count * 32
+    half_width = half_heads * head_width
+
+    def weight_grad(which):
+        blocks = [
+            joined_columns(3 * first + which * half_width, 3 * first + (which + 1) * half_width)
+            for first in range(0, inner_width, half_width)
+        ]
+        return jnp.concatenate(blocks, 1)
+
     return (
         layer_output,
         tokens_grad,
         gains[0],
-        joined_columns(0, inner_width),
-        joined_columns(inner_width, 2 * inner_width),
-        joined_columns(2 * inner_width, 3 * inner_width),
+        weight_grad(0),
+        weight_grad(1),
+        weight_grad(2),
         output_sum.astype(full_type),
         small_sum[:table_size].reshape(head_count, 32).T,
         small_sum[table_size : table_size + head_count],

time: 807 us -> 828 us (1.026)
  waiting for transfers between devices: 113 us -> 72.1 us
  local copies, waits for them, and re-layouts: 46.1 us -> 76.6 us
  starting transfers between devices: 54.2 us -> 76.9 us
  matrix products: 138 us -> 152 us
  other arithmetic: 62.9 us -> 53.5 us
    ppermute x40 -> x48, waiting for transfers between devices: 113 us -> 68.1 us  [swap_over(): lax.ppermute(rows, 'dp', [(i, i ^ 1 << bit) for i in range(lax.axis_size(...]
    ppermute x40 -> x48, starting transfers between devices: 39.2 us -> 56.6 us  [swap_over(): lax.ppermute(rows, 'dp', [(i, i ^ 1 << bit) for i in range(lax.axis_size(...]
    concatenate x4 -> x8, other arithmetic: 23.4 us -> 9.45 us  [the longest x3 4.82 us: weight_grad(): return jnp.concatenate(blocks, 1)]
    unnamed x118 -> x139, local copies, waits for them, and re-layouts: 13.6 us -> 26.6 us
    dot_general x4 -> x6, matrix products: 37.7 us -> 44.7 us  [dot_outer(): lax.dot_general(left, right, (((0,), (0,)), ((), ())), preferred_element_...]
    dot_general x6 -> x8, matrix products: 42.9 us -> 48.2 us  [dot_inner(): lax.dot_general(left, right, (((1,), (1,)), ((), ())), preferred_element_...]
  transfers between devices with their start and end apart: 50 -> 58, of which waited for: 20 -> 19; matrix products, arithmetic and copies ran while one was open for 17% -> 24% of each run, Pallas kernels for 20% -> 19%
where the time goes in v5:
time: 828 us; the launch traced here: 817 us
  Pallas kernels  369 us (45%)
  matrix products  152 us (18%)
  starting transfers between devices  76.9 us (9%)
  local copies, waits for them, and re-layouts  76.6 us (9%)
  waiting for transfers between devices  72.1 us (9%)
  other arithmetic  53.5 us (6%)
  between operations  16 us (2%)
    pallas_call x1, Pallas kernels, gather_found(): pl.pallas_call(functools.partial(gather_kernel, picks, scale), grid=(step...  189 us
    pallas_call x4, Pallas kernels, recall_back(): pl.pallas_call(kernel, grid=(blocks,), in_specs=[pl.BlockSpec(memory_spac...  75 us
    ppermute x48, waiting for transfers between devices, swap_over(): lax.ppermute(rows, 'dp', [(i, i ^ 1 << bit) for i in range(lax.axis_size(...  68.1 us
    dot_general x6, matrix products, dot_rows(): return jnp.dot(left, right, preferred_element_type=full_type)  58.2 us
    ppermute x48, starting transfers between devices, swap_over(): lax.ppermute(rows, 'dp', [(i, i ^ 1 << bit) for i in range(lax.axis_size(...  56.6 us
    dot_general x8, matrix products, dot_inner(): lax.dot_general(left, right, (((1,), (1,)), ((), ())), preferred_element_...  48.2 us
    dot_general x6, matrix products, dot_outer(): lax.dot_general(left, right, (((0,), (0,)), ((), ())), preferred_element_...  44.7 us
    pallas_call x2, Pallas kernels, local_back(): pl.pallas_call(kernel, grid=(count, tokens // seq_len), in_specs=[smem, s...  44.5 us
  transfers between devices with their start and end apart: 58, of which 19 were waited for; matrix products, arithmetic and copies ran while one was open for 24% of the time, Pallas kernels for 19%

profile of v5, /device:TPU:1, one launch (start us, length us, event | category | flops | bytes accessed | tf_op | source)
XLA Modules:
  0.0 816.9 jit_solution(7351122368085015921)
XLA Ops:
  15.7 3.7 copy.141
  19.4 4.2 reshape.191.index_hbm
  28.2 39.3 %interleave.1 = bf16[131072,128]{1,0:T(8,128)(2,1)} custom-call(bf16[4,16384,128]{2,1,0:T(8,128)(2,1)} %key_ref.1, bf16[4,16384,128]{2,1,0:T(8,128)(2,1)} %value_ref.1), custom_call_target="tpu_custom_call" | custom-call | flops 8589934592 | bytes 67108864 | tf_op jit(solution)/shard_map/interleave/pallas_call | solution.py:83
  67.6 11.0 %convolution_convert_fusion.now_ref.before_ref.query_ref.key_ref.value_ref.refs_3_.refs_4_.refs_5_ = bf16[2048,1536]{1,0:T(8,128)(2,1)} fusion(bf16[2048,1024]{1,0:T(8,128)(2,1)} %all-gather.4.cloned.1.call-done, bf16[1024,512]{1,0:T(8,128)(2,1)} %param.24, bf16[1024,512]{1,0:T(8,128)(2,1)} %param.23, bf16[1024,512]{1,0:T(8,128)(2,1)} %param.22), kind=kOutput, calls=%fused_computation.10 | convolution fusion | flops 6455033856 | bytes 13631488 | tf_op jit(solution)/shard_map/dot_general | solution.py:45
  78.5 189.2 %gather_found.1 = (bf16[262144,2,128]{2,1,0:T(2,128)(2,1)}, f32[4096,128]{1,0:T(8,128)}, f32[4096,128]{1,0:T(8,128)}) custom-call(s32[64,32,128]{2,1,0:T(8,128)} %reshape.191.index_hbm, bf16[65536,2,128]{2,1,0:T(2,128)(2,1)} %bitcast.55, bf16[2048,1536]{1,0:T(8,128)(2,1)} %convolution_convert_fusion.now_ref.before_ref.query_ref.key_ref.value_ref.refs_3_.refs_4_.refs_5_, ...), custom_call_target="tpu_custom_call" | custom-call | bytes 536870912 | tf_op jit(solution)/shard_map/gather_found/pallas_call | solution.py:242
  267.8 21.3 %local_read.1 = bf16[2048,512]{1,0:T(8,128)(2,1)} custom-call(f32[4]{0:T(128)} %add_divide_fusion.gate_ref, f32[4,2]{1,0:T(4,128)} %pad_maximum_fusion.11.far_ref, f32[4,1,1024]{2,1,0:T(1,128)} %broadcast_in_dim.33.column_ref, bf16[2048,1536]{1,0:T(8,128)(2,1)} %convolution_convert_fusion.now_ref.before_ref.query_ref.key_ref.value_ref.refs_3_.refs_4_.refs_5_, ...), custom_call_target="tpu_custom_call" | custom-call | bytes 167772160 | tf_op jit(solution)/shard_map/local_read/pallas_call | solution.py:415
  289.0 3.8 convolution_convert_fusion.3
  293.4 4.0 collective-permute-done
  297.3 3.5 multiply_reduce_fusion.2
  312.4 20.9 %add_convert_fusion = (bf16[2048,2048]{1,0:T(8,128)(2,1)}, bf16[2048,2048]{1,0:T(8,128)(2,1)}) fusion(bf16[1024,2048]{1,0:T(8,128)(2,1)S(1)} %copy-done.56, bf16[1024,1024]{1,0:T(8,128)(2,1)} %collective-permute-done.1, bf16[1024,1024]{1,0:T(8,128)(2,1)S(1)} %multiply_convert_fusion.2), kind=kOutput, calls=%fused_computation.1 | convolution fusion | flops 8673820672 | bytes 25165824 | tf_op jit(solution)/shard_map/dot_general | solution.py:45
  333.2 11.7 %convolution_convert_fusion.1 = bf16[2048,1024]{1,0:T(8,128)(2,1)S(1)} fusion(bf16[2048,2048]{1,0:T(8,128)(2,1)} %get-tuple-element.121, bf16[2048,1024]{1,0:T(8,128)(2,1)S(1)} %constant_dynamic-update-slice_fusion.26), kind=kOutput, calls=%fused_computation.43 | convolution fusion | flops 8592031744 | bytes 16777216 | tf_op jit(solution)/shard_map/dot_general | solution.py:49
  345.4 14.3 %multiply_convert_fusion = bf16[2048,2048]{1,0:T(8,128)(2,1)} fusion(bf16[2048,2048]{1,0:T(8,128)(2,1)} %get-tuple-element.120, bf16[2048,1024]{1,0:T(8,128)(2,1)S(1)} %constant_dynamic-update-slice_fusion.26, bf16[2048,1024]{1,0:T(8,128)(2,1)} %param.30), kind=kOutput, calls=%fused_computation | convolution fusion | flops 8602517504 | bytes 25165824 | tf_op jit(solution)/shard_map/dot_general | solution.py:55
  359.7 7.1 fusion.28
  366.8 6.4 fusion.34
  376.0 6.4 fusion.31
  387.6 7.3 fusion.25
  396.2 13.5 %collective-permute-done.6 = bf16[512,1024]{1,0:T(8,128)(2,1)S(1)} collective-permute-done((bf16[512,1024]{1,0:T(8,128)(2,1)S(1)}, bf16[512,1024]{1,0:T(8,128)(2,1)S(1)}, u32[]{:S(2)}, u32[]{:S(2)}) %collective-permute-start.6) | collective-permute-done | bytes 1048608 | tf_op jit(solution)/shard_map/ppermute | solution.py:655
  415.2 9.2 %multiply_reduce_fusion = (bf16[1024]{0:T(1024)(128)(2,1)S(1)}, f32[1024]{0:T(1024)S(1)}, f32[1024,1024]{1,0:T(8,128)}) fusion(f32[1024,1024]{1,0:T(8,128)S(1)} %copy-done.5, f32[1024]{0:T(1024)S(1)} %fusion.94, bf16[1024,1024]{1,0:T(8,128)(2,1)S(1)} %collective-permute-done.4, f32[1024]{0:T(1024)S(1)} %copy-done.50, bf16[1024,2048]{1,0:T(8,128)(2,1)S(1)} %copy-done.58, ...), kind=kOutput, calls=%fused_computation.35 | convolution fusion | flops 4303353856 | bytes 18888704 | tf_op jit(solution)/shard_map/dot_general | solution.py:55
  424.4 11.8 %fusion.104 = (bf16[1024,1024]{1,0:T(8,128)(2,1)}, f32[1024,1024]{1,0:T(8,128)}, bf16[1024,1024]{1,0:T(8,128)(2,1)}) fusion(f32[1024,1024]{1,0:T(8,128)S(1)} %copy-done.5, f32[1024]{0:T(1024)S(1)} %multiply_multiply_fusion.1, f32[1024]{0:T(1024)S(1)} %fusion.94, f32[1024]{0:T(1024)S(1)} %copy-done.50, f32[1024,1024]{1,0:T(8,128)} %get-tuple-element.209, ...), kind=kOutput, calls=%fused_computation.305 | convolution fusion | flops 4309647360 | bytes 31469568 | tf_op jit(solution)/shard_map/dot_general | solution.py:45
  458.8 7.1 collective-permute-done.9
  474.1 3.7 convolution_convert_fusion.2.delta_ref.refs_8_
  487.9 18.7 %recall_back.4 = (f32[2048,256]{1,0:T(8,128)}, f32[1,8,128]{2,1,0:T(8,128)}, bf16[128,1024]{1,0:T(8,128)(2,1)}, bf16[128,1024]{1,0:T(8,128)(2,1)}) custom-call(f32[1]{0:T(128)} %get-tuple-element.203.gate_ref, bf16[524288,128]{1,0:T(8,128)(2,1)} %bitcast.4.found_ref, ...), custom_call_target="tpu_custom_call", output_to_operand_aliasing={{2}: (4, {}), {3}: (5, {})} | custom-call | bytes 67108864 | tf_op jit(solution)/shard_map/recall_back/pallas_call | solution.py:335
  513.8 18.6 %recall_back.5 = (f32[2048,256]{1,0:T(8,128)}, f32[1,8,128]{2,1,0:T(8,128)}, bf16[64,1024]{1,0:T(8,128)(2,1)}, bf16[64,1024]{1,0:T(8,128)(2,1)}) custom-call(f32[1]{0:T(128)} %get-tuple-element.204.gate_ref, bf16[524288,128]{1,0:T(8,128)(2,1)} %bitcast.4.found_ref, ...), custom_call_target="tpu_custom_call", output_to_operand_aliasing={{0}: (4, {}), {2}: (5, {}), {3}: (6, {})} | custom-call | bytes 67108864 | tf_op jit(solution)/shard_map/recall_back/pallas_call | solution.py:335
  536.5 22.3 %local_back.2 = (bf16[2048,256]{1,0:T(8,128)(2,1)}, bf16[2048,256]{1,0:T(8,128)(2,1)}, bf16[2048,256]{1,0:T(8,128)(2,1)}, f32[2,8,1024]{2,1,0:T(8,128)}, f32[2,24,256]{2,1,0:T(8,128)}) custom-call(f32[2]{0:T(128)} %get-tuple-element.206.refs_0_, f32[2,2]{1,0:T(2,128)} %get-tuple-element.198.refs_1_, f32[2,1,1024]{2,1,0:T(1,128)} %slice.213.refs_2_, ...), custom_call_target="tpu_custom_call" | custom-call | bytes 167772160 | tf_op jit(solution)/shard_map/local_back/pallas_call | solution.py:555
  561.7 8.9 %multiply_reduce_fusion.4 = (f32[1024]{0:T(1024)S(1)}, bf16[1024,768]{0,1:T(8,128)(2,1)}) fusion(bf16[1024,256]{0,1:T(8,128)(2,1)S(1)} %copy-done.30, bf16[1024,256]{0,1:T(8,128)(2,1)S(1)} %copy-done.28, bf16[1024,256]{0,1:T(8,128)(2,1)S(1)} %copy-done.27, bf16[2048,1024]{1,0:T(8,128)(2,1)} %all-gather.4.cloned.1.call-done, ...), kind=kOutput, calls=%fused_computation.52 | convolution fusion | flops 3228302336 | bytes 10489856 | tf_op jit(solution)/shard_map/dot_general | solution.py:49
  575.8 3.8 fusion.39
  579.6 3.9 fusion.42
  585.9 18.7 %recall_back.6 = (f32[2048,256]{1,0:T(8,128)}, f32[1,8,128]{2,1,0:T(8,128)}, bf16[256,768]{1,0:T(8,128)(2,1)}, bf16[256,768]{1,0:T(8,128)(2,1)}) custom-call(f32[1]{0:T(128)} %get-tuple-element.201.gate_ref, bf16[524288,128]{1,0:T(8,128)(2,1)} %bitcast.4.found_ref, ...), custom_call_target="tpu_custom_call", output_to_operand_aliasing={{2}: (4, {}), {3}: (5, {})} | custom-call | bytes 67108864 | tf_op jit(solution)/shard_map/recall_back/pallas_call | solution.py:335
  611.7 19.0 %recall_back.7 = (f32[2048,256]{1,0:T(8,128)}, f32[1,8,128]{2,1,0:T(8,128)}, bf16[128,768]{1,0:T(8,128)(2,1)}, bf16[128,768]{1,0:T(8,128)(2,1)}) custom-call(f32[1]{0:T(128)} %get-tuple-element.202.gate_ref, bf16[524288,128]{1,0:T(8,128)(2,1)} %bitcast.4.found_ref, ...), custom_call_target="tpu_custom_call", output_to_operand_aliasing={{0}: (4, {}), {2}: (5, {}), {3}: (6, {})} | custom-call | bytes 67108864 | tf_op jit(solution)/shard_map/recall_back/pallas_call | solution.py:335
  636.5 2.9 collective-permute-start.52
  641.0 2.7 collective-permute-start.27
  645.4 22.3 %local_back.3 = (bf16[2048,256]{1,0:T(8,128)(2,1)}, bf16[2048,256]{1,0:T(8,128)(2,1)}, bf16[2048,256]{1,0:T(8,128)(2,1)}, f32[2,8,1024]{2,1,0:T(8,128)}, f32[2,2...) custom-call(f32[2]{0:T(128)} %get-tuple-element.205.refs_0_, ...), custom_call_target="tpu_custom_call", output_to_operand_aliasing={{5}: (10, {}), {6}: (11, {})} | custom-call | bytes 167772160 | tf_op jit(solution)/shard_map/local_back/pallas_call | solution.py:555
  670.6 9.0 %multiply_reduce_fusion.3 = (f32[1024]{0:T(1024)S(1)}, bf16[1024,768]{0,1:T(8,128)(2,1)}) fusion(bf16[1024,256]{0,1:T(8,128)(2,1)S(1)} %copy-done.25, bf16[1024,256]{0,1:T(8,128)(2,1)S(1)} %copy-done.23, bf16[1024,256]{0,1:T(8,128)(2,1)S(1)} %copy-done.22, bf16[2048,1024]{1,0:T(8,128)(2,1)} %all-gather.4.cloned.1.call-done, ...), kind=kOutput, calls=%fused_computation.51 | convolution fusion | flops 3228302336 | bytes 10489856 | tf_op jit(solution)/shard_map/dot_general | solution.py:49
  687.9 4.0 add_convert_fusion.1
  691.9 9.8 %collective-permute-start.26 = (bf16[1024,1024]{1,0:T(8,128)(2,1)S(1)}, bf16[1024,1024]{1,0:T(8,128)(2,1)S(1)}, u32[]{:S(2)}, u32[]{:S(2)}) collective-permute-start(bf16[1024,1024]{1,0:T(8,128)(2,1)S(1)} %add_convert_fusion.1), channel_id=1, source_target_pairs={{0,1},{1,0},{2,3},{3,2},{4,5},{5,4},{6,7},{7,6},{8,9},{9,8},{10,11... | collective-permute-start | bytes 6291464 | tf_op jit(solution)/shard_map/ppermute | solution.py:640
  702.4 3.8 collective-permute-done.28
  706.2 3.8 collective-permute-done.38
  712.8 3.2 collective-permute-done.30
  728.8 5.2 collective-permute-start.34
  737.9 5.5 collective-permute-start.35
  743.8 5.2 collective-permute-done.35
  757.9 2.8 collective-permute-done.36
  760.8 7.0 collective-permute-done.46
  768.0 7.1 collective-permute-start.47
  780.3 4.4 fusion.106
  785.6 4.5 maximum_convert_fusion.1
  790.1 4.4 maximum_convert_fusion
  797.4 10.8 %collective-permute-done.55 = bf16[256,1024]{1,0:T(8,128)(2,1)S(1)} collective-permute-done((bf16[256,1024]{1,0:T(8,128)(2,1)S(1)}, bf16[256,1024]{1,0:T(8,128)(2,1)S(1)}, u32[]{:S(2)}, u32[]{:S(2)}) %collective-permute-start.55) | collective-permute-done | bytes 524320 | tf_op jit(solution)/shard_map/ppermute | solution.py:655
  (432 shorter events, 169.6 us)
Async XLA Ops:
  7.2 60.4 %all-gather.4.cloned.1.call-start = ((), (), s32[]{:S(2)}) async-start(), calls=%async_computation | async-start | bytes 6291456 | tf_op jit(solution)/shard_map/all_gather | solution.py:760
  13.2 767.1 %all-gather.6.cloned.1.call-start = ((), (), s32[]{:S(2)}) async-start(), calls=%async_computation.1 | async-start | bytes 8912896 | tf_op jit(solution)/shard_map/all_gather | solution.py:712
  293.0 17.1 %collective-permute-start.3 = (bf16[1024,1024]{1,0:T(8,128)(2,1)}, bf16[1024,1024]{1,0:T(8,128)(2,1)}, u32[]{:S(2)}, u32[]{:S(2)}) collective-permute-start(bf16[1024,1024]{1,0:T(8,128)(2,1)} %param.31), channel_id=1, source_target_pairs={{1,0},{0,1},{3,2},{2,3},{5,4},{4,5},{7,6},{6,7},{9,8},{8,9},{11,10... | collective-permute-start | bytes 6291464 | tf_op jit(solution)/shard_map/ppermute | solution.py:617
  302.9 9.5 %collective-permute-start.1 = (bf16[1024,1024]{1,0:T(8,128)(2,1)S(1)}, bf16[1024,1024]{1,0:T(8,128)(2,1)}, u32[]{:S(2)}, u32[]{:S(2)}) collective-permute-start(bf16[1024,1024]{1,0:T(8,128)(2,1)S(1)} %multiply_convert_fusion.2), channel_id=1, source_target_pairs={{1,0},{0,1},{3,2},{2,3},{5,4},{4,5},{7,6},{6,7},{9,8},{8,9},{11,10... | collective-permute-start | bytes 6291464 | tf_op jit(solution)/shard_map/ppermute | solution.py:617
  374.6 39.1 %collective-permute-start.4 = (bf16[1024,1024]{1,0:T(8,128)(2,1)S(1)}, bf16[1024,1024]{1,0:T(8,128)(2,1)S(1)}, u32[]{:S(2)}, u32[]{:S(2)}) collective-permute-start(bf16[1024,1024]{1,0:T(8,128)(2,1)S(1)} %fusion.28), channel_id=1, source_target_pairs={{0,1},{1,0},{2,3},{3,2},{4,5},{5,4},{6,7},{7,6},{8,9},{9,8},{10,11... | collective-permute-start | bytes 6291464 | tf_op jit(solution)/shard_map/ppermute | solution.py:640
  383.7 26.0 %collective-permute-start.6 = (bf16[512,1024]{1,0:T(8,128)(2,1)S(1)}, bf16[512,1024]{1,0:T(8,128)(2,1)S(1)}, u32[]{:S(2)}, u32[]{:S(2)}) collective-permute-start(bf16[512,1024]{1,0:T(8,128)(2,1)S(1)} %get-tuple-element.131), channel_id=1, source_target_pairs={{0,8},{2,10},{4,12},{6,14},{8,0},{10,2},{12,4},{14,6},{16,24},{18,... | collective-permute-start | bytes 3145736 | tf_op jit(solution)/shard_map/ppermute | solution.py:655
  386.4 25.8 %collective-permute-start.5 = (bf16[512,1024]{1,0:T(8,128)(2,1)S(1)}, bf16[512,1024]{1,0:T(8,128)(2,1)S(1)}, u32[]{:S(2)}, u32[]{:S(2)}) collective-permute-start(bf16[512,1024]{1,0:T(8,128)(2,1)S(1)} %get-tuple-element.133), channel_id=1, source_target_pairs={{0,4},{2,6},{4,0},{6,2},{8,12},{10,14},{12,8},{14,10},{16,20},{18,... | collective-permute-start | bytes 3145736 | tf_op jit(solution)/shard_map/ppermute | solution.py:655
  394.9 29.5 %collective-permute-start.2 = (bf16[1024,1024]{1,0:T(8,128)(2,1)S(1)}, bf16[1024,1024]{1,0:T(8,128)(2,1)}, u32[]{:S(2)}, u32[]{:S(2)}) collective-permute-start(bf16[1024,1024]{1,0:T(8,128)(2,1)S(1)} %fusion.25), channel_id=1, source_target_pairs={{0,1},{1,0},{2,3},{3,2},{4,5},{5,4},{6,7},{7,6},{8,9},{9,8},{10,11... | collective-permute-start | bytes 6291464 | tf_op jit(solution)/shard_map/ppermute | solution.py:640
  395.9 58.1 %collective-permute-start.8 = (bf16[512,1024]{1,0:T(8,128)(2,1)}, bf16[512,1024]{1,0:T(8,128)(2,1)}, u32[]{:S(2)}, u32[]{:S(2)}) collective-permute-start(bf16[512,1024]{1,0:T(8,128)(2,1)} %get-tuple-element.129), channel_id=1, source_target_pairs={{0,4},{2,6},{4,0},{6,2},{8,12},{10,14},{12,8},{14,10},{16,20},{18,... | collective-permute-start | bytes 3145736 | tf_op jit(solution)/shard_map/ppermute | solution.py:655
  409.7 46.1 %collective-permute-start.7 = (bf16[512,1024]{1,0:T(8,128)(2,1)}, bf16[512,1024]{1,0:T(8,128)(2,1)}, u32[]{:S(2)}, u32[]{:S(2)}) collective-permute-start(bf16[512,1024]{1,0:T(8,128)(2,1)} %get-tuple-element.136), channel_id=1, source_target_pairs={{0,2},{2,0},{4,6},{6,4},{8,10},{10,8},{12,14},{14,12},{16,18},{18,... | collective-permute-start | bytes 3145736 | tf_op jit(solution)/shard_map/ppermute | solution.py:655
  436.2 36.0 %collective-permute-start.11 = (bf16[1024,1024]{1,0:T(8,128)(2,1)}, bf16[1024,1024]{1,0:T(8,128)(2,1)}, u32[]{:S(2)}, u32[]{:S(2)}) collective-permute-start(bf16[1024,1024]{1,0:T(8,128)(2,1)} %get-tuple-element.70), channel_id=1, source_target_pairs={{1,0},{0,1},{3,2},{2,3},{5,4},{4,5},{7,6},{6,7},{9,8},{8,9},{11,10... | collective-permute-start | bytes 6291464 | tf_op jit(solution)/shard_map/ppermute | solution.py:617
  452.4 15.2 %collective-permute-start.10 = (bf16[256,1024]{1,0:T(8,128)(2,1)}, bf16[256,1024]{1,0:T(8,128)(2,1)S(1)}, u32[]{:S(2)}, u32[]{:S(2)}) collective-permute-start(bf16[256,1024]{1,0:T(8,128)(2,1)} %get-tuple-element.163), channel_id=1, source_target_pairs={{0,2},{2,0},{4,6},{6,4},{8,10},{10,8},{12,14},{14,12},{16,18},{18,... | collective-permute-start | bytes 1572872 | tf_op jit(solution)/shard_map/ppermute | solution.py:655
  452.5 13.4 %collective-permute-start.9 = (bf16[256,1024]{1,0:T(8,128)(2,1)}, bf16[256,1024]{1,0:T(8,128)(2,1)S(1)}, u32[]{:S(2)}, u32[]{:S(2)}) collective-permute-start(bf16[256,1024]{1,0:T(8,128)(2,1)} %get-tuple-element.165), channel_id=1, source_target_pairs={{0,8},{2,10},{4,12},{6,14},{8,0},{10,2},{12,4},{14,6},{16,24},{18,... | collective-permute-start | bytes 1572872 | tf_op jit(solution)/shard_map/ppermute | solution.py:655
  455.6 22.1 %collective-permute-start.13 = (bf16[256,1024]{1,0:T(8,128)(2,1)S(1)}, bf16[256,1024]{1,0:T(8,128)(2,1)S(1)}, u32[]{:S(2)}, u32[]{:S(2)}) collective-permute-start(bf16[256,1024]{1,0:T(8,128)(2,1)S(1)} %get-tuple-element.159), channel_id=1, source_target_pairs={{0,8},{2,10},{4,12},{6,14},{8,0},{10,2},{12,4},{14,6},{16,24},{18,... | collective-permute-start | bytes 1572872 | tf_op jit(solution)/shard_map/ppermute | solution.py:655
  457.5 24.3 %collective-permute-start.12 = (bf16[256,1024]{1,0:T(8,128)(2,1)S(1)}, bf16[256,1024]{1,0:T(8,128)(2,1)S(1)}, u32[]{:S(2)}, u32[]{:S(2)}) collective-permute-start(bf16[256,1024]{1,0:T(8,128)(2,1)S(1)} %get-tuple-element.161), channel_id=1, source_target_pairs={{0,4},{2,6},{4,0},{6,2},{8,12},{10,14},{12,8},{14,10},{16,20},{18,... | collective-permute-start | bytes 1572872 | tf_op jit(solution)/shard_map/ppermute | solution.py:655
  466.2 18.0 %collective-permute-start.18 = (bf16[128,1024]{1,0:T(8,128)(2,1)S(1)}, bf16[128,1024]{1,0:T(8,128)(2,1)S(1)}, u32[]{:S(2)}, u32[]{:S(2)}) collective-permute-start(bf16[128,1024]{1,0:T(8,128)(2,1)S(1)} %get-tuple-element.171), channel_id=1, source_target_pairs={{0,2},{2,0},{4,6},{6,4},{8,10},{10,8},{12,14},{14,12},{16,18},{18,... | collective-permute-start | bytes 786440 | tf_op jit(solution)/shard_map/ppermute | solution.py:655
  467.9 18.8 %collective-permute-start.20 = (bf16[128,1024]{1,0:T(8,128)(2,1)S(1)}, bf16[128,1024]{1,0:T(8,128)(2,1)S(1)}, u32[]{:S(2)}, u32[]{:S(2)}) collective-permute-start(bf16[128,1024]{1,0:T(8,128)(2,1)S(1)} %get-tuple-element.173), channel_id=1, source_target_pairs={{0,4},{2,6},{4,0},{6,2},{8,12},{10,14},{12,8},{14,10},{16,20},{18,... | collective-permute-start | bytes 786440 | tf_op jit(solution)/shard_map/ppermute | solution.py:655
  478.7 33.4 %collective-permute-start.15 = (bf16[128,1024]{1,0:T(8,128)(2,1)S(1)}, bf16[128,1024]{1,0:T(8,128)(2,1)S(1)}, u32[]{:S(2)}, u32[]{:S(2)}) collective-permute-start(bf16[128,1024]{1,0:T(8,128)(2,1)S(1)} %get-tuple-element.175), channel_id=1, source_target_pairs={{0,2},{2,0},{4,6},{6,4},{8,10},{10,8},{12,14},{14,12},{16,18},{18,... | collective-permute-start | bytes 786440 | tf_op jit(solution)/shard_map/ppermute | solution.py:655
  482.9 25.2 %collective-permute-start.14 = (bf16[128,1024]{1,0:T(8,128)(2,1)S(1)}, bf16[128,1024]{1,0:T(8,128)(2,1)S(1)}, u32[]{:S(2)}, u32[]{:S(2)}) collective-permute-start(bf16[128,1024]{1,0:T(8,128)(2,1)S(1)} %get-tuple-element.177), channel_id=1, source_target_pairs={{0,8},{2,10},{4,12},{6,14},{8,0},{10,2},{12,4},{14,6},{16,24},{18,... | collective-permute-start | bytes 786440 | tf_op jit(solution)/shard_map/ppermute | solution.py:655
  484.3 23.6 %collective-permute-start.19 = (bf16[64,1024]{1,0:T(8,128)(2,1)S(1)}, bf16[64,1024]{1,0:T(8,128)(2,1)S(1)}, u32[]{:S(2)}, u32[]{:S(2)}) collective-permute-start(bf16[64,1024]{1,0:T(8,128)(2,1)S(1)} %constant_dynamic-slice_fusion.28), channel_id=1, source_target_pairs={{0,16},{2,18},{4,20},{6,22},{8,24},{10,26},{12,28},{14,30},{16,0},... | collective-permute-start | bytes 393224 | tf_op jit(solution)/shard_map/ppermute | solution.py:655
  486.8 21.2 %collective-permute-start.21 = (bf16[64,1024]{1,0:T(8,128)(2,1)S(1)}, bf16[64,1024]{1,0:T(8,128)(2,1)S(1)}, u32[]{:S(2)}, u32[]{:S(2)}) collective-permute-start(bf16[64,1024]{1,0:T(8,128)(2,1)S(1)} %constant_dynamic-slice_fusion.26), channel_id=1, source_target_pairs={{0,16},{2,18},{4,20},{6,22},{8,24},{10,26},{12,28},{14,30},{16,0},... | collective-permute-start | bytes 393224 | tf_op jit(solution)/shard_map/ppermute | solution.py:655
  487.7 95.7 %collective-permute-start.48 = (bf16[256,1024]{1,0:T(8,128)(2,1)}, bf16[256,1024]{1,0:T(8,128)(2,1)}, u32[]{:S(2)}, u32[]{:S(2)}) collective-permute-start(bf16[256,1024]{1,0:T(8,128)(2,1)} %constant_dynamic-slice_fusion.3), channel_id=1, source_target_pairs={{0,8},{2,10},{4,12},{6,14},{8,0},{10,2},{12,4},{14,6},{16,24},{18,... | collective-permute-start | bytes 1572872 | tf_op jit(solution)/shard_map/ppermute | solution.py:655
  509.7 24.0 %collective-permute-start.16 = (bf16[64,1024]{1,0:T(8,128)(2,1)S(1)}, bf16[64,1024]{1,0:T(8,128)(2,1)S(1)}, u32[]{:S(2)}, u32[]{:S(2)}) collective-permute-start(bf16[64,1024]{1,0:T(8,128)(2,1)S(1)} %get-tuple-element.183), channel_id=1, source_target_pairs={{0,16},{2,18},{4,20},{6,22},{8,24},{10,26},{12,28},{14,30},{16,0},... | collective-permute-start | bytes 393224 | tf_op jit(solution)/shard_map/ppermute | solution.py:655
  513.8 20.9 %collective-permute-start.17 = (bf16[64,1024]{1,0:T(8,128)(2,1)S(1)}, bf16[64,1024]{1,0:T(8,128)(2,1)S(1)}, u32[]{:S(2)}, u32[]{:S(2)}) collective-permute-start(bf16[64,1024]{1,0:T(8,128)(2,1)S(1)} %get-tuple-element.185), channel_id=1, source_target_pairs={{0,16},{2,18},{4,20},{6,22},{8,24},{10,26},{12,28},{14,30},{16,0},... | collective-permute-start | bytes 393224 | tf_op jit(solution)/shard_map/ppermute | solution.py:655
  574.1 32.3 %collective-permute-start.23 = (bf16[256,768]{1,0:T(8,128)(2,1)S(1)}, bf16[256,768]{1,0:T(8,128)(2,1)S(1)}, u32[]{:S(2)}, u32[]{:S(2)}) collective-permute-start(bf16[256,768]{1,0:T(8,128)(2,1)S(1)} %get-tuple-element.167), channel_id=1, source_target_pairs={{0,4},{2,6},{4,0},{6,2},{8,12},{10,14},{12,8},{14,10},{16,20},{18,... | collective-permute-start | bytes 1179656 | tf_op jit(solution)/shard_map/ppermute | solution.py:655
  575.3 34.3 %collective-permute-start.22 = (bf16[256,768]{1,0:T(8,128)(2,1)S(1)}, bf16[256,768]{1,0:T(8,128)(2,1)S(1)}, u32[]{:S(2)}, u32[]{:S(2)}) collective-permute-start(bf16[256,768]{1,0:T(8,128)(2,1)S(1)} %get-tuple-element.169), channel_id=1, source_target_pairs={{0,2},{2,0},{4,6},{6,4},{8,10},{10,8},{12,14},{14,12},{16,18},{18,... | collective-permute-start | bytes 1179656 | tf_op jit(solution)/shard_map/ppermute | solution.py:655
  584.7 21.3 %collective-permute-start.49 = (bf16[128,1024]{1,0:T(8,128)(2,1)S(1)}, bf16[128,1024]{1,0:T(8,128)(2,1)S(1)}, u32[]{:S(2)}, u32[]{:S(2)}) collective-permute-start(bf16[128,1024]{1,0:T(8,128)(2,1)S(1)} %constant_dynamic-slice_fusion.2), channel_id=1, source_target_pairs={{0,2},{2,0},{4,6},{6,4},{8,10},{10,8},{12,14},{14,12},{16,18},{18,... | collective-permute-start | bytes 786440 | tf_op jit(solution)/shard_map/ppermute | solution.py:655
  606.2 24.5 %collective-permute-start.50 = (bf16[64,1024]{1,0:T(8,128)(2,1)S(1)}, bf16[64,1024]{1,0:T(8,128)(2,1)S(1)}, u32[]{:S(2)}, u32[]{:S(2)}) collective-permute-start(bf16[64,1024]{1,0:T(8,128)(2,1)S(1)} %constant_dynamic-slice_fusion.1), channel_id=1, source_target_pairs={{0,4},{2,6},{4,0},{6,2},{8,12},{10,14},{12,8},{14,10},{16,20},{18,... | collective-permute-start | bytes 393224 | tf_op jit(solution)/shard_map/ppermute | solution.py:655
  608.2 35.5 %collective-permute-start.25 = (bf16[128,768]{1,0:T(8,128)(2,1)S(1)}, bf16[128,768]{1,0:T(8,128)(2,1)S(1)}, u32[]{:S(2)}, u32[]{:S(2)}) collective-permute-start(bf16[128,768]{1,0:T(8,128)(2,1)S(1)} %get-tuple-element.179), channel_id=1, source_target_pairs={{0,8},{2,10},{4,12},{6,14},{8,0},{10,2},{12,4},{14,6},{16,24},{18,... | collective-permute-start | bytes 589832 | tf_op jit(solution)/shard_map/ppermute | solution.py:655
  610.3 29.0 %collective-permute-start.24 = (bf16[128,768]{1,0:T(8,128)(2,1)S(1)}, bf16[128,768]{1,0:T(8,128)(2,1)S(1)}, u32[]{:S(2)}, u32[]{:S(2)}) collective-permute-start(bf16[128,768]{1,0:T(8,128)(2,1)S(1)} %get-tuple-element.181), channel_id=1, source_target_pairs={{0,4},{2,6},{4,0},{6,2},{8,12},{10,14},{12,8},{14,10},{16,20},{18,... | collective-permute-start | bytes 589832 | tf_op jit(solution)/shard_map/ppermute | solution.py:655
  636.5 55.4 %collective-permute-start.52 = (bf16[32,1024]{1,0:T(8,128)(2,1)}, bf16[32,1024]{1,0:T(8,128)(2,1)S(1)}, u32[]{:S(2)}, u32[]{:S(2)}) collective-permute-start(bf16[32,1024]{1,0:T(8,128)(2,1)} %get-tuple-element.117), channel_id=1, source_target_pairs={{0,16},{2,18},{4,20},{6,22},{8,24},{10,26},{12,28},{14,30},{16,0},... | collective-permute-start | bytes 196616 | tf_op jit(solution)/shard_map/ppermute | solution.py:655
  641.0 60.8 %collective-permute-start.27 = (bf16[64,768]{1,0:T(8,128)(2,1)S(1)}, bf16[64,768]{1,0:T(8,128)(2,1)S(1)}, u32[]{:S(2)}, u32[]{:S(2)}) collective-permute-start(bf16[64,768]{1,0:T(8,128)(2,1)S(1)} %get-tuple-element.187), channel_id=1, source_target_pairs={{0,8},{2,10},{4,12},{6,14},{8,0},{10,2},{12,4},{14,6},{16,24},{18,... | collective-permute-start | bytes 294920 | tf_op jit(solution)/shard_map/ppermute | solution.py:655
  685.7 25.2 %collective-permute-start.29 = (bf16[256,896]{1,0:T(8,128)(2,1)S(1)}, bf16[256,896]{1,0:T(8,128)(2,1)S(1)}, u32[]{:S(2)}, u32[]{:S(2)}) collective-permute-start(bf16[256,896]{1,0:T(8,128)(2,1)S(1)} %constant_dynamic-slice_fusion.13), channel_id=1, source_target_pairs={{0,2},{2,0},{4,6},{6,4},{8,10},{10,8},{12,14},{14,12},{16,18},{18,... | collective-permute-start | bytes 1376264 | tf_op jit(solution)/shard_map/ppermute | solution.py:655
  686.3 15.9 %collective-permute-start.37 = (bf16[64,768]{1,0:T(8,128)(2,1)S(1)}, bf16[64,768]{1,0:T(8,128)(2,1)S(1)}, u32[]{:S(2)}, u32[]{:S(2)}) collective-permute-start(bf16[64,768]{1,0:T(8,128)(2,1)S(1)} %copy-done.36), channel_id=1, source_target_pairs={{0,2},{2,0},{4,6},{6,4},{8,10},{10,8},{12,14},{14,12},{16,18},{18,... | collective-permute-start | bytes 294920 | tf_op jit(solution)/shard_map/ppermute | solution.py:655
  687.3 25.3 %collective-permute-start.39 = (bf16[256,896]{1,0:T(8,128)(2,1)S(1)}, bf16[256,896]{1,0:T(8,128)(2,1)S(1)}, u32[]{:S(2)}, u32[]{:S(2)}) collective-permute-start(bf16[256,896]{1,0:T(8,128)(2,1)S(1)} %constant_dynamic-slice_fusion.7), channel_id=1, source_target_pairs={{0,4},{2,6},{4,0},{6,2},{8,12},{10,14},{12,8},{14,10},{16,20},{18,... | collective-permute-start | bytes 1376264 | tf_op jit(solution)/shard_map/ppermute | solution.py:655
  691.9 61.0 %collective-permute-start.26 = (bf16[1024,1024]{1,0:T(8,128)(2,1)S(1)}, bf16[1024,1024]{1,0:T(8,128)(2,1)S(1)}, u32[]{:S(2)}, u32[]{:S(2)}) collective-permute-start(bf16[1024,1024]{1,0:T(8,128)(2,1)S(1)} %add_convert_fusion.1), channel_id=1, source_target_pairs={{0,1},{1,0},{2,3},{3,2},{4,5},{5,4},{6,7},{7,6},{8,9},{9,8},{10,11... | collective-permute-start | bytes 6291464 | tf_op jit(solution)/shard_map/ppermute | solution.py:640
  701.8 8.3 %collective-permute-start.53 = (bf16[64,1024]{1,0:T(8,128)(2,1)S(1)}, bf16[64,1024]{1,0:T(8,128)(2,1)S(1)}, u32[]{:S(2)}, u32[]{:S(2)}) collective-permute-start(bf16[64,1024]{1,0:T(8,128)(2,1)S(1)} %constant_dynamic-update-slice_fusion.6), channel_id=1, source_target_pairs={{0,4},{2,6},{4,0},{6,2},{8,12},{10,14},{12,8},{14,10},{16,20},{18,... | collective-permute-start | bytes 393224 | tf_op jit(solution)/shard_map/ppermute | solution.py:655
  710.1 84.5 %collective-permute-start.54 = (bf16[128,1024]{1,0:T(8,128)(2,1)S(1)}, bf16[128,1024]{1,0:T(8,128)(2,1)S(1)}, u32[]{:S(2)}, u32[]{:S(2)}) collective-permute-start(bf16[128,1024]{1,0:T(8,128)(2,1)S(1)} %constant_dynamic-update-slice_fusion.4), channel_id=1, source_target_pairs={{0,2},{2,0},{4,6},{6,4},{8,10},{10,8},{12,14},{14,12},{16,18},{18,... | collective-permute-start | bytes 786440 | tf_op jit(solution)/shard_map/ppermute | solution.py:655
  712.7 5.2 collective-permute-start.40
  726.5 8.8 %collective-permute-start.43 = (bf16[32,1664]{1,0:T(8,128)(2,1)S(1)}, bf16[32,1664]{1,0:T(8,128)(2,1)S(1)}, u32[]{:S(2)}, u32[]{:S(2)}) collective-permute-start(bf16[32,1664]{1,0:T(8,128)(2,1)S(1)} %get-tuple-element.193), channel_id=1, source_target_pairs={{0,16},{2,18},{4,20},{6,22},{8,24},{10,26},{12,28},{14,30},{16,0},... | collective-permute-start | bytes 319496 | tf_op jit(solution)/shard_map/ppermute | solution.py:655
  728.8 9.1 %collective-permute-start.34 = (bf16[64,1664]{1,0:T(8,128)(2,1)S(1)}, bf16[64,1664]{1,0:T(8,128)(2,1)S(1)}, u32[]{:S(2)}, u32[]{:S(2)}) collective-permute-start(bf16[64,1664]{1,0:T(8,128)(2,1)S(1)} %constant_dynamic-update-slice_fusion.22), channel_id=1, source_target_pairs={{0,8},{2,10},{4,12},{6,14},{8,0},{10,2},{12,4},{14,6},{16,24},{18,... | collective-permute-start | bytes 638984 | tf_op jit(solution)/shard_map/ppermute | solution.py:655
  735.3 8.2 %collective-permute-start.44 = (bf16[64,1664]{1,0:T(8,128)(2,1)S(1)}, bf16[64,1664]{1,0:T(8,128)(2,1)S(1)}, u32[]{:S(2)}, u32[]{:S(2)}) collective-permute-start(bf16[64,1664]{1,0:T(8,128)(2,1)S(1)} %constant_dynamic-update-slice_fusion.14), channel_id=1, source_target_pairs={{0,2},{2,0},{4,6},{6,4},{8,10},{10,8},{12,14},{14,12},{16,18},{18,... | collective-permute-start | bytes 638984 | tf_op jit(solution)/shard_map/ppermute | solution.py:655
  737.9 11.1 %collective-permute-start.35 = (bf16[128,1664]{1,0:T(8,128)(2,1)S(1)}, bf16[128,1664]{1,0:T(8,128)(2,1)S(1)}, u32[]{:S(2)}, u32[]{:S(2)}) collective-permute-start(bf16[128,1664]{1,0:T(8,128)(2,1)S(1)} %constant_dynamic-update-slice_fusion.20), channel_id=1, source_target_pairs={{0,4},{2,6},{4,0},{6,2},{8,12},{10,14},{12,8},{14,10},{16,20},{18,... | collective-permute-start | bytes 1277960 | tf_op jit(solution)/shard_map/ppermute | solution.py:655
  743.5 7.0 collective-permute-start.45
  749.0 11.6 %collective-permute-start.36 = (bf16[256,1664]{1,0:T(8,128)(2,1)S(1)}, bf16[256,1664]{1,0:T(8,128)(2,1)S(1)}, u32[]{:S(2)}, u32[]{:S(2)}) collective-permute-start(bf16[256,1664]{1,0:T(8,128)(2,1)S(1)} %constant_dynamic-update-slice_fusion.18), channel_id=1, source_target_pairs={{0,2},{2,0},{4,6},{6,4},{8,10},{10,8},{12,14},{14,12},{16,18},{18,... | collective-permute-start | bytes 2555912 | tf_op jit(solution)/shard_map/ppermute | solution.py:655
  750.6 17.1 %collective-permute-start.46 = (bf16[256,1664]{1,0:T(8,128)(2,1)S(1)}, bf16[256,1664]{1,0:T(8,128)(2,1)S(1)}, u32[]{:S(2)}, u32[]{:S(2)}) collective-permute-start(bf16[256,1664]{1,0:T(8,128)(2,1)S(1)} %constant_dynamic-update-slice_fusion.10), channel_id=1, source_target_pairs={{0,4},{2,6},{4,0},{6,2},{8,12},{10,14},{12,8},{14,10},{16,20},{18,... | collective-permute-start | bytes 2555912 | tf_op jit(solution)/shard_map/ppermute | solution.py:655
  768.0 28.1 %collective-permute-start.47 = (f32[2,1024]{0,1:T(8,128)S(1)}, f32[2,1024]{0,1:T(8,128)S(1)}, u32[]{:S(2)}, u32[]{:S(2)}) collective-permute-start(f32[2,1024]{0,1:T(8,128)S(1)} %fusion.57), channel_id=1, source_target_pairs={{1,0},{0,1},{3,2},{2,3},{5,4},{4,5},{7,6},{6,7},{9,8},{8,9},{11,10... | collective-permute-start | bytes 24584 | tf_op jit(solution)/shard_map/ppermute | solution.py:617
  794.6 13.6 %collective-permute-start.55 = (bf16[256,1024]{1,0:T(8,128)(2,1)S(1)}, bf16[256,1024]{1,0:T(8,128)(2,1)S(1)}, u32[]{:S(2)}, u32[]{:S(2)}) collective-permute-start(bf16[256,1024]{1,0:T(8,128)(2,1)S(1)} %constant_dynamic-update-slice_fusion.2), channel_id=1, source_target_pairs={{0,8},{2,10},{4,12},{6,14},{8,0},{10,2},{12,4},{14,6},{16,24},{18,... | collective-permute-start | bytes 1572872 | tf_op jit(solution)/shard_map/ppermute | solution.py:655
  (74 other events, 1014.9 us)
Sparse Core Ops, SparseCore 0:
  13.4 16.1 all-gather.3
  536.7 130.0 all-gather.5

commit v6 on v4

--- a/solution.py
+++ b/solution.py
@@ -32,6 +32,15 @@
     return rows * lax.rsqrt(jnp.mean(rows * rows, -1, keepdims=True) + eps_norm) * gain
 
 
+def gelu_pair(rows):
+    reach = math.sqrt(2.0 / math.pi)
+    square = rows * rows
+    turn = jnp.tanh(reach * rows * (1.0 + 0.044715 * square))
+    share = 0.5 * (1.0 + turn)
+    steep = 0.5 * (1.0 - turn * turn) * reach * (1.0 + 3.0 * 0.044715 * square)
+    return (rows * share).astype(low_type), (share + rows * steep).astype(low_type)
+
+
 def dot_rows(left, right):
     return jnp.dot(left, right, preferred_element_type=full_type)
 
@@ -53,16 +62,23 @@
     row = lax.broadcasted_iota(jnp.int32, (256, 256), 0)
     column = lax.broadcasted_iota(jnp.int32, (256, 256), 1)
     order = jnp.where(column == (row // 2 + (row % 2) * 128), 1.0, 0.0).astype(low_type)
-    for part in range(rows // 128):
+    for part in range(rows // 256):
+        low, high = pl.ds(part * 256, 128), pl.ds(part * 256 + 128, 128)
         both = jnp.concatenate(
-            [key_ref[0, pl.ds(part * 128, 128)], value_ref[0, pl.ds(part * 128, 128)]], 0
-        )
-        table_ref[pl.ds(part * 256, 256), :] = dot_rows(order, both).astype(low_type)
+            [
+                jnp.concatenate([key_ref[0, low], key_ref[0, high]], 1),
+                jnp.concatenate([value_ref[0, low], value_ref[0, high]], 1),
+            ],
+            0,
+        )
+        mixed = dot_rows(order, both).astype(low_type)
+        table_ref[pl.ds(part * 512, 256), :] = mixed[:, :128]
+        table_ref[pl.ds(part * 512 + 256, 256), :] = mixed[:, 128:]
 
 
 def interleave(memory_keys, memory_values):
     heads, rows, width = memory_keys.shape
-    step = min(2048, rows)
+    step = min(8192, rows)
     spec = pl.BlockSpec((1, step, width), lambda h, i: (h, i, 0))
     return pl.pallas_call(
         interleave_kernel,
@@ -70,6 +86,7 @@
         in_specs=[spec, spec],
         out_specs=pl.BlockSpec((2 * step, width), lambda h, i: (h * (rows // step) + i, 0)),
         out_shape=jax.ShapeDtypeStruct((heads * rows * 2, width), low_type),
+        compiler_params=pltpu.CompilerParams(vmem_limit_bytes=vmem_most),
         cost_estimate=pl.CostEstimate(
             flops=heads * rows * 4 * 256 * width,
             bytes_accessed=heads * rows * width * 8,
@@ -661,10 +678,12 @@
     ]
 
 
-def double_all(parts):
+def double_all(parts, beside):
     orders = bit_orders()
     for step in reversed(range(len(orders[0]))):
         got = [swap_over(part, order[step]) for part, order in zip(parts, orders)]
+        if step == 1:
+            got[2], beside = lax.optimization_barrier((got[2], beside))
         wider = []
         for part, other, order in zip(parts, got, orders):
             rows = part.shape[0]
@@ -673,7 +692,7 @@
             whole = lax.dynamic_update_slice_in_dim(whole, part, side * rows, 0)
             wider.append(lax.dynamic_update_slice_in_dim(whole, other, (1 - side) * rows, 0))
         parts = wider
-    return parts
+    return parts, beside
 
 
 def pack(parts):
@@ -766,32 +785,47 @@
     second_rows = rms_scaled(middle, mlp_gain).astype(low_type)
     grad_full = jnp.concatenate(fetch(grad_output), 0)
     second = jnp.concatenate(fetch(second_rows), 0)
-    hidden = dot_rows(second, hidden_weight)
-    active = jax.nn.gelu(hidden).astype(low_type)
-    return_low = dot_outer(active, grad_full).astype(low_type)
+    active, slope = gelu_pair(dot_rows(second, hidden_weight))
+    slope = lax.optimization_barrier(slope)
     orders = bit_orders()
     steps = len(orders[0])
+
+    return_low = dot_outer(active, grad_full).astype(low_type)
     return_half = return_low.shape[0] // 2
-    return_parts = [return_low[:return_half], return_low[return_half:]]
-    for step in range(steps):
-        return_parts = add_low(*halve_step(return_parts, orders[1:], step))
+    kept_back, sent_back = halve_step(
+        [return_low[:return_half], return_low[return_half:]], orders[1:], 0
+    )
     active_delta = dot_inner(grad_full, return_weight)
-    gelu_back = jax.vjp(jax.nn.gelu, hidden)[1]
-    hidden_delta = gelu_back(active_delta)[0].astype(low_type)
+    hidden_delta = (active_delta * slope.astype(full_type)).astype(low_type)
     second_delta = fold(
         lambda rows: dot_inner(rows, hidden_weight),
         lambda k: lax.slice_in_dim(hidden_delta, k * share_rows, (k + 1) * share_rows),
     )
-    hidden_low = dot_outer(second, hidden_delta).astype(low_type)
-    hidden_half = hidden_low.shape[0] // 2
-    hidden_parts = [hidden_low[:hidden_half], hidden_low[hidden_half:]]
-    hidden_parts = add_low(*halve_step(hidden_parts, orders[:2], 0))
-    kept, sent = halve_step(hidden_parts, orders[:2], 1)
+    hidden_half = hidden_delta.shape[1] // 2
+    hidden_parts = [
+        dot_outer(second, hidden_delta[:, :hidden_half]).astype(low_type),
+        dot_outer(second, hidden_delta[:, hidden_half:]).astype(low_type),
+    ]
+    kept, sent = halve_step(hidden_parts, orders[:2], 0)
+
+    kept_back, kept = lax.optimization_barrier((kept_back, kept))
+    kept_back, sent_back = halve_step(add_low(kept_back, sent_back), orders[1:], 1)
+
     second_back = jax.vjp(rms_scaled, middle, mlp_gain)[1]
     middle_part, mlp_gain_part = second_back(second_delta)
     middle_delta = grad_output.astype(full_type) + middle_part
-    middle_full = in_order(fetch(middle_delta.astype(low_type)))
+    middle_low = middle_delta.astype(low_type)
+    kept, kept_back, middle_low = lax.optimization_barrier((kept, kept_back, middle_low))
+    kept, sent = halve_step(add_low(kept, sent), orders[:2], 1)
+    kept_back, sent_back = halve_step(add_low(kept_back, sent_back), orders[1:], 2)
+    middle_full = in_order(fetch(middle_low))
     mixed_delta = dot_inner(middle_full, output_weight).astype(low_type)
+    kept, kept_back, mixed_delta = lax.optimization_barrier((kept, kept_back, mixed_delta))
+    kept, sent = halve_step(add_low(kept, sent), orders[:2], 2)
+    kept_back, sent_back = halve_step(add_low(kept_back, sent_back), orders[1:], 3)
+    taken = 2
+    for step in range(4, steps):
+        kept_back, sent_back = halve_step(add_low(kept_back, sent_back), orders[1:], step)
     layer_output = (
         middle
         + fold(
@@ -800,7 +834,6 @@
         )
     ).astype(low_type)
 
-    taken = 1
     shards, packed = [], []
     recall_delta = None
     recall_sums = []
@@ -814,19 +847,19 @@
             taken += 1
             kept, sent = halve_step(add_low(kept, sent), orders[:2], taken)
         elif not shards:
-            shards = add_low(kept, sent) + return_parts
+            shards = add_low(kept, sent) + add_low(kept_back, sent_back)
             packed = [pack(shards)]
             kept = []
     while taken < steps - 1:
         taken += 1
         kept, sent = halve_step(add_low(kept, sent), orders[:2], taken)
     if not shards:
-        shards = add_low(kept, sent) + return_parts
+        shards = add_low(kept, sent) + add_low(kept_back, sent_back)
         packed = [pack(shards)]
     hidden_low_sum, hidden_high_sum, return_low_sum, return_high_sum = gather_all(
         packed[0], shards, orders[:2] + orders[1:]
     )
-    hidden_sum = jnp.concatenate([hidden_low_sum, hidden_high_sum], 0)
+    hidden_sum = jnp.concatenate([hidden_low_sum, hidden_high_sum], 1)
     return_sum = jnp.concatenate([return_low_sum, return_high_sum], 0)
     recall_sums = jnp.concatenate(recall_sums, 0)
     half_heads = max(1, head_count // 2)
@@ -869,8 +902,8 @@
     ]
     for step in range(steps):
         last = add_low(*halve_step(last, orders, step))
-    last, hidden_sum, return_sum = lax.optimization_barrier((last, hidden_sum, return_sum))
-    *joined_sum, output_sum = double_all(last)
+    last, (hidden_sum, return_sum) = double_all(last, (hidden_sum, return_sum))
+    *joined_sum, output_sum = last
 
     normed_delta = fold(
         lambda rows: dot_inner(rows, joined), lambda k: share_of(project_delta, k, share_rows)

time: 807 us -> 772 us (0.957)
  waiting for transfers between devices: 113 us -> 89.9 us
  other arithmetic: 62.9 us -> 43.2 us
  starting transfers between devices: 54.2 us -> 67.5 us
  Pallas kernels: 369 us -> 357 us
    ppermute x40, waiting for transfers between devices: 113 us -> 85.9 us  [swap_over(): lax.ppermute(rows, 'dp', [(i, i ^ 1 << bit) for i in range(lax.axis_size(...]
    concatenate x1, other arithmetic: 18.5 us -> 4.42 us  [body(): hidden_sum = jnp.concatenate([hidden_low_sum, hidden_high_sum], 1)]
    pallas_call x1, Pallas kernels: 39.1 us -> 26 us  [interleave(): pl.pallas_call(interleave_kernel, grid=(heads, rows // step), in_specs=[s...]
    dot_general x4 -> x5, matrix products: 37.7 us -> 36.2 us  [dot_outer(): lax.dot_general(left, right, (((0,), (0,)), ((), ())), preferred_element_...]
  transfers between devices with their start and end apart: 50 -> 50, of which waited for: 20 -> 19; matrix products, arithmetic and copies ran while one was open for 17% -> 18% of each run, Pallas kernels for 20% -> 19%
where the time goes in v6:
time: 772 us; the launch traced here: 765 us
  Pallas kernels  357 us (46%)
  matrix products  138 us (18%)
  waiting for transfers between devices  89.9 us (12%)
  starting transfers between devices  67.5 us (9%)
  local copies, waits for them, and re-layouts  53 us (7%)
  other arithmetic  43.2 us (6%)
  between operations  15.9 us (2%)
    pallas_call x1, Pallas kernels, gather_found(): pl.pallas_call(functools.partial(gather_kernel, picks, scale), grid=(step...  190 us
    ppermute x40, waiting for transfers between devices, swap_over(): lax.ppermute(rows, 'dp', [(i, i ^ 1 << bit) for i in range(lax.axis_size(...  85.9 us
    pallas_call x4, Pallas kernels, recall_back(): pl.pallas_call(kernel, grid=(blocks,), in_specs=[pl.BlockSpec(memory_spac...  75.2 us
    dot_general x6, matrix products, dot_rows(): return jnp.dot(left, right, preferred_element_type=full_type)  57.9 us
    pallas_call x2, Pallas kernels, local_back(): pl.pallas_call(kernel, grid=(count, tokens // seq_len), in_specs=[smem, s...  44.8 us
    ppermute x40, starting transfers between devices, swap_over(): lax.ppermute(rows, 'dp', [(i, i ^ 1 << bit) for i in range(lax.axis_size(...  43.6 us
    dot_general x6, matrix products, dot_inner(): lax.dot_general(left, right, (((1,), (1,)), ((), ())), preferred_element_...  42.5 us
    dot_general x5, matrix products, dot_outer(): lax.dot_general(left, right, (((0,), (0,)), ((), ())), preferred_element_...  36.2 us
  transfers between devices with their start and end apart: 50, of which 19 were waited for; matrix products, arithmetic and copies ran while one was open for 18% of the time, Pallas kernels for 19%

profile of v6, /device:TPU:1, one launch (start us, length us, event | category | flops | bytes accessed | tf_op | source)
XLA Modules:
  0.0 764.6 jit_solution(17503710752562091551)
XLA Ops:
  10.7 3.5 fusion.6
  14.4 2.7 copy.59
  17.1 4.2 reshape.187.index_hbm
  28.4 26.0 %interleave.1 = bf16[131072,128]{1,0:T(8,128)(2,1)} custom-call(bf16[4,16384,128]{2,1,0:T(8,128)(2,1)} %key_ref.1, bf16[4,16384,128]{2,1,0:T(8,128)(2,1)} %value_ref.1), custom_call_target="tpu_custom_call" | custom-call | flops 8589934592 | bytes 67108864 | tf_op jit(solution)/shard_map/interleave/pallas_call | solution.py:83
  54.5 11.3 %convolution_convert_fusion.now_ref.before_ref.query_ref.key_ref.value_ref.refs_3_.refs_4_.refs_5_ = bf16[2048,1536]{1,0:T(8,128)(2,1)} fusion(bf16[2048,1024]{1,0:T(8,128)(2,1)} %all-gather.4.cloned.1.call-done, bf16[1024,1536]{1,0:T(8,128)(2,1)} %copy-done.21), kind=kOutput, calls=%fused_computation.10 | convolution fusion | flops 6445596672 | bytes 13631488 | tf_op jit(solution)/shard_map/dot_general | solution.py:45
  65.7 189.8 %gather_found.1 = (bf16[262144,2,128]{2,1,0:T(2,128)(2,1)}, f32[4096,128]{1,0:T(8,128)}, f32[4096,128]{1,0:T(8,128)}) custom-call(s32[64,32,128]{2,1,0:T(8,128)} %reshape.187.index_hbm, bf16[65536,2,128]{2,1,0:T(2,128)(2,1)} %bitcast.52, bf16[2048,1536]{1,0:T(8,128)(2,1)} %convolution_convert_fusion.now_ref.before_ref.query_ref.key_ref.value_ref.refs_3_.refs_4_.refs_5_, ...), custom_call_target="tpu_custom_call" | custom-call | bytes 536870912 | tf_op jit(solution)/shard_map/gather_found/pallas_call | solution.py:243
  255.6 21.2 %local_read.1 = bf16[2048,512]{1,0:T(8,128)(2,1)} custom-call(f32[4]{0:T(128)} %add_divide_fusion.gate_ref, f32[4,2]{1,0:T(4,128)} %pad_maximum_fusion.10.far_ref, f32[4,1,1024]{2,1,0:T(1,128)} %broadcast_in_dim.33.column_ref, bf16[2048,1536]{1,0:T(8,128)(2,1)} %convolution_convert_fusion.now_ref.before_ref.query_ref.key_ref.value_ref.refs_3_.refs_4_.refs_5_, ...), custom_call_target="tpu_custom_call" | custom-call | bytes 167772160 | tf_op jit(solution)/shard_map/local_read/pallas_call | solution.py:414
  276.8 4.0 convolution_convert_fusion.3
  281.2 4.0 collective-permute-done
  285.2 3.5 multiply_reduce_fusion.3
  297.1 20.4 %add_convert_fusion = (bf16[2048,2048]{1,0:T(8,128)(2,1)}, bf16[2048,2048]{1,0:T(8,128)(2,1)}) fusion(bf16[1024,2048]{1,0:T(8,128)(2,1)S(1)} %copy-done.47, bf16[1024,1024]{1,0:T(8,128)(2,1)} %collective-permute-done.1, bf16[1024,1024]{1,0:T(8,128)(2,1)S(1)} %multiply_convert_fusion.2), kind=kOutput, calls=%fused_computation.1 | convolution fusion | flops 8673820672 | bytes 25165824 | tf_op jit(solution)/shard_map/dot_general | solution.py:45
  317.5 11.7 %convolution_convert_fusion.1 = bf16[2048,1024]{1,0:T(8,128)(2,1)S(1)} fusion(bf16[2048,2048]{1,0:T(8,128)(2,1)} %get-tuple-element.111, bf16[2048,1024]{1,0:T(8,128)(2,1)S(1)} %constant_dynamic-update-slice_fusion.3), kind=kOutput, calls=%fused_computation.45 | convolution fusion | flops 8592031744 | bytes 16777216 | tf_op jit(solution)/shard_map/dot_general | solution.py:49
  329.7 14.3 %multiply_convert_fusion = bf16[2048,2048]{1,0:T(8,128)(2,1)} fusion(bf16[2048,2048]{1,0:T(8,128)(2,1)} %get-tuple-element.110, bf16[2048,1024]{1,0:T(8,128)(2,1)S(1)} %constant_dynamic-update-slice_fusion.3, bf16[2048,1024]{1,0:T(8,128)(2,1)} %param.30), kind=kOutput, calls=%fused_computation | convolution fusion | flops 8602517504 | bytes 25165824 | tf_op jit(solution)/shard_map/dot_general | solution.py:55
  344.0 7.1 fusion.28
  351.1 6.4 fusion.34
  359.5 6.8 fusion.31
  367.6 2.7 collective-permute-start.6
  371.5 6.9 fusion.25
  379.6 14.3 %collective-permute-done.6 = bf16[512,1024]{1,0:T(8,128)(2,1)S(1)} collective-permute-done((bf16[512,1024]{1,0:T(8,128)(2,1)S(1)}, bf16[512,1024]{1,0:T(8,128)(2,1)S(1)}, u32[]{:S(2)}, u32[]{:S(2)}) %collective-permute-start.6) | collective-permute-done | bytes 1048608 | tf_op jit(solution)/shard_map/ppermute | solution.py:654
  399.2 9.9 %multiply_reduce_fusion.1 = (bf16[1024]{0:T(1024)(128)(2,1)S(1)}, f32[1024]{0:T(1024)S(1)}, f32[1024,1024]{1,0:T(8,128)}) fusion(f32[1024,1024]{1,0:T(8,128)S(1)} %copy-done.5, f32[1024]{0:T(1024)S(1)} %fusion.89, bf16[1024,1024]{1,0:T(8,128)(2,1)S(1)} %collective-permute-done.4, f32[1024]{0:T(1024)S(1)} %copy-done.37, ...), kind=kOutput, calls=%fused_computation.38 | convolution fusion | flops 4303353856 | bytes 18888704 | tf_op jit(solution)/shard_map/dot_general | solution.py:55
  409.1 11.9 %fusion.98 = (bf16[1024,1024]{1,0:T(8,128)(2,1)}, f32[1024,1024]{1,0:T(8,128)}, bf16[1024,1024]{1,0:T(8,128)(2,1)}) fusion(f32[1024,1024]{1,0:T(8,128)S(1)} %copy-done.5, f32[1024]{0:T(1024)S(1)} %multiply_multiply_fusion.1, f32[1024]{0:T(1024)S(1)} %fusion.89, f32[1024]{0:T(1024)S(1)} %copy-done.37, f32[1024,1024]{1,0:T(8,128)} %get-tuple-element.171, ...), kind=kOutput, calls=%fused_computation.264 | convolution fusion | flops 4309647360 | bytes 31469568 | tf_op jit(solution)/shard_map/dot_general | solution.py:45
  431.3 7.0 collective-permute-done.9
  446.3 3.7 convolution_convert_fusion.2.delta_ref.refs_8_
  460.2 18.6 %recall_back.4 = (f32[2048,512]{1,0:T(8,128)}, f32[1,8,128]{2,1,0:T(8,128)}, bf16[128,1024]{1,0:T(8,128)(2,1)}, bf16[128,1024]{1,0:T(8,128)(2,1)}) custom-call(f32[1]{0:T(128)} %get-tuple-element.165.gate_ref, bf16[524288,128]{1,0:T(8,128)(2,1)} %bitcast.4.found_ref, ...), custom_call_target="tpu_custom_call", output_to_operand_aliasing={{2}: (4, {}), {3}: (5, {})} | custom-call | bytes 67108864 | tf_op jit(solution)/shard_map/recall_back/pallas_call | solution.py:334
  484.7 18.9 %recall_back.5 = (f32[2048,512]{1,0:T(8,128)}, f32[1,8,128]{2,1,0:T(8,128)}, bf16[64,1024]{1,0:T(8,128)(2,1)}, bf16[64,1024]{1,0:T(8,128)(2,1)}) custom-call(f32[1]{0:T(128)} %get-tuple-element.166.gate_ref, bf16[524288,128]{1,0:T(8,128)(2,1)} %bitcast.4.found_ref, ...), custom_call_target="tpu_custom_call", output_to_operand_aliasing={{0}: (4, {}), {2}: (5, {}), {3}: (6, {})} | custom-call | bytes 67108864 | tf_op jit(solution)/shard_map/recall_back/pallas_call | solution.py:334
  506.3 19.1 %recall_back.6 = (f32[2048,512]{1,0:T(8,128)}, f32[1,8,128]{2,1,0:T(8,128)}) custom-call(f32[1]{0:T(128)} %get-tuple-element.167.gate_ref, bf16[524288,128]{1,0:T(8,128)(2,1)} %bitcast.4.found_ref, bf16[2048,1536]{1,0:T(8,128)(2,1)} %convolution_convert_fusion.now_ref.before_ref.query_ref.key_ref.value_ref.refs_3_.refs_4_.refs_5_, ...), custom_call_target="tpu_custom_call", output_to_operand_aliasing={{0}: (4, {})} | custom-call | bytes 67108864 | tf_op jit(solution)/shard_map/recall_back/pallas_call | solution.py:334
  525.4 18.7 %recall_back.7 = (f32[2048,512]{1,0:T(8,128)}, f32[1,8,128]{2,1,0:T(8,128)}) custom-call(f32[1]{0:T(128)} %get-tuple-element.168.gate_ref, bf16[524288,128]{1,0:T(8,128)(2,1)} %bitcast.4.found_ref, bf16[2048,1536]{1,0:T(8,128)(2,1)} %convolution_convert_fusion.now_ref.before_ref.query_ref.key_ref.value_ref.refs_3_.refs_4_.refs_5_, ...), custom_call_target="tpu_custom_call", output_to_operand_aliasing={{0}: (4, {})} | custom-call | bytes 67108864 | tf_op jit(solution)/shard_map/recall_back/pallas_call | solution.py:334
  544.1 22.6 %local_back.2 = (bf16[2048,512]{1,0:T(8,128)(2,1)}, bf16[2048,512]{1,0:T(8,128)(2,1)}, bf16[2048,512]{1,0:T(8,128)(2,1)}, f32[2,8,1024]{2,1,0:T(8,128)}, f32[2,24,256]{2,1,0:T(8,128)}) custom-call(f32[2]{0:T(128)} %get-tuple-element.163.refs_0_, f32[2,2]{1,0:T(2,128)} %get-tuple-element.159.refs_1_, f32[2,1,1024]{2,1,0:T(1,128)} %slice.165.refs_2_, ...), custom_call_target="tpu_custom_call" | custom-call | bytes 167772160 | tf_op jit(solution)/shard_map/local_back/pallas_call | solution.py:553
  566.7 22.2 %local_back.3 = (bf16[2048,512]{1,0:T(8,128)(2,1)}, bf16[2048,512]{1,0:T(8,128)(2,1)}, bf16[2048,512]{1,0:T(8,128)(2,1)}, f32[2,8,1024]{2,1,0:T(8,128)}, f32[2,24,256]{2,1,0:T(8,128)}) custom-call(f32[2]{0:T(128)} %get-tuple-element.164.refs_0_, f32[2,2]{1,0:T(2,128)} %get-tuple-element.160.refs_1_, ...), custom_call_target="tpu_custom_call", output_to_operand_aliasing={{0}: (10, {}), {1}: (11, {}), {2}: (12, {})} | custom-call | bytes 167772160 | tf_op jit(solution)/shard_map/local_back/pallas_call | solution.py:553
  594.6 9.0 %fusion.101 = (bf16[1024,1536]{1,0:T(8,128)(2,1)}, f32[1024]{0:T(1024)S(1)}) fusion(bf16[1024,1536]{1,0:T(8,128)(2,1)S(1)} %copy-done.22, bf16[2048,1024]{1,0:T(8,128)(2,1)S(1)} %copy-done.51, bf16[2048,1536]{1,0:T(8,128)(2,1)S(1)} %constant_dynamic-update-slice_fusion.5), kind=kOutput, calls=%fused_computation.266 | convolution fusion | flops 6448741376 | bytes 16781312 | tf_op jit(solution)/shard_map/dot_general | solution.py:49
  609.3 2.7 collective-permute-done.41
  613.6 2.7 collective-permute-done.42
  619.5 4.3 collective-permute-done.43
  624.0 3.9 fusion.37
  630.4 6.7 collective-permute-start.22
  639.0 6.9 collective-permute-done.31
  646.3 8.8 %collective-permute-done.24 = bf16[128,1664]{1,0:T(8,128)(2,1)S(1)} collective-permute-done((bf16[128,1664]{1,0:T(8,128)(2,1)S(1)}, bf16[128,1664]{1,0:T(8,128)(2,1)S(1)}, u32[]{:S(2)}, u32[]{:S(2)}) %collective-permute-start.24) | collective-permute-done | bytes 426016 | tf_op jit(solution)/shard_map/ppermute | solution.py:654
  657.4 2.9 collective-permute-done.25
  665.9 2.6 collective-permute-start.27
  676.4 2.5 collective-permute-done.28
  681.0 3.7 fusion.7
  692.8 7.9 %collective-permute-done.30 = bf16[256,1664]{1,0:T(8,128)(2,1)S(1)} collective-permute-done((bf16[256,1664]{1,0:T(8,128)(2,1)S(1)}, bf16[256,1664]{1,0:T(8,128)(2,1)S(1)}, u32[]{:S(2)}, u32[]{:S(2)}) %collective-permute-start.30) | collective-permute-done | bytes 852000 | tf_op jit(solution)/shard_map/ppermute | solution.py:654
  700.8 7.0 collective-permute-done.38
  708.0 13.8 %collective-permute-start.39 = (f32[2,1024]{0,1:T(8,128)S(1)}, f32[2,1024]{0,1:T(8,128)S(1)}, u32[]{:S(2)}, u32[]{:S(2)}) collective-permute-start(f32[2,1024]{0,1:T(8,128)S(1)} %fusion.53), channel_id=1, source_target_pairs={{1,0},{0,1},{3,2},{2,3},{5,4},{4,5},{7,6},{6,7},{9,8},{8,9},{11,10... | collective-permute-start | bytes 24584 | tf_op jit(solution)/shard_map/ppermute | solution.py:616
  727.1 4.1 fusion.100
  732.2 4.5 maximum_convert_fusion.1
  736.7 4.4 maximum_convert_fusion
  744.5 10.4 %collective-permute-done.47 = bf16[256,1024]{1,0:T(8,128)(2,1)} collective-permute-done((bf16[256,1024]{1,0:T(8,128)(2,1)S(1)}, bf16[256,1024]{1,0:T(8,128)(2,1)}, u32[]{:S(2)}, u32[]{:S(2)}) %collective-permute-start.47) | collective-permute-done | bytes 524320 | tf_op jit(solution)/shard_map/ppermute | solution.py:654
  (367 shorter events, 126.6 us)
Async XLA Ops:
  7.2 47.3 %all-gather.4.cloned.1.call-start = ((), (), s32[]{:S(2)}) async-start(), calls=%async_computation | async-start | bytes 6291456 | tf_op jit(solution)/shard_map/all_gather | solution.py:759
  14.1 713.0 %all-gather.6.cloned.1.call-start = ((), (), s32[]{:S(2)}) async-start(), calls=%async_computation.1 | async-start | bytes 8912896 | tf_op jit(solution)/shard_map/all_gather | solution.py:711
  280.8 14.5 %collective-permute-start.3 = (bf16[1024,1024]{1,0:T(8,128)(2,1)}, bf16[1024,1024]{1,0:T(8,128)(2,1)}, u32[]{:S(2)}, u32[]{:S(2)}) collective-permute-start(bf16[1024,1024]{1,0:T(8,128)(2,1)} %param.31), channel_id=1, source_target_pairs={{1,0},{0,1},{3,2},{2,3},{5,4},{4,5},{7,6},{6,7},{9,8},{8,9},{11,10... | collective-permute-start | bytes 6291464 | tf_op jit(solution)/shard_map/ppermute | solution.py:616
  291.2 5.9 collective-permute-start.1
  358.8 39.1 %collective-permute-start.4 = (bf16[1024,1024]{1,0:T(8,128)(2,1)S(1)}, bf16[1024,1024]{1,0:T(8,128)(2,1)S(1)}, u32[]{:S(2)}, u32[]{:S(2)}) collective-permute-start(bf16[1024,1024]{1,0:T(8,128)(2,1)S(1)} %fusion.28), channel_id=1, source_target_pairs={{0,1},{1,0},{2,3},{3,2},{4,5},{5,4},{6,7},{7,6},{8,9},{9,8},{10,11... | collective-permute-start | bytes 6291464 | tf_op jit(solution)/shard_map/ppermute | solution.py:639
  367.6 26.2 %collective-permute-start.6 = (bf16[512,1024]{1,0:T(8,128)(2,1)S(1)}, bf16[512,1024]{1,0:T(8,128)(2,1)S(1)}, u32[]{:S(2)}, u32[]{:S(2)}) collective-permute-start(bf16[512,1024]{1,0:T(8,128)(2,1)S(1)} %get-tuple-element.125), channel_id=1, source_target_pairs={{0,8},{2,10},{4,12},{6,14},{8,0},{10,2},{12,4},{14,6},{16,24},{18,... | collective-permute-start | bytes 3145736 | tf_op jit(solution)/shard_map/ppermute | solution.py:654
  370.4 26.0 %collective-permute-start.5 = (bf16[512,1024]{1,0:T(8,128)(2,1)S(1)}, bf16[512,1024]{1,0:T(8,128)(2,1)S(1)}, u32[]{:S(2)}, u32[]{:S(2)}) collective-permute-start(bf16[512,1024]{1,0:T(8,128)(2,1)S(1)} %get-tuple-element.127), channel_id=1, source_target_pairs={{0,4},{2,6},{4,0},{6,2},{8,12},{10,14},{12,8},{14,10},{16,20},{18,... | collective-permute-start | bytes 3145736 | tf_op jit(solution)/shard_map/ppermute | solution.py:654
  378.4 30.6 %collective-permute-start.2 = (bf16[1024,1024]{1,0:T(8,128)(2,1)S(1)}, bf16[1024,1024]{1,0:T(8,128)(2,1)S(1)}, u32[]{:S(2)}, u32[]{:S(2)}) collective-permute-start(bf16[1024,1024]{1,0:T(8,128)(2,1)S(1)} %fusion.25), channel_id=1, source_target_pairs={{0,1},{1,0},{2,3},{3,2},{4,5},{5,4},{6,7},{7,6},{8,9},{9,8},{10,11... | collective-permute-start | bytes 6291464 | tf_op jit(solution)/shard_map/ppermute | solution.py:639
  379.2 47.0 %collective-permute-start.8 = (bf16[512,1024]{1,0:T(8,128)(2,1)}, bf16[512,1024]{1,0:T(8,128)(2,1)}, u32[]{:S(2)}, u32[]{:S(2)}) collective-permute-start(bf16[512,1024]{1,0:T(8,128)(2,1)} %get-tuple-element.123), channel_id=1, source_target_pairs={{0,4},{2,6},{4,0},{6,2},{8,12},{10,14},{12,8},{14,10},{16,20},{18,... | collective-permute-start | bytes 3145736 | tf_op jit(solution)/shard_map/ppermute | solution.py:654
  393.8 34.3 %collective-permute-start.7 = (bf16[512,1024]{1,0:T(8,128)(2,1)}, bf16[512,1024]{1,0:T(8,128)(2,1)}, u32[]{:S(2)}, u32[]{:S(2)}) collective-permute-start(bf16[512,1024]{1,0:T(8,128)(2,1)} %get-tuple-element.130), channel_id=1, source_target_pairs={{0,2},{2,0},{4,6},{6,4},{8,10},{10,8},{12,14},{14,12},{16,18},{18,... | collective-permute-start | bytes 3145736 | tf_op jit(solution)/shard_map/ppermute | solution.py:654
  421.0 23.5 %collective-permute-start.11 = (bf16[1024,1024]{1,0:T(8,128)(2,1)}, bf16[1024,1024]{1,0:T(8,128)(2,1)}, u32[]{:S(2)}, u32[]{:S(2)}) collective-permute-start(bf16[1024,1024]{1,0:T(8,128)(2,1)} %get-tuple-element.64), channel_id=1, source_target_pairs={{1,0},{0,1},{3,2},{2,3},{5,4},{4,5},{7,6},{6,7},{9,8},{8,9},{11,10... | collective-permute-start | bytes 6291464 | tf_op jit(solution)/shard_map/ppermute | solution.py:616
  424.7 15.2 %collective-permute-start.10 = (bf16[256,1024]{1,0:T(8,128)(2,1)}, bf16[256,1024]{1,0:T(8,128)(2,1)S(1)}, u32[]{:S(2)}, u32[]{:S(2)}) collective-permute-start(bf16[256,1024]{1,0:T(8,128)(2,1)} %get-tuple-element.141), channel_id=1, source_target_pairs={{0,2},{2,0},{4,6},{6,4},{8,10},{10,8},{12,14},{14,12},{16,18},{18,... | collective-permute-start | bytes 1572872 | tf_op jit(solution)/shard_map/ppermute | solution.py:654
  424.8 13.4 %collective-permute-start.9 = (bf16[256,1024]{1,0:T(8,128)(2,1)}, bf16[256,1024]{1,0:T(8,128)(2,1)S(1)}, u32[]{:S(2)}, u32[]{:S(2)}) collective-permute-start(bf16[256,1024]{1,0:T(8,128)(2,1)} %get-tuple-element.143), channel_id=1, source_target_pairs={{0,8},{2,10},{4,12},{6,14},{8,0},{10,2},{12,4},{14,6},{16,24},{18,... | collective-permute-start | bytes 1572872 | tf_op jit(solution)/shard_map/ppermute | solution.py:654
  428.0 22.1 %collective-permute-start.13 = (bf16[256,1024]{1,0:T(8,128)(2,1)S(1)}, bf16[256,1024]{1,0:T(8,128)(2,1)S(1)}, u32[]{:S(2)}, u32[]{:S(2)}) collective-permute-start(bf16[256,1024]{1,0:T(8,128)(2,1)S(1)} %get-tuple-element.137), channel_id=1, source_target_pairs={{0,8},{2,10},{4,12},{6,14},{8,0},{10,2},{12,4},{14,6},{16,24},{18,... | collective-permute-start | bytes 1572872 | tf_op jit(solution)/shard_map/ppermute | solution.py:654
  429.9 24.3 %collective-permute-start.12 = (bf16[256,1024]{1,0:T(8,128)(2,1)S(1)}, bf16[256,1024]{1,0:T(8,128)(2,1)S(1)}, u32[]{:S(2)}, u32[]{:S(2)}) collective-permute-start(bf16[256,1024]{1,0:T(8,128)(2,1)S(1)} %get-tuple-element.139), channel_id=1, source_target_pairs={{0,4},{2,6},{4,0},{6,2},{8,12},{10,14},{12,8},{14,10},{16,20},{18,... | collective-permute-start | bytes 1572872 | tf_op jit(solution)/shard_map/ppermute | solution.py:654
  438.5 18.0 %collective-permute-start.18 = (bf16[128,1024]{1,0:T(8,128)(2,1)S(1)}, bf16[128,1024]{1,0:T(8,128)(2,1)S(1)}, u32[]{:S(2)}, u32[]{:S(2)}) collective-permute-start(bf16[128,1024]{1,0:T(8,128)(2,1)S(1)} %get-tuple-element.145), channel_id=1, source_target_pairs={{0,2},{2,0},{4,6},{6,4},{8,10},{10,8},{12,14},{14,12},{16,18},{18,... | collective-permute-start | bytes 786440 | tf_op jit(solution)/shard_map/ppermute | solution.py:654
  440.2 18.8 %collective-permute-start.20 = (bf16[128,1024]{1,0:T(8,128)(2,1)S(1)}, bf16[128,1024]{1,0:T(8,128)(2,1)S(1)}, u32[]{:S(2)}, u32[]{:S(2)}) collective-permute-start(bf16[128,1024]{1,0:T(8,128)(2,1)S(1)} %get-tuple-element.147), channel_id=1, source_target_pairs={{0,4},{2,6},{4,0},{6,2},{8,12},{10,14},{12,8},{14,10},{16,20},{18,... | collective-permute-start | bytes 786440 | tf_op jit(solution)/shard_map/ppermute | solution.py:654
  451.0 31.9 %collective-permute-start.15 = (bf16[128,1024]{1,0:T(8,128)(2,1)S(1)}, bf16[128,1024]{1,0:T(8,128)(2,1)S(1)}, u32[]{:S(2)}, u32[]{:S(2)}) collective-permute-start(bf16[128,1024]{1,0:T(8,128)(2,1)S(1)} %get-tuple-element.149), channel_id=1, source_target_pairs={{0,2},{2,0},{4,6},{6,4},{8,10},{10,8},{12,14},{14,12},{16,18},{18,... | collective-permute-start | bytes 786440 | tf_op jit(solution)/shard_map/ppermute | solution.py:654
  455.2 23.7 %collective-permute-start.14 = (bf16[128,1024]{1,0:T(8,128)(2,1)S(1)}, bf16[128,1024]{1,0:T(8,128)(2,1)S(1)}, u32[]{:S(2)}, u32[]{:S(2)}) collective-permute-start(bf16[128,1024]{1,0:T(8,128)(2,1)S(1)} %get-tuple-element.151), channel_id=1, source_target_pairs={{0,8},{2,10},{4,12},{6,14},{8,0},{10,2},{12,4},{14,6},{16,24},{18,... | collective-permute-start | bytes 786440 | tf_op jit(solution)/shard_map/ppermute | solution.py:654
  456.6 22.2 %collective-permute-start.19 = (bf16[64,1024]{1,0:T(8,128)(2,1)S(1)}, bf16[64,1024]{1,0:T(8,128)(2,1)S(1)}, u32[]{:S(2)}, u32[]{:S(2)}) collective-permute-start(bf16[64,1024]{1,0:T(8,128)(2,1)S(1)} %constant_dynamic-slice_fusion.14), channel_id=1, source_target_pairs={{0,16},{2,18},{4,20},{6,22},{8,24},{10,26},{12,28},{14,30},{16,0},... | collective-permute-start | bytes 393224 | tf_op jit(solution)/shard_map/ppermute | solution.py:654
  459.0 19.8 %collective-permute-start.21 = (bf16[64,1024]{1,0:T(8,128)(2,1)S(1)}, bf16[64,1024]{1,0:T(8,128)(2,1)S(1)}, u32[]{:S(2)}, u32[]{:S(2)}) collective-permute-start(bf16[64,1024]{1,0:T(8,128)(2,1)S(1)} %constant_dynamic-slice_fusion.12), channel_id=1, source_target_pairs={{0,16},{2,18},{4,20},{6,22},{8,24},{10,26},{12,28},{14,30},{16,0},... | collective-permute-start | bytes 393224 | tf_op jit(solution)/shard_map/ppermute | solution.py:654
  460.0 144.9 %collective-permute-start.40 = (bf16[256,1024]{1,0:T(8,128)(2,1)}, bf16[256,1024]{1,0:T(8,128)(2,1)}, u32[]{:S(2)}, u32[]{:S(2)}) collective-permute-start(bf16[256,1024]{1,0:T(8,128)(2,1)} %constant_dynamic-slice_fusion.3), channel_id=1, source_target_pairs={{0,8},{2,10},{4,12},{6,14},{8,0},{10,2},{12,4},{14,6},{16,24},{18,... | collective-permute-start | bytes 1572872 | tf_op jit(solution)/shard_map/ppermute | solution.py:654
  480.6 22.9 %collective-permute-start.16 = (bf16[64,1024]{1,0:T(8,128)(2,1)S(1)}, bf16[64,1024]{1,0:T(8,128)(2,1)S(1)}, u32[]{:S(2)}, u32[]{:S(2)}) collective-permute-start(bf16[64,1024]{1,0:T(8,128)(2,1)S(1)} %get-tuple-element.153), channel_id=1, source_target_pairs={{0,16},{2,18},{4,20},{6,22},{8,24},{10,26},{12,28},{14,30},{16,0},... | collective-permute-start | bytes 393224 | tf_op jit(solution)/shard_map/ppermute | solution.py:654
  484.6 19.9 %collective-permute-start.17 = (bf16[64,1024]{1,0:T(8,128)(2,1)S(1)}, bf16[64,1024]{1,0:T(8,128)(2,1)S(1)}, u32[]{:S(2)}, u32[]{:S(2)}) collective-permute-start(bf16[64,1024]{1,0:T(8,128)(2,1)S(1)} %get-tuple-element.155), channel_id=1, source_target_pairs={{0,16},{2,18},{4,20},{6,22},{8,24},{10,26},{12,28},{14,30},{16,0},... | collective-permute-start | bytes 393224 | tf_op jit(solution)/shard_map/ppermute | solution.py:654
  606.2 5.7 collective-permute-start.41
  616.4 7.4 collective-permute-start.43
  618.6 18.7 %collective-permute-start.23 = (bf16[256,1664]{1,0:T(8,128)(2,1)S(1)}, bf16[256,1664]{1,0:T(8,128)(2,1)S(1)}, u32[]{:S(2)}, u32[]{:S(2)}) collective-permute-start(bf16[256,1664]{1,0:T(8,128)(2,1)S(1)} %constant_dynamic-slice_fusion.11), channel_id=1, source_target_pairs={{0,2},{2,0},{4,6},{6,4},{8,10},{10,8},{12,14},{14,12},{16,18},{18,... | collective-permute-start | bytes 2555912 | tf_op jit(solution)/shard_map/ppermute | solution.py:654
  623.9 4.9 collective-permute-start.44
  628.8 8.4 %collective-permute-start.45 = (bf16[64,1024]{1,0:T(8,128)(2,1)S(1)}, bf16[64,1024]{1,0:T(8,128)(2,1)S(1)}, u32[]{:S(2)}, u32[]{:S(2)}) collective-permute-start(bf16[64,1024]{1,0:T(8,128)(2,1)S(1)} %constant_dynamic-update-slice_fusion.16), channel_id=1, source_target_pairs={{0,4},{2,6},{4,0},{6,2},{8,12},{10,14},{12,8},{14,10},{16,20},{18,... | collective-permute-start | bytes 393224 | tf_op jit(solution)/shard_map/ppermute | solution.py:654
  629.6 16.4 %collective-permute-start.31 = (bf16[256,1664]{1,0:T(8,128)(2,1)S(1)}, bf16[256,1664]{1,0:T(8,128)(2,1)S(1)}, u32[]{:S(2)}, u32[]{:S(2)}) collective-permute-start(bf16[256,1664]{1,0:T(8,128)(2,1)S(1)} %constant_dynamic-slice_fusion.7), channel_id=1, source_target_pairs={{0,4},{2,6},{4,0},{6,2},{8,12},{10,14},{12,8},{14,10},{16,20},{18,... | collective-permute-start | bytes 2555912 | tf_op jit(solution)/shard_map/ppermute | solution.py:654
  630.4 50.5 %collective-permute-start.22 = (bf16[1024,1024]{1,0:T(8,128)(2,1)S(1)}, bf16[1024,1024]{1,0:T(8,128)(2,1)S(1)}, u32[]{:S(2)}, u32[]{:S(2)}) collective-permute-start(bf16[1024,1024]{1,0:T(8,128)(2,1)S(1)} %fusion.37), channel_id=1, source_target_pairs={{0,1},{1,0},{2,3},{3,2},{4,5},{5,4},{6,7},{7,6},{8,9},{9,8},{10,11... | collective-permute-start | bytes 6291464 | tf_op jit(solution)/shard_map/ppermute | solution.py:639
  637.2 104.0 %collective-permute-start.46 = (bf16[128,1024]{1,0:T(8,128)(2,1)S(1)}, bf16[128,1024]{1,0:T(8,128)(2,1)S(1)}, u32[]{:S(2)}, u32[]{:S(2)}) collective-permute-start(bf16[128,1024]{1,0:T(8,128)(2,1)S(1)} %constant_dynamic-update-slice_fusion.14), channel_id=1, source_target_pairs={{0,2},{2,0},{4,6},{6,4},{8,10},{10,8},{12,14},{14,12},{16,18},{18,... | collective-permute-start | bytes 786440 | tf_op jit(solution)/shard_map/ppermute | solution.py:654
  637.6 17.5 %collective-permute-start.24 = (bf16[128,1664]{1,0:T(8,128)(2,1)S(1)}, bf16[128,1664]{1,0:T(8,128)(2,1)S(1)}, u32[]{:S(2)}, u32[]{:S(2)}) collective-permute-start(bf16[128,1664]{1,0:T(8,128)(2,1)S(1)} %constant_dynamic-slice_fusion.10), channel_id=1, source_target_pairs={{0,4},{2,6},{4,0},{6,2},{8,12},{10,14},{12,8},{14,10},{16,20},{18,... | collective-permute-start | bytes 1277960 | tf_op jit(solution)/shard_map/ppermute | solution.py:654
  646.2 9.1 %collective-permute-start.32 = (bf16[128,1664]{1,0:T(8,128)(2,1)S(1)}, bf16[128,1664]{1,0:T(8,128)(2,1)S(1)}, u32[]{:S(2)}, u32[]{:S(2)}) collective-permute-start(bf16[128,1664]{1,0:T(8,128)(2,1)S(1)} %constant_dynamic-slice_fusion.6), channel_id=1, source_target_pairs={{0,8},{2,10},{4,12},{6,14},{8,0},{10,2},{12,4},{14,6},{16,24},{18,... | collective-permute-start | bytes 1277960 | tf_op jit(solution)/shard_map/ppermute | solution.py:654
  655.2 5.1 collective-permute-start.25
  655.5 7.3 collective-permute-start.33
  660.4 5.5 collective-permute-start.26
  662.8 5.7 collective-permute-start.34
  665.9 5.6 collective-permute-start.27
  668.6 5.7 collective-permute-start.35
  671.5 7.4 collective-permute-start.28
  674.3 6.2 collective-permute-start.36
  678.9 7.4 collective-permute-start.29
  680.6 11.0 %collective-permute-start.37 = (bf16[128,1664]{1,0:T(8,128)(2,1)S(1)}, bf16[128,1664]{1,0:T(8,128)(2,1)S(1)}, u32[]{:S(2)}, u32[]{:S(2)}) collective-permute-start(bf16[128,1664]{1,0:T(8,128)(2,1)S(1)} %constant_dynamic-update-slice_fusion.22), channel_id=1, source_target_pairs={{0,8},{2,10},{4,12},{6,14},{8,0},{10,2},{12,4},{14,6},{16,24},{18,... | collective-permute-start | bytes 1277960 | tf_op jit(solution)/shard_map/ppermute | solution.py:654
  686.4 14.3 %collective-permute-start.30 = (bf16[256,1664]{1,0:T(8,128)(2,1)S(1)}, bf16[256,1664]{1,0:T(8,128)(2,1)S(1)}, u32[]{:S(2)}, u32[]{:S(2)}) collective-permute-start(bf16[256,1664]{1,0:T(8,128)(2,1)S(1)} %constant_dynamic-update-slice_fusion.28), channel_id=1, source_target_pairs={{0,2},{2,0},{4,6},{6,4},{8,10},{10,8},{12,14},{14,12},{16,18},{18,... | collective-permute-start | bytes 2555912 | tf_op jit(solution)/shard_map/ppermute | solution.py:654
  691.6 16.2 %collective-permute-start.38 = (bf16[256,1664]{1,0:T(8,128)(2,1)S(1)}, bf16[256,1664]{1,0:T(8,128)(2,1)S(1)}, u32[]{:S(2)}, u32[]{:S(2)}) collective-permute-start(bf16[256,1664]{1,0:T(8,128)(2,1)S(1)} %constant_dynamic-update-slice_fusion.20), channel_id=1, source_target_pairs={{0,4},{2,6},{4,0},{6,2},{8,12},{10,14},{12,8},{14,10},{16,20},{18,... | collective-permute-start | bytes 2555912 | tf_op jit(solution)/shard_map/ppermute | solution.py:654
  708.0 35.1 %collective-permute-start.39 = (f32[2,1024]{0,1:T(8,128)S(1)}, f32[2,1024]{0,1:T(8,128)S(1)}, u32[]{:S(2)}, u32[]{:S(2)}) collective-permute-start(f32[2,1024]{0,1:T(8,128)S(1)} %fusion.53), channel_id=1, source_target_pairs={{1,0},{0,1},{3,2},{2,3},{5,4},{4,5},{7,6},{6,7},{9,8},{8,9},{11,10... | collective-permute-start | bytes 24584 | tf_op jit(solution)/shard_map/ppermute | solution.py:616
  741.2 13.7 %collective-permute-start.47 = (bf16[256,1024]{1,0:T(8,128)(2,1)S(1)}, bf16[256,1024]{1,0:T(8,128)(2,1)}, u32[]{:S(2)}, u32[]{:S(2)}) collective-permute-start(bf16[256,1024]{1,0:T(8,128)(2,1)S(1)} %constant_dynamic-update-slice_fusion.12), channel_id=1, source_target_pairs={{0,8},{2,10},{4,12},{6,14},{8,0},{10,2},{12,4},{14,6},{16,24},{18,... | collective-permute-start | bytes 1572872 | tf_op jit(solution)/shard_map/ppermute | solution.py:654
  (60 other events, 1032.5 us)
Sparse Core Ops, SparseCore 0:
  14.3 16.2 all-gather.3
  506.4 116.2 all-gather.5

commit v7 on v6

--- a/solution.py
+++ b/solution.py
@@ -279,86 +279,6 @@
     )
 
 
-def recall_back_kernel(
-    picks, scale, gate_ref, found_ref, query_ref, delta_ref, query_delta_ref, sums_ref
-):
-    tokens = query_ref.shape[0]
-    wide = 8 * picks * 2
-    own = own_columns(picks)
-    gate = gate_ref[0]
-    groups = range(tokens // 8)
-    both = []
-    for g in groups:
-        rows = jnp.concatenate(
-            [query_ref[pl.ds(g * 8, 8), :], delta_ref[pl.ds(g * 8, 8), :]], 0
-        )
-        both.append(dot_inner(rows, found_ref[pl.ds(g * wide, wide), :]))
-    gained = jnp.zeros((8, 1), full_type)
-    for g in groups:
-        masked = jnp.where(own, both[g][:8] * (scale * log2_e), -jnp.inf)
-        exponent = jnp.exp2(masked - jnp.max(masked, 1, keepdims=True))
-        weights = exponent / jnp.sum(exponent, 1, keepdims=True)
-        reads = pltpu.roll(both[g][8:], wide - 1, 1)
-        expected = jnp.sum(weights * reads, 1, keepdims=True)
-        gained = gained + expected
-        score_delta = (weights * (reads - expected)).astype(low_type)
-        query_delta_ref[pl.ds(g * 8, 8), :] = dot_rows(
-            score_delta, found_ref[pl.ds(g * wide, wide), :]
-        ) * (scale * gate)
-
-    @pl.when(pl.program_id(0) == 0)
-    def clear():
-        sums_ref[...] = jnp.zeros(sums_ref.shape, full_type)
-
-    sums_ref[0] += jnp.broadcast_to(gained, (8, 128))
-
-
-def recall_back(
-    found, queries, mixed_delta, gates, head, carried, after, kept, heads, picks, scale
-):
-    tokens = queries.shape[0]
-    width = mixed_delta.shape[1] // heads
-    step = min(512, tokens)
-    blocks = tokens // step
-    rows_spec = pl.BlockSpec((step, width), lambda i: (i, head))
-    anywhere = pl.BlockSpec(memory_space=pl.ANY)
-    extra = [kept] if kept is not None else []
-    first = 4 + len(extra)
-
-    def kernel(gate_ref, found_ref, query_ref, delta_ref, *rest):
-        query_delta_ref, sums_ref = rest[len(extra) + len(carried) + len(after) :][:2]
-        recall_back_kernel(
-            picks, scale, gate_ref, found_ref, query_ref, delta_ref, query_delta_ref, sums_ref
-        )
-
-    out = pl.pallas_call(
-        kernel,
-        grid=(blocks,),
-        in_specs=[
-            pl.BlockSpec(memory_space=pltpu.SMEM),
-            pl.BlockSpec((step * picks * 2, width), lambda i: (head * blocks + i, 0)),
-            rows_spec,
-            rows_spec,
-        ]
-        + [anywhere] * (len(extra) + len(carried) + len(after)),
-        out_specs=[rows_spec, pl.BlockSpec((1, 8, 128), lambda i: (0, 0, 0))]
-        + [anywhere] * len(carried),
-        out_shape=[
-            jax.ShapeDtypeStruct((tokens, heads * width), full_type),
-            jax.ShapeDtypeStruct((1, 8, 128), full_type),
-        ]
-        + [jax.ShapeDtypeStruct(part.shape, part.dtype) for part in carried],
-        input_output_aliases=({4: 0} if extra else {})
-        | {first + i: 2 + i for i in range(len(carried))},
-        compiler_params=pltpu.CompilerParams(vmem_limit_bytes=vmem_most),
-        cost_estimate=pl.CostEstimate(
-            flops=0, bytes_accessed=tokens * picks * width * 8, transcendentals=0
-        ),
-        name="recall_back",
-    )(gates[head : head + 1], found, queries, mixed_delta, *extra, *carried, *after)
-    return out[0], out[1], list(out[2:])
-
-
 def band(column_ref):
     wide = jnp.broadcast_to(column_ref[0], (tile, ring))
     return pltpu.roll(wide, 0, 1, stride=1, stride_axis=0)[:, :span]
@@ -437,84 +357,183 @@
     )(gates, far, columns, projected, projected, projected, query_mask, key_mask, early, late)
 
 
-def local_back_kernel(
-    scale, gate_ref, far_ref, column_ref, query_ref, key_ref, value_ref, query_mask_ref,
-    key_mask_ref, delta_ref, recall_delta_ref, query_delta_ref, key_delta_ref, value_delta_ref,
-    diagonal_ref, sums_ref, bias_ref, near_ref, key_sum_ref, value_sum_ref,
+def recall_back_rows(
+    picks, scale, own, gate, query_ref, delta_ref, at, rows_ref, read_ref, gains, tokens
 ):
-    head = pl.program_id(0)
-    last = pl.program_id(1) == pl.num_programs(1) - 1
-
-    @pl.when(pl.program_id(1) == 0)
-    def make_band():
+    wide = 8 * picks * 2
+    flight = 8
+    groups = tokens // 8
+    both = {}
+    for first in range(-flight, groups, flight):
+        for g in range(first + flight, min(first + 2 * flight, groups)):
+            where = pl.ds(at + g * 8, 8)
+            pair = jnp.concatenate([query_ref[where, :], delta_ref[where, :]], 0)
+            both[g] = dot_inner(pair, rows_ref[pl.ds(g * wide, wide), :])
+            yield
+        for g in range(max(first, 0), first + flight if first >= 0 else 0):
+            pair = both.pop(g)
+            masked = jnp.where(own, pair[:8] * (scale * log2_e), -jnp.inf)
+            exponent = jnp.exp2(masked - jnp.max(masked, 1, keepdims=True))
+            weights = exponent / jnp.sum(exponent, 1, keepdims=True)
+            reads = pltpu.roll(pair[8:], wide - 1, 1)
+            expected = jnp.sum(weights * reads, 1, keepdims=True)
+            gains.append(expected)
+            score_delta = (weights * (reads - expected)).astype(low_type)
+            rows = rows_ref[pl.ds(g * wide, wide), :]
+            read_ref[pl.ds(g * 8, 8), :] = dot_rows(score_delta, rows) * (scale * gate)
+            yield
+
+
+def local_back_tile(
+    t, scale, gate, far_ref, query_ref, keys, turned, value_ref, query_mask_ref, delta_ref,
+    bias_ref, near_ref, key_sum_ref, value_sum_ref, gains, far_sums, result,
+):
+    count = len(keys)
+    at = [pl.ds(j * tile, tile) for j in range(count)]
+    rows = jnp.concatenate([query_ref[at[t], :], query_mask_ref[0, at[t], :]], 1)
+    delta = ((1.0 - gate) * delta_ref[at[t], :].astype(full_type)).astype(low_type)
+    parts = []
+    for j in range(count):
+        step = j - t
+        if step < -1:
+            bias = far_ref[0, 0]
+        elif step > 1:
+            bias = far_ref[0, 1]
+        else:
+            bias = bias_ref[:, pl.ds((1 - step) * tile, tile)]
+        parts.append(dot_inner(keys[j], rows) * (scale * log2_e) + bias)
+        yield
+    top = jnp.max(functools.reduce(jnp.maximum, parts), 0, keepdims=True)
+    yield
+    for j in range(count):
+        parts[j] = jnp.exp2(parts[j] - top)
+        yield
+    inverse = 1.0 / jnp.sum(functools.reduce(jnp.add, parts), 0, keepdims=True)
+    moves = []
+    products = []
+    for j in range(count):
+        parts[j] = parts[j] * inverse
+        moves.append(dot_inner(value_ref[at[j], :], delta))
+        products.append(parts[j] * moves[j])
+        yield
+    expected = jnp.sum(functools.reduce(jnp.add, products), 0, keepdims=True)
+    gains.append(expected)
+    query_sum = None
+    for j in range(count):
+        step = j - t
+        score_delta = parts[j] * (moves[j] - expected)
+        if abs(step) > 1:
+            side = 0 if step < 0 else 1
+            far_sums[side].append(jnp.sum(score_delta.reshape(tile // 8, 8, tile), 0))
+        else:
+            near_ref[:, pl.ds((1 - step) * tile, tile)] += score_delta
+        yield
+        low_delta = score_delta.astype(low_type)
+        value_part = dot_rows(parts[j].astype(low_type), delta)
+        yield
+        key_part = dot_rows(low_delta, query_ref[at[t], :])
+        yield
+        query_part = dot_rows(turned[j], low_delta)
+        if t == 0:
+            value_sum_ref[at[j], :] = value_part
+            key_sum_ref[at[j], :] = key_part
+        else:
+            value_sum_ref[at[j], :] += value_part
+            key_sum_ref[at[j], :] += key_part
+        query_sum = query_part if j == 0 else query_sum + query_part
+        yield
+    result.append(query_sum.T * scale)
+    yield
+
+
+def run_together(first, second):
+    first, second = list_steps(first), list_steps(second)
+    first_total, second_total = next(first), next(second)
+    done = 0
+    for number in range(second_total):
+        until = (number + 1) * first_total // second_total
+        while done < until:
+            next(first)
+            done += 1
+        next(second)
+
+
+def list_steps(counted):
+    count, steps = counted
+    yield count
+    yield from steps
+
+
+def back_kernel(
+    picks, scale, head, gate_ref, far_ref, column_ref, query_ref, key_ref, value_ref,
+    query_mask_ref, key_mask_ref, delta_ref, found_hbm, query_delta_ref, key_delta_ref,
+    value_delta_ref, diagonal_ref, sums_ref, bias_ref, near_ref, key_sum_ref, value_sum_ref,
+    read_ref, rows_ref, rows_sems,
+):
+    sequence = pl.program_id(0)
+    sequences = pl.num_programs(0)
+    count = query_ref.shape[0] // tile
+    block = rows_ref.shape[1]
+    own = own_columns(picks)
+    gate = gate_ref[0]
+
+    def rows_copy(number, slot):
+        start = (head * sequences * count + number) * block
+        return pltpu.make_async_copy(
+            found_hbm.at[pl.ds(pl.multiple_of(start, block), block)],
+            rows_ref.at[slot],
+            rows_sems.at[slot],
+        )
+
+    @pl.when(sequence == 0)
+    def begin():
+        for slot in range(2):
+            rows_copy(slot, slot).start()
         bias_ref[...] = band(column_ref)
         near_ref[...] = jnp.zeros(near_ref.shape, full_type)
         sums_ref[...] = jnp.zeros(sums_ref.shape, full_type)
 
-    gate = gate_ref[head]
-    count = query_ref.shape[0] // tile
     at = [pl.ds(t * tile, tile) for t in range(count)]
     keys = [jnp.concatenate([key_ref[a, :], key_mask_ref[0, a, :]], 1) for a in at]
     turned = [key_ref[a, :].astype(full_type).T.astype(low_type) for a in at]
-    gained = jnp.zeros((1, tile), full_type)
-    far_sums = [jnp.zeros((8, tile), full_type) for side in range(2)]
+    gains, recall_gains, far_sums = [], [], [[], []]
     for t in range(count):
-        rows = jnp.concatenate([query_ref[at[t], :], query_mask_ref[0, at[t], :]], 1)
-        delta = ((1.0 - gate) * delta_ref[at[t], :].astype(full_type)).astype(low_type)
-        parts = []
-        for j in range(count):
-            step = j - t
-            if step < -1:
-                bias = far_ref[head, 0]
-            elif step > 1:
-                bias = far_ref[head, 1]
-            else:
-                bias = bias_ref[:, pl.ds((1 - step) * tile, tile)]
-            parts.append(dot_inner(keys[j], rows) * (scale * log2_e) + bias)
-        top = jnp.max(functools.reduce(jnp.maximum, parts), 0, keepdims=True)
-        parts = [jnp.exp2(part - top) for part in parts]
-        total = jnp.sum(functools.reduce(jnp.add, parts), 0, keepdims=True)
-        inverse = 1.0 / total
-        parts = [part * inverse for part in parts]
-        moves = [dot_inner(value_ref[at[j], :], delta) for j in range(count)]
-        expected = jnp.sum(
-            functools.reduce(jnp.add, [parts[j] * moves[j] for j in range(count)]),
-            0,
-            keepdims=True,
+        slot = t % 2
+        number = sequence * count + t
+        rows_copy(number, slot).wait()
+        result = []
+        run_together(
+            (
+                2 * (tile // 8),
+                recall_back_rows(
+                    picks, scale, own, gate, query_ref, delta_ref, t * tile, rows_ref.at[slot],
+                    read_ref, recall_gains, tile,
+                ),
+            ),
+            (
+                7 * count + 2,
+                local_back_tile(
+                    t, scale, gate, far_ref, query_ref, keys, turned, value_ref, query_mask_ref,
+                    delta_ref, bias_ref, near_ref, key_sum_ref, value_sum_ref, gains, far_sums,
+                    result,
+                ),
+            ),
         )
-        gained = gained + expected
-        query_sum = None
-        for j in range(count):
-            step = j - t
-            score_delta = parts[j] * (moves[j] - expected)
-            if abs(step) > 1:
-                side = 0 if step < 0 else 1
-                far_sums[side] = far_sums[side] + jnp.sum(
-                    score_delta.reshape(tile // 8, 8, tile), 0
-                )
-            else:
-                near_ref[:, pl.ds((1 - step) * tile, tile)] += score_delta
-            low_delta = score_delta.astype(low_type)
-            value_part = dot_rows(parts[j].astype(low_type), delta)
-            key_part = dot_rows(low_delta, query_ref[at[t], :])
-            query_part = dot_rows(turned[j], low_delta)
-            if t == 0:
-                value_sum_ref[at[j], :] = value_part
-                key_sum_ref[at[j], :] = key_part
-            else:
-                value_sum_ref[at[j], :] += value_part
-                key_sum_ref[at[j], :] += key_part
-            query_sum = query_part if j == 0 else query_sum + query_part
-        query_delta_ref[at[t], :] = (
-            query_sum.T * scale + recall_delta_ref[at[t], :]
-        ).astype(low_type)
+        query_delta_ref[at[t], :] = (result[0] + read_ref[...]).astype(low_type)
+
+        @pl.when(number + 2 < sequences * count)
+        def ahead():
+            rows_copy(number + 2, slot).start()
+
     key_delta_ref[...] = (key_sum_ref[...] * scale).astype(low_type)
     value_delta_ref[...] = value_sum_ref[...].astype(low_type)
-    sums_ref[0, 0:1] += gained
-    sums_ref[0, 8:16] += far_sums[0]
-    sums_ref[0, 16:24] += far_sums[1]
-
-    @pl.when(last)
+    sums_ref[0, 0:1] += functools.reduce(jnp.add, gains)
+    for side in range(2):
+        if far_sums[side]:
+            sums_ref[0, 8 + 8 * side : 16 + 8 * side] += functools.reduce(jnp.add, far_sums[side])
+    sums_ref[0, 24:32] += jnp.broadcast_to(functools.reduce(jnp.add, recall_gains), (8, tile))
+
+    @pl.when(sequence == sequences - 1)
     def fold_diagonals():
         total = jnp.zeros((8, ring), full_type)
         for g in range(tile // 8):
@@ -528,58 +547,58 @@
         diagonal_ref[0] = total
 
 
-def local_back(
-    projected, query_mask, key_mask, mixed_delta, recall_delta, columns, far, gates, seq_len, scale,
-    heads_now, carried, kept, after,
+def back_head(
+    projected, query_mask, key_mask, mixed_delta, found, columns, far, gates, seq_len, picks, scale,
+    head, kept, carried, after,
 ):
     tokens = mixed_delta.shape[0]
     heads = gates.shape[0]
     width = mixed_delta.shape[1] // heads
-    start, count = heads_now
     anywhere = pl.BlockSpec(memory_space=pl.ANY)
-    chosen = slice(start, start + count)
+    chosen = slice(head, head + 1)
+    extra = len(kept) + len(carried) + len(after)
 
     def rows_of(shift):
-        return pl.BlockSpec((seq_len, width), lambda h, s: (s, h + start + shift * heads))
+        return pl.BlockSpec((seq_len, width), lambda s: (s, head + shift * heads))
 
     def kernel(*refs):
-        inputs, rest = refs[:10], refs[10 + len(kept) + len(carried) + len(after) :]
-        local_back_kernel(scale, *inputs, *rest[:5], *rest[5 + len(carried) :])
-
-    mask_spec = pl.BlockSpec((1, seq_len, 128), lambda h, s: (s, 0, 0))
+        outs = refs[10 + extra :]
+        back_kernel(picks, scale, head, *refs[:10], *outs[:5], *outs[5 + len(carried) :])
+
+    mask_spec = pl.BlockSpec((1, seq_len, 128), lambda s: (s, 0, 0))
     smem = pl.BlockSpec(memory_space=pltpu.SMEM)
     rows_shape = jax.ShapeDtypeStruct((tokens, heads * width), low_type)
     first = 10 + len(kept)
     out = pl.pallas_call(
         kernel,
-        grid=(count, tokens // seq_len),
+        grid=(tokens // seq_len,),
         in_specs=[
             smem,
             smem,
-            pl.BlockSpec((1, 1, ring), lambda h, s: (h, 0, 0)),
+            pl.BlockSpec((1, 1, ring), lambda s: (0, 0, 0)),
             rows_of(0),
             rows_of(1),
             rows_of(2),
             mask_spec,
             mask_spec,
             rows_of(0),
-            rows_of(0),
+            anywhere,
         ]
-        + [anywhere] * (len(kept) + len(carried) + len(after)),
+        + [anywhere] * extra,
         out_specs=[
             rows_of(0),
             rows_of(0),
             rows_of(0),
-            pl.BlockSpec((1, 8, ring), lambda h, s: (h, 0, 0)),
-            pl.BlockSpec((1, 24, tile), lambda h, s: (h, 0, 0)),
+            pl.BlockSpec((1, 8, ring), lambda s: (0, 0, 0)),
+            pl.BlockSpec((1, 32, tile), lambda s: (0, 0, 0)),
         ]
         + [anywhere] * len(carried),
         out_shape=[
             rows_shape,
             rows_shape,
             rows_shape,
-            jax.ShapeDtypeStruct((count, 8, ring), full_type),
-            jax.ShapeDtypeStruct((count, 24, tile), full_type),
+            jax.ShapeDtypeStruct((1, 8, ring), full_type),
+            jax.ShapeDtypeStruct((1, 32, tile), full_type),
         ]
         + [jax.ShapeDtypeStruct(part.shape, part.dtype) for part in carried],
         input_output_aliases={10 + i: i for i in range(len(kept))}
@@ -589,15 +608,18 @@
             pltpu.VMEM((tile, span), full_type),
             pltpu.VMEM((seq_len, width), full_type),
             pltpu.VMEM((seq_len, width), full_type),
+            pltpu.VMEM((tile, width), full_type),
+            pltpu.VMEM((2, tile * picks * 2, width), low_type),
+            pltpu.SemaphoreType.DMA((2,)),
         ],
         compiler_params=pltpu.CompilerParams(vmem_limit_bytes=vmem_most),
         cost_estimate=pl.CostEstimate(
-            flops=0, bytes_accessed=count * tokens * seq_len * 40, transcendentals=0
+            flops=0, bytes_accessed=tokens * picks * width * 8, transcendentals=0
         ),
-        name="local_back",
+        name="back_head",
     )(
         gates[chosen], far[chosen], columns[chosen], projected, projected, projected, query_mask,
-        key_mask, mixed_delta, recall_delta, *kept, *carried, *after,
+        key_mask, mixed_delta, found, *kept, *carried, *after,
     )
     return list(out[:3]), out[3], out[4], list(out[5:])
 
@@ -683,7 +705,7 @@
     for step in reversed(range(len(orders[0]))):
         got = [swap_over(part, order[step]) for part, order in zip(parts, orders)]
         if step == 1:
-            got[2], beside = lax.optimization_barrier((got[2], beside))
+            got, beside = lax.optimization_barrier((got, beside))
         wider = []
         for part, other, order in zip(parts, got, orders):
             rows = part.shape[0]
@@ -835,14 +857,16 @@
     ).astype(low_type)
 
     shards, packed = [], []
-    recall_delta = None
-    recall_sums = []
+    deltas = []
+    diagonals = []
+    local_sums = []
     for head in range(head_count):
-        recall_delta, head_sums, kept = recall_back(
-            found, projected, mixed_delta, gates, head, kept, packed, recall_delta, head_count,
-            picks, scale,
+        deltas, diagonal_now, sums_now, kept = back_head(
+            projected, query_mask, key_mask, mixed_delta, found, behind_columns, far, gates,
+            seq_len, picks, scale, head, deltas, kept, packed,
         )
-        recall_sums.append(head_sums)
+        diagonals.append(diagonal_now)
+        local_sums.append(sums_now)
         if taken < steps - 1:
             taken += 1
             kept, sent = halve_step(add_low(kept, sent), orders[:2], taken)
@@ -861,22 +885,10 @@
     )
     hidden_sum = jnp.concatenate([hidden_low_sum, hidden_high_sum], 1)
     return_sum = jnp.concatenate([return_low_sum, return_high_sum], 0)
-    recall_sums = jnp.concatenate(recall_sums, 0)
-    half_heads = max(1, head_count // 2)
-    deltas = []
-    diagonals = []
-    local_sums = []
-    for start in range(0, head_count, half_heads):
-        deltas, diagonal_now, sums_now, unused = local_back(
-            projected, query_mask, key_mask, mixed_delta, recall_delta, behind_columns, far, gates,
-            seq_len, scale, (start, half_heads), [], deltas, packed,
-        )
-        diagonals.append(diagonal_now)
-        local_sums.append(sums_now)
     query_delta, key_delta, value_delta = deltas
     diagonals = jnp.concatenate(diagonals, 0)
     local_sums = jnp.concatenate(local_sums, 0)
-    recall_gain = jnp.sum(recall_sums[:, :, 0], 1)
+    recall_gain = jnp.sum(local_sums[:, 24:32, 0], 1)
     local_gain = jnp.sum(local_sums[:, 0], 1)
     gate_part = gates * (1.0 - gates) * recall_gain - gates * local_gain
     diagonal_sums = jnp.sum(diagonals, 1)

time: 772 us -> 764 us (0.990)
  waiting for transfers between devices: 89.9 us -> 81.4 us
  Pallas kernels: 357 us -> 349 us
    ppermute x40, waiting for transfers between devices: 85.9 us -> 77.3 us  [swap_over(): lax.ppermute(rows, 'dp', [(i, i ^ 1 << bit) for i in range(lax.axis_size(...]
    pallas_call x6 -> x4, Pallas kernels: 120 us -> 112 us  [back_head(): pl.pallas_call(kernel, grid=(tokens // seq_len,), in_specs=[smem, smem, p...]
  transfers between devices with their start and end apart: 50 -> 50, of which waited for: 19 -> 19; matrix products, arithmetic and copies ran while one was open for 18% -> 19% of each run, Pallas kernels for 19% -> 18%
where the time goes in v7:
time: 764 us; the launch traced here: 757 us
  Pallas kernels  349 us (46%)
  matrix products  141 us (18%)
  waiting for transfers between devices  81.4 us (11%)
  starting transfers between devices  72.4 us (9%)
  local copies, waits for them, and re-layouts  53.8 us (7%)
  other arithmetic  43.1 us (6%)
  between operations  16.1 us (2%)
    pallas_call x1, Pallas kernels, gather_found(): pl.pallas_call(functools.partial(gather_kernel, picks, scale), grid=(step...  189 us
    pallas_call x4, Pallas kernels, back_head(): pl.pallas_call(kernel, grid=(tokens // seq_len,), in_specs=[smem, smem, p...  112 us
    ppermute x40, waiting for transfers between devices, swap_over(): lax.ppermute(rows, 'dp', [(i, i ^ 1 << bit) for i in range(lax.axis_size(...  77.3 us
    dot_general x6, matrix products, dot_rows(): return jnp.dot(left, right, preferred_element_type=full_type)  59.4 us
    ppermute x40, starting transfers between devices, swap_over(): lax.ppermute(rows, 'dp', [(i, i ^ 1 << bit) for i in range(lax.axis_size(...  50.7 us
    dot_general x6, matrix products, dot_inner(): lax.dot_general(left, right, (((1,), (1,)), ((), ())), preferred_element_...  42.6 us
    dot_general x5, matrix products, dot_outer(): lax.dot_general(left, right, (((0,), (0,)), ((), ())), preferred_element_...  37.9 us
    pallas_call x1, Pallas kernels, interleave(): pl.pallas_call(interleave_kernel, grid=(heads, rows // step), in_specs=[s...  26 us
  transfers between devices with their start and end apart: 50, of which 19 were waited for; matrix products, arithmetic and copies ran while one was open for 19% of the time, Pallas kernels for 18%

profile of v7, /device:TPU:1, one launch (start us, length us, event | category | flops | bytes accessed | tf_op | source)
XLA Modules:
  0.0 756.8 jit_solution(9514700128369359340)
XLA Ops:
  10.6 3.5 fusion.6
  14.4 2.7 copy.62
  17.1 4.2 reshape.189.index_hbm
  28.4 26.0 %interleave.1 = bf16[131072,128]{1,0:T(8,128)(2,1)} custom-call(bf16[4,16384,128]{2,1,0:T(8,128)(2,1)} %key_ref.1, bf16[4,16384,128]{2,1,0:T(8,128)(2,1)} %value_ref.1), custom_call_target="tpu_custom_call" | custom-call | flops 8589934592 | bytes 67108864 | tf_op jit(solution)/shard_map/interleave/pallas_call | solution.py:83
  54.4 11.3 %convolution_convert_fusion.now_ref.before_ref.query_ref.key_ref.value_ref.refs_3_.refs_4_.refs_5_ = bf16[2048,1536]{1,0:T(8,128)(2,1)} fusion(bf16[2048,1024]{1,0:T(8,128)(2,1)} %all-gather.4.cloned.1.call-done, bf16[1024,1536]{1,0:T(8,128)(2,1)} %copy-done.21), kind=kOutput, calls=%fused_computation.10 | convolution fusion | flops 6445596672 | bytes 13631488 | tf_op jit(solution)/shard_map/dot_general | solution.py:45
  65.7 189.5 %gather_found.1 = (bf16[262144,2,128]{2,1,0:T(2,128)(2,1)}, f32[4096,128]{1,0:T(8,128)}, f32[4096,128]{1,0:T(8,128)}) custom-call(s32[64,32,128]{2,1,0:T(8,128)} %reshape.189.index_hbm, bf16[65536,2,128]{2,1,0:T(2,128)(2,1)} %bitcast.60, bf16[2048,1536]{1,0:T(8,128)(2,1)} %convolution_convert_fusion.now_ref.before_ref.query_ref.key_ref.value_ref.refs_3_.refs_4_.refs_5_, ...), custom_call_target="tpu_custom_call" | custom-call | bytes 536870912 | tf_op jit(solution)/shard_map/gather_found/pallas_call | solution.py:243
  255.1 21.4 %local_read.1 = bf16[2048,512]{1,0:T(8,128)(2,1)} custom-call(f32[4]{0:T(128)} %add_divide_fusion.gate_ref, f32[4,2]{1,0:T(4,128)} %pad_maximum_fusion.7.far_ref, f32[4,1,1024]{2,1,0:T(1,128)} %broadcast_in_dim.33.column_ref, bf16[2048,1536]{1,0:T(8,128)(2,1)} %convolution_convert_fusion.now_ref.before_ref.query_ref.key_ref.value_ref.refs_3_.refs_4_.refs_5_, ...), custom_call_target="tpu_custom_call" | custom-call | bytes 167772160 | tf_op jit(solution)/shard_map/local_read/pallas_call | solution.py:334
  276.6 4.0 convolution_convert_fusion.3
  281.1 4.0 collective-permute-done
  285.1 3.5 multiply_reduce_fusion.3
  296.8 20.4 %add_convert_fusion = (bf16[2048,2048]{1,0:T(8,128)(2,1)}, bf16[2048,2048]{1,0:T(8,128)(2,1)}) fusion(bf16[1024,2048]{1,0:T(8,128)(2,1)S(1)} %copy-done.45, bf16[1024,1024]{1,0:T(8,128)(2,1)} %collective-permute-done.1, bf16[1024,1024]{1,0:T(8,128)(2,1)S(1)} %multiply_convert_fusion.2), kind=kOutput, calls=%fused_computation.1 | convolution fusion | flops 8673820672 | bytes 25165824 | tf_op jit(solution)/shard_map/dot_general | solution.py:45
  317.3 11.7 %convolution_convert_fusion.1 = bf16[2048,1024]{1,0:T(8,128)(2,1)S(1)} fusion(bf16[2048,2048]{1,0:T(8,128)(2,1)} %get-tuple-element.119, bf16[2048,1024]{1,0:T(8,128)(2,1)S(1)} %constant_dynamic-update-slice_fusion.3), kind=kOutput, calls=%fused_computation.45 | convolution fusion | flops 8592031744 | bytes 16777216 | tf_op jit(solution)/shard_map/dot_general | solution.py:49
  329.4 14.1 %multiply_convert_fusion = bf16[2048,2048]{1,0:T(8,128)(2,1)} fusion(bf16[2048,2048]{1,0:T(8,128)(2,1)} %get-tuple-element.118, bf16[2048,1024]{1,0:T(8,128)(2,1)S(1)} %constant_dynamic-update-slice_fusion.3, bf16[2048,1024]{1,0:T(8,128)(2,1)} %param.30), kind=kOutput, calls=%fused_computation | convolution fusion | flops 8602517504 | bytes 25165824 | tf_op jit(solution)/shard_map/dot_general | solution.py:55
  343.6 7.2 fusion.28
  350.7 7.4 fusion.34
  360.1 7.5 fusion.31
  368.9 2.7 collective-permute-start.6
  372.9 8.1 %fusion.25 = bf16[1024,1024]{1,0:T(8,128)(2,1)} fusion(bf16[2048,1024]{1,0:T(8,128)(2,1)S(1)} %copy-done.46, bf16[2048,2048]{1,0:T(8,128)(2,1)} %get-tuple-element.119), kind=kOutput, calls=%fused_computation.56 | convolution fusion | flops 4296015872 | bytes 10485760 | tf_op jit(solution)/shard_map/dot_general | solution.py:45
  382.0 13.1 %collective-permute-done.6 = bf16[512,1024]{1,0:T(8,128)(2,1)S(1)} collective-permute-done((bf16[512,1024]{1,0:T(8,128)(2,1)S(1)}, bf16[512,1024]{1,0:T(8,128)(2,1)S(1)}, u32[]{:S(2)}, u32[]{:S(2)}) %collective-permute-start.6) | collective-permute-done | bytes 1048608 | tf_op jit(solution)/shard_map/ppermute | solution.py:676
  399.2 10.0 %multiply_reduce_fusion.1 = (bf16[1024]{0:T(1024)(128)(2,1)S(1)}, f32[1024]{0:T(1024)S(1)}, f32[1024,1024]{1,0:T(8,128)}) fusion(f32[1024,1024]{1,0:T(8,128)S(1)} %copy-done.7, f32[1024]{0:T(1024)S(1)} %fusion.88, bf16[1024,1024]{1,0:T(8,128)(2,1)S(1)} %collective-permute-done.4, f32[1024]{0:T(1024)S(1)} %copy-done.39, ...), kind=kOutput, calls=%fused_computation.38 | convolution fusion | flops 4303353856 | bytes 18888704 | tf_op jit(solution)/shard_map/dot_general | solution.py:55
  409.2 12.2 %fusion.97 = (bf16[1024,1024]{1,0:T(8,128)(2,1)}, f32[1024,1024]{1,0:T(8,128)}, bf16[1024,1024]{1,0:T(8,128)(2,1)}) fusion(f32[1024,1024]{1,0:T(8,128)S(1)} %copy-done.7, f32[1024]{0:T(1024)S(1)} %multiply_multiply_fusion.1, f32[1024]{0:T(1024)S(1)} %fusion.88, f32[1024]{0:T(1024)S(1)} %copy-done.39, f32[1024,1024]{1,0:T(8,128)} %get-tuple-element.181, ...), kind=kOutput, calls=%fused_computation.267 | convolution fusion | flops 4309647360 | bytes 31469568 | tf_op jit(solution)/shard_map/dot_general | solution.py:45
  430.6 7.1 collective-permute-done.9
  445.6 3.7 convolution_convert_fusion.2.refs_8_
  459.4 28.0 %back_head.4 = (bf16[2048,512]{1,0:T(8,128)(2,1)}, bf16[2048,512]{1,0:T(8,128)(2,1)}, bf16[2048,512]{1,0:T(8,128)(2,1)}, f32[1,8,1024]{2,1,0:T(8,128)}, f32[1,32...) custom-call(f32[1]{0:T(128)} %get-tuple-element.175.refs_0_, ...), custom_call_target="tpu_custom_call", output_to_operand_aliasing={{5}: (10, {}), {6}: (11, {})} | custom-call | bytes 67108864 | tf_op jit(solution)/shard_map/back_head/pallas_call | solution.py:572
  494.1 27.9 %back_head.5 = (bf16[2048,512]{1,0:T(8,128)(2,1)}, bf16[2048,512]{1,0:T(8,128)(2,1)}, bf16[2048,512]{1,0:T(8,128)(2,1)}, f32[1,8,1024]{2,1,0:T(8,128)}, f32[1,32...) custom-call(f32[1]{0:T(128)} %get-tuple-element.176.refs_0_, ...), custom_call_target="tpu_custom_call", output_to_operand_aliasing={{0}: (10, {}), {1}: (11, {}), {2}: (12, {}), {5}: (13, {}),... | custom-call | bytes 67108864 | tf_op jit(solution)/shard_map/back_head/pallas_call | solution.py:572
  525.5 28.2 %back_head.6 = (bf16[2048,512]{1,0:T(8,128)(2,1)}, bf16[2048,512]{1,0:T(8,128)(2,1)}, bf16[2048,512]{1,0:T(8,128)(2,1)}, f32[1,8,1024]{2,1,0:T(8,128)}, f32[1,32,256]{2,1,0:T(8,128)}) custom-call(f32[1]{0:T(128)} %get-tuple-element.177.refs_0_, f32[1,2]{1,0:T(1,128)} %get-tuple-element.171.refs_1_, ...), custom_call_target="tpu_custom_call", output_to_operand_aliasing={{0}: (10, {}), {1}: (11, {}), {2}: (12, {})} | custom-call | bytes 67108864 | tf_op jit(solution)/shard_map/back_head/pallas_call | solution.py:572
  553.7 27.8 %back_head.7 = (bf16[2048,512]{1,0:T(8,128)(2,1)}, bf16[2048,512]{1,0:T(8,128)(2,1)}, bf16[2048,512]{1,0:T(8,128)(2,1)}, f32[1,8,1024]{2,1,0:T(8,128)}, f32[1,32,256]{2,1,0:T(8,128)}) custom-call(f32[1]{0:T(128)} %get-tuple-element.178.refs_0_, f32[1,2]{1,0:T(1,128)} %get-tuple-element.172.refs_1_, ...), custom_call_target="tpu_custom_call", output_to_operand_aliasing={{0}: (10, {}), {1}: (11, {}), {2}: (12, {})} | custom-call | bytes 67108864 | tf_op jit(solution)/shard_map/back_head/pallas_call | solution.py:572
  587.1 9.0 %fusion.100 = (bf16[1024,1536]{1,0:T(8,128)(2,1)}, f32[1024]{0:T(1024)S(1)}) fusion(bf16[1024,1536]{1,0:T(8,128)(2,1)S(1)} %copy-done.22, bf16[2048,1024]{1,0:T(8,128)(2,1)S(1)} %copy-done.48, bf16[2048,1536]{1,0:T(8,128)(2,1)S(1)} %constant_dynamic-update-slice_fusion.5), kind=kOutput, calls=%fused_computation.269 | convolution fusion | flops 6448741376 | bytes 16781312 | tf_op jit(solution)/shard_map/dot_general | solution.py:49
  601.8 9.4 %collective-permute-done.38 = bf16[128,1024]{1,0:T(8,128)(2,1)S(1)} collective-permute-done((bf16[128,1024]{1,0:T(8,128)(2,1)S(1)}, bf16[128,1024]{1,0:T(8,128)(2,1)S(1)}, u32[]{:S(2)}, u32[]{:S(2)}) %collective-permute-start.38) | collective-permute-done | bytes 262176 | tf_op jit(solution)/shard_map/ppermute | solution.py:676
  613.3 5.3 collective-permute-done.39
  622.8 2.9 collective-permute-start.41
  625.7 3.9 fusion.37
  632.2 7.0 collective-permute-start.22
  639.8 5.0 collective-permute-done.23
  648.1 6.6 collective-permute-start.31
  657.2 6.4 collective-permute-start.25
  663.9 5.2 collective-permute-done.25
  671.8 4.2 collective-permute-done.26
  678.7 5.6 collective-permute-done.27
  684.4 3.3 collective-permute-done.34
  687.9 2.8 collective-permute-done.28
  693.2 3.7 fusion.7
  699.5 4.2 fusion.99
  704.6 4.5 maximum_convert_fusion.1
  709.1 4.4 maximum_convert_fusion
  719.8 2.8 collective-permute-done.47
  724.2 4.8 collective-permute-done.44
  730.8 11.4 %collective-permute-start.46 = (f32[2,1024]{0,1:T(8,128)S(1)}, f32[2,1024]{0,1:T(8,128)S(1)}, u32[]{:S(2)}, u32[]{:S(2)}) collective-permute-start(f32[2,1024]{0,1:T(8,128)S(1)} %fusion.53), channel_id=1, source_target_pairs={{1,0},{0,1},{3,2},{2,3},{5,4},{4,5},{7,6},{6,7},{9,8},{8,9},{11,10... | collective-permute-start | bytes 24584 | tf_op jit(solution)/shard_map/ppermute | solution.py:638
  (356 shorter events, 121.3 us)
Async XLA Ops:
  7.2 47.2 %all-gather.4.cloned.1.call-start = ((), (), s32[]{:S(2)}) async-start(), calls=%async_computation | async-start | bytes 6291456 | tf_op jit(solution)/shard_map/all_gather | solution.py:781
  14.1 685.4 %all-gather.6.cloned.1.call-start = ((), (), s32[]{:S(2)}) async-start(), calls=%async_computation.1 | async-start | bytes 8912896 | tf_op jit(solution)/shard_map/all_gather | solution.py:733
  280.6 14.4 %collective-permute-start.3 = (bf16[1024,1024]{1,0:T(8,128)(2,1)}, bf16[1024,1024]{1,0:T(8,128)(2,1)}, u32[]{:S(2)}, u32[]{:S(2)}) collective-permute-start(bf16[1024,1024]{1,0:T(8,128)(2,1)} %param.31), channel_id=1, source_target_pairs={{1,0},{0,1},{3,2},{2,3},{5,4},{4,5},{7,6},{6,7},{9,8},{8,9},{11,10... | collective-permute-start | bytes 6291464 | tf_op jit(solution)/shard_map/ppermute | solution.py:638
  291.0 5.8 collective-permute-start.1
  359.5 39.7 %collective-permute-start.4 = (bf16[1024,1024]{1,0:T(8,128)(2,1)S(1)}, bf16[1024,1024]{1,0:T(8,128)(2,1)S(1)}, u32[]{:S(2)}, u32[]{:S(2)}) collective-permute-start(bf16[1024,1024]{1,0:T(8,128)(2,1)S(1)} %fusion.28), channel_id=1, source_target_pairs={{0,1},{1,0},{2,3},{3,2},{4,5},{5,4},{6,7},{7,6},{8,9},{9,8},{10,11... | collective-permute-start | bytes 6291464 | tf_op jit(solution)/shard_map/ppermute | solution.py:661
  368.9 26.2 %collective-permute-start.6 = (bf16[512,1024]{1,0:T(8,128)(2,1)S(1)}, bf16[512,1024]{1,0:T(8,128)(2,1)S(1)}, u32[]{:S(2)}, u32[]{:S(2)}) collective-permute-start(bf16[512,1024]{1,0:T(8,128)(2,1)S(1)} %get-tuple-element.133), channel_id=1, source_target_pairs={{0,8},{2,10},{4,12},{6,14},{8,0},{10,2},{12,4},{14,6},{16,24},{18,... | collective-permute-start | bytes 3145736 | tf_op jit(solution)/shard_map/ppermute | solution.py:676
  371.7 26.0 %collective-permute-start.5 = (bf16[512,1024]{1,0:T(8,128)(2,1)S(1)}, bf16[512,1024]{1,0:T(8,128)(2,1)S(1)}, u32[]{:S(2)}, u32[]{:S(2)}) collective-permute-start(bf16[512,1024]{1,0:T(8,128)(2,1)S(1)} %get-tuple-element.135), channel_id=1, source_target_pairs={{0,4},{2,6},{4,0},{6,2},{8,12},{10,14},{12,8},{14,10},{16,20},{18,... | collective-permute-start | bytes 3145736 | tf_op jit(solution)/shard_map/ppermute | solution.py:676
  380.9 28.2 %collective-permute-start.2 = (bf16[1024,1024]{1,0:T(8,128)(2,1)}, bf16[1024,1024]{1,0:T(8,128)(2,1)S(1)}, u32[]{:S(2)}, u32[]{:S(2)}) collective-permute-start(bf16[1024,1024]{1,0:T(8,128)(2,1)} %fusion.25), channel_id=1, source_target_pairs={{0,1},{1,0},{2,3},{3,2},{4,5},{5,4},{6,7},{7,6},{8,9},{9,8},{10,11... | collective-permute-start | bytes 6291464 | tf_op jit(solution)/shard_map/ppermute | solution.py:661
  381.7 43.8 %collective-permute-start.8 = (bf16[512,1024]{1,0:T(8,128)(2,1)}, bf16[512,1024]{1,0:T(8,128)(2,1)}, u32[]{:S(2)}, u32[]{:S(2)}) collective-permute-start(bf16[512,1024]{1,0:T(8,128)(2,1)} %get-tuple-element.131), channel_id=1, source_target_pairs={{0,4},{2,6},{4,0},{6,2},{8,12},{10,14},{12,8},{14,10},{16,20},{18,... | collective-permute-start | bytes 3145736 | tf_op jit(solution)/shard_map/ppermute | solution.py:676
  395.1 32.4 %collective-permute-start.7 = (bf16[512,1024]{1,0:T(8,128)(2,1)}, bf16[512,1024]{1,0:T(8,128)(2,1)}, u32[]{:S(2)}, u32[]{:S(2)}) collective-permute-start(bf16[512,1024]{1,0:T(8,128)(2,1)} %get-tuple-element.138), channel_id=1, source_target_pairs={{0,2},{2,0},{4,6},{6,4},{8,10},{10,8},{12,14},{14,12},{16,18},{18,... | collective-permute-start | bytes 3145736 | tf_op jit(solution)/shard_map/ppermute | solution.py:676
  421.4 22.3 %collective-permute-start.11 = (bf16[1024,1024]{1,0:T(8,128)(2,1)}, bf16[1024,1024]{1,0:T(8,128)(2,1)}, u32[]{:S(2)}, u32[]{:S(2)}) collective-permute-start(bf16[1024,1024]{1,0:T(8,128)(2,1)} %get-tuple-element.68), channel_id=1, source_target_pairs={{1,0},{0,1},{3,2},{2,3},{5,4},{4,5},{7,6},{6,7},{9,8},{8,9},{11,10... | collective-permute-start | bytes 6291464 | tf_op jit(solution)/shard_map/ppermute | solution.py:638
  423.9 15.2 %collective-permute-start.10 = (bf16[256,1024]{1,0:T(8,128)(2,1)}, bf16[256,1024]{1,0:T(8,128)(2,1)S(1)}, u32[]{:S(2)}, u32[]{:S(2)}) collective-permute-start(bf16[256,1024]{1,0:T(8,128)(2,1)} %get-tuple-element.149), channel_id=1, source_target_pairs={{0,2},{2,0},{4,6},{6,4},{8,10},{10,8},{12,14},{14,12},{16,18},{18,... | collective-permute-start | bytes 1572872 | tf_op jit(solution)/shard_map/ppermute | solution.py:676
  424.3 13.4 %collective-permute-start.9 = (bf16[256,1024]{1,0:T(8,128)(2,1)}, bf16[256,1024]{1,0:T(8,128)(2,1)S(1)}, u32[]{:S(2)}, u32[]{:S(2)}) collective-permute-start(bf16[256,1024]{1,0:T(8,128)(2,1)} %get-tuple-element.151), channel_id=1, source_target_pairs={{0,8},{2,10},{4,12},{6,14},{8,0},{10,2},{12,4},{14,6},{16,24},{18,... | collective-permute-start | bytes 1572872 | tf_op jit(solution)/shard_map/ppermute | solution.py:676
  427.3 22.0 %collective-permute-start.13 = (bf16[256,1024]{1,0:T(8,128)(2,1)S(1)}, bf16[256,1024]{1,0:T(8,128)(2,1)S(1)}, u32[]{:S(2)}, u32[]{:S(2)}) collective-permute-start(bf16[256,1024]{1,0:T(8,128)(2,1)S(1)} %get-tuple-element.145), channel_id=1, source_target_pairs={{0,8},{2,10},{4,12},{6,14},{8,0},{10,2},{12,4},{14,6},{16,24},{18,... | collective-permute-start | bytes 1572872 | tf_op jit(solution)/shard_map/ppermute | solution.py:676
  429.2 24.1 %collective-permute-start.12 = (bf16[256,1024]{1,0:T(8,128)(2,1)S(1)}, bf16[256,1024]{1,0:T(8,128)(2,1)S(1)}, u32[]{:S(2)}, u32[]{:S(2)}) collective-permute-start(bf16[256,1024]{1,0:T(8,128)(2,1)S(1)} %get-tuple-element.147), channel_id=1, source_target_pairs={{0,4},{2,6},{4,0},{6,2},{8,12},{10,14},{12,8},{14,10},{16,20},{18,... | collective-permute-start | bytes 1572872 | tf_op jit(solution)/shard_map/ppermute | solution.py:676
  437.9 17.8 %collective-permute-start.18 = (bf16[128,1024]{1,0:T(8,128)(2,1)S(1)}, bf16[128,1024]{1,0:T(8,128)(2,1)S(1)}, u32[]{:S(2)}, u32[]{:S(2)}) collective-permute-start(bf16[128,1024]{1,0:T(8,128)(2,1)S(1)} %get-tuple-element.153), channel_id=1, source_target_pairs={{0,2},{2,0},{4,6},{6,4},{8,10},{10,8},{12,14},{14,12},{16,18},{18,... | collective-permute-start | bytes 786440 | tf_op jit(solution)/shard_map/ppermute | solution.py:676
  439.4 18.8 %collective-permute-start.20 = (bf16[128,1024]{1,0:T(8,128)(2,1)S(1)}, bf16[128,1024]{1,0:T(8,128)(2,1)S(1)}, u32[]{:S(2)}, u32[]{:S(2)}) collective-permute-start(bf16[128,1024]{1,0:T(8,128)(2,1)S(1)} %get-tuple-element.155), channel_id=1, source_target_pairs={{0,4},{2,6},{4,0},{6,2},{8,12},{10,14},{12,8},{14,10},{16,20},{18,... | collective-permute-start | bytes 786440 | tf_op jit(solution)/shard_map/ppermute | solution.py:676
  450.3 42.1 %collective-permute-start.15 = (bf16[128,1024]{1,0:T(8,128)(2,1)S(1)}, bf16[128,1024]{1,0:T(8,128)(2,1)S(1)}, u32[]{:S(2)}, u32[]{:S(2)}) collective-permute-start(bf16[128,1024]{1,0:T(8,128)(2,1)S(1)} %get-tuple-element.157), channel_id=1, source_target_pairs={{0,2},{2,0},{4,6},{6,4},{8,10},{10,8},{12,14},{14,12},{16,18},{18,... | collective-permute-start | bytes 786440 | tf_op jit(solution)/shard_map/ppermute | solution.py:676
  454.4 33.9 %collective-permute-start.14 = (bf16[128,1024]{1,0:T(8,128)(2,1)S(1)}, bf16[128,1024]{1,0:T(8,128)(2,1)S(1)}, u32[]{:S(2)}, u32[]{:S(2)}) collective-permute-start(bf16[128,1024]{1,0:T(8,128)(2,1)S(1)} %get-tuple-element.159), channel_id=1, source_target_pairs={{0,8},{2,10},{4,12},{6,14},{8,0},{10,2},{12,4},{14,6},{16,24},{18,... | collective-permute-start | bytes 786440 | tf_op jit(solution)/shard_map/ppermute | solution.py:676
  455.8 32.4 %collective-permute-start.19 = (bf16[64,1024]{1,0:T(8,128)(2,1)S(1)}, bf16[64,1024]{1,0:T(8,128)(2,1)S(1)}, u32[]{:S(2)}, u32[]{:S(2)}) collective-permute-start(bf16[64,1024]{1,0:T(8,128)(2,1)S(1)} %constant_dynamic-slice_fusion.14), channel_id=1, source_target_pairs={{0,16},{2,18},{4,20},{6,22},{8,24},{10,26},{12,28},{14,30},{16,0},... | collective-permute-start | bytes 393224 | tf_op jit(solution)/shard_map/ppermute | solution.py:676
  458.3 29.9 %collective-permute-start.21 = (bf16[64,1024]{1,0:T(8,128)(2,1)S(1)}, bf16[64,1024]{1,0:T(8,128)(2,1)S(1)}, u32[]{:S(2)}, u32[]{:S(2)}) collective-permute-start(bf16[64,1024]{1,0:T(8,128)(2,1)S(1)} %constant_dynamic-slice_fusion.12), channel_id=1, source_target_pairs={{0,16},{2,18},{4,20},{6,22},{8,24},{10,26},{12,28},{14,30},{16,0},... | collective-permute-start | bytes 393224 | tf_op jit(solution)/shard_map/ppermute | solution.py:676
  459.2 138.2 %collective-permute-start.37 = (bf16[256,1024]{1,0:T(8,128)(2,1)}, bf16[256,1024]{1,0:T(8,128)(2,1)}, u32[]{:S(2)}, u32[]{:S(2)}) collective-permute-start(bf16[256,1024]{1,0:T(8,128)(2,1)} %constant_dynamic-slice_fusion.3), channel_id=1, source_target_pairs={{0,8},{2,10},{4,12},{6,14},{8,0},{10,2},{12,4},{14,6},{16,24},{18,... | collective-permute-start | bytes 1572872 | tf_op jit(solution)/shard_map/ppermute | solution.py:676
  490.0 32.8 %collective-permute-start.16 = (bf16[64,1024]{1,0:T(8,128)(2,1)S(1)}, bf16[64,1024]{1,0:T(8,128)(2,1)S(1)}, u32[]{:S(2)}, u32[]{:S(2)}) collective-permute-start(bf16[64,1024]{1,0:T(8,128)(2,1)S(1)} %get-tuple-element.161), channel_id=1, source_target_pairs={{0,16},{2,18},{4,20},{6,22},{8,24},{10,26},{12,28},{14,30},{16,0},... | collective-permute-start | bytes 393224 | tf_op jit(solution)/shard_map/ppermute | solution.py:676
  494.0 29.7 %collective-permute-start.17 = (bf16[64,1024]{1,0:T(8,128)(2,1)S(1)}, bf16[64,1024]{1,0:T(8,128)(2,1)S(1)}, u32[]{:S(2)}, u32[]{:S(2)}) collective-permute-start(bf16[64,1024]{1,0:T(8,128)(2,1)S(1)} %get-tuple-element.163), channel_id=1, source_target_pairs={{0,16},{2,18},{4,20},{6,22},{8,24},{10,26},{12,28},{14,30},{16,0},... | collective-permute-start | bytes 393224 | tf_op jit(solution)/shard_map/ppermute | solution.py:676
  598.7 12.5 %collective-permute-start.38 = (bf16[128,1024]{1,0:T(8,128)(2,1)S(1)}, bf16[128,1024]{1,0:T(8,128)(2,1)S(1)}, u32[]{:S(2)}, u32[]{:S(2)}) collective-permute-start(bf16[128,1024]{1,0:T(8,128)(2,1)S(1)} %constant_dynamic-slice_fusion.2), channel_id=1, source_target_pairs={{0,2},{2,0},{4,6},{6,4},{8,10},{10,8},{12,14},{14,12},{16,18},{18,... | collective-permute-start | bytes 786440 | tf_op jit(solution)/shard_map/ppermute | solution.py:676
  611.4 7.2 collective-permute-start.39
  621.1 23.6 %collective-permute-start.23 = (bf16[256,1664]{1,0:T(8,128)(2,1)S(1)}, bf16[256,1664]{1,0:T(8,128)(2,1)S(1)}, u32[]{:S(2)}, u32[]{:S(2)}) collective-permute-start(bf16[256,1664]{1,0:T(8,128)(2,1)S(1)} %constant_dynamic-slice_fusion.11), channel_id=1, source_target_pairs={{0,2},{2,0},{4,6},{6,4},{8,10},{10,8},{12,14},{14,12},{16,18},{18,... | collective-permute-start | bytes 2555912 | tf_op jit(solution)/shard_map/ppermute | solution.py:676
  622.8 6.8 collective-permute-start.41
  629.6 9.6 %collective-permute-start.42 = (bf16[64,1024]{1,0:T(8,128)(2,1)S(1)}, bf16[64,1024]{1,0:T(8,128)(2,1)S(1)}, u32[]{:S(2)}, u32[]{:S(2)}) collective-permute-start(bf16[64,1024]{1,0:T(8,128)(2,1)S(1)} %constant_dynamic-update-slice_fusion.25), channel_id=1, source_target_pairs={{0,4},{2,6},{4,0},{6,2},{8,12},{10,14},{12,8},{14,10},{16,20},{18,... | collective-permute-start | bytes 393224 | tf_op jit(solution)/shard_map/ppermute | solution.py:676
  632.1 15.7 %collective-permute-start.30 = (bf16[256,1664]{1,0:T(8,128)(2,1)S(1)}, bf16[256,1664]{1,0:T(8,128)(2,1)S(1)}, u32[]{:S(2)}, u32[]{:S(2)}) collective-permute-start(bf16[256,1664]{1,0:T(8,128)(2,1)S(1)} %constant_dynamic-slice_fusion.7), channel_id=1, source_target_pairs={{0,4},{2,6},{4,0},{6,2},{8,12},{10,14},{12,8},{14,10},{16,20},{18,... | collective-permute-start | bytes 2555912 | tf_op jit(solution)/shard_map/ppermute | solution.py:676
  632.2 61.0 %collective-permute-start.22 = (bf16[1024,1024]{1,0:T(8,128)(2,1)S(1)}, bf16[1024,1024]{1,0:T(8,128)(2,1)S(1)}, u32[]{:S(2)}, u32[]{:S(2)}) collective-permute-start(bf16[1024,1024]{1,0:T(8,128)(2,1)S(1)} %fusion.37), channel_id=1, source_target_pairs={{0,1},{1,0},{2,3},{3,2},{4,5},{5,4},{6,7},{7,6},{8,9},{9,8},{10,11... | collective-permute-start | bytes 6291464 | tf_op jit(solution)/shard_map/ppermute | solution.py:661
  639.2 74.3 %collective-permute-start.43 = (bf16[128,1024]{1,0:T(8,128)(2,1)S(1)}, bf16[128,1024]{1,0:T(8,128)(2,1)}, u32[]{:S(2)}, u32[]{:S(2)}) collective-permute-start(bf16[128,1024]{1,0:T(8,128)(2,1)S(1)} %constant_dynamic-update-slice_fusion.23), channel_id=1, source_target_pairs={{0,2},{2,0},{4,6},{6,4},{8,10},{10,8},{12,14},{14,12},{16,18},{18,... | collective-permute-start | bytes 786440 | tf_op jit(solution)/shard_map/ppermute | solution.py:676
  645.0 12.0 %collective-permute-start.24 = (bf16[128,1664]{1,0:T(8,128)(2,1)S(1)}, bf16[128,1664]{1,0:T(8,128)(2,1)S(1)}, u32[]{:S(2)}, u32[]{:S(2)}) collective-permute-start(bf16[128,1664]{1,0:T(8,128)(2,1)S(1)} %constant_dynamic-slice_fusion.10), channel_id=1, source_target_pairs={{0,4},{2,6},{4,0},{6,2},{8,12},{10,14},{12,8},{14,10},{16,20},{18,... | collective-permute-start | bytes 1277960 | tf_op jit(solution)/shard_map/ppermute | solution.py:676
  648.1 15.6 %collective-permute-start.31 = (bf16[128,1664]{1,0:T(8,128)(2,1)S(1)}, bf16[128,1664]{1,0:T(8,128)(2,1)S(1)}, u32[]{:S(2)}, u32[]{:S(2)}) collective-permute-start(bf16[128,1664]{1,0:T(8,128)(2,1)S(1)} %constant_dynamic-slice_fusion.6), channel_id=1, source_target_pairs={{0,8},{2,10},{4,12},{6,14},{8,0},{10,2},{12,4},{14,6},{16,24},{18,... | collective-permute-start | bytes 1277960 | tf_op jit(solution)/shard_map/ppermute | solution.py:676
  657.2 11.9 %collective-permute-start.25 = (bf16[64,1664]{1,0:T(8,128)(2,1)S(1)}, bf16[64,1664]{1,0:T(8,128)(2,1)S(1)}, u32[]{:S(2)}, u32[]{:S(2)}) collective-permute-start(bf16[64,1664]{1,0:T(8,128)(2,1)S(1)} %constant_dynamic-slice_fusion.9), channel_id=1, source_target_pairs={{0,8},{2,10},{4,12},{6,14},{8,0},{10,2},{12,4},{14,6},{16,24},{18,... | collective-permute-start | bytes 638984 | tf_op jit(solution)/shard_map/ppermute | solution.py:676
  663.8 5.5 collective-permute-start.32
  669.3 6.8 collective-permute-start.26
  669.4 7.8 %collective-permute-start.33 = (bf16[32,1664]{1,0:T(8,128)(2,1)S(1)}, bf16[32,1664]{1,0:T(8,128)(2,1)S(1)}, u32[]{:S(2)}, u32[]{:S(2)}) collective-permute-start(bf16[32,1664]{1,0:T(8,128)(2,1)S(1)} %constant_dynamic-slice_fusion.4), channel_id=1, source_target_pairs={{0,16},{2,18},{4,20},{6,22},{8,24},{10,26},{12,28},{14,30},{16,0},... | collective-permute-start | bytes 319496 | tf_op jit(solution)/shard_map/ppermute | solution.py:676
  676.1 8.1 %collective-permute-start.27 = (bf16[32,1664]{1,0:T(8,128)(2,1)S(1)}, bf16[32,1664]{1,0:T(8,128)(2,1)S(1)}, u32[]{:S(2)}, u32[]{:S(2)}) collective-permute-start(bf16[32,1664]{1,0:T(8,128)(2,1)S(1)} %get-tuple-element.113), channel_id=1, source_target_pairs={{0,16},{2,18},{4,20},{6,22},{8,24},{10,26},{12,28},{14,30},{16,0},... | collective-permute-start | bytes 319496 | tf_op jit(solution)/shard_map/ppermute | solution.py:676
  677.3 10.4 %collective-permute-start.34 = (bf16[32,1664]{1,0:T(8,128)(2,1)S(1)}, bf16[32,1664]{1,0:T(8,128)(2,1)S(1)}, u32[]{:S(2)}, u32[]{:S(2)}) collective-permute-start(bf16[32,1664]{1,0:T(8,128)(2,1)S(1)} %get-tuple-element.115), channel_id=1, source_target_pairs={{0,16},{2,18},{4,20},{6,22},{8,24},{10,26},{12,28},{14,30},{16,0},... | collective-permute-start | bytes 319496 | tf_op jit(solution)/shard_map/ppermute | solution.py:676
  684.3 6.5 collective-permute-start.28
  687.7 5.1 collective-permute-start.35
  690.8 22.7 %collective-permute-start.29 = (bf16[128,1664]{1,0:T(8,128)(2,1)S(1)}, bf16[128,1664]{1,0:T(8,128)(2,1)}, u32[]{:S(2)}, u32[]{:S(2)}) collective-permute-start(bf16[128,1664]{1,0:T(8,128)(2,1)S(1)} %constant_dynamic-update-slice_fusion.32), channel_id=1, source_target_pairs={{0,4},{2,6},{4,0},{6,2},{8,12},{10,14},{12,8},{14,10},{16,20},{18,... | collective-permute-start | bytes 1277960 | tf_op jit(solution)/shard_map/ppermute | solution.py:676
  692.8 20.7 %collective-permute-start.36 = (bf16[128,1664]{1,0:T(8,128)(2,1)S(1)}, bf16[128,1664]{1,0:T(8,128)(2,1)}, u32[]{:S(2)}, u32[]{:S(2)}) collective-permute-start(bf16[128,1664]{1,0:T(8,128)(2,1)S(1)} %constant_dynamic-update-slice_fusion.27), channel_id=1, source_target_pairs={{0,8},{2,10},{4,12},{6,14},{8,0},{10,2},{12,4},{14,6},{16,24},{18,... | collective-permute-start | bytes 1277960 | tf_op jit(solution)/shard_map/ppermute | solution.py:676
  714.5 8.1 %collective-permute-start.47 = (bf16[256,1024]{1,0:T(8,128)(2,1)S(1)}, bf16[256,1024]{1,0:T(8,128)(2,1)S(1)}, u32[]{:S(2)}, u32[]{:S(2)}) collective-permute-start(bf16[256,1024]{1,0:T(8,128)(2,1)S(1)} %constant_dynamic-update-slice_fusion.14), channel_id=1, source_target_pairs={{0,8},{2,10},{4,12},{6,14},{8,0},{10,2},{12,4},{14,6},{16,24},{18,... | collective-permute-start | bytes 1572872 | tf_op jit(solution)/shard_map/ppermute | solution.py:676
  717.1 11.9 %collective-permute-start.44 = (bf16[256,1664]{1,0:T(8,128)(2,1)S(1)}, bf16[256,1664]{1,0:T(8,128)(2,1)S(1)}, u32[]{:S(2)}, u32[]{:S(2)}) collective-permute-start(bf16[256,1664]{1,0:T(8,128)(2,1)S(1)} %constant_dynamic-update-slice_fusion.22), channel_id=1, source_target_pairs={{0,2},{2,0},{4,6},{6,4},{8,10},{10,8},{12,14},{14,12},{16,18},{18,... | collective-permute-start | bytes 2555912 | tf_op jit(solution)/shard_map/ppermute | solution.py:676
  718.4 11.9 %collective-permute-start.45 = (bf16[256,1664]{1,0:T(8,128)(2,1)S(1)}, bf16[256,1664]{1,0:T(8,128)(2,1)S(1)}, u32[]{:S(2)}, u32[]{:S(2)}) collective-permute-start(bf16[256,1664]{1,0:T(8,128)(2,1)S(1)} %constant_dynamic-update-slice_fusion.18), channel_id=1, source_target_pairs={{0,4},{2,6},{4,0},{6,2},{8,12},{10,14},{12,8},{14,10},{16,20},{18,... | collective-permute-start | bytes 2555912 | tf_op jit(solution)/shard_map/ppermute | solution.py:676
  730.8 17.6 %collective-permute-start.46 = (f32[2,1024]{0,1:T(8,128)S(1)}, f32[2,1024]{0,1:T(8,128)S(1)}, u32[]{:S(2)}, u32[]{:S(2)}) collective-permute-start(f32[2,1024]{0,1:T(8,128)S(1)} %fusion.53), channel_id=1, source_target_pairs={{1,0},{0,1},{3,2},{2,3},{5,4},{4,5},{7,6},{6,7},{9,8},{8,9},{11,10... | collective-permute-start | bytes 24584 | tf_op jit(solution)/shard_map/ppermute | solution.py:638
  (56 other events, 984.9 us)
Sparse Core Ops, SparseCore 0:
  14.2 16.2 all-gather.3
  525.6 124.7 all-gather.5

commit v8 on v7

--- a/solution.py
+++ b/solution.py
@@ -845,7 +845,8 @@
     kept, kept_back, mixed_delta = lax.optimization_barrier((kept, kept_back, mixed_delta))
     kept, sent = halve_step(add_low(kept, sent), orders[:2], 2)
     kept_back, sent_back = halve_step(add_low(kept_back, sent_back), orders[1:], 3)
-    taken = 2
+    kept, sent = halve_step(add_low(kept, sent), orders[:2], 3)
+    taken = 3
     for step in range(4, steps):
         kept_back, sent_back = halve_step(add_low(kept_back, sent_back), orders[1:], step)
     layer_output = (
@@ -885,7 +886,6 @@
     )
     hidden_sum = jnp.concatenate([hidden_low_sum, hidden_high_sum], 1)
     return_sum = jnp.concatenate([return_low_sum, return_high_sum], 0)
-    query_delta, key_delta, value_delta = deltas
     diagonals = jnp.concatenate(diagonals, 0)
     local_sums = jnp.concatenate(local_sums, 0)
     recall_gain = jnp.sum(local_sums[:, 24:32, 0], 1)
@@ -897,15 +897,18 @@
     far_right = jnp.sum(local_sums[:, 16:24], (1, 2))
     table_part = table_part + far_left[:, None] * (level == 15) + far_right[:, None] * (level == 31)
 
-    project_delta = jnp.concatenate([query_delta, key_delta, value_delta], 1)
-    joined_part = dot_outer(normed, project_delta)
-    attn_gain_part = jnp.sum(joined_part * joined.astype(full_type), 1) / attn_gain
+    joined_parts = [dot_outer(normed, delta) for delta in deltas]
+    weights = (query_weight, key_weight, value_weight)
+    attn_gain_part = sum(
+        jnp.sum(part * weight.astype(full_type), 1) for part, weight in zip(joined_parts, weights)
+    )
+    attn_gain_part = attn_gain_part / attn_gain
     model_width = tokens.shape[1]
     small = jnp.concatenate([table_part.reshape(-1), gate_part])
     small = jnp.pad(small, (0, model_width - small.shape[0]))
     extra = jnp.stack([attn_gain_part, mlp_gain_part, small], 1)
     extra = jnp.pad(extra, ((0, 0), (0, 125)))
-    joined_low = jnp.concatenate([joined_part, extra], 1).astype(low_type)
+    joined_low = jnp.concatenate([part.astype(low_type) for part in joined_parts + [extra]], 1)
     joined_half = joined_low.shape[0] // 2
     last = [
         joined_low[:joined_half],
@@ -917,6 +920,7 @@
     last, (hidden_sum, return_sum) = double_all(last, (hidden_sum, return_sum))
     *joined_sum, output_sum = last
 
+    project_delta = jnp.concatenate(deltas, 1)
     normed_delta = fold(
         lambda rows: dot_inner(rows, joined), lambda k: share_of(project_delta, k, share_rows)
     )

time: 764 us -> 781 us (1.022)
  waiting for transfers between devices: 81.4 us -> 98.8 us
  starting transfers between devices: 72.4 us -> 63 us
    ppermute x40, waiting for transfers between devices: 77.3 us -> 94.7 us  [swap_over(): lax.ppermute(rows, 'dp', [(i, i ^ 1 << bit) for i in range(lax.axis_size(...]
    dot_general x5 -> x7, matrix products: 37.9 us -> 42 us  [dot_outer(): lax.dot_general(left, right, (((0,), (0,)), ((), ())), preferred_element_...]
    unnamed x116 -> x123, local copies, waits for them, and re-layouts: 14.6 us -> 17.6 us
  transfers between devices with their start and end apart: 50 -> 50, of which waited for: 19 -> 19; matrix products, arithmetic and copies ran while one was open for 19% -> 20% of each run, Pallas kernels for 18% -> 18%
where the time goes in v8:
time: 781 us; the launch traced here: 774 us
  Pallas kernels  349 us (45%)
  matrix products  145 us (19%)
  waiting for transfers between devices  98.8 us (13%)
  starting transfers between devices  63 us (8%)
  local copies, waits for them, and re-layouts  61.4 us (8%)
  other arithmetic  40.5 us (5%)
  between operations  16.2 us (2%)
    pallas_call x1, Pallas kernels, gather_found(): pl.pallas_call(functools.partial(gather_kernel, picks, scale), grid=(step...  189 us
    pallas_call x4, Pallas kernels, back_head(): pl.pallas_call(kernel, grid=(tokens // seq_len,), in_specs=[smem, smem, p...  112 us
    ppermute x40, waiting for transfers between devices, swap_over(): lax.ppermute(rows, 'dp', [(i, i ^ 1 << bit) for i in range(lax.axis_size(...  94.7 us
    dot_general x6, matrix products, dot_rows(): return jnp.dot(left, right, preferred_element_type=full_type)  59 us
    ppermute x40, starting transfers between devices, swap_over(): lax.ppermute(rows, 'dp', [(i, i ^ 1 << bit) for i in range(lax.axis_size(...  44.6 us
    dot_general x6, matrix products, dot_inner(): lax.dot_general(left, right, (((1,), (1,)), ((), ())), preferred_element_...  42.6 us
    dot_general x7, matrix products, dot_outer(): lax.dot_general(left, right, (((0,), (0,)), ((), ())), preferred_element_...  42 us
    pallas_call x1, Pallas kernels, interleave(): pl.pallas_call(interleave_kernel, grid=(heads, rows // step), in_specs=[s...  26 us
  transfers between devices with their start and end apart: 50, of which 19 were waited for; matrix products, arithmetic and copies ran while one was open for 20% of the time, Pallas kernels for 18%

profile of v8, /device:TPU:1, one launch (start us, length us, event | category | flops | bytes accessed | tf_op | source)
XLA Modules:
  0.0 773.8 jit_solution(16073245218585612097)
XLA Ops:
  10.7 3.5 fusion.6
  14.4 2.7 copy.102
  17.1 4.2 reshape.189.index_hbm
  29.3 26.0 %interleave.1 = bf16[131072,128]{1,0:T(8,128)(2,1)} custom-call(bf16[4,16384,128]{2,1,0:T(8,128)(2,1)} %key_ref.1, bf16[4,16384,128]{2,1,0:T(8,128)(2,1)} %value_ref.1), custom_call_target="tpu_custom_call" | custom-call | flops 8589934592 | bytes 67108864 | tf_op jit(solution)/shard_map/interleave/pallas_call | solution.py:83
  55.3 11.3 %convolution_convert_fusion.now_ref.before_ref.query_ref.key_ref.value_ref.refs_3_.refs_4_.refs_5_ = bf16[2048,1536]{1,0:T(8,128)(2,1)} fusion(bf16[2048,1024]{1,0:T(8,128)(2,1)} %all-gather.4.cloned.1.call-done, bf16[1024,1536]{1,0:T(8,128)(2,1)} %copy-done.24), kind=kOutput, calls=%fused_computation.10 | convolution fusion | flops 6445596672 | bytes 13631488 | tf_op jit(solution)/shard_map/dot_general | solution.py:45
  66.6 189.5 %gather_found.1 = (bf16[262144,2,128]{2,1,0:T(2,128)(2,1)}, f32[4096,128]{1,0:T(8,128)}, f32[4096,128]{1,0:T(8,128)}) custom-call(s32[64,32,128]{2,1,0:T(8,128)} %reshape.189.index_hbm, bf16[65536,2,128]{2,1,0:T(2,128)(2,1)} %bitcast.64, bf16[2048,1536]{1,0:T(8,128)(2,1)} %convolution_convert_fusion.now_ref.before_ref.query_ref.key_ref.value_ref.refs_3_.refs_4_.refs_5_, ...), custom_call_target="tpu_custom_call" | custom-call | bytes 536870912 | tf_op jit(solution)/shard_map/gather_found/pallas_call | solution.py:243
  256.1 21.4 %local_read.1 = bf16[2048,512]{1,0:T(8,128)(2,1)} custom-call(f32[4]{0:T(128)} %add_divide_fusion.gate_ref, f32[4,2]{1,0:T(4,128)} %pad_maximum_fusion.7.far_ref, f32[4,1,1024]{2,1,0:T(1,128)} %broadcast_in_dim.33.column_ref, bf16[2048,1536]{1,0:T(8,128)(2,1)} %convolution_convert_fusion.now_ref.before_ref.query_ref.key_ref.value_ref.refs_3_.refs_4_.refs_5_, ...), custom_call_target="tpu_custom_call" | custom-call | bytes 167772160 | tf_op jit(solution)/shard_map/local_read/pallas_call | solution.py:334
  277.5 4.0 convolution_convert_fusion.3
  282.0 4.0 collective-permute-done
  286.0 3.5 multiply_reduce_fusion.2
  297.7 20.4 %add_convert_fusion = (bf16[2048,2048]{1,0:T(8,128)(2,1)}, bf16[2048,2048]{1,0:T(8,128)(2,1)}) fusion(bf16[1024,2048]{1,0:T(8,128)(2,1)S(1)} %copy-done.49, bf16[1024,1024]{1,0:T(8,128)(2,1)} %collective-permute-done.1, bf16[1024,1024]{1,0:T(8,128)(2,1)S(1)} %multiply_convert_fusion.2), kind=kOutput, calls=%fused_computation.1 | convolution fusion | flops 8673820672 | bytes 25165824 | tf_op jit(solution)/shard_map/dot_general | solution.py:45
  318.2 11.7 %convolution_convert_fusion.1 = bf16[2048,1024]{1,0:T(8,128)(2,1)S(1)} fusion(bf16[2048,2048]{1,0:T(8,128)(2,1)} %get-tuple-element.115, bf16[2048,1024]{1,0:T(8,128)(2,1)S(1)} %constant_dynamic-update-slice_fusion.3), kind=kOutput, calls=%fused_computation.44 | convolution fusion | flops 8592031744 | bytes 16777216 | tf_op jit(solution)/shard_map/dot_general | solution.py:49
  330.3 14.1 %multiply_convert_fusion = bf16[2048,2048]{1,0:T(8,128)(2,1)} fusion(bf16[2048,2048]{1,0:T(8,128)(2,1)} %get-tuple-element.114, bf16[2048,1024]{1,0:T(8,128)(2,1)S(1)} %constant_dynamic-update-slice_fusion.3, bf16[2048,1024]{1,0:T(8,128)(2,1)} %param.30), kind=kOutput, calls=%fused_computation | convolution fusion | flops 8602517504 | bytes 25165824 | tf_op jit(solution)/shard_map/dot_general | solution.py:55
  344.5 7.2 fusion.28
  351.6 7.4 fusion.34
  361.0 7.5 fusion.31
  369.8 2.7 collective-permute-start.6
  373.8 8.1 %fusion.25 = bf16[1024,1024]{1,0:T(8,128)(2,1)} fusion(bf16[2048,1024]{1,0:T(8,128)(2,1)S(1)} %copy-done.50, bf16[2048,2048]{1,0:T(8,128)(2,1)} %get-tuple-element.115), kind=kOutput, calls=%fused_computation.58 | convolution fusion | flops 4296015872 | bytes 10485760 | tf_op jit(solution)/shard_map/dot_general | solution.py:45
  382.9 13.1 %collective-permute-done.6 = bf16[512,1024]{1,0:T(8,128)(2,1)S(1)} collective-permute-done((bf16[512,1024]{1,0:T(8,128)(2,1)S(1)}, bf16[512,1024]{1,0:T(8,128)(2,1)S(1)}, u32[]{:S(2)}, u32[]{:S(2)}) %collective-permute-start.6) | collective-permute-done | bytes 1048608 | tf_op jit(solution)/shard_map/ppermute | solution.py:676
  400.1 9.9 %multiply_reduce_fusion = (bf16[1024]{0:T(1024)(128)(2,1)S(1)}, f32[1024]{0:T(1024)S(1)}, f32[1024,1024]{1,0:T(8,128)}) fusion(f32[1024,1024]{1,0:T(8,128)S(1)} %copy-done.9, f32[1024]{0:T(1024)S(1)} %fusion.88, bf16[1024,1024]{1,0:T(8,128)(2,1)S(1)} %collective-permute-done.4, f32[1024]{0:T(1024)S(1)} %copy-done.43, bf16[1024,2048]{1,0:T(8,128)(2,1)S(1)} %copy-done.49, ...), kind=kOutput, calls=%fused_computation.37 | convolution fusion | flops 4303353856 | bytes 18888704 | tf_op jit(solution)/shard_map/dot_general | solution.py:55
  410.1 11.8 %fusion.97 = (bf16[1024,1024]{1,0:T(8,128)(2,1)}, f32[1024,1024]{1,0:T(8,128)}, bf16[1024,1024]{1,0:T(8,128)(2,1)}) fusion(f32[1024,1024]{1,0:T(8,128)S(1)} %copy-done.9, f32[1024]{0:T(1024)S(1)} %multiply_multiply_fusion.1, f32[1024]{0:T(1024)S(1)} %fusion.88, f32[1024]{0:T(1024)S(1)} %copy-done.43, f32[1024,1024]{1,0:T(8,128)} %get-tuple-element.171, ...), kind=kOutput, calls=%fused_computation.267 | convolution fusion | flops 4309647360 | bytes 31469568 | tf_op jit(solution)/shard_map/dot_general | solution.py:45
  428.3 2.7 copy.108
  438.3 7.1 collective-permute-done.9
  453.3 3.7 convolution_convert_fusion.2.refs_8_
  468.3 5.2 collective-permute-done.21
  477.5 27.9 %back_head.4 = (bf16[2048,512]{1,0:T(8,128)(2,1)}, bf16[2048,512]{1,0:T(8,128)(2,1)}, bf16[2048,512]{1,0:T(8,128)(2,1)}, f32[1,8,1024]{2,1,0:T(8,128)}, f32[1,32...) custom-call(f32[1]{0:T(128)} %get-tuple-element.165.refs_0_, ...), custom_call_target="tpu_custom_call", output_to_operand_aliasing={{5}: (10, {}), {6}: (11, {})} | custom-call | bytes 67108864 | tf_op jit(solution)/shard_map/back_head/pallas_call | solution.py:572
  509.5 27.8 %back_head.5 = (bf16[2048,512]{1,0:T(8,128)(2,1)}, bf16[2048,512]{1,0:T(8,128)(2,1)}, bf16[2048,512]{1,0:T(8,128)(2,1)}, f32[1,8,1024]{2,1,0:T(8,128)}, f32[1,32,256]{2,1,0:T(8,128)}) custom-call(f32[1]{0:T(128)} %get-tuple-element.166.refs_0_, f32[1,2]{1,0:T(1,128)} %get-tuple-element.160.refs_1_, ...), custom_call_target="tpu_custom_call", output_to_operand_aliasing={{0}: (10, {}), {1}: (11, {}), {2}: (12, {})} | custom-call | bytes 67108864 | tf_op jit(solution)/shard_map/back_head/pallas_call | solution.py:572
  537.4 28.1 %back_head.6 = (bf16[2048,512]{1,0:T(8,128)(2,1)}, bf16[2048,512]{1,0:T(8,128)(2,1)}, bf16[2048,512]{1,0:T(8,128)(2,1)}, f32[1,8,1024]{2,1,0:T(8,128)}, f32[1,32,256]{2,1,0:T(8,128)}) custom-call(f32[1]{0:T(128)} %get-tuple-element.167.refs_0_, f32[1,2]{1,0:T(1,128)} %get-tuple-element.161.refs_1_, ...), custom_call_target="tpu_custom_call", output_to_operand_aliasing={{0}: (10, {}), {1}: (11, {}), {2}: (12, {})} | custom-call | bytes 67108864 | tf_op jit(solution)/shard_map/back_head/pallas_call | solution.py:572
  565.5 28.2 %back_head.7 = (bf16[2048,512]{1,0:T(8,128)(2,1)}, bf16[2048,512]{1,0:T(8,128)(2,1)}, bf16[2048,512]{1,0:T(8,128)(2,1)}, f32[1,8,1024]{2,1,0:T(8,128)}, f32[1,32,256]{2,1,0:T(8,128)}) custom-call(f32[1]{0:T(128)} %get-tuple-element.168.refs_0_, f32[1,2]{1,0:T(1,128)} %get-tuple-element.162.refs_1_, ...), custom_call_target="tpu_custom_call", output_to_operand_aliasing={{0}: (10, {}), {1}: (11, {}), {2}: (12, {})} | custom-call | bytes 67108864 | tf_op jit(solution)/shard_map/back_head/pallas_call | solution.py:572
  593.7 6.3 multiply_reduce_fusion.3
  600.1 3.4 multiply_reduce_fusion.5
  603.6 3.4 multiply_reduce_fusion.4
  620.1 17.9 %collective-permute-done.38 = bf16[128,1024]{1,0:T(8,128)(2,1)S(1)} collective-permute-done((bf16[128,1024]{1,0:T(8,128)(2,1)S(1)}, bf16[128,1024]{1,0:T(8,128)(2,1)S(1)}, u32[]{:S(2)}, u32[]{:S(2)}) %collective-permute-start.38) | collective-permute-done | bytes 262176 | tf_op jit(solution)/shard_map/ppermute | solution.py:676
  639.7 2.5 collective-permute-done.39
  651.5 3.9 fusion.37
  655.5 10.8 %collective-permute-start.22 = (bf16[1024,1024]{1,0:T(8,128)(2,1)S(1)}, bf16[1024,1024]{1,0:T(8,128)(2,1)S(1)}, u32[]{:S(2)}, u32[]{:S(2)}) collective-permute-start(bf16[1024,1024]{1,0:T(8,128)(2,1)S(1)} %fusion.37), channel_id=1, source_target_pairs={{0,1},{1,0},{2,3},{3,2},{4,5},{5,4},{6,7},{7,6},{8,9},{9,8},{10,11... | collective-permute-start | bytes 6291464 | tf_op jit(solution)/shard_map/ppermute | solution.py:661
  669.1 8.6 %collective-permute-done.24 = bf16[128,1664]{1,0:T(8,128)(2,1)S(1)} collective-permute-done((bf16[128,1664]{1,0:T(8,128)(2,1)S(1)}, bf16[128,1664]{1,0:T(8,128)(2,1)S(1)}, u32[]{:S(2)}, u32[]{:S(2)}) %collective-permute-start.24) | collective-permute-done | bytes 426016 | tf_op jit(solution)/shard_map/ppermute | solution.py:676
  690.7 6.2 collective-permute-done.33
  699.2 6.0 collective-permute-done.34
  707.3 4.3 collective-permute-start.29
  712.3 3.7 fusion.7
  716.1 2.5 fusion.3
  718.6 4.2 fusion.99
  723.7 4.5 maximum_convert_fusion.1
  728.2 4.4 maximum_convert_fusion
  738.3 6.9 collective-permute-done.47
  746.8 7.2 collective-permute-done.44
  754.8 4.4 collective-permute-start.46
  (367 shorter events, 131.9 us)
Async XLA Ops:
  7.2 48.1 %all-gather.4.cloned.1.call-start = ((), (), s32[]{:S(2)}) async-start(), calls=%async_computation | async-start | bytes 6291456 | tf_op jit(solution)/shard_map/all_gather | solution.py:781
  14.1 704.5 %all-gather.6.cloned.1.call-start = ((), (), s32[]{:S(2)}) async-start(), calls=%async_computation.1 | async-start | bytes 8912896 | tf_op jit(solution)/shard_map/all_gather | solution.py:733
  281.5 4.5 collective-permute-start
  281.5 14.4 %collective-permute-start.3 = (bf16[1024,1024]{1,0:T(8,128)(2,1)}, bf16[1024,1024]{1,0:T(8,128)(2,1)}, u32[]{:S(2)}, u32[]{:S(2)}) collective-permute-start(bf16[1024,1024]{1,0:T(8,128)(2,1)} %param.31), channel_id=1, source_target_pairs={{1,0},{0,1},{3,2},{2,3},{5,4},{4,5},{7,6},{6,7},{9,8},{8,9},{11,10... | collective-permute-start | bytes 6291464 | tf_op jit(solution)/shard_map/ppermute | solution.py:638
  291.9 5.8 collective-permute-start.1
  360.4 39.7 %collective-permute-start.4 = (bf16[1024,1024]{1,0:T(8,128)(2,1)S(1)}, bf16[1024,1024]{1,0:T(8,128)(2,1)S(1)}, u32[]{:S(2)}, u32[]{:S(2)}) collective-permute-start(bf16[1024,1024]{1,0:T(8,128)(2,1)S(1)} %fusion.28), channel_id=1, source_target_pairs={{0,1},{1,0},{2,3},{3,2},{4,5},{5,4},{6,7},{7,6},{8,9},{9,8},{10,11... | collective-permute-start | bytes 6291464 | tf_op jit(solution)/shard_map/ppermute | solution.py:661
  369.8 26.1 %collective-permute-start.6 = (bf16[512,1024]{1,0:T(8,128)(2,1)S(1)}, bf16[512,1024]{1,0:T(8,128)(2,1)S(1)}, u32[]{:S(2)}, u32[]{:S(2)}) collective-permute-start(bf16[512,1024]{1,0:T(8,128)(2,1)S(1)} %get-tuple-element.127), channel_id=1, source_target_pairs={{0,8},{2,10},{4,12},{6,14},{8,0},{10,2},{12,4},{14,6},{16,24},{18,... | collective-permute-start | bytes 3145736 | tf_op jit(solution)/shard_map/ppermute | solution.py:676
  372.5 26.0 %collective-permute-start.5 = (bf16[512,1024]{1,0:T(8,128)(2,1)S(1)}, bf16[512,1024]{1,0:T(8,128)(2,1)S(1)}, u32[]{:S(2)}, u32[]{:S(2)}) collective-permute-start(bf16[512,1024]{1,0:T(8,128)(2,1)S(1)} %get-tuple-element.129), channel_id=1, source_target_pairs={{0,4},{2,6},{4,0},{6,2},{8,12},{10,14},{12,8},{14,10},{16,20},{18,... | collective-permute-start | bytes 3145736 | tf_op jit(solution)/shard_map/ppermute | solution.py:676
  381.8 28.2 %collective-permute-start.2 = (bf16[1024,1024]{1,0:T(8,128)(2,1)}, bf16[1024,1024]{1,0:T(8,128)(2,1)S(1)}, u32[]{:S(2)}, u32[]{:S(2)}) collective-permute-start(bf16[1024,1024]{1,0:T(8,128)(2,1)} %fusion.25), channel_id=1, source_target_pairs={{0,1},{1,0},{2,3},{3,2},{4,5},{5,4},{6,7},{7,6},{8,9},{9,8},{10,11... | collective-permute-start | bytes 6291464 | tf_op jit(solution)/shard_map/ppermute | solution.py:661
  382.6 50.6 %collective-permute-start.8 = (bf16[512,1024]{1,0:T(8,128)(2,1)}, bf16[512,1024]{1,0:T(8,128)(2,1)}, u32[]{:S(2)}, u32[]{:S(2)}) collective-permute-start(bf16[512,1024]{1,0:T(8,128)(2,1)} %get-tuple-element.125), channel_id=1, source_target_pairs={{0,4},{2,6},{4,0},{6,2},{8,12},{10,14},{12,8},{14,10},{16,20},{18,... | collective-permute-start | bytes 3145736 | tf_op jit(solution)/shard_map/ppermute | solution.py:676
  396.0 39.2 %collective-permute-start.7 = (bf16[512,1024]{1,0:T(8,128)(2,1)}, bf16[512,1024]{1,0:T(8,128)(2,1)}, u32[]{:S(2)}, u32[]{:S(2)}) collective-permute-start(bf16[512,1024]{1,0:T(8,128)(2,1)} %get-tuple-element.132), channel_id=1, source_target_pairs={{0,2},{2,0},{4,6},{6,4},{8,10},{10,8},{12,14},{14,12},{16,18},{18,... | collective-permute-start | bytes 3145736 | tf_op jit(solution)/shard_map/ppermute | solution.py:676
  421.9 29.6 %collective-permute-start.11 = (bf16[1024,1024]{1,0:T(8,128)(2,1)}, bf16[1024,1024]{1,0:T(8,128)(2,1)}, u32[]{:S(2)}, u32[]{:S(2)}) collective-permute-start(bf16[1024,1024]{1,0:T(8,128)(2,1)} %get-tuple-element.66), channel_id=1, source_target_pairs={{1,0},{0,1},{3,2},{2,3},{5,4},{4,5},{7,6},{6,7},{9,8},{8,9},{11,10... | collective-permute-start | bytes 6291464 | tf_op jit(solution)/shard_map/ppermute | solution.py:638
  431.6 15.2 %collective-permute-start.10 = (bf16[256,1024]{1,0:T(8,128)(2,1)}, bf16[256,1024]{1,0:T(8,128)(2,1)S(1)}, u32[]{:S(2)}, u32[]{:S(2)}) collective-permute-start(bf16[256,1024]{1,0:T(8,128)(2,1)} %get-tuple-element.143), channel_id=1, source_target_pairs={{0,2},{2,0},{4,6},{6,4},{8,10},{10,8},{12,14},{14,12},{16,18},{18,... | collective-permute-start | bytes 1572872 | tf_op jit(solution)/shard_map/ppermute | solution.py:676
  432.0 13.4 %collective-permute-start.9 = (bf16[256,1024]{1,0:T(8,128)(2,1)}, bf16[256,1024]{1,0:T(8,128)(2,1)S(1)}, u32[]{:S(2)}, u32[]{:S(2)}) collective-permute-start(bf16[256,1024]{1,0:T(8,128)(2,1)} %get-tuple-element.145), channel_id=1, source_target_pairs={{0,8},{2,10},{4,12},{6,14},{8,0},{10,2},{12,4},{14,6},{16,24},{18,... | collective-permute-start | bytes 1572872 | tf_op jit(solution)/shard_map/ppermute | solution.py:676
  434.9 22.1 %collective-permute-start.14 = (bf16[256,1024]{1,0:T(8,128)(2,1)S(1)}, bf16[256,1024]{1,0:T(8,128)(2,1)S(1)}, u32[]{:S(2)}, u32[]{:S(2)}) collective-permute-start(bf16[256,1024]{1,0:T(8,128)(2,1)S(1)} %get-tuple-element.139), channel_id=1, source_target_pairs={{0,8},{2,10},{4,12},{6,14},{8,0},{10,2},{12,4},{14,6},{16,24},{18,... | collective-permute-start | bytes 1572872 | tf_op jit(solution)/shard_map/ppermute | solution.py:676
  436.9 23.5 %collective-permute-start.12 = (bf16[256,1024]{1,0:T(8,128)(2,1)S(1)}, bf16[256,1024]{1,0:T(8,128)(2,1)S(1)}, u32[]{:S(2)}, u32[]{:S(2)}) collective-permute-start(bf16[256,1024]{1,0:T(8,128)(2,1)S(1)} %get-tuple-element.141), channel_id=1, source_target_pairs={{0,4},{2,6},{4,0},{6,2},{8,12},{10,14},{12,8},{14,10},{16,20},{18,... | collective-permute-start | bytes 1572872 | tf_op jit(solution)/shard_map/ppermute | solution.py:676
  445.7 16.4 %collective-permute-start.18 = (bf16[128,1024]{1,0:T(8,128)(2,1)S(1)}, bf16[128,1024]{1,0:T(8,128)(2,1)S(1)}, u32[]{:S(2)}, u32[]{:S(2)}) collective-permute-start(bf16[128,1024]{1,0:T(8,128)(2,1)S(1)} %get-tuple-element.147), channel_id=1, source_target_pairs={{0,2},{2,0},{4,6},{6,4},{8,10},{10,8},{12,14},{14,12},{16,18},{18,... | collective-permute-start | bytes 786440 | tf_op jit(solution)/shard_map/ppermute | solution.py:676
  447.1 17.5 %collective-permute-start.20 = (bf16[128,1024]{1,0:T(8,128)(2,1)S(1)}, bf16[128,1024]{1,0:T(8,128)(2,1)S(1)}, u32[]{:S(2)}, u32[]{:S(2)}) collective-permute-start(bf16[128,1024]{1,0:T(8,128)(2,1)S(1)} %get-tuple-element.149), channel_id=1, source_target_pairs={{0,4},{2,6},{4,0},{6,2},{8,12},{10,14},{12,8},{14,10},{16,20},{18,... | collective-permute-start | bytes 786440 | tf_op jit(solution)/shard_map/ppermute | solution.py:676
  457.3 17.7 %collective-permute-start.15 = (bf16[128,1024]{1,0:T(8,128)(2,1)S(1)}, bf16[128,1024]{1,0:T(8,128)(2,1)S(1)}, u32[]{:S(2)}, u32[]{:S(2)}) collective-permute-start(bf16[128,1024]{1,0:T(8,128)(2,1)S(1)} %constant_dynamic-slice_fusion.19), channel_id=1, source_target_pairs={{0,2},{2,0},{4,6},{6,4},{8,10},{10,8},{12,14},{14,12},{16,18},{18,... | collective-permute-start | bytes 786440 | tf_op jit(solution)/shard_map/ppermute | solution.py:676
  460.7 12.9 %collective-permute-start.13 = (bf16[128,1024]{1,0:T(8,128)(2,1)S(1)}, bf16[128,1024]{1,0:T(8,128)(2,1)S(1)}, u32[]{:S(2)}, u32[]{:S(2)}) collective-permute-start(bf16[128,1024]{1,0:T(8,128)(2,1)S(1)} %constant_dynamic-slice_fusion.22), channel_id=1, source_target_pairs={{0,8},{2,10},{4,12},{6,14},{8,0},{10,2},{12,4},{14,6},{16,24},{18,... | collective-permute-start | bytes 786440 | tf_op jit(solution)/shard_map/ppermute | solution.py:676
  462.1 6.1 collective-permute-start.19
  464.7 8.8 %collective-permute-start.21 = (bf16[64,1024]{1,0:T(8,128)(2,1)S(1)}, bf16[64,1024]{1,0:T(8,128)(2,1)S(1)}, u32[]{:S(2)}, u32[]{:S(2)}) collective-permute-start(bf16[64,1024]{1,0:T(8,128)(2,1)S(1)} %constant_dynamic-slice_fusion.12), channel_id=1, source_target_pairs={{0,16},{2,18},{4,20},{6,22},{8,24},{10,26},{12,28},{14,30},{16,0},... | collective-permute-start | bytes 393224 | tf_op jit(solution)/shard_map/ppermute | solution.py:676
  465.6 152.2 %collective-permute-start.37 = (bf16[256,1024]{1,0:T(8,128)(2,1)}, bf16[256,1024]{1,0:T(8,128)(2,1)}, u32[]{:S(2)}, u32[]{:S(2)}) collective-permute-start(bf16[256,1024]{1,0:T(8,128)(2,1)} %constant_dynamic-slice_fusion.3), channel_id=1, source_target_pairs={{0,8},{2,10},{4,12},{6,14},{8,0},{10,2},{12,4},{14,6},{16,24},{18,... | collective-permute-start | bytes 1572872 | tf_op jit(solution)/shard_map/ppermute | solution.py:676
  474.3 32.4 %collective-permute-start.16 = (bf16[64,1024]{1,0:T(8,128)(2,1)S(1)}, bf16[64,1024]{1,0:T(8,128)(2,1)S(1)}, u32[]{:S(2)}, u32[]{:S(2)}) collective-permute-start(bf16[64,1024]{1,0:T(8,128)(2,1)S(1)} %get-tuple-element.151), channel_id=1, source_target_pairs={{0,16},{2,18},{4,20},{6,22},{8,24},{10,26},{12,28},{14,30},{16,0},... | collective-permute-start | bytes 393224 | tf_op jit(solution)/shard_map/ppermute | solution.py:676
  475.7 32.0 %collective-permute-start.17 = (bf16[64,1024]{1,0:T(8,128)(2,1)S(1)}, bf16[64,1024]{1,0:T(8,128)(2,1)S(1)}, u32[]{:S(2)}, u32[]{:S(2)}) collective-permute-start(bf16[64,1024]{1,0:T(8,128)(2,1)S(1)} %get-tuple-element.153), channel_id=1, source_target_pairs={{0,16},{2,18},{4,20},{6,22},{8,24},{10,26},{12,28},{14,30},{16,0},... | collective-permute-start | bytes 393224 | tf_op jit(solution)/shard_map/ppermute | solution.py:676
  616.5 50.2 %collective-permute-start.23 = (bf16[256,1664]{1,0:T(8,128)(2,1)S(1)}, bf16[256,1664]{1,0:T(8,128)(2,1)S(1)}, u32[]{:S(2)}, u32[]{:S(2)}) collective-permute-start(bf16[256,1664]{1,0:T(8,128)(2,1)S(1)} %constant_dynamic-slice_fusion.11), channel_id=1, source_target_pairs={{0,2},{2,0},{4,6},{6,4},{8,10},{10,8},{12,14},{14,12},{16,18},{18,... | collective-permute-start | bytes 2555912 | tf_op jit(solution)/shard_map/ppermute | solution.py:676
  619.0 18.9 %collective-permute-start.38 = (bf16[128,1024]{1,0:T(8,128)(2,1)S(1)}, bf16[128,1024]{1,0:T(8,128)(2,1)S(1)}, u32[]{:S(2)}, u32[]{:S(2)}) collective-permute-start(bf16[128,1024]{1,0:T(8,128)(2,1)S(1)} %constant_dynamic-slice_fusion.2), channel_id=1, source_target_pairs={{0,2},{2,0},{4,6},{6,4},{8,10},{10,8},{12,14},{14,12},{16,18},{18,... | collective-permute-start | bytes 786440 | tf_op jit(solution)/shard_map/ppermute | solution.py:676
  638.0 4.2 collective-permute-start.39
  639.1 29.6 %collective-permute-start.30 = (bf16[256,1664]{1,0:T(8,128)(2,1)S(1)}, bf16[256,1664]{1,0:T(8,128)(2,1)S(1)}, u32[]{:S(2)}, u32[]{:S(2)}) collective-permute-start(bf16[256,1664]{1,0:T(8,128)(2,1)S(1)} %constant_dynamic-slice_fusion.7), channel_id=1, source_target_pairs={{0,4},{2,6},{4,0},{6,2},{8,12},{10,14},{12,8},{14,10},{16,20},{18,... | collective-permute-start | bytes 2555912 | tf_op jit(solution)/shard_map/ppermute | solution.py:676
  650.5 15.8 %collective-permute-start.42 = (bf16[64,1024]{1,0:T(8,128)(2,1)S(1)}, bf16[64,1024]{1,0:T(8,128)(2,1)S(1)}, u32[]{:S(2)}, u32[]{:S(2)}) collective-permute-start(bf16[64,1024]{1,0:T(8,128)(2,1)S(1)} %constant_dynamic-update-slice_fusion.25), channel_id=1, source_target_pairs={{0,4},{2,6},{4,0},{6,2},{8,12},{10,14},{12,8},{14,10},{16,20},{18,... | collective-permute-start | bytes 393224 | tf_op jit(solution)/shard_map/ppermute | solution.py:676
  655.5 56.8 %collective-permute-start.22 = (bf16[1024,1024]{1,0:T(8,128)(2,1)S(1)}, bf16[1024,1024]{1,0:T(8,128)(2,1)S(1)}, u32[]{:S(2)}, u32[]{:S(2)}) collective-permute-start(bf16[1024,1024]{1,0:T(8,128)(2,1)S(1)} %fusion.37), channel_id=1, source_target_pairs={{0,1},{1,0},{2,3},{3,2},{4,5},{5,4},{6,7},{7,6},{8,9},{9,8},{10,11... | collective-permute-start | bytes 6291464 | tf_op jit(solution)/shard_map/ppermute | solution.py:661
  666.3 66.3 %collective-permute-start.43 = (bf16[128,1024]{1,0:T(8,128)(2,1)S(1)}, bf16[128,1024]{1,0:T(8,128)(2,1)}, u32[]{:S(2)}, u32[]{:S(2)}) collective-permute-start(bf16[128,1024]{1,0:T(8,128)(2,1)S(1)} %constant_dynamic-update-slice_fusion.23), channel_id=1, source_target_pairs={{0,2},{2,0},{4,6},{6,4},{8,10},{10,8},{12,14},{14,12},{16,18},{18,... | collective-permute-start | bytes 786440 | tf_op jit(solution)/shard_map/ppermute | solution.py:676
  667.0 10.7 %collective-permute-start.24 = (bf16[128,1664]{1,0:T(8,128)(2,1)S(1)}, bf16[128,1664]{1,0:T(8,128)(2,1)S(1)}, u32[]{:S(2)}, u32[]{:S(2)}) collective-permute-start(bf16[128,1664]{1,0:T(8,128)(2,1)S(1)} %constant_dynamic-slice_fusion.10), channel_id=1, source_target_pairs={{0,4},{2,6},{4,0},{6,2},{8,12},{10,14},{12,8},{14,10},{16,20},{18,... | collective-permute-start | bytes 1277960 | tf_op jit(solution)/shard_map/ppermute | solution.py:676
  669.0 10.9 %collective-permute-start.31 = (bf16[128,1664]{1,0:T(8,128)(2,1)S(1)}, bf16[128,1664]{1,0:T(8,128)(2,1)S(1)}, u32[]{:S(2)}, u32[]{:S(2)}) collective-permute-start(bf16[128,1664]{1,0:T(8,128)(2,1)S(1)} %constant_dynamic-slice_fusion.6), channel_id=1, source_target_pairs={{0,8},{2,10},{4,12},{6,14},{8,0},{10,2},{12,4},{14,6},{16,24},{18,... | collective-permute-start | bytes 1277960 | tf_op jit(solution)/shard_map/ppermute | solution.py:676
  677.9 5.8 collective-permute-start.25
  680.0 6.0 collective-permute-start.32
  683.8 4.5 collective-permute-start.26
  686.1 10.8 %collective-permute-start.33 = (bf16[32,1664]{1,0:T(8,128)(2,1)S(1)}, bf16[32,1664]{1,0:T(8,128)(2,1)S(1)}, u32[]{:S(2)}, u32[]{:S(2)}) collective-permute-start(bf16[32,1664]{1,0:T(8,128)(2,1)S(1)} %constant_dynamic-slice_fusion.4), channel_id=1, source_target_pairs={{0,16},{2,18},{4,20},{6,22},{8,24},{10,26},{12,28},{14,30},{16,0},... | collective-permute-start | bytes 319496 | tf_op jit(solution)/shard_map/ppermute | solution.py:676
  688.4 10.8 %collective-permute-start.27 = (bf16[32,1664]{1,0:T(8,128)(2,1)S(1)}, bf16[32,1664]{1,0:T(8,128)(2,1)S(1)}, u32[]{:S(2)}, u32[]{:S(2)}) collective-permute-start(bf16[32,1664]{1,0:T(8,128)(2,1)S(1)} %get-tuple-element.109), channel_id=1, source_target_pairs={{0,16},{2,18},{4,20},{6,22},{8,24},{10,26},{12,28},{14,30},{16,0},... | collective-permute-start | bytes 319496 | tf_op jit(solution)/shard_map/ppermute | solution.py:676
  696.9 8.3 %collective-permute-start.34 = (bf16[32,1664]{1,0:T(8,128)(2,1)S(1)}, bf16[32,1664]{1,0:T(8,128)(2,1)S(1)}, u32[]{:S(2)}, u32[]{:S(2)}) collective-permute-start(bf16[32,1664]{1,0:T(8,128)(2,1)S(1)} %get-tuple-element.111), channel_id=1, source_target_pairs={{0,16},{2,18},{4,20},{6,22},{8,24},{10,26},{12,28},{14,30},{16,0},... | collective-permute-start | bytes 319496 | tf_op jit(solution)/shard_map/ppermute | solution.py:676
  699.2 8.1 %collective-permute-start.28 = (bf16[64,1664]{1,0:T(8,128)(2,1)S(1)}, bf16[64,1664]{1,0:T(8,128)(2,1)S(1)}, u32[]{:S(2)}, u32[]{:S(2)}) collective-permute-start(bf16[64,1664]{1,0:T(8,128)(2,1)S(1)} %constant_dynamic-update-slice_fusion.34), channel_id=1, source_target_pairs={{0,8},{2,10},{4,12},{6,14},{8,0},{10,2},{12,4},{14,6},{16,24},{18,... | collective-permute-start | bytes 638984 | tf_op jit(solution)/shard_map/ppermute | solution.py:676
  705.2 6.4 collective-permute-start.35
  707.3 25.4 %collective-permute-start.29 = (bf16[128,1664]{1,0:T(8,128)(2,1)S(1)}, bf16[128,1664]{1,0:T(8,128)(2,1)}, u32[]{:S(2)}, u32[]{:S(2)}) collective-permute-start(bf16[128,1664]{1,0:T(8,128)(2,1)S(1)} %constant_dynamic-update-slice_fusion.32), channel_id=1, source_target_pairs={{0,4},{2,6},{4,0},{6,2},{8,12},{10,14},{12,8},{14,10},{16,20},{18,... | collective-permute-start | bytes 1277960 | tf_op jit(solution)/shard_map/ppermute | solution.py:676
  711.6 21.0 %collective-permute-start.36 = (bf16[128,1664]{1,0:T(8,128)(2,1)S(1)}, bf16[128,1664]{1,0:T(8,128)(2,1)}, u32[]{:S(2)}, u32[]{:S(2)}) collective-permute-start(bf16[128,1664]{1,0:T(8,128)(2,1)S(1)} %constant_dynamic-update-slice_fusion.27), channel_id=1, source_target_pairs={{0,8},{2,10},{4,12},{6,14},{8,0},{10,2},{12,4},{14,6},{16,24},{18,... | collective-permute-start | bytes 1277960 | tf_op jit(solution)/shard_map/ppermute | solution.py:676
  733.6 11.6 %collective-permute-start.47 = (bf16[256,1024]{1,0:T(8,128)(2,1)S(1)}, bf16[256,1024]{1,0:T(8,128)(2,1)S(1)}, u32[]{:S(2)}, u32[]{:S(2)}) collective-permute-start(bf16[256,1024]{1,0:T(8,128)(2,1)S(1)} %constant_dynamic-update-slice_fusion.14), channel_id=1, source_target_pairs={{0,8},{2,10},{4,12},{6,14},{8,0},{10,2},{12,4},{14,6},{16,24},{18,... | collective-permute-start | bytes 1572872 | tf_op jit(solution)/shard_map/ppermute | solution.py:676
  735.9 18.2 %collective-permute-start.44 = (bf16[256,1664]{1,0:T(8,128)(2,1)S(1)}, bf16[256,1664]{1,0:T(8,128)(2,1)S(1)}, u32[]{:S(2)}, u32[]{:S(2)}) collective-permute-start(bf16[256,1664]{1,0:T(8,128)(2,1)S(1)} %constant_dynamic-update-slice_fusion.22), channel_id=1, source_target_pairs={{0,2},{2,0},{4,6},{6,4},{8,10},{10,8},{12,14},{14,12},{16,18},{18,... | collective-permute-start | bytes 2555912 | tf_op jit(solution)/shard_map/ppermute | solution.py:676
  737.2 17.1 %collective-permute-start.45 = (bf16[256,1664]{1,0:T(8,128)(2,1)S(1)}, bf16[256,1664]{1,0:T(8,128)(2,1)S(1)}, u32[]{:S(2)}, u32[]{:S(2)}) collective-permute-start(bf16[256,1664]{1,0:T(8,128)(2,1)S(1)} %constant_dynamic-update-slice_fusion.18), channel_id=1, source_target_pairs={{0,4},{2,6},{4,0},{6,2},{8,12},{10,14},{12,8},{14,10},{16,20},{18,... | collective-permute-start | bytes 2555912 | tf_op jit(solution)/shard_map/ppermute | solution.py:676
  754.8 10.5 %collective-permute-start.46 = (f32[2,1024]{0,1:T(8,128)S(1)}, f32[2,1024]{0,1:T(8,128)S(1)}, u32[]{:S(2)}, u32[]{:S(2)}) collective-permute-start(f32[2,1024]{0,1:T(8,128)S(1)} %fusion.53), channel_id=1, source_target_pairs={{1,0},{0,1},{3,2},{2,3},{5,4},{4,5},{7,6},{6,7},{9,8},{8,9},{11,10... | collective-permute-start | bytes 24584 | tf_op jit(solution)/shard_map/ppermute | solution.py:638
  (58 other events, 975.5 us)
Sparse Core Ops, SparseCore 0:
  14.3 16.2 all-gather.3
  509.6 116.0 all-gather.5

commit v9 on v7

--- a/solution.py
+++ b/solution.py
@@ -228,7 +228,7 @@
 def gather_found(index_rows, table, queries, picks, scale):
     heads, rows, unused, width = table.shape
     tokens = queries.shape[0]
-    half = 128
+    half = 256
     blocks = tokens // (2 * half)
     steps = heads * blocks
     chunk = half * picks
@@ -314,8 +314,7 @@
         parts = [jnp.exp2(part - top) for part in parts]
         total = jnp.sum(functools.reduce(jnp.add, parts), 1, keepdims=True)
         read = sum(dot_rows(parts[j].astype(low_type), value_ref[at[j], :]) for j in range(count))
-        half = pl.ds(t * (tile // 2), tile // 2)
-        recalled = jnp.concatenate([early_ref[half, :], late_ref[half, :]], 0)
+        recalled = (early_ref, late_ref)[t % 2][pl.ds((t // 2) * tile, tile), :]
         mixed_ref[at[t], :] = (gate * recalled + ((1.0 - gate) / total) * read).astype(low_type)
 
 
@@ -385,7 +384,7 @@
 
 
 def local_back_tile(
-    t, scale, gate, far_ref, query_ref, keys, turned, value_ref, query_mask_ref, delta_ref,
+    t, scale, gate, far, query_ref, keys, turned, value_ref, query_mask_ref, delta_ref,
     bias_ref, near_ref, key_sum_ref, value_sum_ref, gains, far_sums, result,
 ):
     count = len(keys)
@@ -396,9 +395,9 @@
     for j in range(count):
         step = j - t
         if step < -1:
-            bias = far_ref[0, 0]
+            bias = far[0]
         elif step > 1:
-            bias = far_ref[0, 1]
+            bias = far[1]
         else:
             bias = bias_ref[:, pl.ds((1 - step) * tile, tile)]
         parts.append(dot_inner(keys[j], rows) * (scale * log2_e) + bias)
@@ -470,12 +469,15 @@
     value_delta_ref, diagonal_ref, sums_ref, bias_ref, near_ref, key_sum_ref, value_sum_ref,
     read_ref, rows_ref, rows_sems,
 ):
-    sequence = pl.program_id(0)
-    sequences = pl.num_programs(0)
+    place = pl.program_id(0)
+    sequence = pl.program_id(1)
+    sequences = pl.num_programs(1)
+    total_tiles = pl.num_programs(0) * sequences * (query_ref.shape[0] // tile)
     count = query_ref.shape[0] // tile
     block = rows_ref.shape[1]
     own = own_columns(picks)
-    gate = gate_ref[0]
+    gate = gate_ref[place]
+    far_left, far_right = far_ref[place, 0], far_ref[place, 1]
 
     def rows_copy(number, slot):
         start = (head * sequences * count + number) * block
@@ -485,10 +487,13 @@
             rows_sems.at[slot],
         )
 
-    @pl.when(sequence == 0)
+    @pl.when(jnp.logical_and(place == 0, sequence == 0))
     def begin():
         for slot in range(2):
             rows_copy(slot, slot).start()
+
+    @pl.when(sequence == 0)
+    def begin_head():
         bias_ref[...] = band(column_ref)
         near_ref[...] = jnp.zeros(near_ref.shape, full_type)
         sums_ref[...] = jnp.zeros(sums_ref.shape, full_type)
@@ -499,7 +504,7 @@
     gains, recall_gains, far_sums = [], [], [[], []]
     for t in range(count):
         slot = t % 2
-        number = sequence * count + t
+        number = (place * sequences + sequence) * count + t
         rows_copy(number, slot).wait()
         result = []
         run_together(
@@ -513,7 +518,7 @@
             (
                 7 * count + 2,
                 local_back_tile(
-                    t, scale, gate, far_ref, query_ref, keys, turned, value_ref, query_mask_ref,
+                    t, scale, gate, (far_left, far_right), query_ref, keys, turned, value_ref, query_mask_ref,
                     delta_ref, bias_ref, near_ref, key_sum_ref, value_sum_ref, gains, far_sums,
                     result,
                 ),
@@ -521,7 +526,7 @@
         )
         query_delta_ref[at[t], :] = (result[0] + read_ref[...]).astype(low_type)
 
-        @pl.when(number + 2 < sequences * count)
+        @pl.when(number + 2 < total_tiles)
         def ahead():
             rows_copy(number + 2, slot).start()
 
@@ -547,35 +552,36 @@
         diagonal_ref[0] = total
 
 
-def back_head(
+def back_heads(
     projected, query_mask, key_mask, mixed_delta, found, columns, far, gates, seq_len, picks, scale,
-    head, kept, carried, after,
+    heads_now, kept, carried, after,
 ):
     tokens = mixed_delta.shape[0]
     heads = gates.shape[0]
     width = mixed_delta.shape[1] // heads
     anywhere = pl.BlockSpec(memory_space=pl.ANY)
-    chosen = slice(head, head + 1)
+    head, number = heads_now
+    chosen = slice(head, head + number)
     extra = len(kept) + len(carried) + len(after)
 
     def rows_of(shift):
-        return pl.BlockSpec((seq_len, width), lambda s: (s, head + shift * heads))
+        return pl.BlockSpec((seq_len, width), lambda h, s: (s, h + head + shift * heads))
 
     def kernel(*refs):
         outs = refs[10 + extra :]
         back_kernel(picks, scale, head, *refs[:10], *outs[:5], *outs[5 + len(carried) :])
 
-    mask_spec = pl.BlockSpec((1, seq_len, 128), lambda s: (s, 0, 0))
+    mask_spec = pl.BlockSpec((1, seq_len, 128), lambda h, s: (s, 0, 0))
     smem = pl.BlockSpec(memory_space=pltpu.SMEM)
     rows_shape = jax.ShapeDtypeStruct((tokens, heads * width), low_type)
     first = 10 + len(kept)
     out = pl.pallas_call(
         kernel,
-        grid=(tokens // seq_len,),
+        grid=(number, tokens // seq_len),
         in_specs=[
             smem,
             smem,
-            pl.BlockSpec((1, 1, ring), lambda s: (0, 0, 0)),
+            pl.BlockSpec((1, 1, ring), lambda h, s: (h, 0, 0)),
             rows_of(0),
             rows_of(1),
             rows_of(2),
@@ -589,16 +595,16 @@
             rows_of(0),
             rows_of(0),
             rows_of(0),
-            pl.BlockSpec((1, 8, ring), lambda s: (0, 0, 0)),
-            pl.BlockSpec((1, 32, tile), lambda s: (0, 0, 0)),
+            pl.BlockSpec((1, 8, ring), lambda h, s: (h, 0, 0)),
+            pl.BlockSpec((1, 32, tile), lambda h, s: (h, 0, 0)),
         ]
         + [anywhere] * len(carried),
         out_shape=[
             rows_shape,
             rows_shape,
             rows_shape,
-            jax.ShapeDtypeStruct((1, 8, ring), full_type),
-            jax.ShapeDtypeStruct((1, 32, tile), full_type),
+            jax.ShapeDtypeStruct((number, 8, ring), full_type),
+            jax.ShapeDtypeStruct((number, 32, tile), full_type),
         ]
         + [jax.ShapeDtypeStruct(part.shape, part.dtype) for part in carried],
         input_output_aliases={10 + i: i for i in range(len(kept))}
@@ -614,9 +620,9 @@
         ],
         compiler_params=pltpu.CompilerParams(vmem_limit_bytes=vmem_most),
         cost_estimate=pl.CostEstimate(
-            flops=0, bytes_accessed=tokens * picks * width * 8, transcendentals=0
+            flops=0, bytes_accessed=number * tokens * picks * width * 8, transcendentals=0
         ),
-        name="back_head",
+        name="back_heads",
     )(
         gates[chosen], far[chosen], columns[chosen], projected, projected, projected, query_mask,
         key_mask, mixed_delta, found, *kept, *carried, *after,
@@ -860,10 +866,15 @@
     deltas = []
     diagonals = []
     local_sums = []
-    for head in range(head_count):
-        deltas, diagonal_now, sums_now, kept = back_head(
+    heads_in_turn = [(0, 1)]
+    if head_count > 1:
+        heads_in_turn.append((1, 1))
+    if head_count > 2:
+        heads_in_turn.append((2, head_count - 2))
+    for heads_now in heads_in_turn:
+        deltas, diagonal_now, sums_now, kept = back_heads(
             projected, query_mask, key_mask, mixed_delta, found, behind_columns, far, gates,
-            seq_len, picks, scale, head, deltas, kept, packed,
+            seq_len, picks, scale, heads_now, deltas, kept, packed,
         )
         diagonals.append(diagonal_now)
         local_sums.append(sums_now)

time: 764 us -> 772 us (1.010)
  waiting for transfers between devices: 81.4 us -> 97.3 us
    ppermute x40, waiting for transfers between devices: 77.3 us -> 93.2 us  [swap_over(): lax.ppermute(rows, 'dp', [(i, i ^ 1 << bit) for i in range(lax.axis_size(...]
    pallas_call x1, Pallas kernels: 21.4 us -> 33.5 us  [local_read(): pl.pallas_call(functools.partial(local_kernel, scale), grid=(heads, token...]
    pallas_call x4 -> x3, Pallas kernels: 112 us -> 106 us  [back_heads(): pl.pallas_call(kernel, grid=(number, tokens // seq_len), in_specs=[smem,...]
  transfers between devices with their start and end apart: 50 -> 50, of which waited for: 19 -> 20; matrix products, arithmetic and copies ran while one was open for 19% -> 19% of each run, Pallas kernels for 18% -> 17%
where the time goes in v9:
time: 772 us; the launch traced here: 765 us
  Pallas kernels  349 us (45%)
  matrix products  141 us (18%)
  waiting for transfers between devices  97.3 us (13%)
  starting transfers between devices  65 us (8%)
  local copies, waits for them, and re-layouts  54.7 us (7%)
  other arithmetic  42.3 us (5%)
  between operations  16 us (2%)
    pallas_call x1, Pallas kernels, gather_found(): pl.pallas_call(functools.partial(gather_kernel, picks, scale), grid=(step...  183 us
    pallas_call x3, Pallas kernels, back_heads(): pl.pallas_call(kernel, grid=(number, tokens // seq_len), in_specs=[smem,...  106 us
    ppermute x40, waiting for transfers between devices, swap_over(): lax.ppermute(rows, 'dp', [(i, i ^ 1 << bit) for i in range(lax.axis_size(...  93.2 us
    dot_general x6, matrix products, dot_rows(): return jnp.dot(left, right, preferred_element_type=full_type)  59.1 us
    ppermute x40, starting transfers between devices, swap_over(): lax.ppermute(rows, 'dp', [(i, i ^ 1 << bit) for i in range(lax.axis_size(...  50.6 us
    dot_general x6, matrix products, dot_inner(): lax.dot_general(left, right, (((1,), (1,)), ((), ())), preferred_element_...  42.1 us
    dot_general x5, matrix products, dot_outer(): lax.dot_general(left, right, (((0,), (0,)), ((), ())), preferred_element_...  38.2 us
    pallas_call x1, Pallas kernels, local_read(): pl.pallas_call(functools.partial(local_kernel, scale), grid=(heads, token...  33.5 us
  transfers between devices with their start and end apart: 50, of which 20 were waited for; matrix products, arithmetic and copies ran while one was open for 19% of the time, Pallas kernels for 17%

profile of v9, /device:TPU:1, one launch (start us, length us, event | category | flops | bytes accessed | tf_op | source)
XLA Modules:
  0.0 764.5 jit_solution(17391926388349016281)
XLA Ops:
  10.7 3.5 fusion.6
  17.1 4.2 reshape.188.index_hbm
  28.4 26.0 %interleave.1 = bf16[131072,128]{1,0:T(8,128)(2,1)} custom-call(bf16[4,16384,128]{2,1,0:T(8,128)(2,1)} %key_ref.1, bf16[4,16384,128]{2,1,0:T(8,128)(2,1)} %value_ref.1), custom_call_target="tpu_custom_call" | custom-call | flops 8589934592 | bytes 67108864 | tf_op jit(solution)/shard_map/interleave/pallas_call | solution.py:83
  54.4 11.3 %convolution_convert_fusion.now_ref.before_ref.query_ref.key_ref.value_ref.refs_3_.refs_4_.refs_5_ = bf16[2048,1536]{1,0:T(8,128)(2,1)} fusion(bf16[2048,1024]{1,0:T(8,128)(2,1)} %all-gather.4.cloned.1.call-done, bf16[1024,1536]{1,0:T(8,128)(2,1)} %copy-done.19), kind=kOutput, calls=%fused_computation.10 | convolution fusion | flops 6445596672 | bytes 13631488 | tf_op jit(solution)/shard_map/dot_general | solution.py:45
  65.7 183.1 %gather_found.1 = (bf16[262144,2,128]{2,1,0:T(2,128)(2,1)}, f32[4096,128]{1,0:T(8,128)}, f32[4096,128]{1,0:T(8,128)}) custom-call(s32[32,64,128]{2,1,0:T(8,128)} %reshape.188.index_hbm, bf16[65536,2,128]{2,1,0:T(2,128)(2,1)} %bitcast.56, bf16[2048,1536]{1,0:T(8,128)(2,1)} %convolution_convert_fusion.now_ref.before_ref.query_ref.key_ref.value_ref.refs_3_.refs_4_.refs_5_, ...), custom_call_target="tpu_custom_call" | custom-call | bytes 536870912 | tf_op jit(solution)/shard_map/gather_found/pallas_call | solution.py:243
  248.8 33.5 %local_read.1 = bf16[2048,512]{1,0:T(8,128)(2,1)} custom-call(f32[4]{0:T(128)} %add_divide_fusion.gate_ref, f32[4,2]{1,0:T(4,128)} %pad_maximum_fusion.7.far_ref, f32[4,1,1024]{2,1,0:T(1,128)} %broadcast_in_dim.33.column_ref, bf16[2048,1536]{1,0:T(8,128)(2,1)} %convolution_convert_fusion.now_ref.before_ref.query_ref.key_ref.value_ref.refs_3_.refs_4_.refs_5_, ...), custom_call_target="tpu_custom_call" | custom-call | bytes 167772160 | tf_op jit(solution)/shard_map/local_read/pallas_call | solution.py:333
  282.3 4.0 convolution_convert_fusion.3
  286.8 4.0 collective-permute-done
  290.8 3.5 multiply_reduce_fusion.3
  302.5 20.4 %add_convert_fusion = (bf16[2048,2048]{1,0:T(8,128)(2,1)}, bf16[2048,2048]{1,0:T(8,128)(2,1)}) fusion(bf16[1024,2048]{1,0:T(8,128)(2,1)S(1)} %copy-done.41, bf16[1024,1024]{1,0:T(8,128)(2,1)} %collective-permute-done.1, bf16[1024,1024]{1,0:T(8,128)(2,1)S(1)} %multiply_convert_fusion.2), kind=kOutput, calls=%fused_computation.1 | convolution fusion | flops 8673820672 | bytes 25165824 | tf_op jit(solution)/shard_map/dot_general | solution.py:45
  322.9 11.9 %convolution_convert_fusion.1 = bf16[2048,1024]{1,0:T(8,128)(2,1)S(1)} fusion(bf16[2048,2048]{1,0:T(8,128)(2,1)} %get-tuple-element.109, bf16[2048,1024]{1,0:T(8,128)(2,1)S(1)} %constant_dynamic-update-slice_fusion.3), kind=kOutput, calls=%fused_computation.45 | convolution fusion | flops 8592031744 | bytes 16777216 | tf_op jit(solution)/shard_map/dot_general | solution.py:49
  335.3 14.1 %multiply_convert_fusion = bf16[2048,2048]{1,0:T(8,128)(2,1)} fusion(bf16[2048,2048]{1,0:T(8,128)(2,1)} %get-tuple-element.108, bf16[2048,1024]{1,0:T(8,128)(2,1)S(1)} %constant_dynamic-update-slice_fusion.3, bf16[2048,1024]{1,0:T(8,128)(2,1)} %param.30), kind=kOutput, calls=%fused_computation | convolution fusion | flops 8602517504 | bytes 25165824 | tf_op jit(solution)/shard_map/dot_general | solution.py:55
  349.5 6.9 fusion.28
  356.4 7.4 fusion.34
  365.8 7.5 fusion.31
  374.6 2.8 collective-permute-start.6
  378.6 8.0 %fusion.25 = bf16[1024,1024]{1,0:T(8,128)(2,1)} fusion(bf16[2048,1024]{1,0:T(8,128)(2,1)S(1)} %copy-done.42, bf16[2048,2048]{1,0:T(8,128)(2,1)} %get-tuple-element.109), kind=kOutput, calls=%fused_computation.56 | convolution fusion | flops 4296015872 | bytes 10485760 | tf_op jit(solution)/shard_map/dot_general | solution.py:45
  387.6 13.2 %collective-permute-done.6 = bf16[512,1024]{1,0:T(8,128)(2,1)S(1)} collective-permute-done((bf16[512,1024]{1,0:T(8,128)(2,1)S(1)}, bf16[512,1024]{1,0:T(8,128)(2,1)S(1)}, u32[]{:S(2)}, u32[]{:S(2)}) %collective-permute-start.6) | collective-permute-done | bytes 1048608 | tf_op jit(solution)/shard_map/ppermute | solution.py:682
  405.1 9.9 %multiply_reduce_fusion.1 = (bf16[1024]{0:T(1024)(128)(2,1)S(1)}, f32[1024]{0:T(1024)S(1)}, f32[1024,1024]{1,0:T(8,128)}) fusion(f32[1024,1024]{1,0:T(8,128)S(1)} %copy-done.7, f32[1024]{0:T(1024)S(1)} %fusion.88, bf16[1024,1024]{1,0:T(8,128)(2,1)S(1)} %collective-permute-done.4, f32[1024]{0:T(1024)S(1)} %copy-done.35, ...), kind=kOutput, calls=%fused_computation.38 | convolution fusion | flops 4303353856 | bytes 18888704 | tf_op jit(solution)/shard_map/dot_general | solution.py:55
  415.0 12.0 %fusion.97 = (bf16[1024,1024]{1,0:T(8,128)(2,1)}, f32[1024,1024]{1,0:T(8,128)}, bf16[1024,1024]{1,0:T(8,128)(2,1)}) fusion(f32[1024,1024]{1,0:T(8,128)S(1)} %copy-done.7, f32[1024]{0:T(1024)S(1)} %multiply_multiply_fusion.1, f32[1024]{0:T(1024)S(1)} %fusion.88, f32[1024]{0:T(1024)S(1)} %copy-done.35, f32[1024,1024]{1,0:T(8,128)} %get-tuple-element.165, ...), kind=kOutput, calls=%fused_computation.264 | convolution fusion | flops 4309647360 | bytes 31469568 | tf_op jit(solution)/shard_map/dot_general | solution.py:45
  437.7 7.1 collective-permute-done.9
  452.9 3.7 convolution_convert_fusion.2.refs_8_
  465.8 27.9 %back_heads.3 = (bf16[2048,512]{1,0:T(8,128)(2,1)}, bf16[2048,512]{1,0:T(8,128)(2,1)}, bf16[2048,512]{1,0:T(8,128)(2,1)}, f32[1,8,1024]{2,1,0:T(8,128)}, f32[1,3...) custom-call(f32[1]{0:T(128)} %get-tuple-element.161.refs_0_, ...), custom_call_target="tpu_custom_call", output_to_operand_aliasing={{5}: (10, {}), {6}: (11, {})} | custom-call | bytes 67108864 | tf_op jit(solution)/shard_map/back_heads/pallas_call | solution.py:578
  500.4 28.1 %back_heads.4 = (bf16[2048,512]{1,0:T(8,128)(2,1)}, bf16[2048,512]{1,0:T(8,128)(2,1)}, bf16[2048,512]{1,0:T(8,128)(2,1)}, f32[1,8,1024]{2,1,0:T(8,128)}, f32[1,3...) custom-call(f32[1]{0:T(128)} %get-tuple-element.162.refs_0_, ...), custom_call_target="tpu_custom_call", output_to_operand_aliasing={{0}: (10, {}), {1}: (11, {}), {2}: (12, {}), {5}: (13, {}),... | custom-call | bytes 67108864 | tf_op jit(solution)/shard_map/back_heads/pallas_call | solution.py:578
  532.0 50.0 %back_heads.5 = (bf16[2048,512]{1,0:T(8,128)(2,1)}, bf16[2048,512]{1,0:T(8,128)(2,1)}, bf16[2048,512]{1,0:T(8,128)(2,1)}, f32[2,8,1024]{2,1,0:T(8,128)}, f32[2,32,256]{2,1,0:T(8,128)}) custom-call(f32[2]{0:T(128)} %slice.150.refs_0_, f32[2,2]{1,0:T(2,128)} %slice.151.refs_1_, ...), custom_call_target="tpu_custom_call", output_to_operand_aliasing={{0}: (10, {}), {1}: (11, {}), {2}: (12, {})} | custom-call | bytes 134217728 | tf_op jit(solution)/shard_map/back_heads/pallas_call | solution.py:578
  587.8 9.0 %fusion.100 = (bf16[1024,1536]{1,0:T(8,128)(2,1)}, f32[1024]{0:T(1024)S(1)}) fusion(bf16[1024,1536]{1,0:T(8,128)(2,1)S(1)} %copy-done.20, bf16[2048,1024]{1,0:T(8,128)(2,1)S(1)} %copy-done.44, bf16[2048,1536]{1,0:T(8,128)(2,1)S(1)} %constant_dynamic-update-slice_fusion.5), kind=kOutput, calls=%fused_computation.266 | convolution fusion | flops 6448741376 | bytes 16781312 | tf_op jit(solution)/shard_map/dot_general | solution.py:49
  601.5 9.3 %collective-permute-done.38 = bf16[128,1024]{1,0:T(8,128)(2,1)S(1)} collective-permute-done((bf16[128,1024]{1,0:T(8,128)(2,1)S(1)}, bf16[128,1024]{1,0:T(8,128)(2,1)S(1)}, u32[]{:S(2)}, u32[]{:S(2)}) %collective-permute-start.38) | collective-permute-done | bytes 262176 | tf_op jit(solution)/shard_map/ppermute | solution.py:682
  613.0 5.3 collective-permute-done.39
  621.4 5.0 collective-permute-done.40
  626.5 3.7 fusion.37
  632.2 6.2 collective-permute-start.22
  638.5 4.0 collective-permute-start.43
  642.6 9.0 %collective-permute-done.23 = bf16[256,1664]{1,0:T(8,128)(2,1)S(1)} collective-permute-done((bf16[256,1664]{1,0:T(8,128)(2,1)S(1)}, bf16[256,1664]{1,0:T(8,128)(2,1)S(1)}, u32[]{:S(2)}, u32[]{:S(2)}) %collective-permute-start.23) | collective-permute-done | bytes 852000 | tf_op jit(solution)/shard_map/ppermute | solution.py:682
  654.8 4.5 collective-permute-done.24
  659.5 5.1 collective-permute-start.25
  664.6 6.4 collective-permute-done.31
  671.2 4.3 collective-permute-done.25
  675.7 3.3 collective-permute-start.26
  679.6 6.7 collective-permute-done.26
  691.7 4.2 collective-permute-start.28
  697.1 2.9 collective-permute-done.28
  702.9 3.7 fusion.7
  709.4 4.2 fusion.99
  714.5 4.5 maximum_convert_fusion.1
  719.1 4.4 maximum_convert_fusion
  730.0 4.3 collective-permute-done.47
  735.9 8.0 %collective-permute-done.44 = bf16[256,1664]{1,0:T(8,128)(2,1)S(1)} collective-permute-done((bf16[256,1664]{1,0:T(8,128)(2,1)S(1)}, bf16[256,1664]{1,0:T(8,128)(2,1)S(1)}, u32[]{:S(2)}, u32[]{:S(2)}) %collective-permute-start.44) | collective-permute-done | bytes 852000 | tf_op jit(solution)/shard_map/ppermute | solution.py:682
  744.9 5.0 collective-permute-start.46
  (350 shorter events, 121.5 us)
Async XLA Ops:
  7.2 47.2 %all-gather.4.cloned.1.call-start = ((), (), s32[]{:S(2)}) async-start(), calls=%async_computation | async-start | bytes 6291456 | tf_op jit(solution)/shard_map/all_gather | solution.py:787
  14.1 695.3 %all-gather.6.cloned.1.call-start = ((), (), s32[]{:S(2)}) async-start(), calls=%async_computation.1 | async-start | bytes 8912896 | tf_op jit(solution)/shard_map/all_gather | solution.py:739
  286.4 14.3 %collective-permute-start.3 = (bf16[1024,1024]{1,0:T(8,128)(2,1)}, bf16[1024,1024]{1,0:T(8,128)(2,1)}, u32[]{:S(2)}, u32[]{:S(2)}) collective-permute-start(bf16[1024,1024]{1,0:T(8,128)(2,1)} %param.31), channel_id=1, source_target_pairs={{1,0},{0,1},{3,2},{2,3},{5,4},{4,5},{7,6},{6,7},{9,8},{8,9},{11,10... | collective-permute-start | bytes 6291464 | tf_op jit(solution)/shard_map/ppermute | solution.py:644
  296.7 5.8 collective-permute-start.1
  365.2 39.9 %collective-permute-start.4 = (bf16[1024,1024]{1,0:T(8,128)(2,1)S(1)}, bf16[1024,1024]{1,0:T(8,128)(2,1)S(1)}, u32[]{:S(2)}, u32[]{:S(2)}) collective-permute-start(bf16[1024,1024]{1,0:T(8,128)(2,1)S(1)} %fusion.28), channel_id=1, source_target_pairs={{0,1},{1,0},{2,3},{3,2},{4,5},{5,4},{6,7},{7,6},{8,9},{9,8},{10,11... | collective-permute-start | bytes 6291464 | tf_op jit(solution)/shard_map/ppermute | solution.py:667
  374.6 26.2 %collective-permute-start.6 = (bf16[512,1024]{1,0:T(8,128)(2,1)S(1)}, bf16[512,1024]{1,0:T(8,128)(2,1)S(1)}, u32[]{:S(2)}, u32[]{:S(2)}) collective-permute-start(bf16[512,1024]{1,0:T(8,128)(2,1)S(1)} %get-tuple-element.123), channel_id=1, source_target_pairs={{0,8},{2,10},{4,12},{6,14},{8,0},{10,2},{12,4},{14,6},{16,24},{18,... | collective-permute-start | bytes 3145736 | tf_op jit(solution)/shard_map/ppermute | solution.py:682
  377.4 26.1 %collective-permute-start.5 = (bf16[512,1024]{1,0:T(8,128)(2,1)S(1)}, bf16[512,1024]{1,0:T(8,128)(2,1)S(1)}, u32[]{:S(2)}, u32[]{:S(2)}) collective-permute-start(bf16[512,1024]{1,0:T(8,128)(2,1)S(1)} %get-tuple-element.125), channel_id=1, source_target_pairs={{0,4},{2,6},{4,0},{6,2},{8,12},{10,14},{12,8},{14,10},{16,20},{18,... | collective-permute-start | bytes 3145736 | tf_op jit(solution)/shard_map/ppermute | solution.py:682
  386.6 28.4 %collective-permute-start.2 = (bf16[1024,1024]{1,0:T(8,128)(2,1)}, bf16[1024,1024]{1,0:T(8,128)(2,1)S(1)}, u32[]{:S(2)}, u32[]{:S(2)}) collective-permute-start(bf16[1024,1024]{1,0:T(8,128)(2,1)} %fusion.25), channel_id=1, source_target_pairs={{0,1},{1,0},{2,3},{3,2},{4,5},{5,4},{6,7},{7,6},{8,9},{9,8},{10,11... | collective-permute-start | bytes 6291464 | tf_op jit(solution)/shard_map/ppermute | solution.py:667
  387.3 45.4 %collective-permute-start.8 = (bf16[512,1024]{1,0:T(8,128)(2,1)}, bf16[512,1024]{1,0:T(8,128)(2,1)}, u32[]{:S(2)}, u32[]{:S(2)}) collective-permute-start(bf16[512,1024]{1,0:T(8,128)(2,1)} %get-tuple-element.121), channel_id=1, source_target_pairs={{0,4},{2,6},{4,0},{6,2},{8,12},{10,14},{12,8},{14,10},{16,20},{18,... | collective-permute-start | bytes 3145736 | tf_op jit(solution)/shard_map/ppermute | solution.py:682
  400.8 33.8 %collective-permute-start.7 = (bf16[512,1024]{1,0:T(8,128)(2,1)}, bf16[512,1024]{1,0:T(8,128)(2,1)}, u32[]{:S(2)}, u32[]{:S(2)}) collective-permute-start(bf16[512,1024]{1,0:T(8,128)(2,1)} %get-tuple-element.128), channel_id=1, source_target_pairs={{0,2},{2,0},{4,6},{6,4},{8,10},{10,8},{12,14},{14,12},{16,18},{18,... | collective-permute-start | bytes 3145736 | tf_op jit(solution)/shard_map/ppermute | solution.py:682
  427.0 24.0 %collective-permute-start.11 = (bf16[1024,1024]{1,0:T(8,128)(2,1)}, bf16[1024,1024]{1,0:T(8,128)(2,1)}, u32[]{:S(2)}, u32[]{:S(2)}) collective-permute-start(bf16[1024,1024]{1,0:T(8,128)(2,1)} %get-tuple-element.63), channel_id=1, source_target_pairs={{1,0},{0,1},{3,2},{2,3},{5,4},{4,5},{7,6},{6,7},{9,8},{8,9},{11,10... | collective-permute-start | bytes 6291464 | tf_op jit(solution)/shard_map/ppermute | solution.py:644
  431.1 15.2 %collective-permute-start.10 = (bf16[256,1024]{1,0:T(8,128)(2,1)}, bf16[256,1024]{1,0:T(8,128)(2,1)S(1)}, u32[]{:S(2)}, u32[]{:S(2)}) collective-permute-start(bf16[256,1024]{1,0:T(8,128)(2,1)} %get-tuple-element.139), channel_id=1, source_target_pairs={{0,2},{2,0},{4,6},{6,4},{8,10},{10,8},{12,14},{14,12},{16,18},{18,... | collective-permute-start | bytes 1572872 | tf_op jit(solution)/shard_map/ppermute | solution.py:682
  431.4 13.4 %collective-permute-start.9 = (bf16[256,1024]{1,0:T(8,128)(2,1)}, bf16[256,1024]{1,0:T(8,128)(2,1)S(1)}, u32[]{:S(2)}, u32[]{:S(2)}) collective-permute-start(bf16[256,1024]{1,0:T(8,128)(2,1)} %get-tuple-element.141), channel_id=1, source_target_pairs={{0,8},{2,10},{4,12},{6,14},{8,0},{10,2},{12,4},{14,6},{16,24},{18,... | collective-permute-start | bytes 1572872 | tf_op jit(solution)/shard_map/ppermute | solution.py:682
  434.5 22.2 %collective-permute-start.13 = (bf16[256,1024]{1,0:T(8,128)(2,1)S(1)}, bf16[256,1024]{1,0:T(8,128)(2,1)S(1)}, u32[]{:S(2)}, u32[]{:S(2)}) collective-permute-start(bf16[256,1024]{1,0:T(8,128)(2,1)S(1)} %get-tuple-element.135), channel_id=1, source_target_pairs={{0,8},{2,10},{4,12},{6,14},{8,0},{10,2},{12,4},{14,6},{16,24},{18,... | collective-permute-start | bytes 1572872 | tf_op jit(solution)/shard_map/ppermute | solution.py:682
  436.4 24.2 %collective-permute-start.12 = (bf16[256,1024]{1,0:T(8,128)(2,1)S(1)}, bf16[256,1024]{1,0:T(8,128)(2,1)S(1)}, u32[]{:S(2)}, u32[]{:S(2)}) collective-permute-start(bf16[256,1024]{1,0:T(8,128)(2,1)S(1)} %get-tuple-element.137), channel_id=1, source_target_pairs={{0,4},{2,6},{4,0},{6,2},{8,12},{10,14},{12,8},{14,10},{16,20},{18,... | collective-permute-start | bytes 1572872 | tf_op jit(solution)/shard_map/ppermute | solution.py:682
  445.1 17.8 %collective-permute-start.18 = (bf16[128,1024]{1,0:T(8,128)(2,1)S(1)}, bf16[128,1024]{1,0:T(8,128)(2,1)S(1)}, u32[]{:S(2)}, u32[]{:S(2)}) collective-permute-start(bf16[128,1024]{1,0:T(8,128)(2,1)S(1)} %get-tuple-element.143), channel_id=1, source_target_pairs={{0,2},{2,0},{4,6},{6,4},{8,10},{10,8},{12,14},{14,12},{16,18},{18,... | collective-permute-start | bytes 786440 | tf_op jit(solution)/shard_map/ppermute | solution.py:682
  446.6 18.8 %collective-permute-start.20 = (bf16[128,1024]{1,0:T(8,128)(2,1)S(1)}, bf16[128,1024]{1,0:T(8,128)(2,1)S(1)}, u32[]{:S(2)}, u32[]{:S(2)}) collective-permute-start(bf16[128,1024]{1,0:T(8,128)(2,1)S(1)} %get-tuple-element.145), channel_id=1, source_target_pairs={{0,4},{2,6},{4,0},{6,2},{8,12},{10,14},{12,8},{14,10},{16,20},{18,... | collective-permute-start | bytes 786440 | tf_op jit(solution)/shard_map/ppermute | solution.py:682
  457.6 41.1 %collective-permute-start.15 = (bf16[128,1024]{1,0:T(8,128)(2,1)S(1)}, bf16[128,1024]{1,0:T(8,128)(2,1)S(1)}, u32[]{:S(2)}, u32[]{:S(2)}) collective-permute-start(bf16[128,1024]{1,0:T(8,128)(2,1)S(1)} %get-tuple-element.147), channel_id=1, source_target_pairs={{0,2},{2,0},{4,6},{6,4},{8,10},{10,8},{12,14},{14,12},{16,18},{18,... | collective-permute-start | bytes 786440 | tf_op jit(solution)/shard_map/ppermute | solution.py:682
  461.5 33.1 %collective-permute-start.14 = (bf16[128,1024]{1,0:T(8,128)(2,1)S(1)}, bf16[128,1024]{1,0:T(8,128)(2,1)}, u32[]{:S(2)}, u32[]{:S(2)}) collective-permute-start(bf16[128,1024]{1,0:T(8,128)(2,1)S(1)} %get-tuple-element.149), channel_id=1, source_target_pairs={{0,8},{2,10},{4,12},{6,14},{8,0},{10,2},{12,4},{14,6},{16,24},{18,... | collective-permute-start | bytes 786440 | tf_op jit(solution)/shard_map/ppermute | solution.py:682
  463.0 31.5 %collective-permute-start.19 = (bf16[64,1024]{1,0:T(8,128)(2,1)S(1)}, bf16[64,1024]{1,0:T(8,128)(2,1)S(1)}, u32[]{:S(2)}, u32[]{:S(2)}) collective-permute-start(bf16[64,1024]{1,0:T(8,128)(2,1)S(1)} %constant_dynamic-slice_fusion.14), channel_id=1, source_target_pairs={{0,16},{2,18},{4,20},{6,22},{8,24},{10,26},{12,28},{14,30},{16,0},... | collective-permute-start | bytes 393224 | tf_op jit(solution)/shard_map/ppermute | solution.py:682
  465.5 29.0 %collective-permute-start.21 = (bf16[64,1024]{1,0:T(8,128)(2,1)S(1)}, bf16[64,1024]{1,0:T(8,128)(2,1)S(1)}, u32[]{:S(2)}, u32[]{:S(2)}) collective-permute-start(bf16[64,1024]{1,0:T(8,128)(2,1)S(1)} %constant_dynamic-slice_fusion.12), channel_id=1, source_target_pairs={{0,16},{2,18},{4,20},{6,22},{8,24},{10,26},{12,28},{14,30},{16,0},... | collective-permute-start | bytes 393224 | tf_op jit(solution)/shard_map/ppermute | solution.py:682
  465.6 132.4 %collective-permute-start.37 = (bf16[256,1024]{1,0:T(8,128)(2,1)S(1)}, bf16[256,1024]{1,0:T(8,128)(2,1)S(1)}, u32[]{:S(2)}, u32[]{:S(2)}) collective-permute-start(bf16[256,1024]{1,0:T(8,128)(2,1)S(1)} %constant_dynamic-slice_fusion.3), channel_id=1, source_target_pairs={{0,8},{2,10},{4,12},{6,14},{8,0},{10,2},{12,4},{14,6},{16,24},{18,... | collective-permute-start | bytes 1572872 | tf_op jit(solution)/shard_map/ppermute | solution.py:682
  496.4 32.9 %collective-permute-start.16 = (bf16[64,1024]{1,0:T(8,128)(2,1)S(1)}, bf16[64,1024]{1,0:T(8,128)(2,1)S(1)}, u32[]{:S(2)}, u32[]{:S(2)}) collective-permute-start(bf16[64,1024]{1,0:T(8,128)(2,1)S(1)} %get-tuple-element.151), channel_id=1, source_target_pairs={{0,16},{2,18},{4,20},{6,22},{8,24},{10,26},{12,28},{14,30},{16,0},... | collective-permute-start | bytes 393224 | tf_op jit(solution)/shard_map/ppermute | solution.py:682
  500.4 29.8 %collective-permute-start.17 = (bf16[64,1024]{1,0:T(8,128)(2,1)S(1)}, bf16[64,1024]{1,0:T(8,128)(2,1)S(1)}, u32[]{:S(2)}, u32[]{:S(2)}) collective-permute-start(bf16[64,1024]{1,0:T(8,128)(2,1)S(1)} %get-tuple-element.153), channel_id=1, source_target_pairs={{0,16},{2,18},{4,20},{6,22},{8,24},{10,26},{12,28},{14,30},{16,0},... | collective-permute-start | bytes 393224 | tf_op jit(solution)/shard_map/ppermute | solution.py:682
  598.3 12.5 %collective-permute-start.38 = (bf16[128,1024]{1,0:T(8,128)(2,1)S(1)}, bf16[128,1024]{1,0:T(8,128)(2,1)S(1)}, u32[]{:S(2)}, u32[]{:S(2)}) collective-permute-start(bf16[128,1024]{1,0:T(8,128)(2,1)S(1)} %constant_dynamic-slice_fusion.2), channel_id=1, source_target_pairs={{0,2},{2,0},{4,6},{6,4},{8,10},{10,8},{12,14},{14,12},{16,18},{18,... | collective-permute-start | bytes 786440 | tf_op jit(solution)/shard_map/ppermute | solution.py:682
  610.9 7.3 collective-permute-start.39
  618.3 8.0 %collective-permute-start.40 = (bf16[32,1024]{1,0:T(8,128)(2,1)S(1)}, bf16[32,1024]{1,0:T(8,128)(2,1)S(1)}, u32[]{:S(2)}, u32[]{:S(2)}) collective-permute-start(bf16[32,1024]{1,0:T(8,128)(2,1)S(1)} %constant_dynamic-slice_fusion), channel_id=1, source_target_pairs={{0,16},{2,18},{4,20},{6,22},{8,24},{10,26},{12,28},{14,30},{16,0},... | collective-permute-start | bytes 196616 | tf_op jit(solution)/shard_map/ppermute | solution.py:682
  620.8 30.8 %collective-permute-start.23 = (bf16[256,1664]{1,0:T(8,128)(2,1)S(1)}, bf16[256,1664]{1,0:T(8,128)(2,1)S(1)}, u32[]{:S(2)}, u32[]{:S(2)}) collective-permute-start(bf16[256,1664]{1,0:T(8,128)(2,1)S(1)} %constant_dynamic-slice_fusion.11), channel_id=1, source_target_pairs={{0,2},{2,0},{4,6},{6,4},{8,10},{10,8},{12,14},{14,12},{16,18},{18,... | collective-permute-start | bytes 2555912 | tf_op jit(solution)/shard_map/ppermute | solution.py:682
  630.5 7.9 %collective-permute-start.42 = (bf16[64,1024]{1,0:T(8,128)(2,1)S(1)}, bf16[64,1024]{1,0:T(8,128)(2,1)S(1)}, u32[]{:S(2)}, u32[]{:S(2)}) collective-permute-start(bf16[64,1024]{1,0:T(8,128)(2,1)S(1)} %constant_dynamic-update-slice_fusion.24), channel_id=1, source_target_pairs={{0,4},{2,6},{4,0},{6,2},{8,12},{10,14},{12,8},{14,10},{16,20},{18,... | collective-permute-start | bytes 393224 | tf_op jit(solution)/shard_map/ppermute | solution.py:682
  631.7 21.6 %collective-permute-start.30 = (bf16[256,1664]{1,0:T(8,128)(2,1)S(1)}, bf16[256,1664]{1,0:T(8,128)(2,1)S(1)}, u32[]{:S(2)}, u32[]{:S(2)}) collective-permute-start(bf16[256,1664]{1,0:T(8,128)(2,1)S(1)} %constant_dynamic-slice_fusion.7), channel_id=1, source_target_pairs={{0,4},{2,6},{4,0},{6,2},{8,12},{10,14},{12,8},{14,10},{16,20},{18,... | collective-permute-start | bytes 2555912 | tf_op jit(solution)/shard_map/ppermute | solution.py:682
  632.2 70.7 %collective-permute-start.22 = (bf16[1024,1024]{1,0:T(8,128)(2,1)S(1)}, bf16[1024,1024]{1,0:T(8,128)(2,1)S(1)}, u32[]{:S(2)}, u32[]{:S(2)}) collective-permute-start(bf16[1024,1024]{1,0:T(8,128)(2,1)S(1)} %fusion.37), channel_id=1, source_target_pairs={{0,1},{1,0},{2,3},{3,2},{4,5},{5,4},{6,7},{7,6},{8,9},{9,8},{10,11... | collective-permute-start | bytes 6291464 | tf_op jit(solution)/shard_map/ppermute | solution.py:667
  638.5 85.0 %collective-permute-start.43 = (bf16[128,1024]{1,0:T(8,128)(2,1)S(1)}, bf16[128,1024]{1,0:T(8,128)(2,1)}, u32[]{:S(2)}, u32[]{:S(2)}) collective-permute-start(bf16[128,1024]{1,0:T(8,128)(2,1)S(1)} %constant_dynamic-update-slice_fusion.22), channel_id=1, source_target_pairs={{0,2},{2,0},{4,6},{6,4},{8,10},{10,8},{12,14},{14,12},{16,18},{18,... | collective-permute-start | bytes 786440 | tf_op jit(solution)/shard_map/ppermute | solution.py:682
  651.9 7.4 collective-permute-start.24
  653.5 17.5 %collective-permute-start.31 = (bf16[128,1664]{1,0:T(8,128)(2,1)S(1)}, bf16[128,1664]{1,0:T(8,128)(2,1)S(1)}, u32[]{:S(2)}, u32[]{:S(2)}) collective-permute-start(bf16[128,1664]{1,0:T(8,128)(2,1)S(1)} %constant_dynamic-slice_fusion.6), channel_id=1, source_target_pairs={{0,8},{2,10},{4,12},{6,14},{8,0},{10,2},{12,4},{14,6},{16,24},{18,... | collective-permute-start | bytes 1277960 | tf_op jit(solution)/shard_map/ppermute | solution.py:682
  659.5 16.1 %collective-permute-start.25 = (bf16[64,1664]{1,0:T(8,128)(2,1)S(1)}, bf16[64,1664]{1,0:T(8,128)(2,1)S(1)}, u32[]{:S(2)}, u32[]{:S(2)}) collective-permute-start(bf16[64,1664]{1,0:T(8,128)(2,1)S(1)} %constant_dynamic-slice_fusion.9), channel_id=1, source_target_pairs={{0,8},{2,10},{4,12},{6,14},{8,0},{10,2},{12,4},{14,6},{16,24},{18,... | collective-permute-start | bytes 638984 | tf_op jit(solution)/shard_map/ppermute | solution.py:682
  671.2 7.8 %collective-permute-start.32 = (bf16[64,1664]{1,0:T(8,128)(2,1)S(1)}, bf16[64,1664]{1,0:T(8,128)(2,1)S(1)}, u32[]{:S(2)}, u32[]{:S(2)}) collective-permute-start(bf16[64,1664]{1,0:T(8,128)(2,1)S(1)} %constant_dynamic-slice_fusion.5), channel_id=1, source_target_pairs={{0,2},{2,0},{4,6},{6,4},{8,10},{10,8},{12,14},{14,12},{16,18},{18,... | collective-permute-start | bytes 638984 | tf_op jit(solution)/shard_map/ppermute | solution.py:682
  675.7 10.6 %collective-permute-start.26 = (bf16[32,1664]{1,0:T(8,128)(2,1)S(1)}, bf16[32,1664]{1,0:T(8,128)(2,1)S(1)}, u32[]{:S(2)}, u32[]{:S(2)}) collective-permute-start(bf16[32,1664]{1,0:T(8,128)(2,1)S(1)} %constant_dynamic-slice_fusion.8), channel_id=1, source_target_pairs={{0,16},{2,18},{4,20},{6,22},{8,24},{10,26},{12,28},{14,30},{16,0},... | collective-permute-start | bytes 319496 | tf_op jit(solution)/shard_map/ppermute | solution.py:682
  679.0 9.6 %collective-permute-start.33 = (bf16[32,1664]{1,0:T(8,128)(2,1)S(1)}, bf16[32,1664]{1,0:T(8,128)(2,1)S(1)}, u32[]{:S(2)}, u32[]{:S(2)}) collective-permute-start(bf16[32,1664]{1,0:T(8,128)(2,1)S(1)} %constant_dynamic-slice_fusion.4), channel_id=1, source_target_pairs={{0,16},{2,18},{4,20},{6,22},{8,24},{10,26},{12,28},{14,30},{16,0},... | collective-permute-start | bytes 319496 | tf_op jit(solution)/shard_map/ppermute | solution.py:682
  686.4 5.3 collective-permute-start.27
  688.7 8.2 %collective-permute-start.34 = (bf16[32,1664]{1,0:T(8,128)(2,1)S(1)}, bf16[32,1664]{1,0:T(8,128)(2,1)S(1)}, u32[]{:S(2)}, u32[]{:S(2)}) collective-permute-start(bf16[32,1664]{1,0:T(8,128)(2,1)S(1)} %get-tuple-element.105), channel_id=1, source_target_pairs={{0,16},{2,18},{4,20},{6,22},{8,24},{10,26},{12,28},{14,30},{16,0},... | collective-permute-start | bytes 319496 | tf_op jit(solution)/shard_map/ppermute | solution.py:682
  691.7 8.3 %collective-permute-start.28 = (bf16[64,1664]{1,0:T(8,128)(2,1)S(1)}, bf16[64,1664]{1,0:T(8,128)(2,1)S(1)}, u32[]{:S(2)}, u32[]{:S(2)}) collective-permute-start(bf16[64,1664]{1,0:T(8,128)(2,1)S(1)} %constant_dynamic-update-slice_fusion.33), channel_id=1, source_target_pairs={{0,8},{2,10},{4,12},{6,14},{8,0},{10,2},{12,4},{14,6},{16,24},{18,... | collective-permute-start | bytes 638984 | tf_op jit(solution)/shard_map/ppermute | solution.py:682
  696.9 5.1 collective-permute-start.35
  700.0 23.4 %collective-permute-start.29 = (bf16[128,1664]{1,0:T(8,128)(2,1)S(1)}, bf16[128,1664]{1,0:T(8,128)(2,1)}, u32[]{:S(2)}, u32[]{:S(2)}) collective-permute-start(bf16[128,1664]{1,0:T(8,128)(2,1)S(1)} %constant_dynamic-update-slice_fusion.31), channel_id=1, source_target_pairs={{0,4},{2,6},{4,0},{6,2},{8,12},{10,14},{12,8},{14,10},{16,20},{18,... | collective-permute-start | bytes 1277960 | tf_op jit(solution)/shard_map/ppermute | solution.py:682
  702.0 21.5 %collective-permute-start.36 = (bf16[128,1664]{1,0:T(8,128)(2,1)S(1)}, bf16[128,1664]{1,0:T(8,128)(2,1)}, u32[]{:S(2)}, u32[]{:S(2)}) collective-permute-start(bf16[128,1664]{1,0:T(8,128)(2,1)S(1)} %constant_dynamic-update-slice_fusion.26), channel_id=1, source_target_pairs={{0,8},{2,10},{4,12},{6,14},{8,0},{10,2},{12,4},{14,6},{16,24},{18,... | collective-permute-start | bytes 1277960 | tf_op jit(solution)/shard_map/ppermute | solution.py:682
  724.5 9.8 %collective-permute-start.47 = (bf16[256,1024]{1,0:T(8,128)(2,1)S(1)}, bf16[256,1024]{1,0:T(8,128)(2,1)S(1)}, u32[]{:S(2)}, u32[]{:S(2)}) collective-permute-start(bf16[256,1024]{1,0:T(8,128)(2,1)S(1)} %constant_dynamic-update-slice_fusion.13), channel_id=1, source_target_pairs={{0,8},{2,10},{4,12},{6,14},{8,0},{10,2},{12,4},{14,6},{16,24},{18,... | collective-permute-start | bytes 1572872 | tf_op jit(solution)/shard_map/ppermute | solution.py:682
  726.6 17.4 %collective-permute-start.44 = (bf16[256,1664]{1,0:T(8,128)(2,1)S(1)}, bf16[256,1664]{1,0:T(8,128)(2,1)S(1)}, u32[]{:S(2)}, u32[]{:S(2)}) collective-permute-start(bf16[256,1664]{1,0:T(8,128)(2,1)S(1)} %constant_dynamic-update-slice_fusion.21), channel_id=1, source_target_pairs={{0,2},{2,0},{4,6},{6,4},{8,10},{10,8},{12,14},{14,12},{16,18},{18,... | collective-permute-start | bytes 2555912 | tf_op jit(solution)/shard_map/ppermute | solution.py:682
  727.9 16.6 %collective-permute-start.45 = (bf16[256,1664]{1,0:T(8,128)(2,1)S(1)}, bf16[256,1664]{1,0:T(8,128)(2,1)S(1)}, u32[]{:S(2)}, u32[]{:S(2)}) collective-permute-start(bf16[256,1664]{1,0:T(8,128)(2,1)S(1)} %constant_dynamic-update-slice_fusion.17), channel_id=1, source_target_pairs={{0,4},{2,6},{4,0},{6,2},{8,12},{10,14},{12,8},{14,10},{16,20},{18,... | collective-permute-start | bytes 2555912 | tf_op jit(solution)/shard_map/ppermute | solution.py:682
  744.9 11.2 %collective-permute-start.46 = (f32[2,1024]{0,1:T(8,128)S(1)}, f32[2,1024]{0,1:T(8,128)S(1)}, u32[]{:S(2)}, u32[]{:S(2)}) collective-permute-start(f32[2,1024]{0,1:T(8,128)S(1)} %fusion.53), channel_id=1, source_target_pairs={{1,0},{0,1},{3,2},{2,3},{5,4},{4,5},{7,6},{6,7},{9,8},{8,9},{11,10... | collective-permute-start | bytes 24584 | tf_op jit(solution)/shard_map/ppermute | solution.py:644
  (52 other events, 968.9 us)
Sparse Core Ops, SparseCore 0:
  14.3 16.2 all-gather.3
  532.1 130.8 all-gather.5

commit v10 on v9

--- a/solution.py
+++ b/solution.py
@@ -228,7 +228,7 @@
 def gather_found(index_rows, table, queries, picks, scale):
     heads, rows, unused, width = table.shape
     tokens = queries.shape[0]
-    half = 256
+    half = 128
     blocks = tokens // (2 * half)
     steps = heads * blocks
     chunk = half * picks
@@ -314,7 +314,8 @@
         parts = [jnp.exp2(part - top) for part in parts]
         total = jnp.sum(functools.reduce(jnp.add, parts), 1, keepdims=True)
         read = sum(dot_rows(parts[j].astype(low_type), value_ref[at[j], :]) for j in range(count))
-        recalled = (early_ref, late_ref)[t % 2][pl.ds((t // 2) * tile, tile), :]
+        half = pl.ds(t * (tile // 2), tile // 2)
+        recalled = jnp.concatenate([early_ref[half, :], late_ref[half, :]], 0)
         mixed_ref[at[t], :] = (gate * recalled + ((1.0 - gate) / total) * read).astype(low_type)
 
 

time: 772 us -> 767 us (level)
    pallas_call x1, Pallas kernels: 33.5 us -> 21.4 us  [local_read(): pl.pallas_call(functools.partial(local_kernel, scale), grid=(heads, token...]
where the time goes in v10:
time: 767 us; the launch traced here: 758 us
  Pallas kernels  343 us (45%)
  matrix products  141 us (18%)
  waiting for transfers between devices  95.1 us (12%)
  starting transfers between devices  66.7 us (9%)
  local copies, waits for them, and re-layouts  54.8 us (7%)
  other arithmetic  42.2 us (6%)
  between operations  15.8 us (2%)
    pallas_call x1, Pallas kernels, gather_found(): pl.pallas_call(functools.partial(gather_kernel, picks, scale), grid=(step...  190 us
    pallas_call x3, Pallas kernels, back_heads(): pl.pallas_call(kernel, grid=(number, tokens // seq_len), in_specs=[smem,...  106 us
    ppermute x40, waiting for transfers between devices, swap_over(): lax.ppermute(rows, 'dp', [(i, i ^ 1 << bit) for i in range(lax.axis_size(...  91 us
    dot_general x6, matrix products, dot_rows(): return jnp.dot(left, right, preferred_element_type=full_type)  59.5 us
    ppermute x40, starting transfers between devices, swap_over(): lax.ppermute(rows, 'dp', [(i, i ^ 1 << bit) for i in range(lax.axis_size(...  48.2 us
    dot_general x6, matrix products, dot_inner(): lax.dot_general(left, right, (((1,), (1,)), ((), ())), preferred_element_...  42.3 us
    dot_general x5, matrix products, dot_outer(): lax.dot_general(left, right, (((0,), (0,)), ((), ())), preferred_element_...  37.9 us
    pallas_call x1, Pallas kernels, interleave(): pl.pallas_call(interleave_kernel, grid=(heads, rows // step), in_specs=[s...  26 us
  transfers between devices with their start and end apart: 50, of which 20 were waited for; matrix products, arithmetic and copies ran while one was open for 19% of the time, Pallas kernels for 17%

profile of v10, /device:TPU:1, one launch (start us, length us, event | category | flops | bytes accessed | tf_op | source)
XLA Modules:
  0.0 758.2 jit_solution(17353090779230098912)
XLA Ops:
  10.7 3.5 fusion.6
  14.4 2.7 copy.59
  17.1 4.2 reshape.188.index_hbm
  28.4 26.0 %interleave.1 = bf16[131072,128]{1,0:T(8,128)(2,1)} custom-call(bf16[4,16384,128]{2,1,0:T(8,128)(2,1)} %key_ref.1, bf16[4,16384,128]{2,1,0:T(8,128)(2,1)} %value_ref.1), custom_call_target="tpu_custom_call" | custom-call | flops 8589934592 | bytes 67108864 | tf_op jit(solution)/shard_map/interleave/pallas_call | solution.py:83
  54.4 11.3 %convolution_convert_fusion.now_ref.before_ref.query_ref.key_ref.value_ref.refs_3_.refs_4_.refs_5_ = bf16[2048,1536]{1,0:T(8,128)(2,1)} fusion(bf16[2048,1024]{1,0:T(8,128)(2,1)} %all-gather.4.cloned.1.call-done, bf16[1024,1536]{1,0:T(8,128)(2,1)} %copy-done.19), kind=kOutput, calls=%fused_computation.10 | convolution fusion | flops 6445596672 | bytes 13631488 | tf_op jit(solution)/shard_map/dot_general | solution.py:45
  65.7 189.5 %gather_found.1 = (bf16[262144,2,128]{2,1,0:T(2,128)(2,1)}, f32[4096,128]{1,0:T(8,128)}, f32[4096,128]{1,0:T(8,128)}) custom-call(s32[64,32,128]{2,1,0:T(8,128)} %reshape.188.index_hbm, bf16[65536,2,128]{2,1,0:T(2,128)(2,1)} %bitcast.56, bf16[2048,1536]{1,0:T(8,128)(2,1)} %convolution_convert_fusion.now_ref.before_ref.query_ref.key_ref.value_ref.refs_3_.refs_4_.refs_5_, ...), custom_call_target="tpu_custom_call" | custom-call | bytes 536870912 | tf_op jit(solution)/shard_map/gather_found/pallas_call | solution.py:243
  255.2 21.4 %local_read.1 = bf16[2048,512]{1,0:T(8,128)(2,1)} custom-call(f32[4]{0:T(128)} %add_divide_fusion.gate_ref, f32[4,2]{1,0:T(4,128)} %pad_maximum_fusion.7.far_ref, f32[4,1,1024]{2,1,0:T(1,128)} %broadcast_in_dim.33.column_ref, bf16[2048,1536]{1,0:T(8,128)(2,1)} %convolution_convert_fusion.now_ref.before_ref.query_ref.key_ref.value_ref.refs_3_.refs_4_.refs_5_, ...), custom_call_target="tpu_custom_call" | custom-call | bytes 167772160 | tf_op jit(solution)/shard_map/local_read/pallas_call | solution.py:334
  276.7 4.0 convolution_convert_fusion.3
  281.1 4.0 collective-permute-done
  285.1 3.5 multiply_reduce_fusion.3
  296.8 20.5 %add_convert_fusion = (bf16[2048,2048]{1,0:T(8,128)(2,1)}, bf16[2048,2048]{1,0:T(8,128)(2,1)}) fusion(bf16[1024,2048]{1,0:T(8,128)(2,1)S(1)} %copy-done.41, bf16[1024,1024]{1,0:T(8,128)(2,1)} %collective-permute-done.1, bf16[1024,1024]{1,0:T(8,128)(2,1)S(1)} %multiply_convert_fusion.2), kind=kOutput, calls=%fused_computation.1 | convolution fusion | flops 8673820672 | bytes 25165824 | tf_op jit(solution)/shard_map/dot_general | solution.py:45
  317.3 11.7 %convolution_convert_fusion.1 = bf16[2048,1024]{1,0:T(8,128)(2,1)S(1)} fusion(bf16[2048,2048]{1,0:T(8,128)(2,1)} %get-tuple-element.109, bf16[2048,1024]{1,0:T(8,128)(2,1)S(1)} %constant_dynamic-update-slice_fusion.3), kind=kOutput, calls=%fused_computation.45 | convolution fusion | flops 8592031744 | bytes 16777216 | tf_op jit(solution)/shard_map/dot_general | solution.py:49
  329.4 14.1 %multiply_convert_fusion = bf16[2048,2048]{1,0:T(8,128)(2,1)} fusion(bf16[2048,2048]{1,0:T(8,128)(2,1)} %get-tuple-element.108, bf16[2048,1024]{1,0:T(8,128)(2,1)S(1)} %constant_dynamic-update-slice_fusion.3, bf16[2048,1024]{1,0:T(8,128)(2,1)} %param.30), kind=kOutput, calls=%fused_computation | convolution fusion | flops 8602517504 | bytes 25165824 | tf_op jit(solution)/shard_map/dot_general | solution.py:55
  343.6 7.1 fusion.28
  350.7 7.4 fusion.34
  360.1 7.5 fusion.31
  368.9 2.7 collective-permute-start.6
  372.8 8.1 %fusion.25 = bf16[1024,1024]{1,0:T(8,128)(2,1)} fusion(bf16[2048,1024]{1,0:T(8,128)(2,1)S(1)} %copy-done.42, bf16[2048,2048]{1,0:T(8,128)(2,1)} %get-tuple-element.109), kind=kOutput, calls=%fused_computation.56 | convolution fusion | flops 4296015872 | bytes 10485760 | tf_op jit(solution)/shard_map/dot_general | solution.py:45
  382.0 13.1 %collective-permute-done.6 = bf16[512,1024]{1,0:T(8,128)(2,1)S(1)} collective-permute-done((bf16[512,1024]{1,0:T(8,128)(2,1)S(1)}, bf16[512,1024]{1,0:T(8,128)(2,1)S(1)}, u32[]{:S(2)}, u32[]{:S(2)}) %collective-permute-start.6) | collective-permute-done | bytes 1048608 | tf_op jit(solution)/shard_map/ppermute | solution.py:683
  399.3 9.9 %multiply_reduce_fusion.1 = (bf16[1024]{0:T(1024)(128)(2,1)S(1)}, f32[1024]{0:T(1024)S(1)}, f32[1024,1024]{1,0:T(8,128)}) fusion(f32[1024,1024]{1,0:T(8,128)S(1)} %copy-done.7, f32[1024]{0:T(1024)S(1)} %fusion.88, bf16[1024,1024]{1,0:T(8,128)(2,1)S(1)} %collective-permute-done.4, f32[1024]{0:T(1024)S(1)} %copy-done.35, ...), kind=kOutput, calls=%fused_computation.38 | convolution fusion | flops 4303353856 | bytes 18888704 | tf_op jit(solution)/shard_map/dot_general | solution.py:55
  409.2 12.2 %fusion.97 = (bf16[1024,1024]{1,0:T(8,128)(2,1)}, f32[1024,1024]{1,0:T(8,128)}, bf16[1024,1024]{1,0:T(8,128)(2,1)}) fusion(f32[1024,1024]{1,0:T(8,128)S(1)} %copy-done.7, f32[1024]{0:T(1024)S(1)} %multiply_multiply_fusion.1, f32[1024]{0:T(1024)S(1)} %fusion.88, f32[1024]{0:T(1024)S(1)} %copy-done.35, f32[1024,1024]{1,0:T(8,128)} %get-tuple-element.165, ...), kind=kOutput, calls=%fused_computation.264 | convolution fusion | flops 4309647360 | bytes 31469568 | tf_op jit(solution)/shard_map/dot_general | solution.py:45
  432.3 7.1 collective-permute-done.9
  447.3 3.7 convolution_convert_fusion.2.refs_8_
  460.3 27.8 %back_heads.3 = (bf16[2048,512]{1,0:T(8,128)(2,1)}, bf16[2048,512]{1,0:T(8,128)(2,1)}, bf16[2048,512]{1,0:T(8,128)(2,1)}, f32[1,8,1024]{2,1,0:T(8,128)}, f32[1,3...) custom-call(f32[1]{0:T(128)} %get-tuple-element.161.refs_0_, ...), custom_call_target="tpu_custom_call", output_to_operand_aliasing={{5}: (10, {}), {6}: (11, {})} | custom-call | bytes 67108864 | tf_op jit(solution)/shard_map/back_heads/pallas_call | solution.py:579
  494.9 27.8 %back_heads.4 = (bf16[2048,512]{1,0:T(8,128)(2,1)}, bf16[2048,512]{1,0:T(8,128)(2,1)}, bf16[2048,512]{1,0:T(8,128)(2,1)}, f32[1,8,1024]{2,1,0:T(8,128)}, f32[1,3...) custom-call(f32[1]{0:T(128)} %get-tuple-element.162.refs_0_, ...), custom_call_target="tpu_custom_call", output_to_operand_aliasing={{0}: (10, {}), {1}: (11, {}), {2}: (12, {}), {5}: (13, {}),... | custom-call | bytes 67108864 | tf_op jit(solution)/shard_map/back_heads/pallas_call | solution.py:579
  526.2 50.3 %back_heads.5 = (bf16[2048,512]{1,0:T(8,128)(2,1)}, bf16[2048,512]{1,0:T(8,128)(2,1)}, bf16[2048,512]{1,0:T(8,128)(2,1)}, f32[2,8,1024]{2,1,0:T(8,128)}, f32[2,32,256]{2,1,0:T(8,128)}) custom-call(f32[2]{0:T(128)} %slice.150.refs_0_, f32[2,2]{1,0:T(2,128)} %slice.151.refs_1_, ...), custom_call_target="tpu_custom_call", output_to_operand_aliasing={{0}: (10, {}), {1}: (11, {}), {2}: (12, {})} | custom-call | bytes 134217728 | tf_op jit(solution)/shard_map/back_heads/pallas_call | solution.py:579
  582.2 9.0 %fusion.100 = (bf16[1024,1536]{1,0:T(8,128)(2,1)}, f32[1024]{0:T(1024)S(1)}) fusion(bf16[1024,1536]{1,0:T(8,128)(2,1)S(1)} %copy-done.20, bf16[2048,1024]{1,0:T(8,128)(2,1)S(1)} %copy-done.44, bf16[2048,1536]{1,0:T(8,128)(2,1)S(1)} %constant_dynamic-update-slice_fusion.5), kind=kOutput, calls=%fused_computation.266 | convolution fusion | flops 6448741376 | bytes 16781312 | tf_op jit(solution)/shard_map/dot_general | solution.py:49
  595.7 9.5 %collective-permute-done.38 = bf16[128,1024]{1,0:T(8,128)(2,1)S(1)} collective-permute-done((bf16[128,1024]{1,0:T(8,128)(2,1)S(1)}, bf16[128,1024]{1,0:T(8,128)(2,1)S(1)}, u32[]{:S(2)}, u32[]{:S(2)}) %collective-permute-start.38) | collective-permute-done | bytes 262176 | tf_op jit(solution)/shard_map/ppermute | solution.py:683
  607.2 5.3 collective-permute-done.39
  615.6 3.1 collective-permute-done.40
  620.5 3.7 fusion.37
  626.2 9.8 %collective-permute-start.22 = (bf16[1024,1024]{1,0:T(8,128)(2,1)S(1)}, bf16[1024,1024]{1,0:T(8,128)(2,1)S(1)}, u32[]{:S(2)}, u32[]{:S(2)}) collective-permute-start(bf16[1024,1024]{1,0:T(8,128)(2,1)S(1)} %fusion.37), channel_id=1, source_target_pairs={{0,1},{1,0},{2,3},{3,2},{4,5},{5,4},{6,7},{7,6},{8,9},{9,8},{10,11... | collective-permute-start | bytes 6291464 | tf_op jit(solution)/shard_map/ppermute | solution.py:668
  636.7 9.0 %collective-permute-done.23 = bf16[256,1664]{1,0:T(8,128)(2,1)S(1)} collective-permute-done((bf16[256,1664]{1,0:T(8,128)(2,1)S(1)}, bf16[256,1664]{1,0:T(8,128)(2,1)S(1)}, u32[]{:S(2)}, u32[]{:S(2)}) %collective-permute-start.23) | collective-permute-done | bytes 852000 | tf_op jit(solution)/shard_map/ppermute | solution.py:683
  649.0 4.4 collective-permute-done.24
  653.6 5.0 collective-permute-start.25
  658.6 5.9 collective-permute-done.31
  664.7 4.3 collective-permute-done.25
  669.1 3.6 collective-permute-start.26
  673.3 6.9 collective-permute-done.26
  685.1 4.2 collective-permute-start.28
  691.1 2.9 collective-permute-done.28
  696.5 3.7 fusion.7
  700.2 2.8 fusion.3
  703.0 4.2 fusion.99
  708.1 4.5 maximum_convert_fusion.1
  712.6 4.4 maximum_convert_fusion
  728.1 8.4 %collective-permute-done.44 = bf16[256,1664]{1,0:T(8,128)(2,1)S(1)} collective-permute-done((bf16[256,1664]{1,0:T(8,128)(2,1)S(1)}, bf16[256,1664]{1,0:T(8,128)(2,1)S(1)}, u32[]{:S(2)}, u32[]{:S(2)}) %collective-permute-start.44) | collective-permute-done | bytes 852000 | tf_op jit(solution)/shard_map/ppermute | solution.py:683
  738.5 5.4 collective-permute-start.46
  (350 shorter events, 121.6 us)
Async XLA Ops:
  7.2 47.2 %all-gather.4.cloned.1.call-start = ((), (), s32[]{:S(2)}) async-start(), calls=%async_computation | async-start | bytes 6291456 | tf_op jit(solution)/shard_map/all_gather | solution.py:788
  14.1 688.8 %all-gather.6.cloned.1.call-start = ((), (), s32[]{:S(2)}) async-start(), calls=%async_computation.1 | async-start | bytes 8912896 | tf_op jit(solution)/shard_map/all_gather | solution.py:740
  280.6 14.4 %collective-permute-start.3 = (bf16[1024,1024]{1,0:T(8,128)(2,1)}, bf16[1024,1024]{1,0:T(8,128)(2,1)}, u32[]{:S(2)}, u32[]{:S(2)}) collective-permute-start(bf16[1024,1024]{1,0:T(8,128)(2,1)} %param.31), channel_id=1, source_target_pairs={{1,0},{0,1},{3,2},{2,3},{5,4},{4,5},{7,6},{6,7},{9,8},{8,9},{11,10... | collective-permute-start | bytes 6291464 | tf_op jit(solution)/shard_map/ppermute | solution.py:645
  291.1 5.8 collective-permute-start.1
  359.5 39.8 %collective-permute-start.4 = (bf16[1024,1024]{1,0:T(8,128)(2,1)S(1)}, bf16[1024,1024]{1,0:T(8,128)(2,1)S(1)}, u32[]{:S(2)}, u32[]{:S(2)}) collective-permute-start(bf16[1024,1024]{1,0:T(8,128)(2,1)S(1)} %fusion.28), channel_id=1, source_target_pairs={{0,1},{1,0},{2,3},{3,2},{4,5},{5,4},{6,7},{7,6},{8,9},{9,8},{10,11... | collective-permute-start | bytes 6291464 | tf_op jit(solution)/shard_map/ppermute | solution.py:668
  368.9 26.1 %collective-permute-start.6 = (bf16[512,1024]{1,0:T(8,128)(2,1)S(1)}, bf16[512,1024]{1,0:T(8,128)(2,1)S(1)}, u32[]{:S(2)}, u32[]{:S(2)}) collective-permute-start(bf16[512,1024]{1,0:T(8,128)(2,1)S(1)} %get-tuple-element.123), channel_id=1, source_target_pairs={{0,8},{2,10},{4,12},{6,14},{8,0},{10,2},{12,4},{14,6},{16,24},{18,... | collective-permute-start | bytes 3145736 | tf_op jit(solution)/shard_map/ppermute | solution.py:683
  371.6 26.1 %collective-permute-start.5 = (bf16[512,1024]{1,0:T(8,128)(2,1)S(1)}, bf16[512,1024]{1,0:T(8,128)(2,1)S(1)}, u32[]{:S(2)}, u32[]{:S(2)}) collective-permute-start(bf16[512,1024]{1,0:T(8,128)(2,1)S(1)} %get-tuple-element.125), channel_id=1, source_target_pairs={{0,4},{2,6},{4,0},{6,2},{8,12},{10,14},{12,8},{14,10},{16,20},{18,... | collective-permute-start | bytes 3145736 | tf_op jit(solution)/shard_map/ppermute | solution.py:683
  380.9 28.3 %collective-permute-start.2 = (bf16[1024,1024]{1,0:T(8,128)(2,1)}, bf16[1024,1024]{1,0:T(8,128)(2,1)S(1)}, u32[]{:S(2)}, u32[]{:S(2)}) collective-permute-start(bf16[1024,1024]{1,0:T(8,128)(2,1)} %fusion.25), channel_id=1, source_target_pairs={{0,1},{1,0},{2,3},{3,2},{4,5},{5,4},{6,7},{7,6},{8,9},{9,8},{10,11... | collective-permute-start | bytes 6291464 | tf_op jit(solution)/shard_map/ppermute | solution.py:668
  381.7 45.5 %collective-permute-start.8 = (bf16[512,1024]{1,0:T(8,128)(2,1)}, bf16[512,1024]{1,0:T(8,128)(2,1)}, u32[]{:S(2)}, u32[]{:S(2)}) collective-permute-start(bf16[512,1024]{1,0:T(8,128)(2,1)} %get-tuple-element.121), channel_id=1, source_target_pairs={{0,4},{2,6},{4,0},{6,2},{8,12},{10,14},{12,8},{14,10},{16,20},{18,... | collective-permute-start | bytes 3145736 | tf_op jit(solution)/shard_map/ppermute | solution.py:683
  395.1 34.1 %collective-permute-start.7 = (bf16[512,1024]{1,0:T(8,128)(2,1)}, bf16[512,1024]{1,0:T(8,128)(2,1)}, u32[]{:S(2)}, u32[]{:S(2)}) collective-permute-start(bf16[512,1024]{1,0:T(8,128)(2,1)} %get-tuple-element.128), channel_id=1, source_target_pairs={{0,2},{2,0},{4,6},{6,4},{8,10},{10,8},{12,14},{14,12},{16,18},{18,... | collective-permute-start | bytes 3145736 | tf_op jit(solution)/shard_map/ppermute | solution.py:683
  421.4 24.0 %collective-permute-start.11 = (bf16[1024,1024]{1,0:T(8,128)(2,1)}, bf16[1024,1024]{1,0:T(8,128)(2,1)}, u32[]{:S(2)}, u32[]{:S(2)}) collective-permute-start(bf16[1024,1024]{1,0:T(8,128)(2,1)} %get-tuple-element.63), channel_id=1, source_target_pairs={{1,0},{0,1},{3,2},{2,3},{5,4},{4,5},{7,6},{6,7},{9,8},{8,9},{11,10... | collective-permute-start | bytes 6291464 | tf_op jit(solution)/shard_map/ppermute | solution.py:645
  425.6 15.2 %collective-permute-start.10 = (bf16[256,1024]{1,0:T(8,128)(2,1)}, bf16[256,1024]{1,0:T(8,128)(2,1)S(1)}, u32[]{:S(2)}, u32[]{:S(2)}) collective-permute-start(bf16[256,1024]{1,0:T(8,128)(2,1)} %get-tuple-element.139), channel_id=1, source_target_pairs={{0,2},{2,0},{4,6},{6,4},{8,10},{10,8},{12,14},{14,12},{16,18},{18,... | collective-permute-start | bytes 1572872 | tf_op jit(solution)/shard_map/ppermute | solution.py:683
  425.9 13.4 %collective-permute-start.9 = (bf16[256,1024]{1,0:T(8,128)(2,1)}, bf16[256,1024]{1,0:T(8,128)(2,1)S(1)}, u32[]{:S(2)}, u32[]{:S(2)}) collective-permute-start(bf16[256,1024]{1,0:T(8,128)(2,1)} %get-tuple-element.141), channel_id=1, source_target_pairs={{0,8},{2,10},{4,12},{6,14},{8,0},{10,2},{12,4},{14,6},{16,24},{18,... | collective-permute-start | bytes 1572872 | tf_op jit(solution)/shard_map/ppermute | solution.py:683
  428.9 22.1 %collective-permute-start.13 = (bf16[256,1024]{1,0:T(8,128)(2,1)S(1)}, bf16[256,1024]{1,0:T(8,128)(2,1)S(1)}, u32[]{:S(2)}, u32[]{:S(2)}) collective-permute-start(bf16[256,1024]{1,0:T(8,128)(2,1)S(1)} %get-tuple-element.135), channel_id=1, source_target_pairs={{0,8},{2,10},{4,12},{6,14},{8,0},{10,2},{12,4},{14,6},{16,24},{18,... | collective-permute-start | bytes 1572872 | tf_op jit(solution)/shard_map/ppermute | solution.py:683
  430.9 24.2 %collective-permute-start.12 = (bf16[256,1024]{1,0:T(8,128)(2,1)S(1)}, bf16[256,1024]{1,0:T(8,128)(2,1)S(1)}, u32[]{:S(2)}, u32[]{:S(2)}) collective-permute-start(bf16[256,1024]{1,0:T(8,128)(2,1)S(1)} %get-tuple-element.137), channel_id=1, source_target_pairs={{0,4},{2,6},{4,0},{6,2},{8,12},{10,14},{12,8},{14,10},{16,20},{18,... | collective-permute-start | bytes 1572872 | tf_op jit(solution)/shard_map/ppermute | solution.py:683
  439.6 17.8 %collective-permute-start.18 = (bf16[128,1024]{1,0:T(8,128)(2,1)S(1)}, bf16[128,1024]{1,0:T(8,128)(2,1)S(1)}, u32[]{:S(2)}, u32[]{:S(2)}) collective-permute-start(bf16[128,1024]{1,0:T(8,128)(2,1)S(1)} %get-tuple-element.143), channel_id=1, source_target_pairs={{0,2},{2,0},{4,6},{6,4},{8,10},{10,8},{12,14},{14,12},{16,18},{18,... | collective-permute-start | bytes 786440 | tf_op jit(solution)/shard_map/ppermute | solution.py:683
  441.1 18.7 %collective-permute-start.20 = (bf16[128,1024]{1,0:T(8,128)(2,1)S(1)}, bf16[128,1024]{1,0:T(8,128)(2,1)S(1)}, u32[]{:S(2)}, u32[]{:S(2)}) collective-permute-start(bf16[128,1024]{1,0:T(8,128)(2,1)S(1)} %get-tuple-element.145), channel_id=1, source_target_pairs={{0,4},{2,6},{4,0},{6,2},{8,12},{10,14},{12,8},{14,10},{16,20},{18,... | collective-permute-start | bytes 786440 | tf_op jit(solution)/shard_map/ppermute | solution.py:683
  452.0 41.1 %collective-permute-start.15 = (bf16[128,1024]{1,0:T(8,128)(2,1)S(1)}, bf16[128,1024]{1,0:T(8,128)(2,1)S(1)}, u32[]{:S(2)}, u32[]{:S(2)}) collective-permute-start(bf16[128,1024]{1,0:T(8,128)(2,1)S(1)} %get-tuple-element.147), channel_id=1, source_target_pairs={{0,2},{2,0},{4,6},{6,4},{8,10},{10,8},{12,14},{14,12},{16,18},{18,... | collective-permute-start | bytes 786440 | tf_op jit(solution)/shard_map/ppermute | solution.py:683
  456.0 33.0 %collective-permute-start.14 = (bf16[128,1024]{1,0:T(8,128)(2,1)S(1)}, bf16[128,1024]{1,0:T(8,128)(2,1)}, u32[]{:S(2)}, u32[]{:S(2)}) collective-permute-start(bf16[128,1024]{1,0:T(8,128)(2,1)S(1)} %get-tuple-element.149), channel_id=1, source_target_pairs={{0,8},{2,10},{4,12},{6,14},{8,0},{10,2},{12,4},{14,6},{16,24},{18,... | collective-permute-start | bytes 786440 | tf_op jit(solution)/shard_map/ppermute | solution.py:683
  457.5 31.4 %collective-permute-start.19 = (bf16[64,1024]{1,0:T(8,128)(2,1)S(1)}, bf16[64,1024]{1,0:T(8,128)(2,1)S(1)}, u32[]{:S(2)}, u32[]{:S(2)}) collective-permute-start(bf16[64,1024]{1,0:T(8,128)(2,1)S(1)} %constant_dynamic-slice_fusion.14), channel_id=1, source_target_pairs={{0,16},{2,18},{4,20},{6,22},{8,24},{10,26},{12,28},{14,30},{16,0},... | collective-permute-start | bytes 393224 | tf_op jit(solution)/shard_map/ppermute | solution.py:683
  459.9 29.0 %collective-permute-start.21 = (bf16[64,1024]{1,0:T(8,128)(2,1)S(1)}, bf16[64,1024]{1,0:T(8,128)(2,1)S(1)}, u32[]{:S(2)}, u32[]{:S(2)}) collective-permute-start(bf16[64,1024]{1,0:T(8,128)(2,1)S(1)} %constant_dynamic-slice_fusion.12), channel_id=1, source_target_pairs={{0,16},{2,18},{4,20},{6,22},{8,24},{10,26},{12,28},{14,30},{16,0},... | collective-permute-start | bytes 393224 | tf_op jit(solution)/shard_map/ppermute | solution.py:683
  460.1 132.3 %collective-permute-start.37 = (bf16[256,1024]{1,0:T(8,128)(2,1)S(1)}, bf16[256,1024]{1,0:T(8,128)(2,1)S(1)}, u32[]{:S(2)}, u32[]{:S(2)}) collective-permute-start(bf16[256,1024]{1,0:T(8,128)(2,1)S(1)} %constant_dynamic-slice_fusion.3), channel_id=1, source_target_pairs={{0,8},{2,10},{4,12},{6,14},{8,0},{10,2},{12,4},{14,6},{16,24},{18,... | collective-permute-start | bytes 1572872 | tf_op jit(solution)/shard_map/ppermute | solution.py:683
  490.8 32.7 %collective-permute-start.16 = (bf16[64,1024]{1,0:T(8,128)(2,1)S(1)}, bf16[64,1024]{1,0:T(8,128)(2,1)S(1)}, u32[]{:S(2)}, u32[]{:S(2)}) collective-permute-start(bf16[64,1024]{1,0:T(8,128)(2,1)S(1)} %get-tuple-element.151), channel_id=1, source_target_pairs={{0,16},{2,18},{4,20},{6,22},{8,24},{10,26},{12,28},{14,30},{16,0},... | collective-permute-start | bytes 393224 | tf_op jit(solution)/shard_map/ppermute | solution.py:683
  494.8 29.6 %collective-permute-start.17 = (bf16[64,1024]{1,0:T(8,128)(2,1)S(1)}, bf16[64,1024]{1,0:T(8,128)(2,1)S(1)}, u32[]{:S(2)}, u32[]{:S(2)}) collective-permute-start(bf16[64,1024]{1,0:T(8,128)(2,1)S(1)} %get-tuple-element.153), channel_id=1, source_target_pairs={{0,16},{2,18},{4,20},{6,22},{8,24},{10,26},{12,28},{14,30},{16,0},... | collective-permute-start | bytes 393224 | tf_op jit(solution)/shard_map/ppermute | solution.py:683
  592.7 12.6 %collective-permute-start.38 = (bf16[128,1024]{1,0:T(8,128)(2,1)S(1)}, bf16[128,1024]{1,0:T(8,128)(2,1)S(1)}, u32[]{:S(2)}, u32[]{:S(2)}) collective-permute-start(bf16[128,1024]{1,0:T(8,128)(2,1)S(1)} %constant_dynamic-slice_fusion.2), channel_id=1, source_target_pairs={{0,2},{2,0},{4,6},{6,4},{8,10},{10,8},{12,14},{14,12},{16,18},{18,... | collective-permute-start | bytes 786440 | tf_op jit(solution)/shard_map/ppermute | solution.py:683
  605.3 7.2 collective-permute-start.39
  612.6 6.1 collective-permute-start.40
  615.1 30.6 %collective-permute-start.23 = (bf16[256,1664]{1,0:T(8,128)(2,1)S(1)}, bf16[256,1664]{1,0:T(8,128)(2,1)S(1)}, u32[]{:S(2)}, u32[]{:S(2)}) collective-permute-start(bf16[256,1664]{1,0:T(8,128)(2,1)S(1)} %constant_dynamic-slice_fusion.11), channel_id=1, source_target_pairs={{0,2},{2,0},{4,6},{6,4},{8,10},{10,8},{12,14},{14,12},{16,18},{18,... | collective-permute-start | bytes 2555912 | tf_op jit(solution)/shard_map/ppermute | solution.py:683
  618.7 5.8 collective-permute-start.41
  624.5 11.5 %collective-permute-start.42 = (bf16[64,1024]{1,0:T(8,128)(2,1)S(1)}, bf16[64,1024]{1,0:T(8,128)(2,1)S(1)}, u32[]{:S(2)}, u32[]{:S(2)}) collective-permute-start(bf16[64,1024]{1,0:T(8,128)(2,1)S(1)} %constant_dynamic-update-slice_fusion.24), channel_id=1, source_target_pairs={{0,4},{2,6},{4,0},{6,2},{8,12},{10,14},{12,8},{14,10},{16,20},{18,... | collective-permute-start | bytes 393224 | tf_op jit(solution)/shard_map/ppermute | solution.py:683
  626.0 21.5 %collective-permute-start.30 = (bf16[256,1664]{1,0:T(8,128)(2,1)S(1)}, bf16[256,1664]{1,0:T(8,128)(2,1)S(1)}, u32[]{:S(2)}, u32[]{:S(2)}) collective-permute-start(bf16[256,1664]{1,0:T(8,128)(2,1)S(1)} %constant_dynamic-slice_fusion.7), channel_id=1, source_target_pairs={{0,4},{2,6},{4,0},{6,2},{8,12},{10,14},{12,8},{14,10},{16,20},{18,... | collective-permute-start | bytes 2555912 | tf_op jit(solution)/shard_map/ppermute | solution.py:683
  626.2 70.2 %collective-permute-start.22 = (bf16[1024,1024]{1,0:T(8,128)(2,1)S(1)}, bf16[1024,1024]{1,0:T(8,128)(2,1)S(1)}, u32[]{:S(2)}, u32[]{:S(2)}) collective-permute-start(bf16[1024,1024]{1,0:T(8,128)(2,1)S(1)} %fusion.37), channel_id=1, source_target_pairs={{0,1},{1,0},{2,3},{3,2},{4,5},{5,4},{6,7},{7,6},{8,9},{9,8},{10,11... | collective-permute-start | bytes 6291464 | tf_op jit(solution)/shard_map/ppermute | solution.py:668
  636.0 81.0 %collective-permute-start.43 = (bf16[128,1024]{1,0:T(8,128)(2,1)S(1)}, bf16[128,1024]{1,0:T(8,128)(2,1)}, u32[]{:S(2)}, u32[]{:S(2)}) collective-permute-start(bf16[128,1024]{1,0:T(8,128)(2,1)S(1)} %constant_dynamic-update-slice_fusion.22), channel_id=1, source_target_pairs={{0,2},{2,0},{4,6},{6,4},{8,10},{10,8},{12,14},{14,12},{16,18},{18,... | collective-permute-start | bytes 786440 | tf_op jit(solution)/shard_map/ppermute | solution.py:683
  646.0 7.5 collective-permute-start.24
  647.8 16.6 %collective-permute-start.31 = (bf16[128,1664]{1,0:T(8,128)(2,1)S(1)}, bf16[128,1664]{1,0:T(8,128)(2,1)S(1)}, u32[]{:S(2)}, u32[]{:S(2)}) collective-permute-start(bf16[128,1664]{1,0:T(8,128)(2,1)S(1)} %constant_dynamic-slice_fusion.6), channel_id=1, source_target_pairs={{0,8},{2,10},{4,12},{6,14},{8,0},{10,2},{12,4},{14,6},{16,24},{18,... | collective-permute-start | bytes 1277960 | tf_op jit(solution)/shard_map/ppermute | solution.py:683
  653.6 15.4 %collective-permute-start.25 = (bf16[64,1664]{1,0:T(8,128)(2,1)S(1)}, bf16[64,1664]{1,0:T(8,128)(2,1)S(1)}, u32[]{:S(2)}, u32[]{:S(2)}) collective-permute-start(bf16[64,1664]{1,0:T(8,128)(2,1)S(1)} %constant_dynamic-slice_fusion.9), channel_id=1, source_target_pairs={{0,8},{2,10},{4,12},{6,14},{8,0},{10,2},{12,4},{14,6},{16,24},{18,... | collective-permute-start | bytes 638984 | tf_op jit(solution)/shard_map/ppermute | solution.py:683
  664.6 8.1 %collective-permute-start.32 = (bf16[64,1664]{1,0:T(8,128)(2,1)S(1)}, bf16[64,1664]{1,0:T(8,128)(2,1)S(1)}, u32[]{:S(2)}, u32[]{:S(2)}) collective-permute-start(bf16[64,1664]{1,0:T(8,128)(2,1)S(1)} %constant_dynamic-slice_fusion.5), channel_id=1, source_target_pairs={{0,2},{2,0},{4,6},{6,4},{8,10},{10,8},{12,14},{14,12},{16,18},{18,... | collective-permute-start | bytes 638984 | tf_op jit(solution)/shard_map/ppermute | solution.py:683
  669.1 11.2 %collective-permute-start.26 = (bf16[32,1664]{1,0:T(8,128)(2,1)S(1)}, bf16[32,1664]{1,0:T(8,128)(2,1)S(1)}, u32[]{:S(2)}, u32[]{:S(2)}) collective-permute-start(bf16[32,1664]{1,0:T(8,128)(2,1)S(1)} %constant_dynamic-slice_fusion.8), channel_id=1, source_target_pairs={{0,16},{2,18},{4,20},{6,22},{8,24},{10,26},{12,28},{14,30},{16,0},... | collective-permute-start | bytes 319496 | tf_op jit(solution)/shard_map/ppermute | solution.py:683
  672.8 9.7 %collective-permute-start.33 = (bf16[32,1664]{1,0:T(8,128)(2,1)S(1)}, bf16[32,1664]{1,0:T(8,128)(2,1)S(1)}, u32[]{:S(2)}, u32[]{:S(2)}) collective-permute-start(bf16[32,1664]{1,0:T(8,128)(2,1)S(1)} %constant_dynamic-slice_fusion.4), channel_id=1, source_target_pairs={{0,16},{2,18},{4,20},{6,22},{8,24},{10,26},{12,28},{14,30},{16,0},... | collective-permute-start | bytes 319496 | tf_op jit(solution)/shard_map/ppermute | solution.py:683
  682.6 8.2 %collective-permute-start.34 = (bf16[32,1664]{1,0:T(8,128)(2,1)S(1)}, bf16[32,1664]{1,0:T(8,128)(2,1)S(1)}, u32[]{:S(2)}, u32[]{:S(2)}) collective-permute-start(bf16[32,1664]{1,0:T(8,128)(2,1)S(1)} %get-tuple-element.105), channel_id=1, source_target_pairs={{0,16},{2,18},{4,20},{6,22},{8,24},{10,26},{12,28},{14,30},{16,0},... | collective-permute-start | bytes 319496 | tf_op jit(solution)/shard_map/ppermute | solution.py:683
  685.1 8.9 %collective-permute-start.28 = (bf16[64,1664]{1,0:T(8,128)(2,1)S(1)}, bf16[64,1664]{1,0:T(8,128)(2,1)S(1)}, u32[]{:S(2)}, u32[]{:S(2)}) collective-permute-start(bf16[64,1664]{1,0:T(8,128)(2,1)S(1)} %constant_dynamic-update-slice_fusion.33), channel_id=1, source_target_pairs={{0,8},{2,10},{4,12},{6,14},{8,0},{10,2},{12,4},{14,6},{16,24},{18,... | collective-permute-start | bytes 638984 | tf_op jit(solution)/shard_map/ppermute | solution.py:683
  690.8 5.1 collective-permute-start.35
  694.0 23.0 %collective-permute-start.29 = (bf16[128,1664]{1,0:T(8,128)(2,1)S(1)}, bf16[128,1664]{1,0:T(8,128)(2,1)}, u32[]{:S(2)}, u32[]{:S(2)}) collective-permute-start(bf16[128,1664]{1,0:T(8,128)(2,1)S(1)} %constant_dynamic-update-slice_fusion.31), channel_id=1, source_target_pairs={{0,4},{2,6},{4,0},{6,2},{8,12},{10,14},{12,8},{14,10},{16,20},{18,... | collective-permute-start | bytes 1277960 | tf_op jit(solution)/shard_map/ppermute | solution.py:683
  696.0 21.0 %collective-permute-start.36 = (bf16[128,1664]{1,0:T(8,128)(2,1)S(1)}, bf16[128,1664]{1,0:T(8,128)(2,1)}, u32[]{:S(2)}, u32[]{:S(2)}) collective-permute-start(bf16[128,1664]{1,0:T(8,128)(2,1)S(1)} %constant_dynamic-update-slice_fusion.26), channel_id=1, source_target_pairs={{0,8},{2,10},{4,12},{6,14},{8,0},{10,2},{12,4},{14,6},{16,24},{18,... | collective-permute-start | bytes 1277960 | tf_op jit(solution)/shard_map/ppermute | solution.py:683
  718.0 8.5 %collective-permute-start.47 = (bf16[256,1024]{1,0:T(8,128)(2,1)S(1)}, bf16[256,1024]{1,0:T(8,128)(2,1)S(1)}, u32[]{:S(2)}, u32[]{:S(2)}) collective-permute-start(bf16[256,1024]{1,0:T(8,128)(2,1)S(1)} %constant_dynamic-update-slice_fusion.13), channel_id=1, source_target_pairs={{0,8},{2,10},{4,12},{6,14},{8,0},{10,2},{12,4},{14,6},{16,24},{18,... | collective-permute-start | bytes 1572872 | tf_op jit(solution)/shard_map/ppermute | solution.py:683
  720.5 16.0 %collective-permute-start.44 = (bf16[256,1664]{1,0:T(8,128)(2,1)S(1)}, bf16[256,1664]{1,0:T(8,128)(2,1)S(1)}, u32[]{:S(2)}, u32[]{:S(2)}) collective-permute-start(bf16[256,1664]{1,0:T(8,128)(2,1)S(1)} %constant_dynamic-update-slice_fusion.21), channel_id=1, source_target_pairs={{0,2},{2,0},{4,6},{6,4},{8,10},{10,8},{12,14},{14,12},{16,18},{18,... | collective-permute-start | bytes 2555912 | tf_op jit(solution)/shard_map/ppermute | solution.py:683
  721.8 16.2 %collective-permute-start.45 = (bf16[256,1664]{1,0:T(8,128)(2,1)S(1)}, bf16[256,1664]{1,0:T(8,128)(2,1)S(1)}, u32[]{:S(2)}, u32[]{:S(2)}) collective-permute-start(bf16[256,1664]{1,0:T(8,128)(2,1)S(1)} %constant_dynamic-update-slice_fusion.17), channel_id=1, source_target_pairs={{0,4},{2,6},{4,0},{6,2},{8,12},{10,14},{12,8},{14,10},{16,20},{18,... | collective-permute-start | bytes 2555912 | tf_op jit(solution)/shard_map/ppermute | solution.py:683
  738.5 11.5 %collective-permute-start.46 = (f32[2,1024]{0,1:T(8,128)S(1)}, f32[2,1024]{0,1:T(8,128)S(1)}, u32[]{:S(2)}, u32[]{:S(2)}) collective-permute-start(f32[2,1024]{0,1:T(8,128)S(1)} %fusion.53), channel_id=1, source_target_pairs={{1,0},{0,1},{3,2},{2,3},{5,4},{4,5},{7,6},{6,7},{9,8},{8,9},{11,10... | collective-permute-start | bytes 24584 | tf_op jit(solution)/shard_map/ppermute | solution.py:645
  (52 other events, 956.9 us)
Sparse Core Ops, SparseCore 0:
  14.3 16.2 all-gather.3
  526.3 130.5 all-gather.5
